TPU v7x, 512 devices: a whole 4x4x16 slice. The times are simulated.
512 devices in a mesh: acct: 128 (over z, x, core), attr: 4 (over y).
Axes of the slice: x: 4, y: 4, z: 16, core: 2. Of those that a mesh axis runs over, the one named last changes fastest.
Arguments:
- scores0: bfloat16 [65536, 128], P('acct'), may hold values from -6 to 6
- seed_mask: int32 [65536], P('acct'), may hold values 0 or 1
- acct_degree: int32 [65536], P('acct'), may hold values from 1 to 16
- attr_degree: int32 [4, 16384], P('attr', 'acct'), may hold values from 1 to 16
- tile_weight: bfloat16 [4, 2048, 128, 128], P('attr', 'acct'), may hold values from -0.125 to 0.125
- tile_acct: int32 [4, 2048], P('attr', 'acct'), may hold values from 0 to 3
- tile_attr: int32 [4, 2048], P('attr', 'acct'), may hold values from 0 to 127
- attr_owner: int32 [4, 128], P('attr'), may hold values from 0 to 127, each once within a row
- tile_count: int32 [4, 128], P('attr', 'acct'), may hold values from 4 to 16, as said below
Outputs:
- new_scores: float32 [65536, 128], P('acct')
- attr_scores: bfloat16 [4, 16384, 128], P('attr', 'acct')
Inputs may be any that keep to these rules, and one draw needn't show every extreme that they name: `attr_owner`: each row is a permutation of the attribute blocks' owners. `tile_count`: slots at or past a device's count are unused; in every type some device has all 16 slots live.
All inputs are finite; a program needn't handle non-finite values. No bound on the sum of `seed_mask` on one device may be relied on, other than what follows from the above.
Results may differ from a plain program's by a relative error of at most 0.005.
Values may be sent and summed in bfloat16 or wider, within the bound.
No kernel may reach another device: no remote copies, remote signals or barrier semaphores. Data moves between devices by JAX's collectives and lax.ppermute only.
A program may use at most 64 MiB of HBM per device.

v0:
```python
import jax
import jax.numpy as jnp
from jax import lax
from jax.sharding import PartitionSpec as P

ALPHA = 0.8


def per_device(
    scores0,
    seed_mask,
    acct_degree,
    attr_degree,
    tile_weight,
    tile_acct,
    tile_attr,
    attr_owner,
    tile_count,
):
    owners = lax.axis_size("acct")
    tile_side = tile_weight.shape[2]
    slot_total = tile_weight.shape[1]
    score_width = scores0.shape[1]
    acct_scale = lax.rsqrt(acct_degree.astype(jnp.float32))
    prior_scores = scores0.astype(jnp.float32)
    scaled = (prior_scores * acct_scale[:, None]).astype(jnp.bfloat16)
    blocks = scaled.reshape(-1, tile_side, score_width)
    block_count = blocks.shape[0]
    weights = tile_weight[0]
    acct_ids = tile_acct[0]
    owner_table = attr_owner[0]
    lookup = tile_attr[0][:, None] == jnp.arange(owners)[None, :]
    targets = jnp.sum(jnp.where(lookup, owner_table[None, :], 0), axis=1)
    live_count = tile_count[0, 0]

    def slot_pieces(number):
        living = (jnp.arange(number) < live_count).astype(jnp.float32)
        return (weights, acct_ids, targets, living)

    weight_fragment, acct_piece, target_piece, living = slot_pieces(slot_total)
    selected_entries = jnp.take(blocks, acct_piece, axis=0)
    signal_payload = jnp.einsum(
        "und,unq->udq", weight_fragment, selected_entries, preferred_element_type=jnp.float32
    )
    partial_sums = jax.ops.segment_sum(
        signal_payload * living[:, None, None], target_piece, num_segments=owners
    )
    incoming_values = lax.all_to_all(partial_sums, "acct", split_axis=0, concat_axis=0, tiled=True)
    own_sum = jnp.sum(incoming_values, axis=0)
    attr_scale = lax.rsqrt(attr_degree[0].astype(jnp.float32))
    own_scores = (own_sum * attr_scale[:, None]).astype(jnp.bfloat16)
    all_attr = lax.all_gather(own_scores, "acct", axis=0, tiled=True).reshape(
        owners, tile_side, score_width
    )
    weight_fragment, acct_piece, target_piece, living = slot_pieces(slot_total)
    loaded_values = jnp.take(all_attr, target_piece, axis=0)
    reverse_contributions = jnp.einsum(
        "pyb,pbw->pyw", weight_fragment, loaded_values, preferred_element_type=jnp.float32
    )
    returned = jax.ops.segment_sum(
        reverse_contributions * living[:, None, None], acct_piece, num_segments=block_count
    )
    returned_rows = returned.reshape(-1, score_width)
    whole_sum = lax.psum(returned_rows.astype(jnp.bfloat16), "attr").astype(jnp.float32)
    new_scores = jnp.where(
        seed_mask[:, None] == 1,
        prior_scores,
        ALPHA * (whole_sum * acct_scale[:, None]) + (1.0 - ALPHA) * prior_scores,
    )
    return (new_scores, own_scores[None])


def solution(mesh):
    placed = (
        P("acct", None),
        P("acct"),
        P("acct"),
        P("attr", "acct"),
        P("attr", "acct", None, None),
        P("attr", "acct"),
        P("attr", "acct"),
        P("attr", None),
        P("attr", "acct"),
    )
    return jax.shard_map(
        per_device,
        mesh=mesh,
        in_specs=placed,
        out_specs=(P("acct", None), P("attr", "acct", None)),
        check_vma=False,
    )
```

profile of v0, /device:TPU:1, one launch (start us, length us, event | category | flops | bytes accessed | tf_op | source)
XLA Modules:
  0.0 615.4 jit_solution(16985990893490928795)
XLA Ops:
  7.2 0.0 copy-start
  7.9 0.7 fusion.13
  8.5 0.7 compare_convert_fusion
  9.2 0.7 convert_rsqrt_fusion
  9.9 1.0 fusion.8
  10.9 0.6 gather_fusion
  11.6 0.0 copy-done
  11.6 0.4 fusion.1
  12.0 0.3 copy.18
  12.4 0.9 select_reduce_fusion
  13.2 4.3 broadcast_in_dim.63
  17.5 3.4 scatter_fusion
  20.9 0.0 copy-start.4
  20.9 20.9 %all-to-all-start = ((f32[128,128,128]{2,1,0:T(8,128)}), f32[128,128,128]{2,1,0:T(8,128)}, u32[]{:S(2)}, u32[]{:S(2)}) async-start(f32[128,128,128]{2,1,0:T(8,128)} %scatter_fusion), calls=%async_computation | async-start | bytes 16777216 | tf_op jit(solution)/shard_map/all_to_all | solution.py:48
  41.8 0.0 copy-start.2
  41.8 0.0 copy-start.3
  41.8 0.0 all-gather.2.cloned.1.call-start
  41.9 0.0 copy-done.4
  41.9 0.0 copy-start.1
  41.9 364.8 %all-to-all-done = f32[128,128,128]{2,1,0:T(8,128)} async-done(((f32[128,128,128]{2,1,0:T(8,128)}), f32[128,128,128]{2,1,0:T(8,128)}, u32[]{:S(2)}, u32[]{:S(2)}) %all-to-all-start) | async-done | bytes 8388640 | tf_op jit(solution)/shard_map/all_to_all | solution.py:48
  406.7 3.8 reduce_sum.21
  410.5 0.7 multiply_convert_fusion
  411.2 0.0 all-gather.2.cloned.1.call-update
  411.2 0.0 all-reduce.2.cloned.1.call-start
  411.3 0.0 copy-done.2
  411.3 139.1 %all-gather.2.cloned.1.call-done = bf16[16384,128]{1,0:T(8,128)(2,1)} async-done(((bf16[128,128]{1,0:T(8,128)(2,1)}), bf16[16384,128]{1,0:T(8,128)(2,1)}) %all-gather.2.cloned.1.call-update) | async-done | bytes 4194320 | tf_op jit(solution)/shard_map/all_gather | solution.py:52
  550.4 2.8 gather_fusion.1
  553.3 0.6 fusion
  553.8 0.3 copy.20
  554.2 0.0 copy-done.3
  554.2 1.6 scatter_fusion.1
  555.8 0.7 convert_element_type.52
  556.5 0.0 all-reduce.2.cloned.1.call-update
  556.5 0.7 fusion.12
  557.2 49.5 %all-reduce.2.cloned.1.call-done = bf16[512,128]{1,0:T(8,128)(2,1)} async-done(((bf16[512,128]{1,0:T(8,128)(2,1)}), bf16[512,128]{1,0:T(8,128)(2,1)}) %all-reduce.2.cloned.1.call-update) | async-done | bytes 131088 | tf_op jit(solution)/shard_map/psum | solution.py:64
  606.7 0.0 copy-done.1
  606.7 1.8 convert_select_fusion
  (7 shorter events, 0.1 us)
Async XLA Ops:
  7.2 4.4 copy-start
  20.9 21.0 %copy-start.4 = (s32[1,128]{1,0:T(1,128)S(1)}, s32[1,128]{1,0:T(1,128)}, u32[]{:S(2)}) copy-start(s32[1,128]{1,0:T(1,128)} %param.12) | copy-start | bytes 1540
  20.9 385.7 %all-to-all-start = ((f32[128,128,128]{2,1,0:T(8,128)}), f32[128,128,128]{2,1,0:T(8,128)}, u32[]{:S(2)}, u32[]{:S(2)}) async-start(f32[128,128,128]{2,1,0:T(8,128)} %scatter_fusion), calls=%async_computation | async-start | bytes 16777216 | tf_op jit(solution)/shard_map/all_to_all | solution.py:48
  41.8 369.5 %copy-start.2 = (s32[512]{0:T(512)S(1)}, s32[512]{0:T(512)}, u32[]{:S(2)}) copy-start(s32[512]{0:T(512)} %param.10) | copy-start | bytes 6148
  41.8 512.4 %copy-start.3 = (s32[1,16]{1,0:T(1,128)S(1)}, s32[1,16]{1,0:T(1,128)}, u32[]{:S(2)}) copy-start(s32[1,16]{1,0:T(1,128)} %param.14) | copy-start | bytes 196
  41.8 508.6 %all-gather.2.cloned.1.call-start = ((), (), s32[]{:S(2)}) async-start(), calls=%async_computation.1 | async-start | bytes 4227072 | tf_op jit(solution)/shard_map/all_gather | solution.py:52
  41.9 564.8 %copy-start.1 = (bf16[512,128]{1,0:T(8,128)(2,1)S(1)}, bf16[512,128]{1,0:T(8,128)(2,1)}, u32[]{:S(2)}) copy-start(bf16[512,128]{1,0:T(8,128)(2,1)} %param.9) | copy-start | bytes 393220
  411.2 195.5 %all-reduce.2.cloned.1.call-start = ((), (), s32[]{:S(2)}) async-start(), calls=%async_computation.2 | async-start | bytes 262144 | tf_op jit(solution)/shard_map/psum | solution.py:64
Sparse Core Ops, SparseCore 0:
  411.3 139.0 all-gather.1
  556.6 50.0 all-reduce.1
where the time goes:
time: 617 us; the launch traced here: 615 us
  waiting for transfers between devices  553 us (90%)
  starting transfers between devices  21 us (3%)
  other arithmetic  16.7 us (3%)
  between operations  14.9 us (2%)
  local copies, waits for them, and re-layouts  8.46 us (1%)
    all_to_all x1, waiting for transfers between devices, per_device(): lax.all_to_all(partial_sums, 'acct', split_axis=0, concat_axis=0, tiled=T...  365 us
    all_gather x1, waiting for transfers between devices, per_device(): lax.all_gather(own_scores, 'acct', axis=0, tiled=True)  139 us
    psum x1, waiting for transfers between devices, per_device(): lax.psum(returned_rows.astype(jnp.bfloat16), 'attr').astype(jnp.float32)  49.5 us
    all_to_all x1, starting transfers between devices, per_device(): lax.all_to_all(partial_sums, 'acct', split_axis=0, concat_axis=0, tiled=T...  20.9 us
  transfers between devices with their start and end apart: 3, of which 3 were waited for; matrix products, arithmetic and copies ran while one was open for 0% of the time, Pallas kernels for 0%

commit v1 on v0

v1 whole, which is shorter than its diff:
```python
import functools
import jax
import jax.numpy as jnp
from jax import lax
from jax.experimental import pallas as pl
from jax.experimental.pallas import tpu as pltpu
from jax.sharding import Mesh, PartitionSpec as P

ALPHA = 0.8
ACCT = ("zh", "zl", "x", "c")
SIDE = 128
SLOTS = 16
ROWS = 512

AHEAD = [(2 * x + c, 2 * ((x + (1, -1)[c]) % 4) + c) for x in range(4) for c in range(2)]
BACK = [(b, a) for a, b in AHEAD]
SWAP = [(0, 1), (1, 0)]


def place(code, me):
    owner = code & 127
    x = (owner >> 1) & 3
    z = owner >> 3
    away = jnp.where(me[1] == 0, x - me[0], me[0] - x) & 3
    along = (z & 3) * 4 + (z >> 2)
    taken = ((code >> 9) == 1) & ((owner & 1) == me[1])
    return taken, away, along, (code >> 7) & 3


def forward_kernel(me, code0, code1, w0, w1, x0, x1, o0, o1, o2, o3, acc):
    acc[...] = jnp.zeros_like(acc)
    for code, w, rows in ((code0, w0, x0), (code1, w1, x1)):

        def step(s, carry, code=code, w=w, rows=rows):
            taken, away, along, block = place(code[s], me)

            @pl.when(taken)
            def _():
                start = pl.multiple_of(block * SIDE, SIDE)
                acc[away * 16 + along] += lax.dot_general(
                    w[s],
                    rows[pl.ds(start, SIDE), :],
                    (((0,), (0,)), ((), ())),
                    preferred_element_type=jnp.float32,
                )

            return carry

        lax.fori_loop(0, SLOTS, step, 0)
    for n, out in enumerate((o0, o1, o2, o3)):
        out[...] = acc[n * 16 : (n + 1) * 16].astype(out.dtype)


def backward_kernel(me, code0, code1, w0, w1, g0, g1, g2, g3, mine, other, acc):
    acc[...] = jnp.zeros_like(acc)
    for half, (code, w) in enumerate(((code0, w0), (code1, w1))):

        def step(s, carry, half=half, code=code, w=w):
            taken, away, along, block = place(code[s], me)
            for n, blocks in enumerate((g0, g1, g2, g3)):

                @pl.when(taken & (away == n))
                def _(blocks=blocks):
                    start = pl.multiple_of(half * ROWS + block * SIDE, SIDE)
                    acc[pl.ds(start, SIDE), :] += jnp.dot(
                        w[s], blocks[along], preferred_element_type=jnp.float32
                    )

            return carry

        lax.fori_loop(0, SLOTS, step, 0)
    mine[...] = acc[:ROWS]
    other[...] = acc[ROWS:].astype(other.dtype)


def smem(n):
    return [pl.BlockSpec(memory_space=pltpu.SMEM)] * n


def vmem(n):
    return [pl.BlockSpec(memory_space=pltpu.VMEM)] * n


def per_device(
    scores0,
    seed_mask,
    acct_degree,
    attr_degree,
    tile_weight,
    tile_acct,
    tile_attr,
    attr_owner,
    tile_count,
):
    bf16, f32 = jnp.bfloat16, jnp.float32
    weights = tile_weight[0]
    acct_scale = lax.rsqrt(acct_degree.astype(f32))
    prior_scores = scores0.astype(f32)
    scaled = (prior_scores * acct_scale[:, None]).astype(bf16)
    lookup = tile_attr[0][:, None] == jnp.arange(SIDE)[None, :]
    targets = jnp.sum(jnp.where(lookup, attr_owner[0][None, :], 0), axis=1)
    living = (jnp.arange(SLOTS) < tile_count[0, 0]).astype(jnp.int32)
    code = targets + tile_acct[0] * 128 + living * 512
    me = jnp.stack([lax.axis_index("x"), lax.axis_index("c")]).astype(jnp.int32)

    weights1 = lax.ppermute(weights, "c", SWAP)
    code1 = lax.ppermute(code, "c", SWAP)
    scaled1 = lax.ppermute(scaled, "c", SWAP)

    group = jax.ShapeDtypeStruct((16, SIDE, SIDE), bf16)
    o0, o1, o2, o3 = pl.pallas_call(
        forward_kernel,
        out_shape=[group] * 4,
        in_specs=smem(3) + vmem(4),
        out_specs=vmem(4),
        scratch_shapes=[pltpu.VMEM((64, SIDE, SIDE), f32)],
        compiler_params=pltpu.CompilerParams(vmem_limit_bytes=32 * 2**20),
        cost_estimate=pl.CostEstimate(
            flops=2 * 16 * SIDE**3, bytes_accessed=4 * 2**20, transcendentals=0
        ),
    )(me, code, code1, weights, weights1, scaled, scaled1)

    xc = ("x", "c")
    far = lax.ppermute(o2, xc, AHEAD)
    near = lax.ppermute(o3, xc, BACK)
    rest = lax.ppermute((o1.astype(f32) + far.astype(f32)).astype(bf16), xc, AHEAD)
    line = (o0.astype(f32) + near.astype(f32) + rest.astype(f32)).astype(bf16)
    line = line.reshape(4, 4, SIDE, SIDE)
    line = lax.all_to_all(line, "zl", 0, 0, tiled=True)
    quarter = jnp.sum(line.astype(f32), axis=0).astype(bf16)
    quarter = lax.all_to_all(quarter, "zh", 0, 0, tiled=True)
    own_sum = jnp.sum(quarter.astype(f32), axis=0)
    attr_scale = lax.rsqrt(attr_degree[0].astype(f32))
    own_scores = (own_sum * attr_scale[:, None]).astype(bf16)

    spread = jnp.broadcast_to(own_scores[None], (4, SIDE, SIDE))
    spread = lax.all_to_all(spread, "zh", 0, 0, tiled=True)
    spread = jnp.broadcast_to(spread[None], (4, 4, SIDE, SIDE))
    g0 = lax.all_to_all(spread, "zl", 0, 0, tiled=True).reshape(16, SIDE, SIDE)
    g3 = lax.ppermute(g0, xc, AHEAD)
    g1 = lax.ppermute(g0, xc, BACK)
    g2 = lax.ppermute(g3, xc, AHEAD)

    mine, other = pl.pallas_call(
        backward_kernel,
        out_shape=[
            jax.ShapeDtypeStruct((ROWS, SIDE), f32),
            jax.ShapeDtypeStruct((ROWS, SIDE), bf16),
        ],
        in_specs=smem(3) + vmem(6),
        out_specs=vmem(2),
        scratch_shapes=[pltpu.VMEM((2 * ROWS, SIDE), f32)],
        compiler_params=pltpu.CompilerParams(vmem_limit_bytes=32 * 2**20),
        cost_estimate=pl.CostEstimate(
            flops=2 * 16 * SIDE**3, bytes_accessed=4 * 2**20, transcendentals=0
        ),
    )(me, code, code1, weights, weights1, g0, g1, g2, g3)

    returned = (mine + lax.ppermute(other, "c", SWAP).astype(f32)).astype(bf16)
    returned = jnp.broadcast_to(returned[None], (4, ROWS, SIDE))
    returned = lax.all_to_all(returned, "y", 0, 0, tiled=True)
    whole_sum = jnp.sum(returned.astype(f32), axis=0)
    new_scores = jnp.where(
        seed_mask[:, None] == 1,
        prior_scores,
        ALPHA * (whole_sum * acct_scale[:, None]) + (1.0 - ALPHA) * prior_scores,
    )
    return (new_scores, own_scores[None])


def solution(mesh):
    fine = Mesh(mesh.devices.reshape(4, 4, 4, 2, 4), ACCT + ("y",))
    placed = (
        P(ACCT, None),
        P(ACCT),
        P(ACCT),
        P("y", ACCT),
        P("y", ACCT, None, None),
        P("y", ACCT),
        P("y", ACCT),
        P("y", None),
        P("y", ACCT),
    )
    return jax.shard_map(
        per_device,
        mesh=fine,
        in_specs=placed,
        out_specs=(P(ACCT, None), P("y", ACCT, None)),
        check_vma=False,
    )
```

time: 617 us -> 177 us (0.29)
  waiting for transfers between devices: 553 us -> 46.5 us
  starting transfers between devices: 21 us -> 74.4 us
  blocking collectives: 0 us -> 41.3 us
  between operations: 14.9 us -> 1.48 us
  other arithmetic: 16.7 us -> 4.9 us
    all_to_all x1 -> x2, waiting for transfers between devices: 365 us -> 20.2 us  [the longest x1 12 us: per_device(): quarter = lax.all_to_all(quarter, 'zh', 0, 0, tiled=True)]
    all_gather x1 -> x0, waiting for transfers between devices: 139 us -> none  [per_device(): lax.all_gather(own_scores, 'acct', axis=0, tiled=True)]
    ppermute x0 -> x10, starting transfers between devices: none -> 51.3 us  [the longest x1 18.7 us: per_device(): returned = (mine + lax.ppermute(other, 'c', SWAP).astype(f32)).astype(bf16)]
    psum x1 -> x0, waiting for transfers between devices: 49.5 us -> none  [per_device(): lax.psum(returned_rows.astype(jnp.bfloat16), 'attr').astype(jnp.float32)]
    all_to_all x0 -> x3, blocking collectives: none -> 41.3 us  [the longest x1 15.5 us: per_device(): spread = lax.all_to_all(spread, 'zh', 0, 0, tiled=True)]
    ppermute x0 -> x10, waiting for transfers between devices: none -> 26.3 us  [the longest x1 6.55 us: per_device(): g2 = lax.ppermute(g3, xc, AHEAD)]
    all_to_all x1 -> x2, starting transfers between devices: 20.9 us -> 23.2 us  [the longest x1 11.8 us: per_device(): quarter = lax.all_to_all(quarter, 'zh', 0, 0, tiled=True)]
  transfers between devices with their start and end apart: 3 -> 12, of which waited for: 3 -> 9; matrix products, arithmetic and copies ran while one was open for 0% -> 2% of each run, Pallas kernels for 0% -> 0%
where the time goes in v1:
time: 177 us
  starting transfers between devices  74.4 us (42%)
  waiting for transfers between devices  46.5 us (26%)
  blocking collectives  41.3 us (23%)
  other arithmetic  4.9 us (3%)
  Pallas kernels  4.62 us (3%)
  local copies, waits for them, and re-layouts  3.36 us (2%)
    ppermute x1, starting transfers between devices, per_device(): returned = (mine + lax.ppermute(other, 'c', SWAP).astype(f32)).astype(bf16)  18.7 us
    all_to_all x1, blocking collectives, per_device(): spread = lax.all_to_all(spread, 'zh', 0, 0, tiled=True)  15.5 us
    all_to_all x1, blocking collectives, per_device(): g0 = lax.all_to_all(spread, 'zl', 0, 0, tiled=True).reshape(16, SIDE, SIDE)  13.4 us
    all_to_all x1, blocking collectives, per_device(): line = lax.all_to_all(line, 'zl', 0, 0, tiled=True)  12.4 us
    all_to_all x1, waiting for transfers between devices, per_device(): quarter = lax.all_to_all(quarter, 'zh', 0, 0, tiled=True)  12 us
    all_to_all x1, starting transfers between devices, per_device(): quarter = lax.all_to_all(quarter, 'zh', 0, 0, tiled=True)  11.8 us
    all_to_all x1, starting transfers between devices, per_device(): returned = lax.all_to_all(returned, 'y', 0, 0, tiled=True)  11.4 us
    ppermute x1, starting transfers between devices, per_device(): weights1 = lax.ppermute(weights, 'c', SWAP)  8.79 us
  transfers between devices with their start and end apart: 12, of which 9 were waited for; matrix products, arithmetic and copies ran while one was open for 2% of the time, Pallas kernels for 0%

profile of v1, /device:TPU:1, one launch (start us, length us, event | category | flops | bytes accessed | tf_op | source)
XLA Modules:
  0.0 176.6 jit_solution(6220908757147114430)
XLA Ops:
  0.6 8.8 %collective-permute-start.1 = (bf16[16,128,128]{2,1,0:T(8,128)(2,1)}, bf16[16,128,128]{2,1,0:T(8,128)(2,1)S(1)}, u32[]{:S(2)}, u32[]{:S(2)}) collective-permute-start(bf16[16,128,128]{2,1,0:T(8,128)(2,1)} %bitcast.19), channel_id=1, source_target_pairs={{0,4},{4,0},{1,5},{5,1},{2,6},{6,2},{3,7},{7,3},{8,12},{12,8},{9,1... | collective-permute-start | bytes 1572872 | tf_op jit(solution)/shard_map/ppermute | solution.py:106
  9.4 0.7 convert_rsqrt_fusion
  10.1 1.0 fusion.x0
  11.2 1.9 %collective-permute-start.2 = (bf16[512,128]{1,0:T(8,128)(2,1)S(1)}, bf16[512,128]{1,0:T(8,128)(2,1)S(1)}, u32[]{:S(2)}, u32[]{:S(2)}) collective-permute-start(bf16[512,128]{1,0:T(8,128)(2,1)S(1)} %fusion.x0), channel_id=1, source_target_pairs={{0,4},{4,0},{1,5},{5,1},{2,6},{6,2},{3,7},{7,3},{8,12},{12,8},{9,1... | collective-permute-start | bytes 393224 | tf_op jit(solution)/shard_map/ppermute | solution.py:108
  13.7 0.0 copy-start.5
  13.7 0.0 copy-start.6
  13.8 0.6 copy-done.5
  14.4 0.0 copy-done.6
  14.4 0.2 select_reduce_fusion
  14.6 0.7 copy-done.4
  15.3 2.4 %collective-permute-start = (s32[16]{0:T(128)S(1)}, s32[16]{0:T(128)S(1)}, u32[]{:S(2)}, u32[]{:S(2)}) collective-permute-start(s32[16]{0:T(128)S(1)} %fusion.3.code0), channel_id=1, source_target_pairs={{0,4},{4,0},{1,5},{5,1},{2,6},{6,2},{3,7},{7,3},{8,12},{12,8},{9,1... | collective-permute-start | bytes 200 | tf_op jit(solution)/shard_map/ppermute | solution.py:107
  17.7 0.1 pad_add_fusion.me
  17.7 0.7 collective-permute-done.code1
  18.5 0.0 collective-permute-done.2.x1
  18.5 1.0 copy-done
  19.5 2.5 %shard_map.104 = (bf16[16,128,128]{2,1,0:T(8,128)(2,1)S(1)}, bf16[16,128,128]{2,1,0:T(8,128)(2,1)S(1)}, bf16[16,128,128]{2,1,0:T(8,128)(2,1)S(1)}, bf16[16,128,128]{2,1,0:T(8,128)(2,1)S(1)}) custom-call(s32[2]{0:T(128)S(1)} %pad_add_fusion.me, s32[16]{0:T(128)S(1)} %fusion.3.code0, s32[16]{0:T(128)S(1)} %collective-permute-done.code1, ...), custom_call_target="tpu_custom_call" | custom-call | flops 67108864 | bytes 4194304 | tf_op jit(solution)/shard_map/pallas_call | solution.py:111
  22.0 1.9 %collective-permute-start.4 = (bf16[16,128,128]{2,1,0:T(8,128)(2,1)S(1)}, bf16[16,128,128]{2,1,0:T(8,128)(2,1)S(1)}, u32[]{:S(2)}, u32[]{:S(2)}) collective-permute-start(bf16[16,128,128]{2,1,0:T(8,128)(2,1)S(1)} %get-tuple-element.11), channel_id=1, source_target_pairs={{0,8},{4,28},{8,16},{12,4},{16,24},{20,12},{24,0},{28,20},{1,9},{5... | collective-permute-start | bytes 1572872 | tf_op jit(solution)/shard_map/ppermute | solution.py:124
  24.0 3.4 %collective-permute-start.3 = (bf16[16,128,128]{2,1,0:T(8,128)(2,1)S(1)}, bf16[16,128,128]{2,1,0:T(8,128)(2,1)S(1)}, u32[]{:S(2)}, u32[]{:S(2)}) collective-permute-start(bf16[16,128,128]{2,1,0:T(8,128)(2,1)S(1)} %get-tuple-element.9), channel_id=1, source_target_pairs={{8,0},{28,4},{16,8},{4,12},{24,16},{12,20},{0,24},{20,28},{9,1},{2... | collective-permute-start | bytes 1572872 | tf_op jit(solution)/shard_map/ppermute | solution.py:125
  27.3 5.8 %collective-permute-done.4 = bf16[16,128,128]{2,1,0:T(8,128)(2,1)S(1)} collective-permute-done((bf16[16,128,128]{2,1,0:T(8,128)(2,1)S(1)}, bf16[16,128,128]{2,1,0:T(8,128)(2,1)S(1)}, u32[]{:S(2)}, u32[]{:S(2)}) %collective-permute-start.4) | collective-permute-done | bytes 524320 | tf_op jit(solution)/shard_map/ppermute | solution.py:124
  33.2 0.1 add_convert_fusion.1
  33.3 1.9 %collective-permute-start.5 = (bf16[16,128,128]{2,1,0:T(8,128)(2,1)S(1)}, bf16[16,128,128]{2,1,0:T(8,128)(2,1)S(1)}, u32[]{:S(2)}, u32[]{:S(2)}) collective-permute-start(bf16[16,128,128]{2,1,0:T(8,128)(2,1)S(1)} %add_convert_fusion.1), channel_id=1, source_target_pairs={{0,8},{4,28},{8,16},{12,4},{16,24},{20,12},{24,0},{28,20},{1,9},{5... | collective-permute-start | bytes 1572872 | tf_op jit(solution)/shard_map/ppermute | solution.py:126
  35.2 5.0 %collective-permute-done.3 = bf16[16,128,128]{2,1,0:T(8,128)(2,1)S(1)} collective-permute-done((bf16[16,128,128]{2,1,0:T(8,128)(2,1)S(1)}, bf16[16,128,128]{2,1,0:T(8,128)(2,1)S(1)}, u32[]{:S(2)}, u32[]{:S(2)}) %collective-permute-start.3) | collective-permute-done | bytes 524320 | tf_op jit(solution)/shard_map/ppermute | solution.py:125
  40.3 3.0 %collective-permute-done.5 = bf16[16,128,128]{2,1,0:T(8,128)(2,1)S(1)} collective-permute-done((bf16[16,128,128]{2,1,0:T(8,128)(2,1)S(1)}, bf16[16,128,128]{2,1,0:T(8,128)(2,1)S(1)}, u32[]{:S(2)}, u32[]{:S(2)}) %collective-permute-start.5) | collective-permute-done | bytes 524320 | tf_op jit(solution)/shard_map/ppermute | solution.py:126
  43.2 0.2 add_convert_fusion
  43.5 12.4 %all_to_all.25 = bf16[4,4,128,128]{3,2,1,0:T(8,128)(2,1)S(1)} all-to-all(bf16[4,4,128,128]{3,2,1,0:T(8,128)(2,1)S(1)} %bitcast.25), channel_id=1, replica_groups=mesh['zh'=4,'zl'=4,'x'=4,'c'=2,'y'=4] {'zl'}, dimensions={0} | all-to-all | bytes 1048576 | tf_op jit(solution)/shard_map/all_to_all | solution.py:129
  55.8 0.7 reduce_sum.42
  56.6 11.8 %all-to-all-start.1 = ((bf16[4,128,128]{2,1,0:T(8,128)(2,1)}), bf16[4,128,128]{2,1,0:T(8,128)(2,1)S(1)}, u32[]{:S(2)}, u32[]{:S(2)}) async-start(bf16[4,128,128]{2,1,0:T(8,128)(2,1)} %reduce_sum.42), calls=%async_computation.1 | async-start | bytes 262144 | tf_op jit(solution)/shard_map/all_to_all | solution.py:131
  68.4 12.0 %all-to-all-done.1 = bf16[4,128,128]{2,1,0:T(8,128)(2,1)S(1)} async-done(((bf16[4,128,128]{2,1,0:T(8,128)(2,1)}), bf16[4,128,128]{2,1,0:T(8,128)(2,1)S(1)}, u32[]{:S(2)}, u32[]{:S(2)}) %all-to-all-start.1) | async-done | bytes 131104 | tf_op jit(solution)/shard_map/all_to_all | solution.py:131
  80.4 0.1 multiply_convert_fusion
  80.6 15.5 %all_to_all.26 = bf16[4,128,128]{2,1,0:T(8,128)(2,1)S(1)} all-to-all(bf16[4,128,128]{2,1,0:T(8,128)(2,1)S(1)} %broadcast_in_dim.50), channel_id=1, replica_groups=mesh['zh'=4,'zl'=4,'x'=4,'c'=2,'y'=4] {'zh'}, dimensions={0} | all-to-all | bytes 262144 | tf_op jit(solution)/shard_map/all_to_all | solution.py:137
  96.1 0.1 broadcast_in_dim.51
  96.2 0.0 copy-start.1
  96.2 13.4 %all_to_all.27 = bf16[4,4,128,128]{3,2,1,0:T(8,128)(2,1)S(1)} all-to-all(bf16[4,4,128,128]{3,2,1,0:T(8,128)(2,1)S(1)} %broadcast_in_dim.51), channel_id=1, replica_groups=mesh['zh'=4,'zl'=4,'x'=4,'c'=2,'y'=4] {'zl'}, dimensions={0} | all-to-all | bytes 1048576 | tf_op jit(solution)/shard_map/all_to_all | solution.py:139
  109.6 5.3 %collective-permute-start.7 = (bf16[16,128,128]{2,1,0:T(8,128)(2,1)S(1)}, bf16[16,128,128]{2,1,0:T(8,128)(2,1)S(1)}, u32[]{:S(2)}, u32[]{:S(2)}) collective-permute-start(bf16[16,128,128]{2,1,0:T(8,128)(2,1)S(1)} %bitcast.22), channel_id=1, source_target_pairs={{0,8},{4,28},{8,16},{12,4},{16,24},{20,12},{24,0},{28,20},{1,9},{5... | collective-permute-start | bytes 1572872 | tf_op jit(solution)/shard_map/ppermute | solution.py:140
  114.9 1.9 %collective-permute-start.6 = (bf16[16,128,128]{2,1,0:T(8,128)(2,1)S(1)}, bf16[16,128,128]{2,1,0:T(8,128)(2,1)S(1)}, u32[]{:S(2)}, u32[]{:S(2)}) collective-permute-start(bf16[16,128,128]{2,1,0:T(8,128)(2,1)S(1)} %bitcast.23), channel_id=1, source_target_pairs={{8,0},{28,4},{16,8},{4,12},{24,16},{12,20},{0,24},{20,28},{9,1},{2... | collective-permute-start | bytes 1572872 | tf_op jit(solution)/shard_map/ppermute | solution.py:141
  116.8 4.2 %collective-permute-done.7.g3 = bf16[16,128,128]{2,1,0:T(8,128)(2,1)S(1)} collective-permute-done((bf16[16,128,128]{2,1,0:T(8,128)(2,1)S(1)}, bf16[16,128,128]{2,1,0:T(8,128)(2,1)S(1)}, u32[]{:S(2)}, u32[]{:S(2)}) %collective-permute-start.7) | collective-permute-done | bytes 524320 | tf_op jit(solution)/shard_map/ppermute | solution.py:140
  121.0 5.0 %collective-permute-start.8 = (bf16[16,128,128]{2,1,0:T(8,128)(2,1)S(1)}, bf16[16,128,128]{2,1,0:T(8,128)(2,1)S(1)}, u32[]{:S(2)}, u32[]{:S(2)}) collective-permute-start(bf16[16,128,128]{2,1,0:T(8,128)(2,1)S(1)} %collective-permute-done.7.g3), channel_id=1, source_target_pairs={{0,8},{4,28},{8,16},{12,4},{16,24},{20,12},{24,0},{28,20},{1,9},{5... | collective-permute-start | bytes 1572872 | tf_op jit(solution)/shard_map/ppermute | solution.py:142
  126.0 0.0 collective-permute-done.6.g1
  126.0 6.6 %collective-permute-done.8.g2 = bf16[16,128,128]{2,1,0:T(8,128)(2,1)S(1)} collective-permute-done((bf16[16,128,128]{2,1,0:T(8,128)(2,1)S(1)}, bf16[16,128,128]{2,1,0:T(8,128)(2,1)S(1)}, u32[]{:S(2)}, u32[]{:S(2)}) %collective-permute-start.8) | collective-permute-done | bytes 524320 | tf_op jit(solution)/shard_map/ppermute | solution.py:142
  132.6 2.1 %shard_map.105 = (f32[512,128]{1,0:T(8,128)S(1)}, bf16[512,128]{1,0:T(8,128)(2,1)S(1)}) custom-call(s32[2]{0:T(128)S(1)} %pad_add_fusion.me, s32[16]{0:T(128)S(1)} %fusion.3.code0, s32[16]{0:T(128)S(1)} %collective-permute-done.code1, bf16[16,128,128]{2,1,0:T(8,128)(2,1)S(1)} %bitcast.21, bf16[16,128,128]{2,1,0:T(8,128)(2,1)S(1)} %collective-permute-done.1.w1, ...), custom_call_target="tpu_custom_call" | custom-call | flops 67108864 | bytes 4194304 | tf_op jit(solution)/shard_map/pallas_call | solution.py:144
  134.7 18.7 %collective-permute-start.9 = (bf16[512,128]{1,0:T(8,128)(2,1)S(1)}, bf16[512,128]{1,0:T(8,128)(2,1)S(1)}, u32[]{:S(2)}, u32[]{:S(2)}) collective-permute-start(bf16[512,128]{1,0:T(8,128)(2,1)S(1)} %get-tuple-element.13), channel_id=1, source_target_pairs={{0,4},{4,0},{1,5},{5,1},{2,6},{6,2},{3,7},{7,3},{8,12},{12,8},{9,1... | collective-permute-start | bytes 393224 | tf_op jit(solution)/shard_map/ppermute | solution.py:159
  153.5 1.0 collective-permute-done.9
  154.5 0.9 broadcast_in_dim.52
  155.3 11.4 %all-to-all-start.4 = ((bf16[4,512,128]{2,1,0:T(8,128)(2,1)}), bf16[4,512,128]{2,1,0:T(8,128)(2,1)S(1)}, u32[]{:S(2)}, u32[]{:S(2)}) async-start(bf16[4,512,128]{2,1,0:T(8,128)(2,1)} %broadcast_in_dim.52), calls=%async_computation.4 | async-start | bytes 1048576 | tf_op jit(solution)/shard_map/all_to_all | solution.py:161
  166.7 0.7 fusion.2
  167.4 8.2 %all-to-all-done.4 = bf16[4,512,128]{2,1,0:T(8,128)(2,1)S(1)} async-done(((bf16[4,512,128]{2,1,0:T(8,128)(2,1)}), bf16[4,512,128]{2,1,0:T(8,128)(2,1)S(1)}, u32[]{:S(2)}, u32[]{:S(2)}) %all-to-all-start.4) | async-done | bytes 524320 | tf_op jit(solution)/shard_map/all_to_all | solution.py:161
  175.6 0.1 convert_reduce_fusion
  175.7 0.9 convert_select_fusion
  (16 shorter events, 0.1 us)
Async XLA Ops:
  0.6 17.8 %collective-permute-start.1 = (bf16[16,128,128]{2,1,0:T(8,128)(2,1)}, bf16[16,128,128]{2,1,0:T(8,128)(2,1)S(1)}, u32[]{:S(2)}, u32[]{:S(2)}) collective-permute-start(bf16[16,128,128]{2,1,0:T(8,128)(2,1)} %bitcast.19), channel_id=1, source_target_pairs={{0,4},{4,0},{1,5},{5,1},{2,6},{6,2},{3,7},{7,3},{8,12},{12,8},{9,1... | collective-permute-start | bytes 1572872 | tf_op jit(solution)/shard_map/ppermute | solution.py:106
  11.2 7.3 %collective-permute-start.2 = (bf16[512,128]{1,0:T(8,128)(2,1)S(1)}, bf16[512,128]{1,0:T(8,128)(2,1)S(1)}, u32[]{:S(2)}, u32[]{:S(2)}) collective-permute-start(bf16[512,128]{1,0:T(8,128)(2,1)S(1)} %fusion.x0), channel_id=1, source_target_pairs={{0,4},{4,0},{1,5},{5,1},{2,6},{6,2},{3,7},{7,3},{8,12},{12,8},{9,1... | collective-permute-start | bytes 393224 | tf_op jit(solution)/shard_map/ppermute | solution.py:108
  13.7 0.7 copy-start.5
  13.7 0.7 copy-start.6
  14.6 0.7 copy-start.4
  15.3 3.2 %collective-permute-start = (s32[16]{0:T(128)S(1)}, s32[16]{0:T(128)S(1)}, u32[]{:S(2)}, u32[]{:S(2)}) collective-permute-start(s32[16]{0:T(128)S(1)} %fusion.3.code0), channel_id=1, source_target_pairs={{0,4},{4,0},{1,5},{5,1},{2,6},{6,2},{3,7},{7,3},{8,12},{12,8},{9,1... | collective-permute-start | bytes 200 | tf_op jit(solution)/shard_map/ppermute | solution.py:107
  18.5 1.0 copy-start
  22.0 11.1 %collective-permute-start.4 = (bf16[16,128,128]{2,1,0:T(8,128)(2,1)S(1)}, bf16[16,128,128]{2,1,0:T(8,128)(2,1)S(1)}, u32[]{:S(2)}, u32[]{:S(2)}) collective-permute-start(bf16[16,128,128]{2,1,0:T(8,128)(2,1)S(1)} %get-tuple-element.11), channel_id=1, source_target_pairs={{0,8},{4,28},{8,16},{12,4},{16,24},{20,12},{24,0},{28,20},{1,9},{5... | collective-permute-start | bytes 1572872 | tf_op jit(solution)/shard_map/ppermute | solution.py:124
  24.0 16.3 %collective-permute-start.3 = (bf16[16,128,128]{2,1,0:T(8,128)(2,1)S(1)}, bf16[16,128,128]{2,1,0:T(8,128)(2,1)S(1)}, u32[]{:S(2)}, u32[]{:S(2)}) collective-permute-start(bf16[16,128,128]{2,1,0:T(8,128)(2,1)S(1)} %get-tuple-element.9), channel_id=1, source_target_pairs={{8,0},{28,4},{16,8},{4,12},{24,16},{12,20},{0,24},{20,28},{9,1},{2... | collective-permute-start | bytes 1572872 | tf_op jit(solution)/shard_map/ppermute | solution.py:125
  33.3 9.9 %collective-permute-start.5 = (bf16[16,128,128]{2,1,0:T(8,128)(2,1)S(1)}, bf16[16,128,128]{2,1,0:T(8,128)(2,1)S(1)}, u32[]{:S(2)}, u32[]{:S(2)}) collective-permute-start(bf16[16,128,128]{2,1,0:T(8,128)(2,1)S(1)} %add_convert_fusion.1), channel_id=1, source_target_pairs={{0,8},{4,28},{8,16},{12,4},{16,24},{20,12},{24,0},{28,20},{1,9},{5... | collective-permute-start | bytes 1572872 | tf_op jit(solution)/shard_map/ppermute | solution.py:126
  56.6 11.8 %copy-start.7 = (s32[1,128]{1,0:T(1,128)S(1)}, s32[1,128]{1,0:T(1,128)}, u32[]{:S(2)}) copy-start(s32[1,128]{1,0:T(1,128)} %param.12) | copy-start | bytes 1540
  56.6 23.8 %all-to-all-start.1 = ((bf16[4,128,128]{2,1,0:T(8,128)(2,1)}), bf16[4,128,128]{2,1,0:T(8,128)(2,1)S(1)}, u32[]{:S(2)}, u32[]{:S(2)}) async-start(bf16[4,128,128]{2,1,0:T(8,128)(2,1)} %reduce_sum.42), calls=%async_computation.1 | async-start | bytes 262144 | tf_op jit(solution)/shard_map/all_to_all | solution.py:131
  96.2 36.4 %copy-start.1 = (bf16[1,16,128,128]{3,2,1,0:T(8,128)(2,1)S(1)}, bf16[1,16,128,128]{3,2,1,0:T(8,128)(2,1)}, u32[]{:S(2)}) copy-start(bf16[1,16,128,128]{3,2,1,0:T(8,128)(2,1)} %param.13) | copy-start | bytes 1572868
  109.6 11.4 %collective-permute-start.7 = (bf16[16,128,128]{2,1,0:T(8,128)(2,1)S(1)}, bf16[16,128,128]{2,1,0:T(8,128)(2,1)S(1)}, u32[]{:S(2)}, u32[]{:S(2)}) collective-permute-start(bf16[16,128,128]{2,1,0:T(8,128)(2,1)S(1)} %bitcast.22), channel_id=1, source_target_pairs={{0,8},{4,28},{8,16},{12,4},{16,24},{20,12},{24,0},{28,20},{1,9},{5... | collective-permute-start | bytes 1572872 | tf_op jit(solution)/shard_map/ppermute | solution.py:140
  114.9 11.1 %collective-permute-start.6 = (bf16[16,128,128]{2,1,0:T(8,128)(2,1)S(1)}, bf16[16,128,128]{2,1,0:T(8,128)(2,1)S(1)}, u32[]{:S(2)}, u32[]{:S(2)}) collective-permute-start(bf16[16,128,128]{2,1,0:T(8,128)(2,1)S(1)} %bitcast.23), channel_id=1, source_target_pairs={{8,0},{28,4},{16,8},{4,12},{24,16},{12,20},{0,24},{20,28},{9,1},{2... | collective-permute-start | bytes 1572872 | tf_op jit(solution)/shard_map/ppermute | solution.py:141
  121.0 11.6 %collective-permute-start.8 = (bf16[16,128,128]{2,1,0:T(8,128)(2,1)S(1)}, bf16[16,128,128]{2,1,0:T(8,128)(2,1)S(1)}, u32[]{:S(2)}, u32[]{:S(2)}) collective-permute-start(bf16[16,128,128]{2,1,0:T(8,128)(2,1)S(1)} %collective-permute-done.7.g3), channel_id=1, source_target_pairs={{0,8},{4,28},{8,16},{12,4},{16,24},{20,12},{24,0},{28,20},{1,9},{5... | collective-permute-start | bytes 1572872 | tf_op jit(solution)/shard_map/ppermute | solution.py:142
  134.7 19.7 %collective-permute-start.9 = (bf16[512,128]{1,0:T(8,128)(2,1)S(1)}, bf16[512,128]{1,0:T(8,128)(2,1)S(1)}, u32[]{:S(2)}, u32[]{:S(2)}) collective-permute-start(bf16[512,128]{1,0:T(8,128)(2,1)S(1)} %get-tuple-element.13), channel_id=1, source_target_pairs={{0,4},{4,0},{1,5},{5,1},{2,6},{6,2},{3,7},{7,3},{8,12},{12,8},{9,1... | collective-permute-start | bytes 393224 | tf_op jit(solution)/shard_map/ppermute | solution.py:159
  155.3 11.4 %copy-start.3 = (s32[512]{0:T(512)S(1)}, s32[512]{0:T(512)}, u32[]{:S(2)}) copy-start(s32[512]{0:T(512)} %param.10) | copy-start | bytes 6148
  155.3 20.3 %all-to-all-start.4 = ((bf16[4,512,128]{2,1,0:T(8,128)(2,1)}), bf16[4,512,128]{2,1,0:T(8,128)(2,1)S(1)}, u32[]{:S(2)}, u32[]{:S(2)}) async-start(bf16[4,512,128]{2,1,0:T(8,128)(2,1)} %broadcast_in_dim.52), calls=%async_computation.4 | async-start | bytes 1048576 | tf_op jit(solution)/shard_map/all_to_all | solution.py:161
  167.4 8.3 %copy-start.2 = (bf16[512,128]{1,0:T(8,128)(2,1)S(1)}, bf16[512,128]{1,0:T(8,128)(2,1)}, u32[]{:S(2)}) copy-start(bf16[512,128]{1,0:T(8,128)(2,1)} %param.9) | copy-start | bytes 393220

commit v2 on v1

v2 whole, which is shorter than its diff:
```python
import functools
import jax
import jax.numpy as jnp
from jax import lax
from jax.experimental import pallas as pl
from jax.experimental.pallas import tpu as pltpu
from jax.sharding import Mesh, PartitionSpec as P

ALPHA = 0.8
ACCT = ("z", "x", "c")
SIDE = 128
SLOTS = 16
ROWS = 512
LINE = 16
MEBI = 2**20

AHEAD = [(2 * x + c, 2 * ((x + (1, -1)[c]) % 4) + c) for x in range(4) for c in range(2)]
BACK = [(b, a) for a, b in AHEAD]
SWAP = [(0, 1), (1, 0)]


def place(code, me):
    owner = code & 127
    x = (owner >> 1) & 3
    away = jnp.where(me[1] == 0, x - me[0], me[0] - x) & 3
    taken = ((code >> 9) == 1) & ((owner & 1) == me[1])
    return taken, away, owner >> 3, (code >> 7) & 3


def column(row):
    return jnp.broadcast_to(row, (SIDE, SIDE)).T


def prepare_kernel(table, attr, acct, count, scores, degree, payload, code):
    lane = lax.broadcasted_iota(jnp.int32, (SLOTS, SIDE), 1)
    tail = jnp.zeros((SLOTS, SIDE), jnp.int32)
    for s in range(SLOTS):
        owner = table[0, attr[0, s]]
        placing = acct[0, s] + jnp.where(s < count[0, 0], 4, 0)
        code[s] = owner + placing * 128
        tail = jnp.where(lane == s, owner, tail)
        tail = jnp.where(lane == s + SLOTS, placing, tail)
    payload[ROWS:] = tail.astype(jnp.float32).astype(payload.dtype)
    for n in range(4):
        rows = pl.ds(n * SIDE, SIDE)
        scale = column(lax.rsqrt(degree[n : n + 1, :].astype(jnp.float32)))
        payload[rows, :] = (scores[rows, :].astype(jnp.float32) * scale).astype(payload.dtype)


def finish_kernel(t0, t1, t2, t3, scores, degree, seed, new):
    for n in range(4):
        rows = pl.ds(n * SIDE, SIDE)
        scale = column(lax.rsqrt(degree[n : n + 1, :].astype(jnp.float32)))
        prior = scores[rows, :].astype(jnp.float32)
        f32 = [t[rows, :].astype(jnp.float32) for t in (t0, t1, t2, t3)]
        whole = (f32[0] + f32[2]) + (f32[1] + f32[3])
        mixed = ALPHA * (whole * scale) + (1.0 - ALPHA) * prior
        kept = column(seed[n : n + 1, :].astype(jnp.float32))
        new[rows, :] = jnp.where(kept == 1.0, prior, mixed)


def forward_kernel(offsets, me, code0, code1, w0, w1, x0, x1, *refs):
    outs, acc = refs[:-1], refs[-1]
    acc[...] = jnp.zeros_like(acc)
    for code, w, rows in ((code0, w0, x0), (code1, w1, x1)):

        def step(s, carry, code=code, w=w, rows=rows):
            taken, away, z, block = place(code[s], me)
            index = jnp.int32(0)
            wanted = jnp.bool_(False)
            for n, offset in enumerate(offsets):
                index = jnp.where(away == offset, n * LINE, index)
                wanted = wanted | (away == offset)

            @pl.when(taken & wanted)
            def _():
                start = pl.multiple_of(block * SIDE, SIDE)
                acc[index + z] += lax.dot_general(
                    w[s],
                    rows[pl.ds(start, SIDE), :],
                    (((0,), (0,)), ((), ())),
                    preferred_element_type=jnp.float32,
                )

            return carry

        lax.fori_loop(0, SLOTS, step, 0)
    for n, out in enumerate(outs):
        out[...] = acc[n * LINE : (n + 1) * LINE].astype(out.dtype)


def owner_kernel(parts, degree, own, spread):
    scale = column(lax.rsqrt(degree[...].astype(jnp.float32)))
    total = parts[0].astype(jnp.float32)
    for n in range(1, LINE):
        total += parts[n].astype(jnp.float32)
    scores = (total * scale).astype(own.dtype)
    own[...] = scores
    for n in range(LINE):
        spread[n] = scores


def backward_kernel(me, code0, code1, w0, w1, g0, g1, g2, g3, mine, other, acc):
    acc[...] = jnp.zeros_like(acc)
    for half, (code, w) in enumerate(((code0, w0), (code1, w1))):

        def step(s, carry, half=half, code=code, w=w):
            taken, away, z, block = place(code[s], me)
            for n, blocks in enumerate((g0, g1, g2, g3)):

                @pl.when(taken & (away == n))
                def _(blocks=blocks):
                    start = pl.multiple_of(half * ROWS + block * SIDE, SIDE)
                    acc[pl.ds(start, SIDE), :] += jnp.dot(
                        w[s], blocks[z], preferred_element_type=jnp.float32
                    )

            return carry

        lax.fori_loop(0, SLOTS, step, 0)
    mine[...] = acc[:ROWS]
    other[...] = acc[ROWS:].astype(other.dtype)


def smem(n):
    return [pl.BlockSpec(memory_space=pltpu.SMEM)] * n


def vmem(n):
    return [pl.BlockSpec(memory_space=pltpu.VMEM)] * n


def call(kernel, outs, specs, scratch, flops, moved, out_specs=None):
    return pl.pallas_call(
        kernel,
        out_shape=outs,
        in_specs=specs,
        out_specs=out_specs or vmem(len(outs)),
        scratch_shapes=scratch,
        compiler_params=pltpu.CompilerParams(vmem_limit_bytes=24 * MEBI),
        cost_estimate=pl.CostEstimate(flops=flops, bytes_accessed=moved, transcendentals=0),
    )


def per_device(
    scores0,
    seed_mask,
    acct_degree,
    attr_degree,
    tile_weight,
    tile_acct,
    tile_attr,
    attr_owner,
    tile_count,
):
    bf16, f32, i32 = jnp.bfloat16, jnp.float32, jnp.int32
    group = jax.ShapeDtypeStruct((LINE, SIDE, SIDE), bf16)
    block = jax.ShapeDtypeStruct((SIDE, SIDE), bf16)
    weights = tile_weight[0]
    weights1 = lax.ppermute(weights, "c", SWAP)

    degree = acct_degree.reshape(4, SIDE)
    payload, code = call(
        prepare_kernel,
        [
            jax.ShapeDtypeStruct((ROWS + SLOTS, SIDE), bf16),
            jax.ShapeDtypeStruct((SLOTS,), i32),
        ],
        smem(4) + vmem(2),
        [],
        ROWS * SIDE,
        MEBI // 4,
        vmem(1) + smem(1),
    )(attr_owner, tile_attr, tile_acct, tile_count, scores0, degree)
    payload1 = lax.ppermute(payload, "c", SWAP)
    tail1 = payload1[ROWS].astype(i32)
    code1 = tail1[:SLOTS] + tail1[SLOTS : 2 * SLOTS] * 128
    me = jnp.stack([lax.axis_index("x"), lax.axis_index("c")]).astype(i32)

    tiles = 2 * 10 * SIDE**3
    slots = (me, code, code1, weights, weights1)

    def forward(offsets):
        return call(
            functools.partial(forward_kernel, offsets),
            [group] * len(offsets),
            smem(3) + vmem(4),
            [pltpu.VMEM((len(offsets) * LINE, SIDE, SIDE), f32)],
            tiles,
            3 * MEBI,
        )(*slots, payload, payload1)

    (o2,) = forward((2,))
    far = lax.ppermute(o2, ("x", "c"), AHEAD)
    o3, o1, o0 = forward((3, 1, 0))
    near = lax.ppermute(o3, ("x", "c"), BACK)
    rest = (o1.astype(f32) + far.astype(f32)).astype(bf16)
    rest = lax.ppermute(rest, ("x", "c"), AHEAD)
    line = (o0.astype(f32) + near.astype(f32) + rest.astype(f32)).astype(bf16)
    line = lax.all_to_all(line, "z", 0, 0, tiled=True)
    own_scores, spread = call(
        owner_kernel, [block, group], vmem(2), [], SIDE * SIDE * LINE, MEBI
    )(line, attr_degree)

    g0 = lax.all_to_all(spread, "z", 0, 0, tiled=True)
    g3 = lax.ppermute(g0, ("x", "c"), AHEAD)
    g1 = lax.ppermute(g0, ("x", "c"), BACK)
    g2 = lax.ppermute(g3, ("x", "c"), AHEAD)
    mine, other = call(
        backward_kernel,
        [jax.ShapeDtypeStruct((ROWS, SIDE), f32), jax.ShapeDtypeStruct((ROWS, SIDE), bf16)],
        smem(3) + vmem(6),
        [pltpu.VMEM((2 * ROWS, SIDE), f32)],
        tiles,
        4 * MEBI,
    )(*slots, g0, g1, g2, g3)

    returned = (mine + lax.ppermute(other, "c", SWAP).astype(f32)).astype(bf16)
    types = [returned]
    for shift in (1, 2, 3):
        ring = [(y, (y + shift) % 4) for y in range(4)]
        types.append(lax.ppermute(returned, "y", ring))
    (new_scores,) = call(
        finish_kernel,
        [jax.ShapeDtypeStruct((ROWS, SIDE), f32)],
        vmem(7),
        [],
        ROWS * SIDE * 8,
        MEBI,
    )(*types, scores0, degree, seed_mask.reshape(4, SIDE))
    return (new_scores, own_scores[None])


def solution(mesh):
    fine = Mesh(mesh.devices.reshape(LINE, 4, 2, 4), ACCT + ("y",))
    placed = (
        P(ACCT, None),
        P(ACCT),
        P(ACCT),
        P("y", ACCT),
        P("y", ACCT, None, None),
        P("y", ACCT),
        P("y", ACCT),
        P("y", None),
        P("y", ACCT),
    )
    return jax.shard_map(
        per_device,
        mesh=fine,
        in_specs=placed,
        out_specs=(P(ACCT, None), P("y", ACCT, None)),
        check_vma=False,
    )
```

time: 177 us -> 172 us (0.972); the launches traced: 177 us -> 169 us
  blocking collectives: 41.3 us -> 64.8 us
  starting transfers between devices: 74.4 us -> 53.7 us
  waiting for transfers between devices: 46.5 us -> 35.2 us
  Pallas kernels: 4.62 us -> 10.6 us
  other arithmetic: 4.9 us -> 0.57 us
    all_to_all x3 -> x2, blocking collectives: 41.3 us -> 64.8 us  [the longest x1 35.1 us: per_device(): g0 = lax.all_to_all(spread, 'z', 0, 0, tiled=True)]
    all_to_all x2 -> x0, starting transfers between devices: 23.2 us -> none  [the longest x1 11.8 us: per_device(): quarter = lax.all_to_all(quarter, 'zh', 0, 0, tiled=True)]
    all_to_all x2 -> x0, waiting for transfers between devices: 20.2 us -> none  [the longest x1 12 us: per_device(): quarter = lax.all_to_all(quarter, 'zh', 0, 0, tiled=True)]
    ppermute x8 -> x10, starting transfers between devices: 23.7 us -> 41.7 us  [the longest x3 10.1 us: per_device(): types.append(lax.ppermute(returned, 'y', ring))]
    ppermute x1, starting transfers between devices: 18.7 us -> 10.1 us  [per_device(): returned = (mine + lax.ppermute(other, 'c', SWAP).astype(f32)).astype(bf16)]
    ppermute x8 -> x10, waiting for transfers between devices: 25.3 us -> 32.3 us  [the longest x1 6.95 us: per_device(): g2 = lax.ppermute(g3, ('x', 'c'), AHEAD)]
    ppermute x1, starting transfers between devices: 8.79 us -> 1.92 us  [per_device(): weights1 = lax.ppermute(weights, 'c', SWAP)]
    pallas_call x2 -> x6, Pallas kernels: 4.62 us -> 10.6 us  [the longest x2 5 us: forward(): call(functools.partial(forward_kernel, offsets), [group] * len(offsets),...]
  transfers between devices with their start and end apart: 12 -> 12, of which waited for: 9 -> 10; matrix products, arithmetic and copies ran while one was open for 2% -> 0% of each run, Pallas kernels for 0% -> 2%
where the time goes in v2:
time: 172 us; the launch traced here: 169 us
  blocking collectives  64.8 us (38%)
  starting transfers between devices  53.7 us (31%)
  waiting for transfers between devices  35.2 us (20%)
  Pallas kernels  10.6 us (6%)
  local copies, waits for them, and re-layouts  2.62 us (2%)
    all_to_all x1, blocking collectives, per_device(): g0 = lax.all_to_all(spread, 'z', 0, 0, tiled=True)  35.1 us
    all_to_all x1, blocking collectives, per_device(): line = lax.all_to_all(line, 'z', 0, 0, tiled=True)  29.7 us
    ppermute x3, starting transfers between devices, per_device(): types.append(lax.ppermute(returned, 'y', ring))  10.1 us
    ppermute x1, starting transfers between devices, per_device(): returned = (mine + lax.ppermute(other, 'c', SWAP).astype(f32)).astype(bf16)  10.1 us
    ppermute x1, starting transfers between devices, per_device(): payload1 = lax.ppermute(payload, 'c', SWAP)  8.79 us
    ppermute x1, starting transfers between devices, per_device(): g3 = lax.ppermute(g0, ('x', 'c'), AHEAD)  8.09 us
    ppermute x1, waiting for transfers between devices, per_device(): g2 = lax.ppermute(g3, ('x', 'c'), AHEAD)  6.95 us
    ppermute x3, waiting for transfers between devices, per_device(): types.append(lax.ppermute(returned, 'y', ring))  6.87 us
  transfers between devices with their start and end apart: 12, of which 10 were waited for; matrix products, arithmetic and copies ran while one was open for 0% of the time, Pallas kernels for 2%

profile of v2, /device:TPU:1, one launch (start us, length us, event | category | flops | bytes accessed | tf_op | source)
XLA Modules:
  0.0 169.0 jit_solution(3785806949089886493)
XLA Ops:
  0.6 0.0 copy-start.4
  1.3 0.0 copy-start.6
  1.3 0.0 copy-start.7
  1.3 0.0 copy-start.8
  1.3 0.0 copy-done.4
  1.3 0.6 copy-done.6
  2.0 0.0 copy-done.7
  2.0 0.0 copy-done.8
  2.0 0.9 copy-done.2
  2.9 1.2 shard_map.104
  4.1 8.8 %collective-permute-start = (bf16[528,128]{1,0:T(8,128)(2,1)S(1)}, bf16[528,128]{1,0:T(8,128)(2,1)S(1)}, u32[]{:S(2)}, u32[]{:S(2)}) collective-permute-start(bf16[528,128]{1,0:T(8,128)(2,1)S(1)} %get-tuple-element.12.x0), channel_id=1, source_target_pairs={{0,4},{4,0},{1,5},{5,1},{2,6},{6,2},{3,7},{7,3},{8,12},{12,8},{9,1... | collective-permute-start | bytes 405512 | tf_op jit(solution)/shard_map/ppermute | solution.py:175
  12.9 1.9 %collective-permute-start.1 = (bf16[16,128,128]{2,1,0:T(8,128)(2,1)}, bf16[16,128,128]{2,1,0:T(8,128)(2,1)S(1)}, u32[]{:S(2)}, u32[]{:S(2)}) collective-permute-start(bf16[16,128,128]{2,1,0:T(8,128)(2,1)} %bitcast.8), channel_id=1, source_target_pairs={{0,4},{4,0},{1,5},{5,1},{2,6},{6,2},{3,7},{7,3},{8,12},{12,8},{9,1... | collective-permute-start | bytes 1572872 | tf_op jit(solution)/shard_map/ppermute | solution.py:160
  14.9 0.1 pad_add_fusion.me
  14.9 0.0 collective-permute-done.x1
  14.9 0.1 add_bitcast_fusion.code1
  15.0 1.9 %collective-permute-done.1.w1 = bf16[16,128,128]{2,1,0:T(8,128)(2,1)S(1)} collective-permute-done((bf16[16,128,128]{2,1,0:T(8,128)(2,1)}, bf16[16,128,128]{2,1,0:T(8,128)(2,1)S(1)}, u32[]{:S(2)}, u32[]{:S(2)}) %collective-permute-start.1) | collective-permute-done | bytes 524320 | tf_op jit(solution)/shard_map/ppermute | solution.py:160
  16.9 1.0 copy-done
  18.0 1.6 shard_map.106
  19.6 1.9 %collective-permute-start.3 = (bf16[16,128,128]{2,1,0:T(8,128)(2,1)S(1)}, bf16[16,128,128]{2,1,0:T(8,128)(2,1)S(1)}, u32[]{:S(2)}, u32[]{:S(2)}) collective-permute-start(bf16[16,128,128]{2,1,0:T(8,128)(2,1)S(1)} %shard_map.106), channel_id=1, source_target_pairs={{0,8},{4,28},{8,16},{12,4},{16,24},{20,12},{24,0},{28,20},{1,9},{5... | collective-permute-start | bytes 1572872 | tf_op jit(solution)/shard_map/ppermute | solution.py:194
  21.6 3.4 %shard_map.105 = (bf16[16,128,128]{2,1,0:T(8,128)(2,1)S(1)}, bf16[16,128,128]{2,1,0:T(8,128)(2,1)S(1)}, bf16[16,128,128]{2,1,0:T(8,128)(2,1)S(1)}) custom-call(s32[2]{0:T(128)S(1)} %pad_add_fusion.me, s32[16]{0:T(128)S(1)} %get-tuple-element.11.code0, s32[16]{0:T(128)S(1)} %add_bitcast_fusion.code1, bf16[16,128,128]{2,1,0:T(8,128)(2,1)S(1)} %bitcast.10, ...), custom_call_target="tpu_custom_call" | custom-call | flops 41943040 | bytes 3145728 | tf_op jit(solution)/shard_map/pallas_call | solution.py:184
  24.9 3.2 %collective-permute-start.2 = (bf16[16,128,128]{2,1,0:T(8,128)(2,1)S(1)}, bf16[16,128,128]{2,1,0:T(8,128)(2,1)S(1)}, u32[]{:S(2)}, u32[]{:S(2)}) collective-permute-start(bf16[16,128,128]{2,1,0:T(8,128)(2,1)S(1)} %get-tuple-element.14), channel_id=1, source_target_pairs={{8,0},{28,4},{16,8},{4,12},{24,16},{12,20},{0,24},{20,28},{9,1},{2... | collective-permute-start | bytes 1572872 | tf_op jit(solution)/shard_map/ppermute | solution.py:196
  28.1 1.9 %collective-permute-done.3 = bf16[16,128,128]{2,1,0:T(8,128)(2,1)S(1)} collective-permute-done((bf16[16,128,128]{2,1,0:T(8,128)(2,1)S(1)}, bf16[16,128,128]{2,1,0:T(8,128)(2,1)S(1)}, u32[]{:S(2)}, u32[]{:S(2)}) %collective-permute-start.3) | collective-permute-done | bytes 524320 | tf_op jit(solution)/shard_map/ppermute | solution.py:194
  30.0 0.1 add_convert_fusion.1
  30.2 2.7 %collective-permute-start.4 = (bf16[16,128,128]{2,1,0:T(8,128)(2,1)S(1)}, bf16[16,128,128]{2,1,0:T(8,128)(2,1)S(1)}, u32[]{:S(2)}, u32[]{:S(2)}) collective-permute-start(bf16[16,128,128]{2,1,0:T(8,128)(2,1)S(1)} %add_convert_fusion.1), channel_id=1, source_target_pairs={{0,8},{4,28},{8,16},{12,4},{16,24},{20,12},{24,0},{28,20},{1,9},{5... | collective-permute-start | bytes 1572872 | tf_op jit(solution)/shard_map/ppermute | solution.py:198
  32.8 4.5 %collective-permute-done.2 = bf16[16,128,128]{2,1,0:T(8,128)(2,1)S(1)} collective-permute-done((bf16[16,128,128]{2,1,0:T(8,128)(2,1)S(1)}, bf16[16,128,128]{2,1,0:T(8,128)(2,1)S(1)}, u32[]{:S(2)}, u32[]{:S(2)}) %collective-permute-start.2) | collective-permute-done | bytes 524320 | tf_op jit(solution)/shard_map/ppermute | solution.py:196
  37.3 4.8 %collective-permute-done.4 = bf16[16,128,128]{2,1,0:T(8,128)(2,1)S(1)} collective-permute-done((bf16[16,128,128]{2,1,0:T(8,128)(2,1)S(1)}, bf16[16,128,128]{2,1,0:T(8,128)(2,1)S(1)}, u32[]{:S(2)}, u32[]{:S(2)}) %collective-permute-start.4) | collective-permute-done | bytes 524320 | tf_op jit(solution)/shard_map/ppermute | solution.py:198
  42.1 0.2 add_convert_fusion
  42.3 0.0 copy-start.9
  42.4 29.7 %all_to_all.10.parts = bf16[16,128,128]{2,1,0:T(8,128)(2,1)S(1)} all-to-all(bf16[16,128,128]{2,1,0:T(8,128)(2,1)S(1)} %add_convert_fusion), channel_id=1, replica_groups=mesh['z'=16,'x'=4,'c'=2,'y'=4] {'z'}, dimensions={0} | all-to-all | bytes 1048576 | tf_op jit(solution)/shard_map/all_to_all | solution.py:200
  72.1 0.0 copy-done.9
  72.1 0.8 shard_map.107
  72.8 35.1 %all_to_all.11.g0 = bf16[16,128,128]{2,1,0:T(8,128)(2,1)S(1)} all-to-all(bf16[16,128,128]{2,1,0:T(8,128)(2,1)S(1)} %get-tuple-element.16), channel_id=1, replica_groups=mesh['z'=16,'x'=4,'c'=2,'y'=4] {'z'}, dimensions={0} | all-to-all | bytes 1048576 | tf_op jit(solution)/shard_map/all_to_all | solution.py:205
  107.9 8.1 %collective-permute-start.6 = (bf16[16,128,128]{2,1,0:T(8,128)(2,1)S(1)}, bf16[16,128,128]{2,1,0:T(8,128)(2,1)S(1)}, u32[]{:S(2)}, u32[]{:S(2)}) collective-permute-start(bf16[16,128,128]{2,1,0:T(8,128)(2,1)S(1)} %all_to_all.11.g0), channel_id=1, source_target_pairs={{0,8},{4,28},{8,16},{12,4},{16,24},{20,12},{24,0},{28,20},{1,9},{5... | collective-permute-start | bytes 1572872 | tf_op jit(solution)/shard_map/ppermute | solution.py:206
  116.0 1.9 %collective-permute-start.5 = (bf16[16,128,128]{2,1,0:T(8,128)(2,1)S(1)}, bf16[16,128,128]{2,1,0:T(8,128)(2,1)S(1)}, u32[]{:S(2)}, u32[]{:S(2)}) collective-permute-start(bf16[16,128,128]{2,1,0:T(8,128)(2,1)S(1)} %all_to_all.11.g0), channel_id=1, source_target_pairs={{8,0},{28,4},{16,8},{4,12},{24,16},{12,20},{0,24},{20,28},{9,1},{2... | collective-permute-start | bytes 1572872 | tf_op jit(solution)/shard_map/ppermute | solution.py:207
  117.9 4.2 %collective-permute-done.6.g3 = bf16[16,128,128]{2,1,0:T(8,128)(2,1)S(1)} collective-permute-done((bf16[16,128,128]{2,1,0:T(8,128)(2,1)S(1)}, bf16[16,128,128]{2,1,0:T(8,128)(2,1)S(1)}, u32[]{:S(2)}, u32[]{:S(2)}) %collective-permute-start.6) | collective-permute-done | bytes 524320 | tf_op jit(solution)/shard_map/ppermute | solution.py:206
  122.1 5.0 %collective-permute-start.7 = (bf16[16,128,128]{2,1,0:T(8,128)(2,1)S(1)}, bf16[16,128,128]{2,1,0:T(8,128)(2,1)S(1)}, u32[]{:S(2)}, u32[]{:S(2)}) collective-permute-start(bf16[16,128,128]{2,1,0:T(8,128)(2,1)S(1)} %collective-permute-done.6.g3), channel_id=1, source_target_pairs={{0,8},{4,28},{8,16},{12,4},{16,24},{20,12},{24,0},{28,20},{1,9},{5... | collective-permute-start | bytes 1572872 | tf_op jit(solution)/shard_map/ppermute | solution.py:208
  127.1 3.1 %collective-permute-done.5.g1 = bf16[16,128,128]{2,1,0:T(8,128)(2,1)S(1)} collective-permute-done((bf16[16,128,128]{2,1,0:T(8,128)(2,1)S(1)}, bf16[16,128,128]{2,1,0:T(8,128)(2,1)S(1)}, u32[]{:S(2)}, u32[]{:S(2)}) %collective-permute-start.5) | collective-permute-done | bytes 524320 | tf_op jit(solution)/shard_map/ppermute | solution.py:207
  130.2 7.0 %collective-permute-done.7.g2 = bf16[16,128,128]{2,1,0:T(8,128)(2,1)S(1)} collective-permute-done((bf16[16,128,128]{2,1,0:T(8,128)(2,1)S(1)}, bf16[16,128,128]{2,1,0:T(8,128)(2,1)S(1)}, u32[]{:S(2)}, u32[]{:S(2)}) %collective-permute-start.7) | collective-permute-done | bytes 524320 | tf_op jit(solution)/shard_map/ppermute | solution.py:208
  137.2 2.7 %shard_map.108 = (f32[512,128]{1,0:T(8,128)S(1)}, bf16[512,128]{1,0:T(8,128)(2,1)S(1)}) custom-call(s32[2]{0:T(128)S(1)} %pad_add_fusion.me, s32[16]{0:T(128)S(1)} %get-tuple-element.11.code0, s32[16]{0:T(128)S(1)} %add_bitcast_fusion.code1, bf16[16,128,128]{2,1,0:T(8,128)(2,1)S(1)} %bitcast.11, bf16[16,128,128]{2,1,0:T(8,128)(2,1)S(1)} %collective-permute-done.1.w1, ...), custom_call_target="tpu_custom_call" | custom-call | flops 41943040 | bytes 4194304 | tf_op jit(solution)/shard_map/pallas_call | solution.py:209
  139.9 10.1 %collective-permute-start.8 = (bf16[512,128]{1,0:T(8,128)(2,1)S(1)}, bf16[512,128]{1,0:T(8,128)(2,1)S(1)}, u32[]{:S(2)}, u32[]{:S(2)}) collective-permute-start(bf16[512,128]{1,0:T(8,128)(2,1)S(1)} %get-tuple-element.18), channel_id=1, source_target_pairs={{0,4},{4,0},{1,5},{5,1},{2,6},{6,2},{3,7},{7,3},{8,12},{12,8},{9,1... | collective-permute-start | bytes 393224 | tf_op jit(solution)/shard_map/ppermute | solution.py:218
  150.0 1.0 collective-permute-done.8
  151.0 5.7 %collective-permute-start.11 = (bf16[512,128]{1,0:T(8,128)(2,1)S(1)}, bf16[512,128]{1,0:T(8,128)(2,1)S(1)}, u32[]{:S(2)}, u32[]{:S(2)}) collective-permute-start(bf16[512,128]{1,0:T(8,128)(2,1)S(1)} %add_convert_fusion.2.t0), channel_id=1, source_target_pairs={{0,3},{1,0},{2,1},{3,2},{4,7},{5,4},{6,5},{7,6},{8,11},{9,8},{10,9... | collective-permute-start | bytes 393224 | tf_op jit(solution)/shard_map/ppermute | solution.py:222
  156.7 1.9 %collective-permute-start.10 = (bf16[512,128]{1,0:T(8,128)(2,1)S(1)}, bf16[512,128]{1,0:T(8,128)(2,1)S(1)}, u32[]{:S(2)}, u32[]{:S(2)}) collective-permute-start(bf16[512,128]{1,0:T(8,128)(2,1)S(1)} %add_convert_fusion.2.t0), channel_id=1, source_target_pairs={{0,2},{1,3},{2,0},{3,1},{4,6},{5,7},{6,4},{7,5},{8,10},{9,11},{10,... | collective-permute-start | bytes 393224 | tf_op jit(solution)/shard_map/ppermute | solution.py:222
  158.7 2.5 %collective-permute-start.9 = (bf16[512,128]{1,0:T(8,128)(2,1)S(1)}, bf16[512,128]{1,0:T(8,128)(2,1)S(1)}, u32[]{:S(2)}, u32[]{:S(2)}) collective-permute-start(bf16[512,128]{1,0:T(8,128)(2,1)S(1)} %add_convert_fusion.2.t0), channel_id=1, source_target_pairs={{0,1},{1,2},{2,3},{3,0},{4,5},{5,6},{6,7},{7,4},{8,9},{9,10},{10,1... | collective-permute-start | bytes 393224 | tf_op jit(solution)/shard_map/ppermute | solution.py:222
  161.2 0.0 collective-permute-done.11.t3
  161.2 3.4 %collective-permute-done.10.t2 = bf16[512,128]{1,0:T(8,128)(2,1)S(1)} collective-permute-done((bf16[512,128]{1,0:T(8,128)(2,1)S(1)}, bf16[512,128]{1,0:T(8,128)(2,1)S(1)}, u32[]{:S(2)}, u32[]{:S(2)}) %collective-permute-start.10) | collective-permute-done | bytes 131104 | tf_op jit(solution)/shard_map/ppermute | solution.py:222
  164.5 3.5 %collective-permute-done.9.t1 = bf16[512,128]{1,0:T(8,128)(2,1)S(1)} collective-permute-done((bf16[512,128]{1,0:T(8,128)(2,1)S(1)}, bf16[512,128]{1,0:T(8,128)(2,1)S(1)}, u32[]{:S(2)}, u32[]{:S(2)}) %collective-permute-start.9) | collective-permute-done | bytes 131104 | tf_op jit(solution)/shard_map/ppermute | solution.py:222
  168.0 0.9 shard_map.109
  (10 shorter events, 0.1 us)
Async XLA Ops:
  0.6 0.7 copy-start.4
  1.3 0.7 copy-start.6
  1.3 0.7 copy-start.7
  1.3 0.7 copy-start.8
  2.0 0.9 copy-start.2
  4.1 10.8 %collective-permute-start = (bf16[528,128]{1,0:T(8,128)(2,1)S(1)}, bf16[528,128]{1,0:T(8,128)(2,1)S(1)}, u32[]{:S(2)}, u32[]{:S(2)}) collective-permute-start(bf16[528,128]{1,0:T(8,128)(2,1)S(1)} %get-tuple-element.12.x0), channel_id=1, source_target_pairs={{0,4},{4,0},{1,5},{5,1},{2,6},{6,2},{3,7},{7,3},{8,12},{12,8},{9,1... | collective-permute-start | bytes 405512 | tf_op jit(solution)/shard_map/ppermute | solution.py:175
  12.9 4.0 %collective-permute-start.1 = (bf16[16,128,128]{2,1,0:T(8,128)(2,1)}, bf16[16,128,128]{2,1,0:T(8,128)(2,1)S(1)}, u32[]{:S(2)}, u32[]{:S(2)}) collective-permute-start(bf16[16,128,128]{2,1,0:T(8,128)(2,1)} %bitcast.8), channel_id=1, source_target_pairs={{0,4},{4,0},{1,5},{5,1},{2,6},{6,2},{3,7},{7,3},{8,12},{12,8},{9,1... | collective-permute-start | bytes 1572872 | tf_op jit(solution)/shard_map/ppermute | solution.py:160
  16.9 1.0 copy-start
  19.6 10.4 %collective-permute-start.3 = (bf16[16,128,128]{2,1,0:T(8,128)(2,1)S(1)}, bf16[16,128,128]{2,1,0:T(8,128)(2,1)S(1)}, u32[]{:S(2)}, u32[]{:S(2)}) collective-permute-start(bf16[16,128,128]{2,1,0:T(8,128)(2,1)S(1)} %shard_map.106), channel_id=1, source_target_pairs={{0,8},{4,28},{8,16},{12,4},{16,24},{20,12},{24,0},{28,20},{1,9},{5... | collective-permute-start | bytes 1572872 | tf_op jit(solution)/shard_map/ppermute | solution.py:194
  24.9 12.4 %collective-permute-start.2 = (bf16[16,128,128]{2,1,0:T(8,128)(2,1)S(1)}, bf16[16,128,128]{2,1,0:T(8,128)(2,1)S(1)}, u32[]{:S(2)}, u32[]{:S(2)}) collective-permute-start(bf16[16,128,128]{2,1,0:T(8,128)(2,1)S(1)} %get-tuple-element.14), channel_id=1, source_target_pairs={{8,0},{28,4},{16,8},{4,12},{24,16},{12,20},{0,24},{20,28},{9,1},{2... | collective-permute-start | bytes 1572872 | tf_op jit(solution)/shard_map/ppermute | solution.py:196
  30.2 11.9 %collective-permute-start.4 = (bf16[16,128,128]{2,1,0:T(8,128)(2,1)S(1)}, bf16[16,128,128]{2,1,0:T(8,128)(2,1)S(1)}, u32[]{:S(2)}, u32[]{:S(2)}) collective-permute-start(bf16[16,128,128]{2,1,0:T(8,128)(2,1)S(1)} %add_convert_fusion.1), channel_id=1, source_target_pairs={{0,8},{4,28},{8,16},{12,4},{16,24},{20,12},{24,0},{28,20},{1,9},{5... | collective-permute-start | bytes 1572872 | tf_op jit(solution)/shard_map/ppermute | solution.py:198
  42.3 29.7 %copy-start.9 = (s32[1,128]{1,0:T(1,128)S(1)}, s32[1,128]{1,0:T(1,128)}, u32[]{:S(2)}) copy-start(s32[1,128]{1,0:T(1,128)} %degree.1) | copy-start | bytes 1540
  72.8 64.4 %copy-start.1 = (bf16[1,16,128,128]{3,2,1,0:T(8,128)(2,1)S(1)}, bf16[1,16,128,128]{3,2,1,0:T(8,128)(2,1)}, u32[]{:S(2)}) copy-start(bf16[1,16,128,128]{3,2,1,0:T(8,128)(2,1)} %param.13) | copy-start | bytes 1572868
  107.9 14.2 %collective-permute-start.6 = (bf16[16,128,128]{2,1,0:T(8,128)(2,1)S(1)}, bf16[16,128,128]{2,1,0:T(8,128)(2,1)S(1)}, u32[]{:S(2)}, u32[]{:S(2)}) collective-permute-start(bf16[16,128,128]{2,1,0:T(8,128)(2,1)S(1)} %all_to_all.11.g0), channel_id=1, source_target_pairs={{0,8},{4,28},{8,16},{12,4},{16,24},{20,12},{24,0},{28,20},{1,9},{5... | collective-permute-start | bytes 1572872 | tf_op jit(solution)/shard_map/ppermute | solution.py:206
  116.0 14.3 %collective-permute-start.5 = (bf16[16,128,128]{2,1,0:T(8,128)(2,1)S(1)}, bf16[16,128,128]{2,1,0:T(8,128)(2,1)S(1)}, u32[]{:S(2)}, u32[]{:S(2)}) collective-permute-start(bf16[16,128,128]{2,1,0:T(8,128)(2,1)S(1)} %all_to_all.11.g0), channel_id=1, source_target_pairs={{8,0},{28,4},{16,8},{4,12},{24,16},{12,20},{0,24},{20,28},{9,1},{2... | collective-permute-start | bytes 1572872 | tf_op jit(solution)/shard_map/ppermute | solution.py:207
  122.1 15.1 %collective-permute-start.7 = (bf16[16,128,128]{2,1,0:T(8,128)(2,1)S(1)}, bf16[16,128,128]{2,1,0:T(8,128)(2,1)S(1)}, u32[]{:S(2)}, u32[]{:S(2)}) collective-permute-start(bf16[16,128,128]{2,1,0:T(8,128)(2,1)S(1)} %collective-permute-done.6.g3), channel_id=1, source_target_pairs={{0,8},{4,28},{8,16},{12,4},{16,24},{20,12},{24,0},{28,20},{1,9},{5... | collective-permute-start | bytes 1572872 | tf_op jit(solution)/shard_map/ppermute | solution.py:208
  139.9 11.1 %collective-permute-start.8 = (bf16[512,128]{1,0:T(8,128)(2,1)S(1)}, bf16[512,128]{1,0:T(8,128)(2,1)S(1)}, u32[]{:S(2)}, u32[]{:S(2)}) collective-permute-start(bf16[512,128]{1,0:T(8,128)(2,1)S(1)} %get-tuple-element.18), channel_id=1, source_target_pairs={{0,4},{4,0},{1,5},{5,1},{2,6},{6,2},{3,7},{7,3},{8,12},{12,8},{9,1... | collective-permute-start | bytes 393224 | tf_op jit(solution)/shard_map/ppermute | solution.py:218
  151.0 17.1 %copy-start.3 = (bf16[512,128]{1,0:T(8,128)(2,1)S(1)}, bf16[512,128]{1,0:T(8,128)(2,1)}, u32[]{:S(2)}) copy-start(bf16[512,128]{1,0:T(8,128)(2,1)} %scores.3) | copy-start | bytes 393220
  151.0 17.1 %copy-start.5 = (s32[512]{0:T(512)S(1)}, s32[512]{0:T(512)}, u32[]{:S(2)}) copy-start(s32[512]{0:T(512)} %param.10) | copy-start | bytes 6148
  151.0 10.2 %collective-permute-start.11 = (bf16[512,128]{1,0:T(8,128)(2,1)S(1)}, bf16[512,128]{1,0:T(8,128)(2,1)S(1)}, u32[]{:S(2)}, u32[]{:S(2)}) collective-permute-start(bf16[512,128]{1,0:T(8,128)(2,1)S(1)} %add_convert_fusion.2.t0), channel_id=1, source_target_pairs={{0,3},{1,0},{2,1},{3,2},{4,7},{5,4},{6,5},{7,6},{8,11},{9,8},{10,9... | collective-permute-start | bytes 393224 | tf_op jit(solution)/shard_map/ppermute | solution.py:222
  156.7 7.8 %collective-permute-start.10 = (bf16[512,128]{1,0:T(8,128)(2,1)S(1)}, bf16[512,128]{1,0:T(8,128)(2,1)S(1)}, u32[]{:S(2)}, u32[]{:S(2)}) collective-permute-start(bf16[512,128]{1,0:T(8,128)(2,1)S(1)} %add_convert_fusion.2.t0), channel_id=1, source_target_pairs={{0,2},{1,3},{2,0},{3,1},{4,6},{5,7},{6,4},{7,5},{8,10},{9,11},{10,... | collective-permute-start | bytes 393224 | tf_op jit(solution)/shard_map/ppermute | solution.py:222
  158.7 9.4 %collective-permute-start.9 = (bf16[512,128]{1,0:T(8,128)(2,1)S(1)}, bf16[512,128]{1,0:T(8,128)(2,1)S(1)}, u32[]{:S(2)}, u32[]{:S(2)}) collective-permute-start(bf16[512,128]{1,0:T(8,128)(2,1)S(1)} %add_convert_fusion.2.t0), channel_id=1, source_target_pairs={{0,1},{1,2},{2,3},{3,0},{4,5},{5,6},{6,7},{7,4},{8,9},{9,10},{10,1... | collective-permute-start | bytes 393224 | tf_op jit(solution)/shard_map/ppermute | solution.py:222

commit v3 on v2

v3 whole, which is shorter than its diff:
```python
import functools
import jax
import jax.numpy as jnp
from jax import lax
from jax.experimental import pallas as pl
from jax.experimental.pallas import tpu as pltpu
from jax.sharding import Mesh, PartitionSpec as P

ALPHA = 0.8
ACCT = ("zh", "zl", "x", "c")
SIDE = 128
SLOTS = 16
ROWS = 512
LINE = 16
MEBI = 2**20

SWAP = [(0, 1), (1, 0)]
TILES = SLOTS * SIDE
SENT = TILES + ROWS + SLOTS
FOUR = 4 * SIDE
FIRST = [(2 * h + c, 2 * (3 - h if c else h ^ 1) + c) for h in range(4) for c in range(2)]
SECOND = [(2 * h + c, 2 * (h ^ 1 if c else 3 - h) + c) for h in range(4) for c in range(2)]


def shift(n):
    return [(i, (i + n) % 4) for i in range(4)]


def place(code, me):
    owner = code & 127
    z = owner >> 3
    away = (((owner >> 1) & 3) - me[0]) & 3
    taken = ((code >> 9) == 1) & ((owner & 1) == me[1])
    return taken, away, (z & 3) * 4 + (z >> 2), (code >> 7) & 3


def column(row):
    return jnp.broadcast_to(row, (SIDE, SIDE)).T


def prepare_kernel(table, attr, acct, count, weights, scores, degree, payload, code):
    lane = lax.broadcasted_iota(jnp.int32, (SLOTS, SIDE), 1)
    tail = jnp.zeros((SLOTS, SIDE), jnp.int32)
    for s in range(SLOTS):
        owner = table[0, attr[0, s]]
        placing = acct[0, s] + jnp.where(s < count[0, 0], 4, 0)
        code[s] = owner + placing * 128
        tail = jnp.where(lane == s, owner, tail)
        tail = jnp.where(lane == s + SLOTS, placing, tail)
        payload[s * SIDE : (s + 1) * SIDE, :] = weights[0, s]
    payload[TILES + ROWS :, :] = tail.astype(jnp.float32).astype(payload.dtype)
    for n in range(4):
        rows = pl.ds(n * SIDE, SIDE)
        scale = column(lax.rsqrt(degree[n : n + 1, :].astype(jnp.float32)))
        scaled = scores[rows, :].astype(jnp.float32) * scale
        payload[pl.ds(TILES + n * SIDE, SIDE), :] = scaled.astype(payload.dtype)


def tile(sent, s):
    return sent[pl.ds(pl.multiple_of(s * SIDE, SIDE), SIDE), :]


def forward_kernel(offsets, me, code0, code1, sent0, sent1, *refs):
    outs, acc = refs[:-1], refs[-1]
    acc[...] = jnp.zeros_like(acc)
    for code, sent in ((code0, sent0), (code1, sent1)):

        def step(s, carry, code=code, sent=sent):
            taken, away, along, block = place(code[s], me)
            index = jnp.int32(0)
            wanted = jnp.bool_(False)
            for n, offset in enumerate(offsets):
                index = jnp.where(away == offset, n * LINE, index)
                wanted = wanted | (away == offset)

            @pl.when(taken & wanted)
            def _():
                acc[index + along] += lax.dot_general(
                    tile(sent, s),
                    tile(sent, SLOTS + block),
                    (((0,), (0,)), ((), ())),
                    preferred_element_type=jnp.float32,
                )

            return carry

        lax.fori_loop(0, SLOTS, step, 0)
    for n, out in enumerate(outs):
        out[...] = acc[n * LINE : (n + 1) * LINE].astype(out.dtype)


def near_kernel(me, parts, degree, sums):
    for n in range(4):
        total = parts[0, n].astype(jnp.float32)
        for k in range(1, 4):
            total += parts[k, n].astype(jnp.float32)
        sums[n * SIDE : (n + 1) * SIDE, :] = total.astype(sums.dtype)
    row = lax.broadcasted_iota(jnp.int32, (SLOTS, SIDE), 0)
    mine = jnp.where(row == me[2], degree[...].astype(jnp.float32), 0.0)
    sums[FOUR:, :] = mine.astype(sums.dtype)


def far_kernel(me, mine, other, own, scores):
    degree = mine[FOUR:, :].astype(jnp.float32) + other[FOUR:, :].astype(jnp.float32)
    for n in range(4):
        rows = pl.ds(n * SIDE, SIDE)
        total = mine[rows, :].astype(jnp.float32) + other[rows, :].astype(jnp.float32)
        scale = column(lax.rsqrt(degree[n : n + 1, :]))
        scores[rows, :] = (total * scale).astype(scores.dtype)
    own[...] = scores[pl.ds(pl.multiple_of(me[2] * SIDE, SIDE), SIDE), :]


def backward_kernel(me, code0, code1, sent0, sent1, g0, g1, g2, g3, mine, other, acc):
    acc[...] = jnp.zeros_like(acc)
    for half, (code, sent) in enumerate(((code0, sent0), (code1, sent1))):

        def step(s, carry, half=half, code=code, sent=sent):
            taken, away, along, block = place(code[s], me)
            for n, blocks in enumerate((g0, g1, g2, g3)):

                @pl.when(taken & (away == n))
                def _(blocks=blocks):
                    start = pl.multiple_of(half * ROWS + block * SIDE, SIDE)
                    acc[pl.ds(start, SIDE), :] += jnp.dot(
                        tile(sent, s), tile(blocks, along), preferred_element_type=jnp.float32
                    )

            return carry

        lax.fori_loop(0, SLOTS, step, 0)
    mine[...] = acc[:ROWS]
    other[...] = acc[ROWS:].astype(other.dtype)


def finish_kernel(types, scores, degree, seed, new):
    for n in range(4):
        rows = pl.ds(n * SIDE, SIDE)
        scale = column(lax.rsqrt(degree[n : n + 1, :].astype(jnp.float32)))
        prior = scores[rows, :].astype(jnp.float32)
        whole = types[0, rows, :].astype(jnp.float32)
        for k in range(1, 4):
            whole += types[k, rows, :].astype(jnp.float32)
        mixed = ALPHA * (whole * scale) + (1.0 - ALPHA) * prior
        kept = column(seed[n : n + 1, :].astype(jnp.float32))
        new[rows, :] = jnp.where(kept == 1.0, prior, mixed)


def smem(n):
    return [pl.BlockSpec(memory_space=pltpu.SMEM)] * n


def vmem(n):
    return [pl.BlockSpec(memory_space=pltpu.VMEM)] * n


def call(kernel, outs, specs, scratch, flops, moved, out_specs=None):
    return pl.pallas_call(
        kernel,
        out_shape=outs,
        in_specs=specs,
        out_specs=out_specs or vmem(len(outs)),
        scratch_shapes=scratch,
        compiler_params=pltpu.CompilerParams(vmem_limit_bytes=24 * MEBI),
        cost_estimate=pl.CostEstimate(flops=flops, bytes_accessed=moved, transcendentals=0),
    )


def per_device(
    scores0,
    seed_mask,
    acct_degree,
    attr_degree,
    tile_weight,
    tile_acct,
    tile_attr,
    attr_owner,
    tile_count,
):
    bf16, f32, i32 = jnp.bfloat16, jnp.float32, jnp.int32
    group = jax.ShapeDtypeStruct((LINE, SIDE, SIDE), bf16)
    degree = acct_degree.reshape(4, SIDE)
    payload, code = call(
        prepare_kernel,
        [jax.ShapeDtypeStruct((SENT, SIDE), bf16), jax.ShapeDtypeStruct((SLOTS,), i32)],
        smem(4) + vmem(3),
        [],
        ROWS * SIDE,
        MEBI,
        vmem(1) + smem(1),
    )(attr_owner, tile_attr, tile_acct, tile_count, tile_weight, scores0, degree)
    payload1 = lax.ppermute(payload, "c", SWAP)
    tail1 = payload1[TILES + ROWS].astype(i32)
    code1 = tail1[:SLOTS] + tail1[SLOTS : 2 * SLOTS] * 128
    me = jnp.stack([lax.axis_index(axis) for axis in ("x", "c", "zh")]).astype(i32)

    tiles = 2 * 10 * SIDE**3
    slots = (me, code, code1, payload, payload1)

    def forward(offsets):
        return call(
            functools.partial(forward_kernel, offsets),
            [group] * len(offsets),
            smem(3) + vmem(2),
            [pltpu.VMEM((len(offsets) * LINE, SIDE, SIDE), f32)],
            tiles,
            3 * MEBI,
        )(*slots)

    (o2,) = forward((2,))
    r2 = lax.ppermute(o2, "x", shift(2))
    o1, o3, o0 = forward((1, 3, 0))
    r1 = lax.ppermute(o1, "x", shift(1))
    r3 = lax.ppermute(o3, "x", shift(3))
    line = o0.astype(f32) + r1.astype(f32) + r2.astype(f32) + r3.astype(f32)
    line = line.astype(bf16).reshape(4, 4, SIDE, SIDE)
    line = lax.all_to_all(line, "zl", 0, 0, tiled=True)
    sums = jax.ShapeDtypeStruct((FOUR + SLOTS, SIDE), bf16)
    (near,) = call(
        near_kernel, [sums], smem(1) + vmem(2), [], SIDE * SIDE * LINE, MEBI
    )(me, line, attr_degree)
    half = near.astype(f32) + lax.ppermute(near, ("zh", "c"), FIRST).astype(f32)
    half = half.astype(bf16)
    rest = lax.ppermute(half, ("zh", "c"), SECOND)
    own_scores, scores = call(
        far_kernel,
        [jax.ShapeDtypeStruct((SIDE, SIDE), bf16), jax.ShapeDtypeStruct((FOUR, SIDE), bf16)],
        smem(1) + vmem(2),
        [],
        SIDE * SIDE * LINE,
        MEBI // 2,
    )(me, half, rest)

    g0 = lax.all_gather(scores, "zl", axis=0, tiled=True)
    g2 = lax.ppermute(g0, "x", shift(2))
    g3 = lax.ppermute(g0, "x", shift(1))
    g1 = lax.ppermute(g0, "x", shift(3))
    mine, other = call(
        backward_kernel,
        [jax.ShapeDtypeStruct((ROWS, SIDE), f32), jax.ShapeDtypeStruct((ROWS, SIDE), bf16)],
        smem(3) + vmem(6),
        [pltpu.VMEM((2 * ROWS, SIDE), f32)],
        tiles,
        4 * MEBI,
    )(*slots, g0, g1, g2, g3)

    returned = (mine + lax.ppermute(other, "c", SWAP).astype(f32)).astype(bf16)
    types = jnp.broadcast_to(returned[None], (4, ROWS, SIDE))
    types = lax.all_to_all(types, "y", 0, 0, tiled=True)
    (new_scores,) = call(
        finish_kernel,
        [jax.ShapeDtypeStruct((ROWS, SIDE), f32)],
        vmem(4),
        [],
        ROWS * SIDE * 8,
        MEBI,
    )(types, scores0, degree, seed_mask.reshape(4, SIDE))
    return (new_scores, own_scores[None])


def solution(mesh):
    fine = Mesh(mesh.devices.reshape(4, 4, 4, 2, 4), ACCT + ("y",))
    placed = (
        P(ACCT, None),
        P(ACCT),
        P(ACCT),
        P("y", ACCT),
        P("y", ACCT, None, None),
        P("y", ACCT),
        P("y", ACCT),
        P("y", None),
        P("y", ACCT),
    )
    return jax.shard_map(
        per_device,
        mesh=fine,
        in_specs=placed,
        out_specs=(P(ACCT, None), P("y", ACCT, None)),
        check_vma=False,
    )
```

time: 172 us -> 156 us (0.907)
  blocking collectives: 64.8 us -> 42.2 us
  waiting for transfers between devices: 35.2 us -> 45.5 us
  starting transfers between devices: 53.7 us -> 47.4 us
  Pallas kernels: 10.6 us -> 14 us
    all_to_all x2, blocking collectives: 64.8 us -> 30 us  [the longest x1 16.6 us: per_device(): line = lax.all_to_all(line, 'zl', 0, 0, tiled=True)]
    all_gather x0 -> x1, blocking collectives: none -> 12.2 us  [per_device(): g0 = lax.all_gather(scores, 'zl', axis=0, tiled=True)]
    ppermute x10 -> x8, waiting for transfers between devices: 34.2 us -> 42.9 us  [the longest x1 12 us: per_device(): g2 = lax.ppermute(g0, 'x', shift(2))]
    ppermute x1, starting transfers between devices: 10.1 us -> 4.21 us  [per_device(): returned = (mine + lax.ppermute(other, 'c', SWAP).astype(f32)).astype(bf16)]
    pallas_call x3 -> x4, Pallas kernels: 2.9 us -> 4.06 us  [the longest x1 1.3 us: per_device(): call(far_kernel, [jax.ShapeDtypeStruct((SIDE, SIDE), bf16), jax.ShapeDtyp...]
    ppermute x10 -> x8, starting transfers between devices: 34.9 us -> 34.4 us  [the longest x1 7.7 us: per_device(): half = near.astype(f32) + lax.ppermute(near, ('zh', 'c'), FIRST).astype(f32)]
  transfers between devices with their start and end apart: 12 -> 10, of which waited for: 10 -> 9; matrix products, arithmetic and copies ran while one was open for 0% -> 0% of each run, Pallas kernels for 2% -> 3%
where the time goes in v3:
time: 156 us; the launch traced here: 154 us
  starting transfers between devices  47.4 us (30%)
  waiting for transfers between devices  45.5 us (29%)
  blocking collectives  42.2 us (27%)
  Pallas kernels  14 us (9%)
  local copies, waits for them, and re-layouts  2.69 us (2%)
    all_to_all x1, blocking collectives, per_device(): line = lax.all_to_all(line, 'zl', 0, 0, tiled=True)  16.6 us
    all_to_all x1, blocking collectives, per_device(): types = lax.all_to_all(types, 'y', 0, 0, tiled=True)  13.4 us
    all_gather x1, blocking collectives, per_device(): g0 = lax.all_gather(scores, 'zl', axis=0, tiled=True)  12.2 us
    ppermute x1, waiting for transfers between devices, per_device(): g2 = lax.ppermute(g0, 'x', shift(2))  12 us
    ppermute x1, waiting for transfers between devices, per_device(): r1 = lax.ppermute(o1, 'x', shift(1))  11.9 us
    ppermute x1, starting transfers between devices, per_device(): payload1 = lax.ppermute(payload, 'c', SWAP)  8.79 us
    ppermute x1, starting transfers between devices, per_device(): half = near.astype(f32) + lax.ppermute(near, ('zh', 'c'), FIRST).astype(f32)  7.7 us
    ppermute x1, starting transfers between devices, per_device(): rest = lax.ppermute(half, ('zh', 'c'), SECOND)  7.43 us
  transfers between devices with their start and end apart: 10, of which 9 were waited for; matrix products, arithmetic and copies ran while one was open for 0% of the time, Pallas kernels for 3%

profile of v3, /device:TPU:1, one launch (start us, length us, event | category | flops | bytes accessed | tf_op | source)
XLA Modules:
  0.0 153.9 jit_solution(3300409767228075039)
XLA Ops:
  0.6 0.0 copy-start.3
  1.3 0.0 copy-start.5
  1.3 0.0 copy-start.6
  1.3 0.0 copy-start.7
  1.3 0.0 copy-done.3
  1.3 0.6 copy-done.5
  2.0 0.0 copy-done.6
  2.0 0.0 copy-done.7
  2.0 0.9 copy-done
  2.9 1.0 copy-done.2
  3.9 1.2 shard_map.104
  5.2 8.8 %collective-permute-start = (bf16[2576,128]{1,0:T(8,128)(2,1)S(1)}, bf16[2576,128]{1,0:T(8,128)(2,1)S(1)}, u32[]{:S(2)}, u32[]{:S(2)}) collective-permute-start(bf16[2576,128]{1,0:T(8,128)(2,1)S(1)} %get-tuple-element.12.sent0), channel_id=1, source_target_pairs={{0,4},{4,0},{1,5},{5,1},{2,6},{6,2},{3,7},{7,3},{8,12},{12,8},{9,1... | collective-permute-start | bytes 1978376 | tf_op jit(solution)/shard_map/ppermute | solution.py:191
  14.0 0.1 pad_add_fusion.me
  14.1 1.6 %collective-permute-done.sent1 = bf16[2576,128]{1,0:T(8,128)(2,1)S(1)} collective-permute-done((bf16[2576,128]{1,0:T(8,128)(2,1)S(1)}, bf16[2576,128]{1,0:T(8,128)(2,1)S(1)}, u32[]{:S(2)}, u32[]{:S(2)}) %collective-permute-start) | collective-permute-done | bytes 659488 | tf_op jit(solution)/shard_map/ppermute | solution.py:191
  15.7 0.1 add_bitcast_fusion.code1
  15.8 1.6 %shard_map.106 = bf16[16,128,128]{2,1,0:T(8,128)(2,1)S(1)} custom-call(s32[3]{0:T(128)S(1)} %pad_add_fusion.me, s32[16]{0:T(128)S(1)} %get-tuple-element.11.code0, s32[16]{0:T(128)S(1)} %add_bitcast_fusion.code1, bf16[2576,128]{1,0:T(8,128)(2,1)S(1)} %get-tuple-element.12.sent0, bf16[2576,128]{1,0:T(8,128)(2,1)S(1)} %collective-permute-done.sent1), custom_call_target="tpu_custom_call" | custom-call | flops 41943040 | bytes 3145728 | tf_op jit(solution)/shard_map/pallas_call | solution.py:200
  17.4 1.9 %collective-permute-start.2 = (bf16[16,128,128]{2,1,0:T(8,128)(2,1)S(1)}, bf16[16,128,128]{2,1,0:T(8,128)(2,1)S(1)}, u32[]{:S(2)}, u32[]{:S(2)}) collective-permute-start(bf16[16,128,128]{2,1,0:T(8,128)(2,1)S(1)} %shard_map.106), channel_id=1, source_target_pairs={{0,16},{8,24},{16,0},{24,8},{1,17},{9,25},{17,1},{25,9},{2,18},{10... | collective-permute-start | bytes 1572872 | tf_op jit(solution)/shard_map/ppermute | solution.py:210
  19.3 4.8 %shard_map.105 = (bf16[16,128,128]{2,1,0:T(8,128)(2,1)S(1)}, bf16[16,128,128]{2,1,0:T(8,128)(2,1)S(1)}, bf16[16,128,128]{2,1,0:T(8,128)(2,1)S(1)}) custom-call(s32[3]{0:T(128)S(1)} %pad_add_fusion.me, s32[16]{0:T(128)S(1)} %get-tuple-element.11.code0, s32[16]{0:T(128)S(1)} %add_bitcast_fusion.code1, bf16[2576,128]{1,0:T(8,128)(2,1)S(1)} %get-tuple-element.12.sent0, ...), custom_call_target="tpu_custom_call" | custom-call | flops 41943040 | bytes 3145728 | tf_op jit(solution)/shard_map/pallas_call | solution.py:200
  24.1 1.9 %collective-permute-start.1 = (bf16[16,128,128]{2,1,0:T(8,128)(2,1)S(1)}, bf16[16,128,128]{2,1,0:T(8,128)(2,1)S(1)}, u32[]{:S(2)}, u32[]{:S(2)}) collective-permute-start(bf16[16,128,128]{2,1,0:T(8,128)(2,1)S(1)} %get-tuple-element.14), channel_id=1, source_target_pairs={{0,8},{8,16},{16,24},{24,0},{1,9},{9,17},{17,25},{25,1},{2,10},{10... | collective-permute-start | bytes 1572872 | tf_op jit(solution)/shard_map/ppermute | solution.py:212
  26.1 4.6 %collective-permute-start.3 = (bf16[16,128,128]{2,1,0:T(8,128)(2,1)S(1)}, bf16[16,128,128]{2,1,0:T(8,128)(2,1)S(1)}, u32[]{:S(2)}, u32[]{:S(2)}) collective-permute-start(bf16[16,128,128]{2,1,0:T(8,128)(2,1)S(1)} %get-tuple-element.15), channel_id=1, source_target_pairs={{0,24},{8,0},{16,8},{24,16},{1,25},{9,1},{17,9},{25,17},{2,26},{10... | collective-permute-start | bytes 1572872 | tf_op jit(solution)/shard_map/ppermute | solution.py:213
  30.7 3.3 %collective-permute-done.2 = bf16[16,128,128]{2,1,0:T(8,128)(2,1)S(1)} collective-permute-done((bf16[16,128,128]{2,1,0:T(8,128)(2,1)S(1)}, bf16[16,128,128]{2,1,0:T(8,128)(2,1)S(1)}, u32[]{:S(2)}, u32[]{:S(2)}) %collective-permute-start.2) | collective-permute-done | bytes 524320 | tf_op jit(solution)/shard_map/ppermute | solution.py:210
  34.0 11.9 %collective-permute-done.1 = bf16[16,128,128]{2,1,0:T(8,128)(2,1)S(1)} collective-permute-done((bf16[16,128,128]{2,1,0:T(8,128)(2,1)S(1)}, bf16[16,128,128]{2,1,0:T(8,128)(2,1)S(1)}, u32[]{:S(2)}, u32[]{:S(2)}) %collective-permute-start.1) | collective-permute-done | bytes 524320 | tf_op jit(solution)/shard_map/ppermute | solution.py:212
  45.9 0.0 collective-permute-done.3
  45.9 0.3 add_convert_fusion
  46.2 0.0 copy-start.8
  46.2 16.6 %all_to_all.10.parts = bf16[4,4,128,128]{3,2,1,0:T(8,128)(2,1)S(1)} all-to-all(bf16[4,4,128,128]{3,2,1,0:T(8,128)(2,1)S(1)} %bitcast.12), channel_id=1, replica_groups=mesh['zh'=4,'zl'=4,'x'=4,'c'=2,'y'=4] {'zl'}, dimensions={0} | all-to-all | bytes 1048576 | tf_op jit(solution)/shard_map/all_to_all | solution.py:216
  62.9 0.6 shard_map.107
  63.5 7.7 %collective-permute-start.4 = (bf16[528,128]{1,0:T(8,128)(2,1)S(1)}, bf16[528,128]{1,0:T(8,128)(2,1)S(1)}, u32[]{:S(2)}, u32[]{:S(2)}) collective-permute-start(bf16[528,128]{1,0:T(8,128)(2,1)S(1)} %shard_map.107), channel_id=1, source_target_pairs={{0,128},{4,388},{128,0},{132,260},{256,384},{260,132},{384,256},{3... | collective-permute-start | bytes 405512 | tf_op jit(solution)/shard_map/ppermute | solution.py:221
  71.2 5.6 %collective-permute-done.4 = bf16[528,128]{1,0:T(8,128)(2,1)S(1)} collective-permute-done((bf16[528,128]{1,0:T(8,128)(2,1)S(1)}, bf16[528,128]{1,0:T(8,128)(2,1)S(1)}, u32[]{:S(2)}, u32[]{:S(2)}) %collective-permute-start.4) | collective-permute-done | bytes 135200 | tf_op jit(solution)/shard_map/ppermute | solution.py:221
  76.8 7.4 %collective-permute-start.5 = (bf16[528,128]{1,0:T(8,128)(2,1)S(1)}, bf16[528,128]{1,0:T(8,128)(2,1)S(1)}, u32[]{:S(2)}, u32[]{:S(2)}) collective-permute-start(bf16[528,128]{1,0:T(8,128)(2,1)S(1)} %add_convert_fusion.1.mine), channel_id=1, source_target_pairs={{0,384},{4,132},{128,256},{132,4},{256,128},{260,388},{384,0},{388... | collective-permute-start | bytes 405512 | tf_op jit(solution)/shard_map/ppermute | solution.py:223
  84.2 5.6 %collective-permute-done.5.other = bf16[528,128]{1,0:T(8,128)(2,1)S(1)} collective-permute-done((bf16[528,128]{1,0:T(8,128)(2,1)S(1)}, bf16[528,128]{1,0:T(8,128)(2,1)S(1)}, u32[]{:S(2)}, u32[]{:S(2)}) %collective-permute-start.5) | collective-permute-done | bytes 135200 | tf_op jit(solution)/shard_map/ppermute | solution.py:223
  89.9 1.3 shard_map.108
  91.2 12.2 %all_gather.3.g0 = bf16[2048,128]{1,0:T(8,128)(2,1)S(1)} all-gather(bf16[512,128]{1,0:T(8,128)(2,1)S(1)} %get-tuple-element.16), channel_id=1, replica_groups=mesh['zh'=4,'zl'=4,'x'=4,'c'=2,'y'=4] {'zl'}, dimensions={0}, use_global_device_ids=true | all-gather | bytes 655360 | tf_op jit(solution)/shard_map/all_gather | solution.py:233
  103.3 4.6 %collective-permute-start.8 = (bf16[2048,128]{1,0:T(8,128)(2,1)S(1)}, bf16[2048,128]{1,0:T(8,128)(2,1)S(1)}, u32[]{:S(2)}, u32[]{:S(2)}) collective-permute-start(bf16[2048,128]{1,0:T(8,128)(2,1)S(1)} %all_gather.3.g0), channel_id=1, source_target_pairs={{0,8},{8,16},{16,24},{24,0},{1,9},{9,17},{17,25},{25,1},{2,10},{10... | collective-permute-start | bytes 1572872 | tf_op jit(solution)/shard_map/ppermute | solution.py:235
  108.0 2.7 %collective-permute-start.7 = (bf16[2048,128]{1,0:T(8,128)(2,1)S(1)}, bf16[2048,128]{1,0:T(8,128)(2,1)S(1)}, u32[]{:S(2)}, u32[]{:S(2)}) collective-permute-start(bf16[2048,128]{1,0:T(8,128)(2,1)S(1)} %all_gather.3.g0), channel_id=1, source_target_pairs={{0,16},{8,24},{16,0},{24,8},{1,17},{9,25},{17,1},{25,9},{2,18},{10... | collective-permute-start | bytes 1572872 | tf_op jit(solution)/shard_map/ppermute | solution.py:234
  110.7 3.5 %collective-permute-start.6 = (bf16[2048,128]{1,0:T(8,128)(2,1)S(1)}, bf16[2048,128]{1,0:T(8,128)(2,1)S(1)}, u32[]{:S(2)}, u32[]{:S(2)}) collective-permute-start(bf16[2048,128]{1,0:T(8,128)(2,1)S(1)} %all_gather.3.g0), channel_id=1, source_target_pairs={{0,24},{8,0},{16,8},{24,16},{1,25},{9,1},{17,9},{25,17},{2,26},{10... | collective-permute-start | bytes 1572872 | tf_op jit(solution)/shard_map/ppermute | solution.py:236
  114.2 1.1 collective-permute-done.8.g3
  115.4 12.0 %collective-permute-done.7.g2 = bf16[2048,128]{1,0:T(8,128)(2,1)S(1)} collective-permute-done((bf16[2048,128]{1,0:T(8,128)(2,1)S(1)}, bf16[2048,128]{1,0:T(8,128)(2,1)S(1)}, u32[]{:S(2)}, u32[]{:S(2)}) %collective-permute-start.7) | collective-permute-done | bytes 524320 | tf_op jit(solution)/shard_map/ppermute | solution.py:234
  127.4 3.3 %collective-permute-done.6.g1 = bf16[2048,128]{1,0:T(8,128)(2,1)S(1)} collective-permute-done((bf16[2048,128]{1,0:T(8,128)(2,1)S(1)}, bf16[2048,128]{1,0:T(8,128)(2,1)S(1)}, u32[]{:S(2)}, u32[]{:S(2)}) %collective-permute-start.6) | collective-permute-done | bytes 524320 | tf_op jit(solution)/shard_map/ppermute | solution.py:236
  130.7 3.5 %shard_map.109 = (f32[512,128]{1,0:T(8,128)S(1)}, bf16[512,128]{1,0:T(8,128)(2,1)S(1)}) custom-call(s32[3]{0:T(128)S(1)} %pad_add_fusion.me, s32[16]{0:T(128)S(1)} %get-tuple-element.11.code0, s32[16]{0:T(128)S(1)} %add_bitcast_fusion.code1, bf16[2576,128]{1,0:T(8,128)(2,1)S(1)} %get-tuple-element.12.sent0, ...), custom_call_target="tpu_custom_call" | custom-call | flops 41943040 | bytes 4194304 | tf_op jit(solution)/shard_map/pallas_call | solution.py:237
  134.2 4.2 %collective-permute-start.9 = (bf16[512,128]{1,0:T(8,128)(2,1)S(1)}, bf16[512,128]{1,0:T(8,128)(2,1)S(1)}, u32[]{:S(2)}, u32[]{:S(2)}) collective-permute-start(bf16[512,128]{1,0:T(8,128)(2,1)S(1)} %get-tuple-element.18), channel_id=1, source_target_pairs={{0,4},{4,0},{1,5},{5,1},{2,6},{6,2},{3,7},{7,3},{8,12},{12,8},{9,1... | collective-permute-start | bytes 393224 | tf_op jit(solution)/shard_map/ppermute | solution.py:246
  138.5 1.0 collective-permute-done.9
  139.5 0.1 broadcast_in_dim.4
  139.5 0.0 copy-start.1
  139.5 0.0 copy-start.4
  139.6 13.4 %all_to_all.11.types = bf16[4,512,128]{2,1,0:T(8,128)(2,1)S(1)} all-to-all(bf16[4,512,128]{2,1,0:T(8,128)(2,1)S(1)} %broadcast_in_dim.4), channel_id=1, replica_groups=mesh['zh'=4,'zl'=4,'x'=4,'c'=2,'y'=4] {'y'}, dimensions={0} | all-to-all | bytes 1048576 | tf_op jit(solution)/shard_map/all_to_all | solution.py:248
  153.0 0.0 copy-done.1
  153.0 0.9 shard_map.110
  (7 shorter events, 0.1 us)
Async XLA Ops:
  0.6 0.7 copy-start.3
  1.3 0.7 copy-start.5
  1.3 0.7 copy-start.6
  1.3 0.7 copy-start.7
  2.0 0.9 copy-start
  2.9 1.0 copy-start.2
  5.2 10.5 %collective-permute-start = (bf16[2576,128]{1,0:T(8,128)(2,1)S(1)}, bf16[2576,128]{1,0:T(8,128)(2,1)S(1)}, u32[]{:S(2)}, u32[]{:S(2)}) collective-permute-start(bf16[2576,128]{1,0:T(8,128)(2,1)S(1)} %get-tuple-element.12.sent0), channel_id=1, source_target_pairs={{0,4},{4,0},{1,5},{5,1},{2,6},{6,2},{3,7},{7,3},{8,12},{12,8},{9,1... | collective-permute-start | bytes 1978376 | tf_op jit(solution)/shard_map/ppermute | solution.py:191
  17.4 16.6 %collective-permute-start.2 = (bf16[16,128,128]{2,1,0:T(8,128)(2,1)S(1)}, bf16[16,128,128]{2,1,0:T(8,128)(2,1)S(1)}, u32[]{:S(2)}, u32[]{:S(2)}) collective-permute-start(bf16[16,128,128]{2,1,0:T(8,128)(2,1)S(1)} %shard_map.106), channel_id=1, source_target_pairs={{0,16},{8,24},{16,0},{24,8},{1,17},{9,25},{17,1},{25,9},{2,18},{10... | collective-permute-start | bytes 1572872 | tf_op jit(solution)/shard_map/ppermute | solution.py:210
  24.1 21.7 %collective-permute-start.1 = (bf16[16,128,128]{2,1,0:T(8,128)(2,1)S(1)}, bf16[16,128,128]{2,1,0:T(8,128)(2,1)S(1)}, u32[]{:S(2)}, u32[]{:S(2)}) collective-permute-start(bf16[16,128,128]{2,1,0:T(8,128)(2,1)S(1)} %get-tuple-element.14), channel_id=1, source_target_pairs={{0,8},{8,16},{16,24},{24,0},{1,9},{9,17},{17,25},{25,1},{2,10},{10... | collective-permute-start | bytes 1572872 | tf_op jit(solution)/shard_map/ppermute | solution.py:212
  26.1 19.8 %collective-permute-start.3 = (bf16[16,128,128]{2,1,0:T(8,128)(2,1)S(1)}, bf16[16,128,128]{2,1,0:T(8,128)(2,1)S(1)}, u32[]{:S(2)}, u32[]{:S(2)}) collective-permute-start(bf16[16,128,128]{2,1,0:T(8,128)(2,1)S(1)} %get-tuple-element.15), channel_id=1, source_target_pairs={{0,24},{8,0},{16,8},{24,16},{1,25},{9,1},{17,9},{25,17},{2,26},{10... | collective-permute-start | bytes 1572872 | tf_op jit(solution)/shard_map/ppermute | solution.py:213
  46.2 16.6 %copy-start.8 = (s32[1,128]{1,0:T(1,128)S(1)}, s32[1,128]{1,0:T(1,128)}, u32[]{:S(2)}) copy-start(s32[1,128]{1,0:T(1,128)} %degree.1) | copy-start | bytes 1540
  63.5 13.3 %collective-permute-start.4 = (bf16[528,128]{1,0:T(8,128)(2,1)S(1)}, bf16[528,128]{1,0:T(8,128)(2,1)S(1)}, u32[]{:S(2)}, u32[]{:S(2)}) collective-permute-start(bf16[528,128]{1,0:T(8,128)(2,1)S(1)} %shard_map.107), channel_id=1, source_target_pairs={{0,128},{4,388},{128,0},{132,260},{256,384},{260,132},{384,256},{3... | collective-permute-start | bytes 405512 | tf_op jit(solution)/shard_map/ppermute | solution.py:221
  76.8 13.1 %collective-permute-start.5 = (bf16[528,128]{1,0:T(8,128)(2,1)S(1)}, bf16[528,128]{1,0:T(8,128)(2,1)S(1)}, u32[]{:S(2)}, u32[]{:S(2)}) collective-permute-start(bf16[528,128]{1,0:T(8,128)(2,1)S(1)} %add_convert_fusion.1.mine), channel_id=1, source_target_pairs={{0,384},{4,132},{128,256},{132,4},{256,128},{260,388},{384,0},{388... | collective-permute-start | bytes 405512 | tf_op jit(solution)/shard_map/ppermute | solution.py:223
  103.3 12.0 %collective-permute-start.8 = (bf16[2048,128]{1,0:T(8,128)(2,1)S(1)}, bf16[2048,128]{1,0:T(8,128)(2,1)S(1)}, u32[]{:S(2)}, u32[]{:S(2)}) collective-permute-start(bf16[2048,128]{1,0:T(8,128)(2,1)S(1)} %all_gather.3.g0), channel_id=1, source_target_pairs={{0,8},{8,16},{16,24},{24,0},{1,9},{9,17},{17,25},{25,1},{2,10},{10... | collective-permute-start | bytes 1572872 | tf_op jit(solution)/shard_map/ppermute | solution.py:235
  108.0 19.4 %collective-permute-start.7 = (bf16[2048,128]{1,0:T(8,128)(2,1)S(1)}, bf16[2048,128]{1,0:T(8,128)(2,1)S(1)}, u32[]{:S(2)}, u32[]{:S(2)}) collective-permute-start(bf16[2048,128]{1,0:T(8,128)(2,1)S(1)} %all_gather.3.g0), channel_id=1, source_target_pairs={{0,16},{8,24},{16,0},{24,8},{1,17},{9,25},{17,1},{25,9},{2,18},{10... | collective-permute-start | bytes 1572872 | tf_op jit(solution)/shard_map/ppermute | solution.py:234
  110.7 20.0 %collective-permute-start.6 = (bf16[2048,128]{1,0:T(8,128)(2,1)S(1)}, bf16[2048,128]{1,0:T(8,128)(2,1)S(1)}, u32[]{:S(2)}, u32[]{:S(2)}) collective-permute-start(bf16[2048,128]{1,0:T(8,128)(2,1)S(1)} %all_gather.3.g0), channel_id=1, source_target_pairs={{0,24},{8,0},{16,8},{24,16},{1,25},{9,1},{17,9},{25,17},{2,26},{10... | collective-permute-start | bytes 1572872 | tf_op jit(solution)/shard_map/ppermute | solution.py:236
  134.2 5.2 %collective-permute-start.9 = (bf16[512,128]{1,0:T(8,128)(2,1)S(1)}, bf16[512,128]{1,0:T(8,128)(2,1)S(1)}, u32[]{:S(2)}, u32[]{:S(2)}) collective-permute-start(bf16[512,128]{1,0:T(8,128)(2,1)S(1)} %get-tuple-element.18), channel_id=1, source_target_pairs={{0,4},{4,0},{1,5},{5,1},{2,6},{6,2},{3,7},{7,3},{8,12},{12,8},{9,1... | collective-permute-start | bytes 393224 | tf_op jit(solution)/shard_map/ppermute | solution.py:246
  139.5 13.4 %copy-start.1 = (bf16[512,128]{1,0:T(8,128)(2,1)S(1)}, bf16[512,128]{1,0:T(8,128)(2,1)}, u32[]{:S(2)}) copy-start(bf16[512,128]{1,0:T(8,128)(2,1)} %scores.3) | copy-start | bytes 393220
  139.5 13.4 %copy-start.4 = (s32[512]{0:T(512)S(1)}, s32[512]{0:T(512)}, u32[]{:S(2)}) copy-start(s32[512]{0:T(512)} %param.10) | copy-start | bytes 6148

commit v4 on v3

v4 whole, which is shorter than its diff:
```python
import functools
import jax
import jax.numpy as jnp
from jax import lax
from jax.experimental import pallas as pl
from jax.experimental.pallas import tpu as pltpu
from jax.sharding import PartitionSpec as P

ALPHA = 0.8
SIDE = 128
SLOTS = 16
ROWS = 512
LINE = 16
MEBI = 2**20
TILES = SLOTS * SIDE
SENT = TILES + ROWS + SLOTS
FOUR = 4 * SIDE


def device(core, u, v):
    return (((u + core) % 16) * 4 + (v + core) % 4) * 2 + core


def pairs(meet):
    return [
        (device(c, u, v), device(c, *meet(c, u, v)))
        for c in range(2)
        for u in range(16)
        for v in range(4)
    ]


SWAP = [(i, i ^ 1) for i in range(128)]
BESIDE = pairs(lambda c, u, v: (u ^ 1, v))
ACROSS = pairs(lambda c, u, v: (u, v ^ 1))
DIAGONAL = pairs(lambda c, u, v: (u ^ 1, v ^ 1))
FIRST = pairs(lambda c, u, v: (u ^ 4 if c == 0 else 12 - (u & 12) + (u & 3), v))
SECOND = pairs(lambda c, u, v: (u ^ 4 if c == 1 else 12 - (u & 12) + (u & 3), v))
QUADS = [
    [device(c, far * 4 + step * 2 + odd, (0, 3, 1, 2)[side * 2 + end]) for end in (0, 1) for step in (0, 1)]
    for c in (0, 1)
    for side in (0, 1)
    for odd in (0, 1)
    for far in range(4)
]


def where(index):
    core = index & 1
    return core, ((index >> 3) - core) & 15, ((index >> 1) - core) & 3


def place(code, me):
    core, u, v = where(me[0])
    core1, u1, v1 = where(code & 127)
    side = (v ^ (v >> 1) ^ v1 ^ (v1 >> 1)) & 1
    taken = ((code >> 9) == 1) & (core1 == core)
    along = (v1 >> 1) * 8 + ((u1 >> 1) & 1) * 4 + (u1 >> 2)
    return taken, side * 2 + ((u ^ u1) & 1), along, (code >> 7) & 3


def column(row):
    return jnp.broadcast_to(row, (SIDE, SIDE)).T


def prepare_kernel(table, attr, acct, count, weights, scores, degree, payload, code, rows, sems):
    tiles = pltpu.make_async_copy(weights, payload.at[pl.ds(0, TILES), :], sems.at[0])
    prior = pltpu.make_async_copy(scores, rows, sems.at[1])
    prior.start()
    tiles.start()
    lane = lax.broadcasted_iota(jnp.int32, (SLOTS, SIDE), 1)
    tail = jnp.zeros((SLOTS, SIDE), jnp.int32)
    for s in range(SLOTS):
        owner = table[0, attr[0, s]]
        placing = acct[0, s] + jnp.where(s < count[0, 0], 4, 0)
        code[s] = owner + placing * 128
        tail = jnp.where(lane == s, owner, tail)
        tail = jnp.where(lane == s + SLOTS, placing, tail)
    payload[TILES + ROWS :, :] = tail.astype(jnp.float32).astype(payload.dtype)
    prior.wait()
    for n in range(4):
        scale = column(lax.rsqrt(degree[n : n + 1, :].astype(jnp.float32)))
        scaled = rows[pl.ds(n * SIDE, SIDE), :].astype(jnp.float32) * scale
        payload[pl.ds(TILES + n * SIDE, SIDE), :] = scaled.astype(payload.dtype)
    tiles.wait()


def tile(sent, s):
    return sent[pl.ds(pl.multiple_of(s * SIDE, SIDE), SIDE), :]


def forward_kernel(offsets, me, code0, code1, sent0, sent1, *refs):
    outs, acc = refs[:-1], refs[-1]
    acc[...] = jnp.zeros_like(acc)
    for code, sent in ((code0, sent0), (code1, sent1)):

        def step(s, carry, code=code, sent=sent):
            taken, away, along, block = place(code[s], me)
            index = jnp.int32(0)
            wanted = jnp.bool_(False)
            for n, offset in enumerate(offsets):
                index = jnp.where(away == offset, n * LINE, index)
                wanted = wanted | (away == offset)

            @pl.when(taken & wanted)
            def _():
                acc[index + along] += lax.dot_general(
                    tile(sent, s),
                    tile(sent, SLOTS + block),
                    (((0,), (0,)), ((), ())),
                    preferred_element_type=jnp.float32,
                )

            return carry

        lax.fori_loop(0, SLOTS, step, 0)
    for n, out in enumerate(outs):
        out[...] = acc[n * LINE : (n + 1) * LINE].astype(out.dtype)


def near_kernel(me, parts, degree, sums):
    for n in range(4):
        total = parts[0, n].astype(jnp.float32)
        for k in range(1, 4):
            total += parts[k, n].astype(jnp.float32)
        sums[n * SIDE : (n + 1) * SIDE, :] = total.astype(sums.dtype)
    row = lax.broadcasted_iota(jnp.int32, (SLOTS, SIDE), 0)
    mine = jnp.where(row == where(me[0])[1] >> 2, degree[...].astype(jnp.float32), 0.0)
    sums[FOUR:, :] = mine.astype(sums.dtype)


def far_kernel(me, mine, other, own, spread):
    degree = mine[FOUR:, :].astype(jnp.float32) + other[FOUR:, :].astype(jnp.float32)
    for n in range(4):
        rows = pl.ds(n * SIDE, SIDE)
        total = mine[rows, :].astype(jnp.float32) + other[rows, :].astype(jnp.float32)
        scores = (total * column(lax.rsqrt(degree[n : n + 1, :]))).astype(spread.dtype)
        for k in range(4):
            spread[k, rows, :] = scores
    far = where(me[0])[1] >> 2
    own[...] = spread[0, pl.ds(pl.multiple_of(far * SIDE, SIDE), SIDE), :]


def backward_kernel(chips, me, code0, code1, sent0, sent1, *refs):
    groups, refs = refs[: len(chips)], refs[len(chips) :]
    if len(refs) == 1:
        (acc,) = refs
        acc[...] = jnp.zeros_like(acc)
    else:
        before, mine, other, acc = refs
        acc[...] = before[...]
    for half, (code, sent) in enumerate(((code0, sent0), (code1, sent1))):

        def step(s, carry, half=half, code=code, sent=sent):
            taken, chip, along, block = place(code[s], me)
            for n, blocks in zip(chips, groups):

                @pl.when(taken & (chip == n))
                def _(blocks=blocks):
                    start = pl.multiple_of(half * ROWS + block * SIDE, SIDE)
                    acc[pl.ds(start, SIDE), :] += jnp.dot(
                        tile(sent, s), tile(blocks, along), preferred_element_type=jnp.float32
                    )

            return carry

        lax.fori_loop(0, SLOTS, step, 0)
    if len(refs) > 1:
        mine[...] = acc[:ROWS]
        other[...] = acc[ROWS:].astype(other.dtype)


def finish_kernel(types, scores, degree, seed, new):
    for n in range(4):
        rows = pl.ds(n * SIDE, SIDE)
        scale = column(lax.rsqrt(degree[n : n + 1, :].astype(jnp.float32)))
        prior = scores[rows, :].astype(jnp.float32)
        whole = types[0, rows, :].astype(jnp.float32)
        for k in range(1, 4):
            whole += types[k, rows, :].astype(jnp.float32)
        mixed = ALPHA * (whole * scale) + (1.0 - ALPHA) * prior
        kept = column(seed[n : n + 1, :].astype(jnp.float32))
        new[rows, :] = jnp.where(kept == 1.0, prior, mixed)


def smem(n):
    return [pl.BlockSpec(memory_space=pltpu.SMEM)] * n


def vmem(n):
    return [pl.BlockSpec(memory_space=pltpu.VMEM)] * n


def call(kernel, outs, specs, scratch, flops, moved, out_specs=None):
    return pl.pallas_call(
        kernel,
        out_shape=outs,
        in_specs=specs,
        out_specs=out_specs or vmem(len(outs)),
        scratch_shapes=scratch,
        compiler_params=pltpu.CompilerParams(vmem_limit_bytes=24 * MEBI),
        cost_estimate=pl.CostEstimate(flops=flops, bytes_accessed=moved, transcendentals=0),
    )


def per_device(
    scores0,
    seed_mask,
    acct_degree,
    attr_degree,
    tile_weight,
    tile_acct,
    tile_attr,
    attr_owner,
    tile_count,
):
    bf16, f32, i32 = jnp.bfloat16, jnp.float32, jnp.int32
    group = jax.ShapeDtypeStruct((LINE, SIDE, SIDE), bf16)
    degree = acct_degree.reshape(4, SIDE)
    payload, code = call(
        prepare_kernel,
        [jax.ShapeDtypeStruct((SENT, SIDE), bf16), jax.ShapeDtypeStruct((SLOTS,), i32)],
        smem(4) + [pl.BlockSpec(memory_space=pl.ANY)] * 2 + vmem(1),
        [pltpu.VMEM((ROWS, SIDE), bf16), pltpu.SemaphoreType.DMA((2,))],
        ROWS * SIDE,
        MEBI,
        vmem(1) + smem(1),
    )(
        attr_owner,
        tile_attr,
        tile_acct,
        tile_count,
        tile_weight.reshape(TILES, SIDE),
        scores0,
        degree,
    )
    payload1 = lax.ppermute(payload, "acct", SWAP)
    tail1 = payload1[TILES + ROWS].astype(i32)
    code1 = tail1[:SLOTS] + tail1[SLOTS : 2 * SLOTS] * 128
    me = lax.axis_index("acct").astype(i32).reshape(1)

    flops = 2 * 10 * SIDE**3
    slots = (me, code, code1, payload, payload1)

    def forward(chips):
        return call(
            functools.partial(forward_kernel, chips),
            [group] * len(chips),
            smem(3) + vmem(2),
            [pltpu.VMEM((len(chips) * LINE, SIDE, SIDE), f32)],
            flops,
            3 * MEBI,
        )(*slots)

    (o3,) = forward((3,))
    r3 = lax.ppermute(o3, "acct", DIAGONAL)
    o1, o2, o0 = forward((1, 2, 0))
    r1 = lax.ppermute(o1, "acct", BESIDE)
    r2 = lax.ppermute(o2, "acct", ACROSS)
    line = o0.astype(f32) + r1.astype(f32) + r2.astype(f32) + r3.astype(f32)
    line = line.astype(bf16).reshape(4, 4, SIDE, SIDE)
    line = lax.all_to_all(line, "acct", 0, 0, tiled=True, axis_index_groups=QUADS)
    sums = jax.ShapeDtypeStruct((FOUR + SLOTS, SIDE), bf16)
    (near,) = call(
        near_kernel, [sums], smem(1) + vmem(2), [], SIDE * SIDE * LINE, MEBI
    )(me, line, attr_degree)
    half = near.astype(f32) + lax.ppermute(near, "acct", FIRST).astype(f32)
    half = half.astype(bf16)
    rest = lax.ppermute(half, "acct", SECOND)
    own_scores, spread = call(
        far_kernel,
        [
            jax.ShapeDtypeStruct((SIDE, SIDE), bf16),
            jax.ShapeDtypeStruct((4, FOUR, SIDE), bf16),
        ],
        smem(1) + vmem(2),
        [],
        SIDE * SIDE * LINE,
        MEBI // 2,
    )(me, half, rest)

    g0 = lax.all_to_all(spread, "acct", 0, 0, tiled=True, axis_index_groups=QUADS)
    g0 = g0.reshape(LINE * SIDE, SIDE)
    g3 = lax.ppermute(g0, "acct", DIAGONAL)
    g1 = lax.ppermute(g0, "acct", BESIDE)
    g2 = lax.ppermute(g0, "acct", ACROSS)
    acc = jax.ShapeDtypeStruct((2 * ROWS, SIDE), f32)
    (before,) = call(
        functools.partial(backward_kernel, (0,)), [acc], smem(3) + vmem(3), [], flops, 4 * MEBI
    )(*slots, g0)
    mine, other = call(
        functools.partial(backward_kernel, (1, 2, 3)),
        [jax.ShapeDtypeStruct((ROWS, SIDE), f32), jax.ShapeDtypeStruct((ROWS, SIDE), bf16)],
        smem(3) + vmem(6),
        [pltpu.VMEM(acc.shape, f32)],
        flops,
        4 * MEBI,
    )(*slots, g1, g2, g3, before)

    returned = (mine + lax.ppermute(other, "acct", SWAP).astype(f32)).astype(bf16)
    types = jnp.broadcast_to(returned[None], (4, ROWS, SIDE))
    types = lax.all_to_all(types, "attr", 0, 0, tiled=True)
    (new_scores,) = call(
        finish_kernel,
        [jax.ShapeDtypeStruct((ROWS, SIDE), f32)],
        vmem(4),
        [],
        ROWS * SIDE * 8,
        MEBI,
    )(types, scores0, degree, seed_mask.reshape(4, SIDE))
    return (new_scores, own_scores[None])


def solution(mesh):
    placed = (
        P("acct", None),
        P("acct"),
        P("acct"),
        P("attr", "acct"),
        P("attr", "acct", None, None),
        P("attr", "acct"),
        P("attr", "acct"),
        P("attr", None),
        P("attr", "acct"),
    )
    return jax.shard_map(
        per_device,
        mesh=mesh,
        in_specs=placed,
        out_specs=(P("acct", None), P("attr", "acct", None)),
        check_vma=False,
    )
```

time: 156 us -> 143 us (0.917)
  waiting for transfers between devices: 45.5 us -> 39.3 us
  starting transfers between devices: 47.4 us -> 41.8 us
    all_to_all x2 -> x3, blocking collectives: 30 us -> 43 us  [the longest x1 16.4 us: per_device(): types = lax.all_to_all(types, 'attr', 0, 0, tiled=True)]
    all_gather x1 -> x0, blocking collectives: 12.2 us -> none  [per_device(): g0 = lax.all_gather(scores, 'zl', axis=0, tiled=True)]
    ppermute x10, waiting for transfers between devices: 45.5 us -> 39.3 us  [the longest x1 10.6 us: per_device(): half = near.astype(f32) + lax.ppermute(near, 'acct', FIRST).astype(f32)]
    ppermute x10, starting transfers between devices: 47.4 us -> 41.8 us  [the longest x1 8.79 us: per_device(): payload1 = lax.ppermute(payload, 'acct', SWAP)]
    pallas_call x3 -> x4, Pallas kernels: 9.97 us -> 9.3 us  [the longest x2 5.36 us: forward(): call(functools.partial(forward_kernel, chips), [group] * len(chips), smem...]
  transfers between devices with their start and end apart: 10 -> 10, of which waited for: 9 -> 8; matrix products, arithmetic and copies ran while one was open for 0% -> 0% of each run, Pallas kernels for 3% -> 4%
where the time goes in v4:
time: 143 us; the launch traced here: 141 us
  blocking collectives  43 us (30%)
  starting transfers between devices  41.8 us (29%)
  waiting for transfers between devices  39.3 us (27%)
  Pallas kernels  12.6 us (9%)
  local copies, waits for them, and re-layouts  2.7 us (2%)
  between operations  1.51 us (1%)
    all_to_all x1, blocking collectives, per_device(): types = lax.all_to_all(types, 'attr', 0, 0, tiled=True)  16.4 us
    all_to_all x1, blocking collectives, per_device(): lax.all_to_all(line, 'acct', 0, 0, tiled=True, axis_index_groups=QUADS)  14.1 us
    all_to_all x1, blocking collectives, per_device(): lax.all_to_all(spread, 'acct', 0, 0, tiled=True, axis_index_groups=QUADS)  12.4 us
    ppermute x1, waiting for transfers between devices, per_device(): half = near.astype(f32) + lax.ppermute(near, 'acct', FIRST).astype(f32)  10.6 us
    ppermute x1, waiting for transfers between devices, per_device(): rest = lax.ppermute(half, 'acct', SECOND)  9.71 us
    ppermute x1, starting transfers between devices, per_device(): payload1 = lax.ppermute(payload, 'acct', SWAP)  8.79 us
    ppermute x1, starting transfers between devices, per_device(): r3 = lax.ppermute(o3, 'acct', DIAGONAL)  8.3 us
    ppermute x1, waiting for transfers between devices, per_device(): r2 = lax.ppermute(o2, 'acct', ACROSS)  7.26 us
  transfers between devices with their start and end apart: 10, of which 8 were waited for; matrix products, arithmetic and copies ran while one was open for 0% of the time, Pallas kernels for 4%

profile of v4, /device:TPU:1, one launch (start us, length us, event | category | flops | bytes accessed | tf_op | source)
XLA Modules:
  0.0 141.3 jit_solution(17120332234597734624)
XLA Ops:
  1.3 0.0 copy-start.3
  1.3 0.0 copy-start.5
  1.3 0.0 copy-start.6
  1.3 0.0 copy-start.7
  1.3 0.6 copy-done.3
  2.0 0.0 copy-done.5
  2.0 0.0 copy-done.6
  2.0 0.0 copy-done.7
  2.0 0.9 copy-done
  2.9 1.0 copy-done.2
  3.9 1.6 %shard_map.104 = (bf16[2576,128]{1,0:T(8,128)(2,1)S(1)}, s32[16]{0:T(128)S(1)}) custom-call(s32[1,128]{1,0:T(1,128)S(1)} %copy-done.5, s32[1,16]{1,0:T(1,128)S(1)} %copy-done.6, s32[1,16]{1,0:T(1,128)S(1)} %copy-done.7, s32[1,1]{1,0:T(1,128)S(6)} %copy.11.count, bf16[2048,128]{1,0:T(8,128)(2,1)S(1)} %bitcast.13, bf16[512,128]{1,0:T(8,128)(2,1)S(1)} %copy-done, ...), custom_call_target="tpu_custom_call" | custom-call | flops 65536 | bytes 1048576 | tf_op jit(solution)/shard_map/pallas_call | solution.py:220
  5.5 8.8 %collective-permute-start = (bf16[2576,128]{1,0:T(8,128)(2,1)S(1)}, bf16[2576,128]{1,0:T(8,128)(2,1)S(1)}, u32[]{:S(2)}, u32[]{:S(2)}) collective-permute-start(bf16[2576,128]{1,0:T(8,128)(2,1)S(1)} %get-tuple-element.12.sent0), channel_id=1, source_target_pairs={{0,4},{4,0},{8,12},{12,8},{16,20},{20,16},{24,28},{28,24},{32,36},... | collective-permute-start | bytes 1978376 | tf_op jit(solution)/shard_map/ppermute | solution.py:237
  14.3 1.7 %collective-permute-done.sent1 = bf16[2576,128]{1,0:T(8,128)(2,1)S(1)} collective-permute-done((bf16[2576,128]{1,0:T(8,128)(2,1)S(1)}, bf16[2576,128]{1,0:T(8,128)(2,1)S(1)}, u32[]{:S(2)}, u32[]{:S(2)}) %collective-permute-start) | collective-permute-done | bytes 659488 | tf_op jit(solution)/shard_map/ppermute | solution.py:237
  16.0 0.1 add_bitcast_fusion.code1
  16.1 2.0 %shard_map.106 = bf16[16,128,128]{2,1,0:T(8,128)(2,1)S(1)} custom-call(s32[1]{0:T(128)} %bitcast.me, s32[16]{0:T(128)S(1)} %get-tuple-element.11.code0, s32[16]{0:T(128)S(1)} %add_bitcast_fusion.code1, bf16[2576,128]{1,0:T(8,128)(2,1)S(1)} %get-tuple-element.12.sent0, bf16[2576,128]{1,0:T(8,128)(2,1)S(1)} %collective-permute-done.sent1), custom_call_target="tpu_custom_call" | custom-call | flops 41943040 | bytes 3145728 | tf_op jit(solution)/shard_map/pallas_call | solution.py:246
  18.1 8.3 %collective-permute-start.3 = (bf16[16,128,128]{2,1,0:T(8,128)(2,1)S(1)}, bf16[16,128,128]{2,1,0:T(8,128)(2,1)S(1)}, u32[]{:S(2)}, u32[]{:S(2)}) collective-permute-start(bf16[16,128,128]{2,1,0:T(8,128)(2,1)S(1)} %shard_map.106), channel_id=1, source_target_pairs={{0,40},{8,32},{16,56},{24,48},{32,8},{40,0},{48,24},{56,16},{64,10... | collective-permute-start | bytes 1572872 | tf_op jit(solution)/shard_map/ppermute | solution.py:256
  26.4 3.4 %shard_map.105 = (bf16[16,128,128]{2,1,0:T(8,128)(2,1)S(1)}, bf16[16,128,128]{2,1,0:T(8,128)(2,1)S(1)}, bf16[16,128,128]{2,1,0:T(8,128)(2,1)S(1)}) custom-call(s32[1]{0:T(128)} %bitcast.me, s32[16]{0:T(128)S(1)} %get-tuple-element.11.code0, s32[16]{0:T(128)S(1)} %add_bitcast_fusion.code1, bf16[2576,128]{1,0:T(8,128)(2,1)S(1)} %get-tuple-element.12.sent0, ...), custom_call_target="tpu_custom_call" | custom-call | flops 41943040 | bytes 3145728 | tf_op jit(solution)/shard_map/pallas_call | solution.py:246
  29.8 1.9 %collective-permute-start.2 = (bf16[16,128,128]{2,1,0:T(8,128)(2,1)S(1)}, bf16[16,128,128]{2,1,0:T(8,128)(2,1)S(1)}, u32[]{:S(2)}, u32[]{:S(2)}) collective-permute-start(bf16[16,128,128]{2,1,0:T(8,128)(2,1)S(1)} %get-tuple-element.15), channel_id=1, source_target_pairs={{0,8},{8,0},{16,24},{24,16},{32,40},{40,32},{48,56},{56,48},{64,72... | collective-permute-start | bytes 1572872 | tf_op jit(solution)/shard_map/ppermute | solution.py:259
  31.7 1.9 %collective-permute-start.1 = (bf16[16,128,128]{2,1,0:T(8,128)(2,1)S(1)}, bf16[16,128,128]{2,1,0:T(8,128)(2,1)S(1)}, u32[]{:S(2)}, u32[]{:S(2)}) collective-permute-start(bf16[16,128,128]{2,1,0:T(8,128)(2,1)S(1)} %get-tuple-element.14), channel_id=1, source_target_pairs={{0,32},{8,40},{16,48},{24,56},{32,0},{40,8},{48,16},{56,24},{64,96... | collective-permute-start | bytes 1572872 | tf_op jit(solution)/shard_map/ppermute | solution.py:258
  33.6 0.0 collective-permute-done.3
  33.6 7.3 %collective-permute-done.2 = bf16[16,128,128]{2,1,0:T(8,128)(2,1)S(1)} collective-permute-done((bf16[16,128,128]{2,1,0:T(8,128)(2,1)S(1)}, bf16[16,128,128]{2,1,0:T(8,128)(2,1)S(1)}, u32[]{:S(2)}, u32[]{:S(2)}) %collective-permute-start.2) | collective-permute-done | bytes 524320 | tf_op jit(solution)/shard_map/ppermute | solution.py:259
  40.9 1.9 %collective-permute-done.1 = bf16[16,128,128]{2,1,0:T(8,128)(2,1)S(1)} collective-permute-done((bf16[16,128,128]{2,1,0:T(8,128)(2,1)S(1)}, bf16[16,128,128]{2,1,0:T(8,128)(2,1)S(1)}, u32[]{:S(2)}, u32[]{:S(2)}) %collective-permute-start.1) | collective-permute-done | bytes 524320 | tf_op jit(solution)/shard_map/ppermute | solution.py:258
  42.8 0.3 add_convert_fusion
  43.2 0.0 copy-start.8
  43.2 14.1 %all_to_all.15.parts = bf16[4,4,128,128]{3,2,1,0:T(8,128)(2,1)S(1)} all-to-all(bf16[4,4,128,128]{3,2,1,0:T(8,128)(2,1)S(1)} %bitcast.17), channel_id=1, replica_groups={{0,64,24,88},{128,192,152,216},{256,320,280,344},{384,448,408,472},{32,..., dimensions={0} | all-to-all | bytes 1048576 | tf_op jit(solution)/shard_map/all_to_all | solution.py:262
  57.3 0.0 copy-done.8
  57.3 0.1 shard_map.107
  57.4 1.9 %collective-permute-start.4 = (bf16[528,128]{1,0:T(8,128)(2,1)S(1)}, bf16[528,128]{1,0:T(8,128)(2,1)S(1)}, u32[]{:S(2)}, u32[]{:S(2)}) collective-permute-start(bf16[528,128]{1,0:T(8,128)(2,1)S(1)} %shard_map.107), channel_id=1, source_target_pairs={{0,128},{8,136},{16,144},{24,152},{32,160},{40,168},{48,176},{56,1... | collective-permute-start | bytes 405512 | tf_op jit(solution)/shard_map/ppermute | solution.py:267
  59.3 10.6 %collective-permute-done.4 = bf16[528,128]{1,0:T(8,128)(2,1)S(1)} collective-permute-done((bf16[528,128]{1,0:T(8,128)(2,1)S(1)}, bf16[528,128]{1,0:T(8,128)(2,1)S(1)}, u32[]{:S(2)}, u32[]{:S(2)}) %collective-permute-start.4) | collective-permute-done | bytes 135200 | tf_op jit(solution)/shard_map/ppermute | solution.py:267
  70.0 1.9 %collective-permute-start.5 = (bf16[528,128]{1,0:T(8,128)(2,1)S(1)}, bf16[528,128]{1,0:T(8,128)(2,1)S(1)}, u32[]{:S(2)}, u32[]{:S(2)}) collective-permute-start(bf16[528,128]{1,0:T(8,128)(2,1)S(1)} %add_convert_fusion.1.mine), channel_id=1, source_target_pairs={{0,384},{8,392},{16,400},{24,408},{32,416},{40,424},{48,432},{56,4... | collective-permute-start | bytes 405512 | tf_op jit(solution)/shard_map/ppermute | solution.py:269
  71.9 9.7 %collective-permute-done.5.other = bf16[528,128]{1,0:T(8,128)(2,1)S(1)} collective-permute-done((bf16[528,128]{1,0:T(8,128)(2,1)S(1)}, bf16[528,128]{1,0:T(8,128)(2,1)S(1)}, u32[]{:S(2)}, u32[]{:S(2)}) %collective-permute-start.5) | collective-permute-done | bytes 135200 | tf_op jit(solution)/shard_map/ppermute | solution.py:269
  81.6 0.8 shard_map.108
  82.4 12.4 %all_to_all.16 = bf16[4,512,128]{2,1,0:T(8,128)(2,1)S(1)} all-to-all(bf16[4,512,128]{2,1,0:T(8,128)(2,1)S(1)} %get-tuple-element.16), channel_id=1, replica_groups={{0,64,24,88},{128,192,152,216},{256,320,280,344},{384,448,408,472},{32,..., dimensions={0} | all-to-all | bytes 1048576 | tf_op jit(solution)/shard_map/all_to_all | solution.py:282
  94.9 1.9 %collective-permute-start.6 = (bf16[2048,128]{1,0:T(8,128)(2,1)S(1)}, bf16[2048,128]{1,0:T(8,128)(2,1)S(1)}, u32[]{:S(2)}, u32[]{:S(2)}) collective-permute-start(bf16[2048,128]{1,0:T(8,128)(2,1)S(1)} %bitcast.9), channel_id=1, source_target_pairs={{0,32},{8,40},{16,48},{24,56},{32,0},{40,8},{48,16},{56,24},{64,96... | collective-permute-start | bytes 1572872 | tf_op jit(solution)/shard_map/ppermute | solution.py:285
  96.8 4.9 %collective-permute-start.7 = (bf16[2048,128]{1,0:T(8,128)(2,1)S(1)}, bf16[2048,128]{1,0:T(8,128)(2,1)S(1)}, u32[]{:S(2)}, u32[]{:S(2)}) collective-permute-start(bf16[2048,128]{1,0:T(8,128)(2,1)S(1)} %bitcast.10), channel_id=1, source_target_pairs={{0,8},{8,0},{16,24},{24,16},{32,40},{40,32},{48,56},{56,48},{64,72... | collective-permute-start | bytes 1572872 | tf_op jit(solution)/shard_map/ppermute | solution.py:286
  101.7 4.3 %collective-permute-start.8 = (bf16[2048,128]{1,0:T(8,128)(2,1)S(1)}, bf16[2048,128]{1,0:T(8,128)(2,1)S(1)}, u32[]{:S(2)}, u32[]{:S(2)}) collective-permute-start(bf16[2048,128]{1,0:T(8,128)(2,1)S(1)} %bitcast.11), channel_id=1, source_target_pairs={{0,40},{8,32},{16,56},{24,48},{32,8},{40,0},{48,24},{56,16},{64,10... | collective-permute-start | bytes 1572872 | tf_op jit(solution)/shard_map/ppermute | solution.py:284
  106.0 1.9 %shard_map.109.refs_3_ = f32[1024,128]{1,0:T(8,128)S(1)} custom-call(s32[1]{0:T(128)} %bitcast.me, s32[16]{0:T(128)S(1)} %get-tuple-element.11.code0, s32[16]{0:T(128)S(1)} %add_bitcast_fusion.code1, bf16[2576,128]{1,0:T(8,128)(2,1)S(1)} %get-tuple-element.12.sent0, bf16[2576,128]{1,0:T(8,128)(2,1)S(1)} %collective-permute-done.sent1, ...), custom_call_target="tpu_custom_call" | custom-call | flops 41943040 | bytes 4194304 | tf_op jit(solution)/shard_map/pallas_call | solution.py:288
  107.9 0.0 collective-permute-done.6.refs_0_
  107.9 5.5 %collective-permute-done.7.refs_1_ = bf16[2048,128]{1,0:T(8,128)(2,1)S(1)} collective-permute-done((bf16[2048,128]{1,0:T(8,128)(2,1)S(1)}, bf16[2048,128]{1,0:T(8,128)(2,1)S(1)}, u32[]{:S(2)}, u32[]{:S(2)}) %collective-permute-start.7) | collective-permute-done | bytes 524320 | tf_op jit(solution)/shard_map/ppermute | solution.py:286
  113.4 1.5 %collective-permute-done.8.refs_2_ = bf16[2048,128]{1,0:T(8,128)(2,1)S(1)} collective-permute-done((bf16[2048,128]{1,0:T(8,128)(2,1)S(1)}, bf16[2048,128]{1,0:T(8,128)(2,1)S(1)}, u32[]{:S(2)}, u32[]{:S(2)}) %collective-permute-start.8) | collective-permute-done | bytes 524320 | tf_op jit(solution)/shard_map/ppermute | solution.py:284
  114.9 2.1 %shard_map.110 = (f32[512,128]{1,0:T(8,128)S(1)}, bf16[512,128]{1,0:T(8,128)(2,1)S(1)}) custom-call(s32[1]{0:T(128)} %bitcast.me, s32[16]{0:T(128)S(1)} %get-tuple-element.11.code0, s32[16]{0:T(128)S(1)} %add_bitcast_fusion.code1, bf16[2576,128]{1,0:T(8,128)(2,1)S(1)} %get-tuple-element.12.sent0, bf16[2576,128]{1,0:T(8,128)(2,1)S(1)} %collective-permute-done.sent1, ...), custom_call_target="tpu_custom_call" | custom-call | flops 41943040 | bytes 4194304 | tf_op jit(solution)/shard_map/pallas_call | solution.py:291
  117.0 5.8 %collective-permute-start.9 = (bf16[512,128]{1,0:T(8,128)(2,1)S(1)}, bf16[512,128]{1,0:T(8,128)(2,1)S(1)}, u32[]{:S(2)}, u32[]{:S(2)}) collective-permute-start(bf16[512,128]{1,0:T(8,128)(2,1)S(1)} %get-tuple-element.18), channel_id=1, source_target_pairs={{0,4},{4,0},{8,12},{12,8},{16,20},{20,16},{24,28},{28,24},{32,36},... | collective-permute-start | bytes 393224 | tf_op jit(solution)/shard_map/ppermute | solution.py:300
  122.9 1.0 collective-permute-done.9
  123.9 0.1 broadcast_in_dim.4
  124.0 0.0 copy-start.1
  124.0 0.0 copy-start.4
  124.0 16.4 %all_to_all.17.types = bf16[4,512,128]{2,1,0:T(8,128)(2,1)S(1)} all-to-all(bf16[4,512,128]{2,1,0:T(8,128)(2,1)S(1)} %broadcast_in_dim.4), channel_id=1, replica_groups=mesh['acct'=128,'attr'=4] {'attr'}, dimensions={0} | all-to-all | bytes 1048576 | tf_op jit(solution)/shard_map/all_to_all | solution.py:302
  140.4 0.9 shard_map.111
  (7 shorter events, 0.1 us)
Async XLA Ops:
  1.3 0.7 copy-start.3
  1.3 0.7 copy-start.5
  1.3 0.7 copy-start.6
  1.3 0.7 copy-start.7
  2.0 0.9 copy-start
  2.9 1.0 copy-start.2
  5.5 10.5 %collective-permute-start = (bf16[2576,128]{1,0:T(8,128)(2,1)S(1)}, bf16[2576,128]{1,0:T(8,128)(2,1)S(1)}, u32[]{:S(2)}, u32[]{:S(2)}) collective-permute-start(bf16[2576,128]{1,0:T(8,128)(2,1)S(1)} %get-tuple-element.12.sent0), channel_id=1, source_target_pairs={{0,4},{4,0},{8,12},{12,8},{16,20},{20,16},{24,28},{28,24},{32,36},... | collective-permute-start | bytes 1978376 | tf_op jit(solution)/shard_map/ppermute | solution.py:237
  18.1 15.5 %collective-permute-start.3 = (bf16[16,128,128]{2,1,0:T(8,128)(2,1)S(1)}, bf16[16,128,128]{2,1,0:T(8,128)(2,1)S(1)}, u32[]{:S(2)}, u32[]{:S(2)}) collective-permute-start(bf16[16,128,128]{2,1,0:T(8,128)(2,1)S(1)} %shard_map.106), channel_id=1, source_target_pairs={{0,40},{8,32},{16,56},{24,48},{32,8},{40,0},{48,24},{56,16},{64,10... | collective-permute-start | bytes 1572872 | tf_op jit(solution)/shard_map/ppermute | solution.py:256
  29.8 11.1 %collective-permute-start.2 = (bf16[16,128,128]{2,1,0:T(8,128)(2,1)S(1)}, bf16[16,128,128]{2,1,0:T(8,128)(2,1)S(1)}, u32[]{:S(2)}, u32[]{:S(2)}) collective-permute-start(bf16[16,128,128]{2,1,0:T(8,128)(2,1)S(1)} %get-tuple-element.15), channel_id=1, source_target_pairs={{0,8},{8,0},{16,24},{24,16},{32,40},{40,32},{48,56},{56,48},{64,72... | collective-permute-start | bytes 1572872 | tf_op jit(solution)/shard_map/ppermute | solution.py:259
  31.7 11.1 %collective-permute-start.1 = (bf16[16,128,128]{2,1,0:T(8,128)(2,1)S(1)}, bf16[16,128,128]{2,1,0:T(8,128)(2,1)S(1)}, u32[]{:S(2)}, u32[]{:S(2)}) collective-permute-start(bf16[16,128,128]{2,1,0:T(8,128)(2,1)S(1)} %get-tuple-element.14), channel_id=1, source_target_pairs={{0,32},{8,40},{16,48},{24,56},{32,0},{40,8},{48,16},{56,24},{64,96... | collective-permute-start | bytes 1572872 | tf_op jit(solution)/shard_map/ppermute | solution.py:258
  43.2 14.2 %copy-start.8 = (s32[1,128]{1,0:T(1,128)S(1)}, s32[1,128]{1,0:T(1,128)}, u32[]{:S(2)}) copy-start(s32[1,128]{1,0:T(1,128)} %degree.1) | copy-start | bytes 1540
  57.4 12.6 %collective-permute-start.4 = (bf16[528,128]{1,0:T(8,128)(2,1)S(1)}, bf16[528,128]{1,0:T(8,128)(2,1)S(1)}, u32[]{:S(2)}, u32[]{:S(2)}) collective-permute-start(bf16[528,128]{1,0:T(8,128)(2,1)S(1)} %shard_map.107), channel_id=1, source_target_pairs={{0,128},{8,136},{16,144},{24,152},{32,160},{40,168},{48,176},{56,1... | collective-permute-start | bytes 405512 | tf_op jit(solution)/shard_map/ppermute | solution.py:267
  70.0 11.6 %collective-permute-start.5 = (bf16[528,128]{1,0:T(8,128)(2,1)S(1)}, bf16[528,128]{1,0:T(8,128)(2,1)S(1)}, u32[]{:S(2)}, u32[]{:S(2)}) collective-permute-start(bf16[528,128]{1,0:T(8,128)(2,1)S(1)} %add_convert_fusion.1.mine), channel_id=1, source_target_pairs={{0,384},{8,392},{16,400},{24,408},{32,416},{40,424},{48,432},{56,4... | collective-permute-start | bytes 405512 | tf_op jit(solution)/shard_map/ppermute | solution.py:269
  94.9 13.0 %collective-permute-start.6 = (bf16[2048,128]{1,0:T(8,128)(2,1)S(1)}, bf16[2048,128]{1,0:T(8,128)(2,1)S(1)}, u32[]{:S(2)}, u32[]{:S(2)}) collective-permute-start(bf16[2048,128]{1,0:T(8,128)(2,1)S(1)} %bitcast.9), channel_id=1, source_target_pairs={{0,32},{8,40},{16,48},{24,56},{32,0},{40,8},{48,16},{56,24},{64,96... | collective-permute-start | bytes 1572872 | tf_op jit(solution)/shard_map/ppermute | solution.py:285
  96.8 16.6 %collective-permute-start.7 = (bf16[2048,128]{1,0:T(8,128)(2,1)S(1)}, bf16[2048,128]{1,0:T(8,128)(2,1)S(1)}, u32[]{:S(2)}, u32[]{:S(2)}) collective-permute-start(bf16[2048,128]{1,0:T(8,128)(2,1)S(1)} %bitcast.10), channel_id=1, source_target_pairs={{0,8},{8,0},{16,24},{24,16},{32,40},{40,32},{48,56},{56,48},{64,72... | collective-permute-start | bytes 1572872 | tf_op jit(solution)/shard_map/ppermute | solution.py:286
  101.7 13.2 %collective-permute-start.8 = (bf16[2048,128]{1,0:T(8,128)(2,1)S(1)}, bf16[2048,128]{1,0:T(8,128)(2,1)S(1)}, u32[]{:S(2)}, u32[]{:S(2)}) collective-permute-start(bf16[2048,128]{1,0:T(8,128)(2,1)S(1)} %bitcast.11), channel_id=1, source_target_pairs={{0,40},{8,32},{16,56},{24,48},{32,8},{40,0},{48,24},{56,16},{64,10... | collective-permute-start | bytes 1572872 | tf_op jit(solution)/shard_map/ppermute | solution.py:284
  117.0 6.8 %collective-permute-start.9 = (bf16[512,128]{1,0:T(8,128)(2,1)S(1)}, bf16[512,128]{1,0:T(8,128)(2,1)S(1)}, u32[]{:S(2)}, u32[]{:S(2)}) collective-permute-start(bf16[512,128]{1,0:T(8,128)(2,1)S(1)} %get-tuple-element.18), channel_id=1, source_target_pairs={{0,4},{4,0},{8,12},{12,8},{16,20},{20,16},{24,28},{28,24},{32,36},... | collective-permute-start | bytes 393224 | tf_op jit(solution)/shard_map/ppermute | solution.py:300
  124.0 16.4 %copy-start.1 = (bf16[512,128]{1,0:T(8,128)(2,1)S(1)}, bf16[512,128]{1,0:T(8,128)(2,1)}, u32[]{:S(2)}) copy-start(bf16[512,128]{1,0:T(8,128)(2,1)} %scores.3) | copy-start | bytes 393220
  124.0 16.4 %copy-start.4 = (s32[512]{0:T(512)S(1)}, s32[512]{0:T(512)}, u32[]{:S(2)}) copy-start(s32[512]{0:T(512)} %param.10) | copy-start | bytes 6148

commit v5 on v4

--- a/solution.py
+++ b/solution.py
@@ -50,32 +50,33 @@
     return core, ((index >> 3) - core) & 15, ((index >> 1) - core) & 3
 
 
-def place(code, me):
-    core, u, v = where(me[0])
-    core1, u1, v1 = where(code & 127)
+def decode(owner, core, u, v):
+    core1, u1, v1 = where(owner)
     side = (v ^ (v >> 1) ^ v1 ^ (v1 >> 1)) & 1
-    taken = ((code >> 9) == 1) & (core1 == core)
-    along = (v1 >> 1) * 8 + ((u1 >> 1) & 1) * 4 + (u1 >> 2)
-    return taken, side * 2 + ((u ^ u1) & 1), along, (code >> 7) & 3
+    chip = jnp.where(core1 == core, side * 2 + ((u ^ u1) & 1), 7)
+    return chip * 16 + (v1 >> 1) * 8 + ((u1 >> 1) & 1) * 4 + (u1 >> 2)
 
 
 def column(row):
     return jnp.broadcast_to(row, (SIDE, SIDE)).T
 
 
-def prepare_kernel(table, attr, acct, count, weights, scores, degree, payload, code, rows, sems):
+def prepare_kernel(me, table, attr, acct, count, weights, scores, degree, payload, rows, sems):
     tiles = pltpu.make_async_copy(weights, payload.at[pl.ds(0, TILES), :], sems.at[0])
     prior = pltpu.make_async_copy(scores, rows, sems.at[1])
     prior.start()
     tiles.start()
+    core, u, v = where(me[0])
+    twin, twin_u, twin_v = where(me[0] ^ 1)
     lane = lax.broadcasted_iota(jnp.int32, (SLOTS, SIDE), 1)
     tail = jnp.zeros((SLOTS, SIDE), jnp.int32)
     for s in range(SLOTS):
         owner = table[0, attr[0, s]]
-        placing = acct[0, s] + jnp.where(s < count[0, 0], 4, 0)
-        code[s] = owner + placing * 128
-        tail = jnp.where(lane == s, owner, tail)
-        tail = jnp.where(lane == s + SLOTS, placing, tail)
+        live = s < count[0, 0]
+        tail = jnp.where(lane == s, jnp.where(live, decode(owner, core, u, v), 112), tail)
+        sent = jnp.where(live, decode(owner, twin, twin_u, twin_v), 112)
+        tail = jnp.where(lane == s + SLOTS, sent, tail)
+        tail = jnp.where(lane == s + 2 * SLOTS, acct[0, s], tail)
     payload[TILES + ROWS :, :] = tail.astype(jnp.float32).astype(payload.dtype)
     prior.wait()
     for n in range(4):
@@ -89,20 +90,21 @@
     return sent[pl.ds(pl.multiple_of(s * SIDE, SIDE), SIDE), :]
 
 
-def forward_kernel(offsets, me, code0, code1, sent0, sent1, *refs):
+def forward_kernel(offsets, tail0, tail1, sent0, sent1, *refs):
     outs, acc = refs[:-1], refs[-1]
     acc[...] = jnp.zeros_like(acc)
-    for code, sent in ((code0, sent0), (code1, sent1)):
-
-        def step(s, carry, code=code, sent=sent):
-            taken, away, along, block = place(code[s], me)
+    for half, (tail, sent) in enumerate(((tail0, sent0), (tail1, sent1))):
+
+        def step(s, carry, half=half, tail=tail, sent=sent):
+            code, block = tail[0, half * SLOTS + s], tail[0, 2 * SLOTS + s]
+            chip, along = code >> 4, code & 15
             index = jnp.int32(0)
             wanted = jnp.bool_(False)
             for n, offset in enumerate(offsets):
-                index = jnp.where(away == offset, n * LINE, index)
-                wanted = wanted | (away == offset)
-
-            @pl.when(taken & wanted)
+                index = jnp.where(chip == offset, n * LINE, index)
+                wanted = wanted | (chip == offset)
+
+            @pl.when(wanted)
             def _():
                 acc[index + along] += lax.dot_general(
                     tile(sent, s),
@@ -141,7 +143,7 @@
     own[...] = spread[0, pl.ds(pl.multiple_of(far * SIDE, SIDE), SIDE), :]
 
 
-def backward_kernel(chips, me, code0, code1, sent0, sent1, *refs):
+def backward_kernel(chips, tail0, tail1, sent0, sent1, *refs):
     groups, refs = refs[: len(chips)], refs[len(chips) :]
     if len(refs) == 1:
         (acc,) = refs
@@ -149,13 +151,14 @@
     else:
         before, mine, other, acc = refs
         acc[...] = before[...]
-    for half, (code, sent) in enumerate(((code0, sent0), (code1, sent1))):
-
-        def step(s, carry, half=half, code=code, sent=sent):
-            taken, chip, along, block = place(code[s], me)
+    for half, (tail, sent) in enumerate(((tail0, sent0), (tail1, sent1))):
+
+        def step(s, carry, half=half, tail=tail, sent=sent):
+            code, block = tail[0, half * SLOTS + s], tail[0, 2 * SLOTS + s]
+            chip, along = code >> 4, code & 15
             for n, blocks in zip(chips, groups):
 
-                @pl.when(taken & (chip == n))
+                @pl.when(chip == n)
                 def _(blocks=blocks):
                     start = pl.multiple_of(half * ROWS + block * SIDE, SIDE)
                     acc[pl.ds(start, SIDE), :] += jnp.dot(
@@ -191,12 +194,12 @@
     return [pl.BlockSpec(memory_space=pltpu.VMEM)] * n
 
 
-def call(kernel, outs, specs, scratch, flops, moved, out_specs=None):
+def call(kernel, outs, specs, scratch, flops, moved):
     return pl.pallas_call(
         kernel,
         out_shape=outs,
         in_specs=specs,
-        out_specs=out_specs or vmem(len(outs)),
+        out_specs=vmem(len(outs)),
         scratch_shapes=scratch,
         compiler_params=pltpu.CompilerParams(vmem_limit_bytes=24 * MEBI),
         cost_estimate=pl.CostEstimate(flops=flops, bytes_accessed=moved, transcendentals=0),
@@ -217,36 +220,34 @@
     bf16, f32, i32 = jnp.bfloat16, jnp.float32, jnp.int32
     group = jax.ShapeDtypeStruct((LINE, SIDE, SIDE), bf16)
     degree = acct_degree.reshape(4, SIDE)
-    payload, code = call(
+    me = lax.axis_index("acct").astype(i32).reshape(1)
+    (payload,) = call(
         prepare_kernel,
-        [jax.ShapeDtypeStruct((SENT, SIDE), bf16), jax.ShapeDtypeStruct((SLOTS,), i32)],
-        smem(4) + [pl.BlockSpec(memory_space=pl.ANY)] * 2 + vmem(1),
+        [jax.ShapeDtypeStruct((SENT, SIDE), bf16)],
+        smem(5) + [pl.BlockSpec(memory_space=pltpu.HBM)] * 2 + vmem(1),
         [pltpu.VMEM((ROWS, SIDE), bf16), pltpu.SemaphoreType.DMA((2,))],
         ROWS * SIDE,
         MEBI,
-        vmem(1) + smem(1),
     )(
+        me,
         attr_owner,
         tile_attr,
         tile_acct,
         tile_count,
-        tile_weight.reshape(TILES, SIDE),
-        scores0,
+        pltpu.with_memory_space_constraint(tile_weight.reshape(TILES, SIDE), pltpu.HBM),
+        pltpu.with_memory_space_constraint(scores0, pltpu.HBM),
         degree,
     )
     payload1 = lax.ppermute(payload, "acct", SWAP)
-    tail1 = payload1[TILES + ROWS].astype(i32)
-    code1 = tail1[:SLOTS] + tail1[SLOTS : 2 * SLOTS] * 128
-    me = lax.axis_index("acct").astype(i32).reshape(1)
-
     flops = 2 * 10 * SIDE**3
-    slots = (me, code, code1, payload, payload1)
+    tails = [sent[TILES + ROWS :][:1].astype(i32) for sent in (payload, payload1)]
+    slots = (*tails, payload, payload1)
 
     def forward(chips):
         return call(
             functools.partial(forward_kernel, chips),
             [group] * len(chips),
-            smem(3) + vmem(2),
+            smem(2) + vmem(2),
             [pltpu.VMEM((len(chips) * LINE, SIDE, SIDE), f32)],
             flops,
             3 * MEBI,
@@ -254,9 +255,10 @@
 
     (o3,) = forward((3,))
     r3 = lax.ppermute(o3, "acct", DIAGONAL)
-    o1, o2, o0 = forward((1, 2, 0))
+    o1, o2 = forward((1, 2))
     r1 = lax.ppermute(o1, "acct", BESIDE)
     r2 = lax.ppermute(o2, "acct", ACROSS)
+    (o0,) = forward((0,))
     line = o0.astype(f32) + r1.astype(f32) + r2.astype(f32) + r3.astype(f32)
     line = line.astype(bf16).reshape(4, 4, SIDE, SIDE)
     line = lax.all_to_all(line, "acct", 0, 0, tiled=True, axis_index_groups=QUADS)
@@ -286,12 +288,12 @@
     g2 = lax.ppermute(g0, "acct", ACROSS)
     acc = jax.ShapeDtypeStruct((2 * ROWS, SIDE), f32)
     (before,) = call(
-        functools.partial(backward_kernel, (0,)), [acc], smem(3) + vmem(3), [], flops, 4 * MEBI
+        functools.partial(backward_kernel, (0,)), [acc], smem(2) + vmem(3), [], flops, 4 * MEBI
     )(*slots, g0)
     mine, other = call(
         functools.partial(backward_kernel, (1, 2, 3)),
         [jax.ShapeDtypeStruct((ROWS, SIDE), f32), jax.ShapeDtypeStruct((ROWS, SIDE), bf16)],
-        smem(3) + vmem(6),
+        smem(2) + vmem(6),
         [pltpu.VMEM(acc.shape, f32)],
         flops,
         4 * MEBI,

time: 143 us -> 137 us (0.958)
  waiting for transfers between devices: 39.3 us -> 28.3 us
  starting transfers between devices: 41.8 us -> 51.7 us
  blocking collectives: 43 us -> 40.4 us
  local copies, waits for them, and re-layouts: 2.7 us -> 0.76 us
    ppermute x1, starting transfers between devices: 1.92 us -> 9.59 us  [per_device(): rest = lax.ppermute(half, 'acct', SECOND)]
    ppermute x1, waiting for transfers between devices: 9.71 us -> 5.29 us  [per_device(): rest = lax.ppermute(half, 'acct', SECOND)]
    all_to_all x1, blocking collectives: 16.4 us -> 12 us  [per_device(): types = lax.all_to_all(types, 'attr', 0, 0, tiled=True)]
    ppermute x1, waiting for transfers between devices: 7.26 us -> 3.55 us  [per_device(): r2 = lax.ppermute(o2, 'acct', ACROSS)]
    ppermute x1, waiting for transfers between devices: 10.6 us -> 7.86 us  [per_device(): half = near.astype(f32) + lax.ppermute(near, 'acct', FIRST).astype(f32)]
    unnamed x18 -> x14, local copies, waits for them, and re-layouts: 2.63 us -> 0.69 us
    ppermute x1, starting transfers between devices: 1.92 us -> 3.44 us  [per_device(): r1 = lax.ppermute(o1, 'acct', BESIDE)]
    pallas_call x2 -> x3, Pallas kernels: 5.36 us -> 5.52 us  [forward(): call(functools.partial(forward_kernel, chips), [group] * len(chips), smem...]
where the time goes in v5:
time: 137 us; the launch traced here: 135 us
  starting transfers between devices  51.7 us (38%)
  blocking collectives  40.4 us (29%)
  waiting for transfers between devices  28.3 us (21%)
  Pallas kernels  12.2 us (9%)
  between operations  1.52 us (1%)
    all_to_all x1, blocking collectives, per_device(): lax.all_to_all(line, 'acct', 0, 0, tiled=True, axis_index_groups=QUADS)  14.7 us
    all_to_all x1, blocking collectives, per_device(): lax.all_to_all(spread, 'acct', 0, 0, tiled=True, axis_index_groups=QUADS)  13.7 us
    all_to_all x1, blocking collectives, per_device(): types = lax.all_to_all(types, 'attr', 0, 0, tiled=True)  12 us
    ppermute x1, starting transfers between devices, per_device(): r3 = lax.ppermute(o3, 'acct', DIAGONAL)  9.72 us
    ppermute x1, starting transfers between devices, per_device(): rest = lax.ppermute(half, 'acct', SECOND)  9.59 us
    ppermute x1, starting transfers between devices, per_device(): payload1 = lax.ppermute(payload, 'acct', SWAP)  8.79 us
    ppermute x1, waiting for transfers between devices, per_device(): half = near.astype(f32) + lax.ppermute(near, 'acct', FIRST).astype(f32)  7.86 us
    ppermute x1, starting transfers between devices, per_device(): lax.ppermute(other, 'acct', SWAP).astype(f32)  5.55 us
  transfers between devices with their start and end apart: 10, of which 8 were waited for; matrix products, arithmetic and copies ran while one was open for 0% of the time, Pallas kernels for 4%

profile of v5, /device:TPU:1, one launch (start us, length us, event | category | flops | bytes accessed | tf_op | source)
XLA Modules:
  0.0 135.3 jit_solution(4939866032399384949)
XLA Ops:
  1.3 0.0 copy-start.1
  1.3 0.0 copy-start.3
  1.3 0.0 copy-start.4
  1.3 0.0 copy-start.5
  1.3 0.6 copy-done.1
  2.0 0.0 copy-done.3
  2.0 0.0 copy-done.4
  2.0 0.0 copy-done.5
  2.0 1.7 %shard_map.104.sent0 = bf16[2576,128]{1,0:T(8,128)(2,1)S(1)} custom-call(s32[1]{0:T(128)} %bitcast.me, s32[1,128]{1,0:T(1,128)S(1)} %copy-done.3, s32[1,16]{1,0:T(1,128)S(1)} %copy-done.4, s32[1,16]{1,0:T(1,128)S(1)} %copy-done.5, s32[1,1]{1,0:T(1,128)S(6)} %copy.11.count, bf16[2048,128]{1,0:T(8,128)(2,1)} %bitcast.15, bf16[512,128]{1,0:T(8,128)(2,1)} %scores.3, ...), custom_call_target="tpu_custom_call" | custom-call | flops 65536 | bytes 1048576 | tf_op jit(solution)/shard_map/pallas_call | solution.py:224
  3.7 8.8 %collective-permute-start = (bf16[2576,128]{1,0:T(8,128)(2,1)S(1)}, bf16[2576,128]{1,0:T(8,128)(2,1)S(1)}, u32[]{:S(2)}, u32[]{:S(2)}) collective-permute-start(bf16[2576,128]{1,0:T(8,128)(2,1)S(1)} %shard_map.104.sent0), channel_id=1, source_target_pairs={{0,4},{4,0},{8,12},{12,8},{16,20},{20,16},{24,28},{28,24},{32,36},... | collective-permute-start | bytes 1978376 | tf_op jit(solution)/shard_map/ppermute | solution.py:241
  12.5 1.7 %collective-permute-done.sent1 = bf16[2576,128]{1,0:T(8,128)(2,1)S(1)} collective-permute-done((bf16[2576,128]{1,0:T(8,128)(2,1)S(1)}, bf16[2576,128]{1,0:T(8,128)(2,1)S(1)}, u32[]{:S(2)}, u32[]{:S(2)}) %collective-permute-start) | collective-permute-done | bytes 659488 | tf_op jit(solution)/shard_map/ppermute | solution.py:241
  14.2 1.3 shard_map.107
  15.5 9.7 %collective-permute-start.3 = (bf16[16,128,128]{2,1,0:T(8,128)(2,1)S(1)}, bf16[16,128,128]{2,1,0:T(8,128)(2,1)S(1)}, u32[]{:S(2)}, u32[]{:S(2)}) collective-permute-start(bf16[16,128,128]{2,1,0:T(8,128)(2,1)S(1)} %shard_map.107), channel_id=1, source_target_pairs={{0,40},{8,32},{16,56},{24,48},{32,8},{40,0},{48,24},{56,16},{64,10... | collective-permute-start | bytes 1572872 | tf_op jit(solution)/shard_map/ppermute | solution.py:257
  25.2 2.0 %shard_map.106 = (bf16[16,128,128]{2,1,0:T(8,128)(2,1)S(1)}, bf16[16,128,128]{2,1,0:T(8,128)(2,1)S(1)}) custom-call(s32[1,128]{1,0:T(1,128)S(1)} %slice_convert_fusion.1.tail0, s32[1,128]{1,0:T(1,128)S(1)} %slice_convert_fusion.tail1, bf16[2576,128]{1,0:T(8,128)(2,1)S(1)} %shard_map.104.sent0, bf16[2576,128]{1,0:T(8,128)(2,1)S(1)} %collective-permute-done.sent1), custom_call_target="tpu_custom_call" | custom-call | flops 41943040 | bytes 3145728 | tf_op jit(solution)/shard_map/pallas_call | solution.py:247
  27.2 1.9 %collective-permute-start.2 = (bf16[16,128,128]{2,1,0:T(8,128)(2,1)S(1)}, bf16[16,128,128]{2,1,0:T(8,128)(2,1)S(1)}, u32[]{:S(2)}, u32[]{:S(2)}) collective-permute-start(bf16[16,128,128]{2,1,0:T(8,128)(2,1)S(1)} %get-tuple-element.9), channel_id=1, source_target_pairs={{0,8},{8,0},{16,24},{24,16},{32,40},{40,32},{48,56},{56,48},{64,72... | collective-permute-start | bytes 1572872 | tf_op jit(solution)/shard_map/ppermute | solution.py:260
  29.2 3.4 %collective-permute-start.1 = (bf16[16,128,128]{2,1,0:T(8,128)(2,1)S(1)}, bf16[16,128,128]{2,1,0:T(8,128)(2,1)S(1)}, u32[]{:S(2)}, u32[]{:S(2)}) collective-permute-start(bf16[16,128,128]{2,1,0:T(8,128)(2,1)S(1)} %get-tuple-element.8), channel_id=1, source_target_pairs={{0,32},{8,40},{16,48},{24,56},{32,0},{40,8},{48,16},{56,24},{64,96... | collective-permute-start | bytes 1572872 | tf_op jit(solution)/shard_map/ppermute | solution.py:259
  32.6 2.2 %shard_map.105 = bf16[16,128,128]{2,1,0:T(8,128)(2,1)S(1)} custom-call(s32[1,128]{1,0:T(1,128)S(1)} %slice_convert_fusion.1.tail0, s32[1,128]{1,0:T(1,128)S(1)} %slice_convert_fusion.tail1, bf16[2576,128]{1,0:T(8,128)(2,1)S(1)} %shard_map.104.sent0, bf16[2576,128]{1,0:T(8,128)(2,1)S(1)} %collective-permute-done.sent1), custom_call_target="tpu_custom_call" | custom-call | flops 41943040 | bytes 3145728 | tf_op jit(solution)/shard_map/pallas_call | solution.py:247
  34.8 0.0 collective-permute-done.3
  34.8 3.5 %collective-permute-done.2 = bf16[16,128,128]{2,1,0:T(8,128)(2,1)S(1)} collective-permute-done((bf16[16,128,128]{2,1,0:T(8,128)(2,1)S(1)}, bf16[16,128,128]{2,1,0:T(8,128)(2,1)S(1)}, u32[]{:S(2)}, u32[]{:S(2)}) %collective-permute-start.2) | collective-permute-done | bytes 524320 | tf_op jit(solution)/shard_map/ppermute | solution.py:260
  38.4 1.9 %collective-permute-done.1 = bf16[16,128,128]{2,1,0:T(8,128)(2,1)S(1)} collective-permute-done((bf16[16,128,128]{2,1,0:T(8,128)(2,1)S(1)}, bf16[16,128,128]{2,1,0:T(8,128)(2,1)S(1)}, u32[]{:S(2)}, u32[]{:S(2)}) %collective-permute-start.1) | collective-permute-done | bytes 524320 | tf_op jit(solution)/shard_map/ppermute | solution.py:259
  40.3 0.3 add_convert_fusion
  40.6 0.0 copy-start.6
  40.7 14.7 %all_to_all.15.parts = bf16[4,4,128,128]{3,2,1,0:T(8,128)(2,1)S(1)} all-to-all(bf16[4,4,128,128]{3,2,1,0:T(8,128)(2,1)S(1)} %bitcast.14), channel_id=1, replica_groups={{0,64,24,88},{128,192,152,216},{256,320,280,344},{384,448,408,472},{32,..., dimensions={0} | all-to-all | bytes 1048576 | tf_op jit(solution)/shard_map/all_to_all | solution.py:264
  55.3 0.0 copy-done.6
  55.3 0.1 shard_map.108
  55.4 1.9 %collective-permute-start.4 = (bf16[528,128]{1,0:T(8,128)(2,1)S(1)}, bf16[528,128]{1,0:T(8,128)(2,1)S(1)}, u32[]{:S(2)}, u32[]{:S(2)}) collective-permute-start(bf16[528,128]{1,0:T(8,128)(2,1)S(1)} %shard_map.108), channel_id=1, source_target_pairs={{0,128},{8,136},{16,144},{24,152},{32,160},{40,168},{48,176},{56,1... | collective-permute-start | bytes 405512 | tf_op jit(solution)/shard_map/ppermute | solution.py:269
  57.3 7.9 %collective-permute-done.4 = bf16[528,128]{1,0:T(8,128)(2,1)S(1)} collective-permute-done((bf16[528,128]{1,0:T(8,128)(2,1)S(1)}, bf16[528,128]{1,0:T(8,128)(2,1)S(1)}, u32[]{:S(2)}, u32[]{:S(2)}) %collective-permute-start.4) | collective-permute-done | bytes 135200 | tf_op jit(solution)/shard_map/ppermute | solution.py:269
  65.2 9.6 %collective-permute-start.5 = (bf16[528,128]{1,0:T(8,128)(2,1)S(1)}, bf16[528,128]{1,0:T(8,128)(2,1)S(1)}, u32[]{:S(2)}, u32[]{:S(2)}) collective-permute-start(bf16[528,128]{1,0:T(8,128)(2,1)S(1)} %add_convert_fusion.1.mine), channel_id=1, source_target_pairs={{0,384},{8,392},{16,400},{24,408},{32,416},{40,424},{48,432},{56,4... | collective-permute-start | bytes 405512 | tf_op jit(solution)/shard_map/ppermute | solution.py:271
  74.8 5.3 %collective-permute-done.5.other = bf16[528,128]{1,0:T(8,128)(2,1)S(1)} collective-permute-done((bf16[528,128]{1,0:T(8,128)(2,1)S(1)}, bf16[528,128]{1,0:T(8,128)(2,1)S(1)}, u32[]{:S(2)}, u32[]{:S(2)}) %collective-permute-start.5) | collective-permute-done | bytes 135200 | tf_op jit(solution)/shard_map/ppermute | solution.py:271
  80.1 0.8 shard_map.109
  80.9 13.7 %all_to_all.16 = bf16[4,512,128]{2,1,0:T(8,128)(2,1)S(1)} all-to-all(bf16[4,512,128]{2,1,0:T(8,128)(2,1)S(1)} %get-tuple-element.10), channel_id=1, replica_groups={{0,64,24,88},{128,192,152,216},{256,320,280,344},{384,448,408,472},{32,..., dimensions={0} | all-to-all | bytes 1048576 | tf_op jit(solution)/shard_map/all_to_all | solution.py:284
  94.6 1.9 %collective-permute-start.6 = (bf16[2048,128]{1,0:T(8,128)(2,1)S(1)}, bf16[2048,128]{1,0:T(8,128)(2,1)S(1)}, u32[]{:S(2)}, u32[]{:S(2)}) collective-permute-start(bf16[2048,128]{1,0:T(8,128)(2,1)S(1)} %bitcast.7), channel_id=1, source_target_pairs={{0,32},{8,40},{16,48},{24,56},{32,0},{40,8},{48,16},{56,24},{64,96... | collective-permute-start | bytes 1572872 | tf_op jit(solution)/shard_map/ppermute | solution.py:287
  96.5 4.2 %collective-permute-start.7 = (bf16[2048,128]{1,0:T(8,128)(2,1)S(1)}, bf16[2048,128]{1,0:T(8,128)(2,1)S(1)}, u32[]{:S(2)}, u32[]{:S(2)}) collective-permute-start(bf16[2048,128]{1,0:T(8,128)(2,1)S(1)} %bitcast.8), channel_id=1, source_target_pairs={{0,8},{8,0},{16,24},{24,16},{32,40},{40,32},{48,56},{56,48},{64,72... | collective-permute-start | bytes 1572872 | tf_op jit(solution)/shard_map/ppermute | solution.py:288
  100.7 4.7 %collective-permute-start.8 = (bf16[2048,128]{1,0:T(8,128)(2,1)S(1)}, bf16[2048,128]{1,0:T(8,128)(2,1)S(1)}, u32[]{:S(2)}, u32[]{:S(2)}) collective-permute-start(bf16[2048,128]{1,0:T(8,128)(2,1)S(1)} %bitcast.9), channel_id=1, source_target_pairs={{0,40},{8,32},{16,56},{24,48},{32,8},{40,0},{48,24},{56,16},{64,10... | collective-permute-start | bytes 1572872 | tf_op jit(solution)/shard_map/ppermute | solution.py:286
  105.4 1.5 %shard_map.110.refs_3_ = f32[1024,128]{1,0:T(8,128)S(1)} custom-call(s32[1,128]{1,0:T(1,128)S(1)} %slice_convert_fusion.1.tail0, s32[1,128]{1,0:T(1,128)S(1)} %slice_convert_fusion.tail1, bf16[2576,128]{1,0:T(8,128)(2,1)S(1)} %shard_map.104.sent0, bf16[2576,128]{1,0:T(8,128)(2,1)S(1)} %collective-permute-done.sent1, bf16[2048,128]{1,0:T(8,128)(2,1)S(1)} %bitcast.10), custom_call_target="tpu_custom_call" | custom-call | flops 41943040 | bytes 4194304 | tf_op jit(solution)/shard_map/pallas_call | solution.py:290
  107.0 0.0 collective-permute-done.6.refs_0_
  107.0 5.5 %collective-permute-done.7.refs_1_ = bf16[2048,128]{1,0:T(8,128)(2,1)S(1)} collective-permute-done((bf16[2048,128]{1,0:T(8,128)(2,1)S(1)}, bf16[2048,128]{1,0:T(8,128)(2,1)S(1)}, u32[]{:S(2)}, u32[]{:S(2)}) %collective-permute-start.7) | collective-permute-done | bytes 524320 | tf_op jit(solution)/shard_map/ppermute | solution.py:288
  112.5 1.5 %collective-permute-done.8.refs_2_ = bf16[2048,128]{1,0:T(8,128)(2,1)S(1)} collective-permute-done((bf16[2048,128]{1,0:T(8,128)(2,1)S(1)}, bf16[2048,128]{1,0:T(8,128)(2,1)S(1)}, u32[]{:S(2)}, u32[]{:S(2)}) %collective-permute-start.8) | collective-permute-done | bytes 524320 | tf_op jit(solution)/shard_map/ppermute | solution.py:286
  114.0 1.7 %shard_map.111 = (f32[512,128]{1,0:T(8,128)S(1)}, bf16[512,128]{1,0:T(8,128)(2,1)S(1)}) custom-call(s32[1,128]{1,0:T(1,128)S(1)} %slice_convert_fusion.1.tail0, s32[1,128]{1,0:T(1,128)S(1)} %slice_convert_fusion.tail1, bf16[2576,128]{1,0:T(8,128)(2,1)S(1)} %shard_map.104.sent0, bf16[2576,128]{1,0:T(8,128)(2,1)S(1)} %collective-permute-done.sent1, ...), custom_call_target="tpu_custom_call" | custom-call | flops 41943040 | bytes 4194304 | tf_op jit(solution)/shard_map/pallas_call | solution.py:293
  115.7 5.5 %collective-permute-start.9 = (bf16[512,128]{1,0:T(8,128)(2,1)S(1)}, bf16[512,128]{1,0:T(8,128)(2,1)S(1)}, u32[]{:S(2)}, u32[]{:S(2)}) collective-permute-start(bf16[512,128]{1,0:T(8,128)(2,1)S(1)} %get-tuple-element.12), channel_id=1, source_target_pairs={{0,4},{4,0},{8,12},{12,8},{16,20},{20,16},{24,28},{28,24},{32,36},... | collective-permute-start | bytes 393224 | tf_op jit(solution)/shard_map/ppermute | solution.py:302
  121.2 1.0 collective-permute-done.9
  122.2 0.1 broadcast_in_dim.4
  122.3 0.0 copy-start
  122.3 0.0 copy-start.2
  122.3 12.0 %all_to_all.17.types = bf16[4,512,128]{2,1,0:T(8,128)(2,1)S(1)} all-to-all(bf16[4,512,128]{2,1,0:T(8,128)(2,1)S(1)} %broadcast_in_dim.4), channel_id=1, replica_groups=mesh['acct'=128,'attr'=4] {'attr'}, dimensions={0} | all-to-all | bytes 1048576 | tf_op jit(solution)/shard_map/all_to_all | solution.py:304
  134.4 0.0 copy-done
  134.4 0.0 copy-done.2
  134.4 0.9 shard_map.112
  (4 shorter events, 0.1 us)
Async XLA Ops:
  1.3 0.7 copy-start.1
  1.3 0.7 copy-start.3
  1.3 0.7 copy-start.4
  1.3 0.7 copy-start.5
  3.7 10.5 %collective-permute-start = (bf16[2576,128]{1,0:T(8,128)(2,1)S(1)}, bf16[2576,128]{1,0:T(8,128)(2,1)S(1)}, u32[]{:S(2)}, u32[]{:S(2)}) collective-permute-start(bf16[2576,128]{1,0:T(8,128)(2,1)S(1)} %shard_map.104.sent0), channel_id=1, source_target_pairs={{0,4},{4,0},{8,12},{12,8},{16,20},{20,16},{24,28},{28,24},{32,36},... | collective-permute-start | bytes 1978376 | tf_op jit(solution)/shard_map/ppermute | solution.py:241
  15.5 19.3 %collective-permute-start.3 = (bf16[16,128,128]{2,1,0:T(8,128)(2,1)S(1)}, bf16[16,128,128]{2,1,0:T(8,128)(2,1)S(1)}, u32[]{:S(2)}, u32[]{:S(2)}) collective-permute-start(bf16[16,128,128]{2,1,0:T(8,128)(2,1)S(1)} %shard_map.107), channel_id=1, source_target_pairs={{0,40},{8,32},{16,56},{24,48},{32,8},{40,0},{48,24},{56,16},{64,10... | collective-permute-start | bytes 1572872 | tf_op jit(solution)/shard_map/ppermute | solution.py:257
  27.2 11.1 %collective-permute-start.2 = (bf16[16,128,128]{2,1,0:T(8,128)(2,1)S(1)}, bf16[16,128,128]{2,1,0:T(8,128)(2,1)S(1)}, u32[]{:S(2)}, u32[]{:S(2)}) collective-permute-start(bf16[16,128,128]{2,1,0:T(8,128)(2,1)S(1)} %get-tuple-element.9), channel_id=1, source_target_pairs={{0,8},{8,0},{16,24},{24,16},{32,40},{40,32},{48,56},{56,48},{64,72... | collective-permute-start | bytes 1572872 | tf_op jit(solution)/shard_map/ppermute | solution.py:260
  29.2 11.1 %collective-permute-start.1 = (bf16[16,128,128]{2,1,0:T(8,128)(2,1)S(1)}, bf16[16,128,128]{2,1,0:T(8,128)(2,1)S(1)}, u32[]{:S(2)}, u32[]{:S(2)}) collective-permute-start(bf16[16,128,128]{2,1,0:T(8,128)(2,1)S(1)} %get-tuple-element.8), channel_id=1, source_target_pairs={{0,32},{8,40},{16,48},{24,56},{32,0},{40,8},{48,16},{56,24},{64,96... | collective-permute-start | bytes 1572872 | tf_op jit(solution)/shard_map/ppermute | solution.py:259
  40.6 14.7 %copy-start.6 = (s32[1,128]{1,0:T(1,128)S(1)}, s32[1,128]{1,0:T(1,128)}, u32[]{:S(2)}) copy-start(s32[1,128]{1,0:T(1,128)} %degree.1) | copy-start | bytes 1540
  55.4 9.8 %collective-permute-start.4 = (bf16[528,128]{1,0:T(8,128)(2,1)S(1)}, bf16[528,128]{1,0:T(8,128)(2,1)S(1)}, u32[]{:S(2)}, u32[]{:S(2)}) collective-permute-start(bf16[528,128]{1,0:T(8,128)(2,1)S(1)} %shard_map.108), channel_id=1, source_target_pairs={{0,128},{8,136},{16,144},{24,152},{32,160},{40,168},{48,176},{56,1... | collective-permute-start | bytes 405512 | tf_op jit(solution)/shard_map/ppermute | solution.py:269
  65.2 14.9 %collective-permute-start.5 = (bf16[528,128]{1,0:T(8,128)(2,1)S(1)}, bf16[528,128]{1,0:T(8,128)(2,1)S(1)}, u32[]{:S(2)}, u32[]{:S(2)}) collective-permute-start(bf16[528,128]{1,0:T(8,128)(2,1)S(1)} %add_convert_fusion.1.mine), channel_id=1, source_target_pairs={{0,384},{8,392},{16,400},{24,408},{32,416},{40,424},{48,432},{56,4... | collective-permute-start | bytes 405512 | tf_op jit(solution)/shard_map/ppermute | solution.py:271
  94.6 12.4 %collective-permute-start.6 = (bf16[2048,128]{1,0:T(8,128)(2,1)S(1)}, bf16[2048,128]{1,0:T(8,128)(2,1)S(1)}, u32[]{:S(2)}, u32[]{:S(2)}) collective-permute-start(bf16[2048,128]{1,0:T(8,128)(2,1)S(1)} %bitcast.7), channel_id=1, source_target_pairs={{0,32},{8,40},{16,48},{24,56},{32,0},{40,8},{48,16},{56,24},{64,96... | collective-permute-start | bytes 1572872 | tf_op jit(solution)/shard_map/ppermute | solution.py:287
  96.5 15.9 %collective-permute-start.7 = (bf16[2048,128]{1,0:T(8,128)(2,1)S(1)}, bf16[2048,128]{1,0:T(8,128)(2,1)S(1)}, u32[]{:S(2)}, u32[]{:S(2)}) collective-permute-start(bf16[2048,128]{1,0:T(8,128)(2,1)S(1)} %bitcast.8), channel_id=1, source_target_pairs={{0,8},{8,0},{16,24},{24,16},{32,40},{40,32},{48,56},{56,48},{64,72... | collective-permute-start | bytes 1572872 | tf_op jit(solution)/shard_map/ppermute | solution.py:288
  100.7 13.2 %collective-permute-start.8 = (bf16[2048,128]{1,0:T(8,128)(2,1)S(1)}, bf16[2048,128]{1,0:T(8,128)(2,1)S(1)}, u32[]{:S(2)}, u32[]{:S(2)}) collective-permute-start(bf16[2048,128]{1,0:T(8,128)(2,1)S(1)} %bitcast.9), channel_id=1, source_target_pairs={{0,40},{8,32},{16,56},{24,48},{32,8},{40,0},{48,24},{56,16},{64,10... | collective-permute-start | bytes 1572872 | tf_op jit(solution)/shard_map/ppermute | solution.py:286
  115.7 6.5 %collective-permute-start.9 = (bf16[512,128]{1,0:T(8,128)(2,1)S(1)}, bf16[512,128]{1,0:T(8,128)(2,1)S(1)}, u32[]{:S(2)}, u32[]{:S(2)}) collective-permute-start(bf16[512,128]{1,0:T(8,128)(2,1)S(1)} %get-tuple-element.12), channel_id=1, source_target_pairs={{0,4},{4,0},{8,12},{12,8},{16,20},{20,16},{24,28},{28,24},{32,36},... | collective-permute-start | bytes 393224 | tf_op jit(solution)/shard_map/ppermute | solution.py:302
  122.3 12.0 %copy-start = (bf16[512,128]{1,0:T(8,128)(2,1)S(1)}, bf16[512,128]{1,0:T(8,128)(2,1)}, u32[]{:S(2)}) copy-start(bf16[512,128]{1,0:T(8,128)(2,1)} %scores.3) | copy-start | bytes 393220
  122.3 12.0 %copy-start.2 = (s32[512]{0:T(512)S(1)}, s32[512]{0:T(512)}, u32[]{:S(2)}) copy-start(s32[512]{0:T(512)} %param.10) | copy-start | bytes 6148

commit v6 on v5

--- a/solution.py
+++ b/solution.py
@@ -34,14 +34,18 @@
 BESIDE = pairs(lambda c, u, v: (u ^ 1, v))
 ACROSS = pairs(lambda c, u, v: (u, v ^ 1))
 DIAGONAL = pairs(lambda c, u, v: (u ^ 1, v ^ 1))
-FIRST = pairs(lambda c, u, v: (u ^ 4 if c == 0 else 12 - (u & 12) + (u & 3), v))
-SECOND = pairs(lambda c, u, v: (u ^ 4 if c == 1 else 12 - (u & 12) + (u & 3), v))
 QUADS = [
     [device(c, far * 4 + step * 2 + odd, (0, 3, 1, 2)[side * 2 + end]) for end in (0, 1) for step in (0, 1)]
     for c in (0, 1)
     for side in (0, 1)
     for odd in (0, 1)
     for far in range(4)
+]
+FARS = [
+    [device(c, far * 4 + step, v) for far in range(4)]
+    for c in (0, 1)
+    for step in range(4)
+    for v in range(4)
 ]
 
 
@@ -120,23 +124,23 @@
         out[...] = acc[n * LINE : (n + 1) * LINE].astype(out.dtype)
 
 
-def near_kernel(me, parts, degree, sums):
+def near_kernel(parts, degree, sums):
     for n in range(4):
         total = parts[0, n].astype(jnp.float32)
         for k in range(1, 4):
             total += parts[k, n].astype(jnp.float32)
         sums[n * SIDE : (n + 1) * SIDE, :] = total.astype(sums.dtype)
-    row = lax.broadcasted_iota(jnp.int32, (SLOTS, SIDE), 0)
-    mine = jnp.where(row == where(me[0])[1] >> 2, degree[...].astype(jnp.float32), 0.0)
-    sums[FOUR:, :] = mine.astype(sums.dtype)
-
-
-def far_kernel(me, mine, other, own, spread):
-    degree = mine[FOUR:, :].astype(jnp.float32) + other[FOUR:, :].astype(jnp.float32)
+    sums[FOUR:, :] = jnp.broadcast_to(degree[...].astype(jnp.float32), (SLOTS, SIDE)).astype(sums.dtype)
+
+
+def far_kernel(me, parts, own, spread):
     for n in range(4):
         rows = pl.ds(n * SIDE, SIDE)
-        total = mine[rows, :].astype(jnp.float32) + other[rows, :].astype(jnp.float32)
-        scores = (total * column(lax.rsqrt(degree[n : n + 1, :]))).astype(spread.dtype)
+        total = parts[0, rows, :].astype(jnp.float32)
+        for k in range(1, 4):
+            total += parts[k, rows, :].astype(jnp.float32)
+        degree = parts[n, FOUR:, :].astype(jnp.float32)[:1]
+        scores = (total * column(lax.rsqrt(degree))).astype(spread.dtype)
         for k in range(4):
             spread[k, rows, :] = scores
     far = where(me[0])[1] >> 2
@@ -263,23 +267,19 @@
     line = line.astype(bf16).reshape(4, 4, SIDE, SIDE)
     line = lax.all_to_all(line, "acct", 0, 0, tiled=True, axis_index_groups=QUADS)
     sums = jax.ShapeDtypeStruct((FOUR + SLOTS, SIDE), bf16)
-    (near,) = call(
-        near_kernel, [sums], smem(1) + vmem(2), [], SIDE * SIDE * LINE, MEBI
-    )(me, line, attr_degree)
-    half = near.astype(f32) + lax.ppermute(near, "acct", FIRST).astype(f32)
-    half = half.astype(bf16)
-    rest = lax.ppermute(half, "acct", SECOND)
+    (near,) = call(near_kernel, [sums], vmem(2), [], SIDE * SIDE * LINE, MEBI)(line, attr_degree)
+    fars = lax.all_gather(near, "acct", axis=0, tiled=False, axis_index_groups=FARS)
     own_scores, spread = call(
         far_kernel,
         [
             jax.ShapeDtypeStruct((SIDE, SIDE), bf16),
             jax.ShapeDtypeStruct((4, FOUR, SIDE), bf16),
         ],
-        smem(1) + vmem(2),
+        smem(1) + vmem(1),
         [],
         SIDE * SIDE * LINE,
         MEBI // 2,
-    )(me, half, rest)
+    )(me, fars)
 
     g0 = lax.all_to_all(spread, "acct", 0, 0, tiled=True, axis_index_groups=QUADS)
     g0 = g0.reshape(LINE * SIDE, SIDE)
@@ -291,13 +291,13 @@
         functools.partial(backward_kernel, (0,)), [acc], smem(2) + vmem(3), [], flops, 4 * MEBI
     )(*slots, g0)
     mine, other = call(
-        functools.partial(backward_kernel, (1, 2, 3)),
+        functools.partial(backward_kernel, (3, 1, 2)),
         [jax.ShapeDtypeStruct((ROWS, SIDE), f32), jax.ShapeDtypeStruct((ROWS, SIDE), bf16)],
         smem(2) + vmem(6),
         [pltpu.VMEM(acc.shape, f32)],
         flops,
         4 * MEBI,
-    )(*slots, g1, g2, g3, before)
+    )(*slots, g3, g1, g2, before)
 
     returned = (mine + lax.ppermute(other, "acct", SWAP).astype(f32)).astype(bf16)
     types = jnp.broadcast_to(returned[None], (4, ROWS, SIDE))

time: 137 us -> 137 us (level)
  blocking collectives: 40.4 us -> 62.3 us
  waiting for transfers between devices: 28.3 us -> 17.6 us
  starting transfers between devices: 51.7 us -> 42.8 us
    all_gather x0 -> x1, blocking collectives: none -> 23.5 us  [per_device(): lax.all_gather(near, 'acct', axis=0, tiled=False, axis_index_groups=FARS)]
    ppermute x2 -> x0, waiting for transfers between devices: 13.2 us -> none  [the longest x1 7.86 us: per_device(): half = near.astype(f32) + lax.ppermute(near, 'acct', FIRST).astype(f32)]
    ppermute x2 -> x0, starting transfers between devices: 11.5 us -> none  [the longest x1 9.59 us: per_device(): rest = lax.ppermute(half, 'acct', SECOND)]
    ppermute x1, starting transfers between devices: 4.69 us -> 11 us  [per_device(): g3 = lax.ppermute(g0, 'acct', DIAGONAL)]
    ppermute x1, waiting for transfers between devices: 0.01 us -> 5.17 us  [per_device(): g1 = lax.ppermute(g0, 'acct', BESIDE)]
    all_to_all x1, blocking collectives: 14.7 us -> 10.3 us  [per_device(): lax.all_to_all(line, 'acct', 0, 0, tiled=True, axis_index_groups=QUADS)]
    ppermute x1, waiting for transfers between devices: 5.46 us -> 1.34 us  [per_device(): g2 = lax.ppermute(g0, 'acct', ACROSS)]
    all_to_all x1, blocking collectives: 12 us -> 14.1 us  [per_device(): types = lax.all_to_all(types, 'attr', 0, 0, tiled=True)]
  transfers between devices with their start and end apart: 10 -> 8, of which waited for: 8 -> 7; matrix products, arithmetic and copies ran while one was open for 0% -> 0% of each run, Pallas kernels for 4% -> 4%
where the time goes in v6:
time: 137 us
  blocking collectives  62.3 us (45%)
  starting transfers between devices  42.8 us (31%)
  waiting for transfers between devices  17.6 us (13%)
  Pallas kernels  11.1 us (8%)
  between operations  1.49 us (1%)
    all_gather x1, blocking collectives, per_device(): lax.all_gather(near, 'acct', axis=0, tiled=False, axis_index_groups=FARS)  23.5 us
    all_to_all x1, blocking collectives, per_device(): lax.all_to_all(spread, 'acct', 0, 0, tiled=True, axis_index_groups=QUADS)  14.4 us
    all_to_all x1, blocking collectives, per_device(): types = lax.all_to_all(types, 'attr', 0, 0, tiled=True)  14.1 us
    ppermute x1, starting transfers between devices, per_device(): g3 = lax.ppermute(g0, 'acct', DIAGONAL)  11 us
    all_to_all x1, blocking collectives, per_device(): lax.all_to_all(line, 'acct', 0, 0, tiled=True, axis_index_groups=QUADS)  10.3 us
    ppermute x1, starting transfers between devices, per_device(): payload1 = lax.ppermute(payload, 'acct', SWAP)  8.79 us
    ppermute x1, starting transfers between devices, per_device(): r3 = lax.ppermute(o3, 'acct', DIAGONAL)  8.3 us
    ppermute x1, starting transfers between devices, per_device(): lax.ppermute(other, 'acct', SWAP).astype(f32)  6.09 us
  transfers between devices with their start and end apart: 8, of which 7 were waited for; matrix products, arithmetic and copies ran while one was open for 0% of the time, Pallas kernels for 4%

profile of v6, /device:TPU:1, one launch (start us, length us, event | category | flops | bytes accessed | tf_op | source)
XLA Modules:
  0.0 136.5 jit_solution(688628499881835358)
XLA Ops:
  1.3 0.0 copy-start.1
  1.3 0.0 copy-start.3
  1.3 0.0 copy-start.4
  1.3 0.0 copy-start.5
  1.3 0.6 copy-done.1
  2.0 0.0 copy-done.3
  2.0 0.0 copy-done.4
  2.0 0.0 copy-done.5
  2.0 1.7 %shard_map.104.sent0 = bf16[2576,128]{1,0:T(8,128)(2,1)S(1)} custom-call(s32[1]{0:T(128)} %bitcast.me, s32[1,128]{1,0:T(1,128)S(1)} %copy-done.3, s32[1,16]{1,0:T(1,128)S(1)} %copy-done.4, s32[1,16]{1,0:T(1,128)S(1)} %copy-done.5, s32[1,1]{1,0:T(1,128)S(6)} %copy.11.count, bf16[2048,128]{1,0:T(8,128)(2,1)} %bitcast.17, bf16[512,128]{1,0:T(8,128)(2,1)} %scores.3, ...), custom_call_target="tpu_custom_call" | custom-call | flops 65536 | bytes 1048576 | tf_op jit(solution)/shard_map/pallas_call | solution.py:228
  3.7 8.8 %collective-permute-start = (bf16[2576,128]{1,0:T(8,128)(2,1)S(1)}, bf16[2576,128]{1,0:T(8,128)(2,1)S(1)}, u32[]{:S(2)}, u32[]{:S(2)}) collective-permute-start(bf16[2576,128]{1,0:T(8,128)(2,1)S(1)} %shard_map.104.sent0), channel_id=1, source_target_pairs={{0,4},{4,0},{8,12},{12,8},{16,20},{20,16},{24,28},{28,24},{32,36},... | collective-permute-start | bytes 1978376 | tf_op jit(solution)/shard_map/ppermute | solution.py:245
  12.5 1.7 %collective-permute-done.sent1 = bf16[2576,128]{1,0:T(8,128)(2,1)S(1)} collective-permute-done((bf16[2576,128]{1,0:T(8,128)(2,1)S(1)}, bf16[2576,128]{1,0:T(8,128)(2,1)S(1)}, u32[]{:S(2)}, u32[]{:S(2)}) %collective-permute-start) | collective-permute-done | bytes 659488 | tf_op jit(solution)/shard_map/ppermute | solution.py:245
  14.2 1.3 shard_map.107
  15.5 8.3 %collective-permute-start.3 = (bf16[16,128,128]{2,1,0:T(8,128)(2,1)S(1)}, bf16[16,128,128]{2,1,0:T(8,128)(2,1)S(1)}, u32[]{:S(2)}, u32[]{:S(2)}) collective-permute-start(bf16[16,128,128]{2,1,0:T(8,128)(2,1)S(1)} %shard_map.107), channel_id=1, source_target_pairs={{0,40},{8,32},{16,56},{24,48},{32,8},{40,0},{48,24},{56,16},{64,10... | collective-permute-start | bytes 1572872 | tf_op jit(solution)/shard_map/ppermute | solution.py:261
  23.8 1.7 %shard_map.106 = (bf16[16,128,128]{2,1,0:T(8,128)(2,1)S(1)}, bf16[16,128,128]{2,1,0:T(8,128)(2,1)S(1)}) custom-call(s32[1,128]{1,0:T(1,128)S(1)} %slice_convert_fusion.1.tail0, s32[1,128]{1,0:T(1,128)S(1)} %slice_convert_fusion.tail1, bf16[2576,128]{1,0:T(8,128)(2,1)S(1)} %shard_map.104.sent0, bf16[2576,128]{1,0:T(8,128)(2,1)S(1)} %collective-permute-done.sent1), custom_call_target="tpu_custom_call" | custom-call | flops 41943040 | bytes 3145728 | tf_op jit(solution)/shard_map/pallas_call | solution.py:251
  25.5 2.6 %collective-permute-start.2 = (bf16[16,128,128]{2,1,0:T(8,128)(2,1)S(1)}, bf16[16,128,128]{2,1,0:T(8,128)(2,1)S(1)}, u32[]{:S(2)}, u32[]{:S(2)}) collective-permute-start(bf16[16,128,128]{2,1,0:T(8,128)(2,1)S(1)} %get-tuple-element.9), channel_id=1, source_target_pairs={{0,8},{8,0},{16,24},{24,16},{32,40},{40,32},{48,56},{56,48},{64,72... | collective-permute-start | bytes 1572872 | tf_op jit(solution)/shard_map/ppermute | solution.py:264
  28.1 1.9 %collective-permute-start.1 = (bf16[16,128,128]{2,1,0:T(8,128)(2,1)S(1)}, bf16[16,128,128]{2,1,0:T(8,128)(2,1)S(1)}, u32[]{:S(2)}, u32[]{:S(2)}) collective-permute-start(bf16[16,128,128]{2,1,0:T(8,128)(2,1)S(1)} %get-tuple-element.8), channel_id=1, source_target_pairs={{0,32},{8,40},{16,48},{24,56},{32,0},{40,8},{48,16},{56,24},{64,96... | collective-permute-start | bytes 1572872 | tf_op jit(solution)/shard_map/ppermute | solution.py:263
  30.0 1.8 %shard_map.105 = bf16[16,128,128]{2,1,0:T(8,128)(2,1)S(1)} custom-call(s32[1,128]{1,0:T(1,128)S(1)} %slice_convert_fusion.1.tail0, s32[1,128]{1,0:T(1,128)S(1)} %slice_convert_fusion.tail1, bf16[2576,128]{1,0:T(8,128)(2,1)S(1)} %shard_map.104.sent0, bf16[2576,128]{1,0:T(8,128)(2,1)S(1)} %collective-permute-done.sent1), custom_call_target="tpu_custom_call" | custom-call | flops 41943040 | bytes 3145728 | tf_op jit(solution)/shard_map/pallas_call | solution.py:251
  31.9 0.0 collective-permute-done.3
  31.9 4.7 %collective-permute-done.2 = bf16[16,128,128]{2,1,0:T(8,128)(2,1)S(1)} collective-permute-done((bf16[16,128,128]{2,1,0:T(8,128)(2,1)S(1)}, bf16[16,128,128]{2,1,0:T(8,128)(2,1)S(1)}, u32[]{:S(2)}, u32[]{:S(2)}) %collective-permute-start.2) | collective-permute-done | bytes 524320 | tf_op jit(solution)/shard_map/ppermute | solution.py:264
  36.6 2.6 %collective-permute-done.1 = bf16[16,128,128]{2,1,0:T(8,128)(2,1)S(1)} collective-permute-done((bf16[16,128,128]{2,1,0:T(8,128)(2,1)S(1)}, bf16[16,128,128]{2,1,0:T(8,128)(2,1)S(1)}, u32[]{:S(2)}, u32[]{:S(2)}) %collective-permute-start.1) | collective-permute-done | bytes 524320 | tf_op jit(solution)/shard_map/ppermute | solution.py:263
  39.3 0.3 add_convert_fusion
  39.6 0.0 copy-start.6
  39.6 10.3 %all_to_all.15.parts = bf16[4,4,128,128]{3,2,1,0:T(8,128)(2,1)S(1)} all-to-all(bf16[4,4,128,128]{3,2,1,0:T(8,128)(2,1)S(1)} %bitcast.16), channel_id=1, replica_groups={{0,64,24,88},{128,192,152,216},{256,320,280,344},{384,448,408,472},{32,..., dimensions={0} | all-to-all | bytes 1048576 | tf_op jit(solution)/shard_map/all_to_all | solution.py:268
  49.9 0.0 copy-done.6
  49.9 0.1 shard_map.108
  50.0 23.5 %all-gather = bf16[2112,128]{1,0:T(8,128)(2,1)S(1)} all-gather(bf16[528,128]{1,0:T(8,128)(2,1)S(1)} %shard_map.108), channel_id=2, replica_groups={{0,128,256,384},{8,136,264,392},{16,144,272,400},{24,152,280,408},{32,1..., dimensions={0}, use_global_device_ids=true | all-gather | bytes 675840 | tf_op jit(solution)/shard_map/all_gather | solution.py:271
  73.5 0.8 shard_map.109
  74.3 14.4 %all_to_all.16 = bf16[4,512,128]{2,1,0:T(8,128)(2,1)S(1)} all-to-all(bf16[4,512,128]{2,1,0:T(8,128)(2,1)S(1)} %get-tuple-element.10), channel_id=1, replica_groups={{0,64,24,88},{128,192,152,216},{256,320,280,344},{384,448,408,472},{32,..., dimensions={0} | all-to-all | bytes 1048576 | tf_op jit(solution)/shard_map/all_to_all | solution.py:284
  88.7 11.0 %collective-permute-start.4 = (bf16[2048,128]{1,0:T(8,128)(2,1)S(1)}, bf16[2048,128]{1,0:T(8,128)(2,1)S(1)}, u32[]{:S(2)}, u32[]{:S(2)}) collective-permute-start(bf16[2048,128]{1,0:T(8,128)(2,1)S(1)} %bitcast.9), channel_id=1, source_target_pairs={{0,40},{8,32},{16,56},{24,48},{32,8},{40,0},{48,24},{56,16},{64,10... | collective-permute-start | bytes 1572872 | tf_op jit(solution)/shard_map/ppermute | solution.py:286
  99.7 1.9 %collective-permute-start.5 = (bf16[2048,128]{1,0:T(8,128)(2,1)S(1)}, bf16[2048,128]{1,0:T(8,128)(2,1)S(1)}, u32[]{:S(2)}, u32[]{:S(2)}) collective-permute-start(bf16[2048,128]{1,0:T(8,128)(2,1)S(1)} %bitcast.10), channel_id=1, source_target_pairs={{0,32},{8,40},{16,48},{24,56},{32,0},{40,8},{48,16},{56,24},{64,96... | collective-permute-start | bytes 1572872 | tf_op jit(solution)/shard_map/ppermute | solution.py:287
  101.6 2.2 %collective-permute-start.6 = (bf16[2048,128]{1,0:T(8,128)(2,1)S(1)}, bf16[2048,128]{1,0:T(8,128)(2,1)S(1)}, u32[]{:S(2)}, u32[]{:S(2)}) collective-permute-start(bf16[2048,128]{1,0:T(8,128)(2,1)S(1)} %bitcast.11), channel_id=1, source_target_pairs={{0,8},{8,0},{16,24},{24,16},{32,40},{40,32},{48,56},{56,48},{64,72... | collective-permute-start | bytes 1572872 | tf_op jit(solution)/shard_map/ppermute | solution.py:288
  103.8 1.3 shard_map.110.refs_3_
  105.1 1.1 collective-permute-done.4.refs_0_
  106.2 5.2 %collective-permute-done.5.refs_1_ = bf16[2048,128]{1,0:T(8,128)(2,1)S(1)} collective-permute-done((bf16[2048,128]{1,0:T(8,128)(2,1)S(1)}, bf16[2048,128]{1,0:T(8,128)(2,1)S(1)}, u32[]{:S(2)}, u32[]{:S(2)}) %collective-permute-start.5) | collective-permute-done | bytes 524320 | tf_op jit(solution)/shard_map/ppermute | solution.py:287
  111.4 1.3 collective-permute-done.6.refs_2_
  112.7 1.5 %shard_map.111 = (f32[512,128]{1,0:T(8,128)S(1)}, bf16[512,128]{1,0:T(8,128)(2,1)S(1)}) custom-call(s32[1,128]{1,0:T(1,128)S(1)} %slice_convert_fusion.1.tail0, s32[1,128]{1,0:T(1,128)S(1)} %slice_convert_fusion.tail1, bf16[2576,128]{1,0:T(8,128)(2,1)S(1)} %shard_map.104.sent0, bf16[2576,128]{1,0:T(8,128)(2,1)S(1)} %collective-permute-done.sent1, ...), custom_call_target="tpu_custom_call" | custom-call | flops 41943040 | bytes 4194304 | tf_op jit(solution)/shard_map/pallas_call | solution.py:293
  114.3 6.1 %collective-permute-start.7 = (bf16[512,128]{1,0:T(8,128)(2,1)S(1)}, bf16[512,128]{1,0:T(8,128)(2,1)S(1)}, u32[]{:S(2)}, u32[]{:S(2)}) collective-permute-start(bf16[512,128]{1,0:T(8,128)(2,1)S(1)} %get-tuple-element.12), channel_id=1, source_target_pairs={{0,4},{4,0},{8,12},{12,8},{16,20},{20,16},{24,28},{28,24},{32,36},... | collective-permute-start | bytes 393224 | tf_op jit(solution)/shard_map/ppermute | solution.py:302
  120.4 1.0 collective-permute-done.7
  121.4 0.1 broadcast_in_dim.4
  121.4 0.0 copy-start
  121.4 0.0 copy-start.2
  121.5 14.1 %all_to_all.17.types = bf16[4,512,128]{2,1,0:T(8,128)(2,1)S(1)} all-to-all(bf16[4,512,128]{2,1,0:T(8,128)(2,1)S(1)} %broadcast_in_dim.4), channel_id=1, replica_groups=mesh['acct'=128,'attr'=4] {'attr'}, dimensions={0} | all-to-all | bytes 1048576 | tf_op jit(solution)/shard_map/all_to_all | solution.py:304
  135.6 0.0 copy-done
  135.6 0.0 copy-done.2
  135.6 0.9 shard_map.112
  (3 shorter events, 0.0 us)
Async XLA Ops:
  1.3 0.7 copy-start.1
  1.3 0.7 copy-start.3
  1.3 0.7 copy-start.4
  1.3 0.7 copy-start.5
  3.7 10.5 %collective-permute-start = (bf16[2576,128]{1,0:T(8,128)(2,1)S(1)}, bf16[2576,128]{1,0:T(8,128)(2,1)S(1)}, u32[]{:S(2)}, u32[]{:S(2)}) collective-permute-start(bf16[2576,128]{1,0:T(8,128)(2,1)S(1)} %shard_map.104.sent0), channel_id=1, source_target_pairs={{0,4},{4,0},{8,12},{12,8},{16,20},{20,16},{24,28},{28,24},{32,36},... | collective-permute-start | bytes 1978376 | tf_op jit(solution)/shard_map/ppermute | solution.py:245
  15.5 16.4 %collective-permute-start.3 = (bf16[16,128,128]{2,1,0:T(8,128)(2,1)S(1)}, bf16[16,128,128]{2,1,0:T(8,128)(2,1)S(1)}, u32[]{:S(2)}, u32[]{:S(2)}) collective-permute-start(bf16[16,128,128]{2,1,0:T(8,128)(2,1)S(1)} %shard_map.107), channel_id=1, source_target_pairs={{0,40},{8,32},{16,56},{24,48},{32,8},{40,0},{48,24},{56,16},{64,10... | collective-permute-start | bytes 1572872 | tf_op jit(solution)/shard_map/ppermute | solution.py:261
  25.5 11.1 %collective-permute-start.2 = (bf16[16,128,128]{2,1,0:T(8,128)(2,1)S(1)}, bf16[16,128,128]{2,1,0:T(8,128)(2,1)S(1)}, u32[]{:S(2)}, u32[]{:S(2)}) collective-permute-start(bf16[16,128,128]{2,1,0:T(8,128)(2,1)S(1)} %get-tuple-element.9), channel_id=1, source_target_pairs={{0,8},{8,0},{16,24},{24,16},{32,40},{40,32},{48,56},{56,48},{64,72... | collective-permute-start | bytes 1572872 | tf_op jit(solution)/shard_map/ppermute | solution.py:264
  28.1 11.1 %collective-permute-start.1 = (bf16[16,128,128]{2,1,0:T(8,128)(2,1)S(1)}, bf16[16,128,128]{2,1,0:T(8,128)(2,1)S(1)}, u32[]{:S(2)}, u32[]{:S(2)}) collective-permute-start(bf16[16,128,128]{2,1,0:T(8,128)(2,1)S(1)} %get-tuple-element.8), channel_id=1, source_target_pairs={{0,32},{8,40},{16,48},{24,56},{32,0},{40,8},{48,16},{56,24},{64,96... | collective-permute-start | bytes 1572872 | tf_op jit(solution)/shard_map/ppermute | solution.py:263
  39.6 10.3 %copy-start.6 = (s32[1,128]{1,0:T(1,128)S(1)}, s32[1,128]{1,0:T(1,128)}, u32[]{:S(2)}) copy-start(s32[1,128]{1,0:T(1,128)} %degree.1) | copy-start | bytes 1540
  88.7 17.5 %collective-permute-start.4 = (bf16[2048,128]{1,0:T(8,128)(2,1)S(1)}, bf16[2048,128]{1,0:T(8,128)(2,1)S(1)}, u32[]{:S(2)}, u32[]{:S(2)}) collective-permute-start(bf16[2048,128]{1,0:T(8,128)(2,1)S(1)} %bitcast.9), channel_id=1, source_target_pairs={{0,40},{8,32},{16,56},{24,48},{32,8},{40,0},{48,24},{56,16},{64,10... | collective-permute-start | bytes 1572872 | tf_op jit(solution)/shard_map/ppermute | solution.py:286
  99.7 11.7 %collective-permute-start.5 = (bf16[2048,128]{1,0:T(8,128)(2,1)S(1)}, bf16[2048,128]{1,0:T(8,128)(2,1)S(1)}, u32[]{:S(2)}, u32[]{:S(2)}) collective-permute-start(bf16[2048,128]{1,0:T(8,128)(2,1)S(1)} %bitcast.10), channel_id=1, source_target_pairs={{0,32},{8,40},{16,48},{24,56},{32,0},{40,8},{48,16},{56,24},{64,96... | collective-permute-start | bytes 1572872 | tf_op jit(solution)/shard_map/ppermute | solution.py:287
  101.6 11.1 %collective-permute-start.6 = (bf16[2048,128]{1,0:T(8,128)(2,1)S(1)}, bf16[2048,128]{1,0:T(8,128)(2,1)S(1)}, u32[]{:S(2)}, u32[]{:S(2)}) collective-permute-start(bf16[2048,128]{1,0:T(8,128)(2,1)S(1)} %bitcast.11), channel_id=1, source_target_pairs={{0,8},{8,0},{16,24},{24,16},{32,40},{40,32},{48,56},{56,48},{64,72... | collective-permute-start | bytes 1572872 | tf_op jit(solution)/shard_map/ppermute | solution.py:288
  114.3 7.1 %collective-permute-start.7 = (bf16[512,128]{1,0:T(8,128)(2,1)S(1)}, bf16[512,128]{1,0:T(8,128)(2,1)S(1)}, u32[]{:S(2)}, u32[]{:S(2)}) collective-permute-start(bf16[512,128]{1,0:T(8,128)(2,1)S(1)} %get-tuple-element.12), channel_id=1, source_target_pairs={{0,4},{4,0},{8,12},{12,8},{16,20},{20,16},{24,28},{28,24},{32,36},... | collective-permute-start | bytes 393224 | tf_op jit(solution)/shard_map/ppermute | solution.py:302
  121.4 14.2 %copy-start = (bf16[512,128]{1,0:T(8,128)(2,1)S(1)}, bf16[512,128]{1,0:T(8,128)(2,1)}, u32[]{:S(2)}) copy-start(bf16[512,128]{1,0:T(8,128)(2,1)} %scores.3) | copy-start | bytes 393220
  121.4 14.1 %copy-start.2 = (s32[512]{0:T(512)S(1)}, s32[512]{0:T(512)}, u32[]{:S(2)}) copy-start(s32[512]{0:T(512)} %param.10) | copy-start | bytes 6148

commit v7 on v5

--- a/solution.py
+++ b/solution.py
@@ -43,8 +43,6 @@
     for odd in (0, 1)
     for far in range(4)
 ]
-
-
 def where(index):
     core = index & 1
     return core, ((index >> 3) - core) & 15, ((index >> 1) - core) & 3
@@ -61,9 +59,11 @@
     return jnp.broadcast_to(row, (SIDE, SIDE)).T
 
 
-def prepare_kernel(me, table, attr, acct, count, weights, scores, degree, payload, rows, sems):
+def prepare_kernel(me, table, attr, acct, count, weights, scores, degrees, payload, rows, degree, sems):
     tiles = pltpu.make_async_copy(weights, payload.at[pl.ds(0, TILES), :], sems.at[0])
     prior = pltpu.make_async_copy(scores, rows, sems.at[1])
+    small = pltpu.make_async_copy(degrees, degree, sems.at[2])
+    small.start()
     prior.start()
     tiles.start()
     core, u, v = where(me[0])
@@ -78,6 +78,7 @@
         tail = jnp.where(lane == s + SLOTS, sent, tail)
         tail = jnp.where(lane == s + 2 * SLOTS, acct[0, s], tail)
     payload[TILES + ROWS :, :] = tail.astype(jnp.float32).astype(payload.dtype)
+    small.wait()
     prior.wait()
     for n in range(4):
         scale = column(lax.rsqrt(degree[n : n + 1, :].astype(jnp.float32)))
@@ -143,15 +144,18 @@
     own[...] = spread[0, pl.ds(pl.multiple_of(far * SIDE, SIDE), SIDE), :]
 
 
-def backward_kernel(chips, tail0, tail1, sent0, sent1, *refs):
+def backward_kernel(chips, halves, *refs):
+    tails, sents, refs = refs[: len(halves)], refs[len(halves) : 2 * len(halves)], refs[2 * len(halves) :]
     groups, refs = refs[: len(chips)], refs[len(chips) :]
     if len(refs) == 1:
         (acc,) = refs
         acc[...] = jnp.zeros_like(acc)
+        base = 0
     else:
-        before, mine, other, acc = refs
-        acc[...] = before[...]
-    for half, (tail, sent) in enumerate(((tail0, sent0), (tail1, sent1))):
+        before, out, acc = refs
+        base = halves[0] * ROWS
+        acc[...] = before[base : base + ROWS, :]
+    for half, tail, sent in zip(halves, tails, sents):
 
         def step(s, carry, half=half, tail=tail, sent=sent):
             code, block = tail[0, half * SLOTS + s], tail[0, 2 * SLOTS + s]
@@ -160,7 +164,7 @@
 
                 @pl.when(chip == n)
                 def _(blocks=blocks):
-                    start = pl.multiple_of(half * ROWS + block * SIDE, SIDE)
+                    start = pl.multiple_of(half * ROWS - base + block * SIDE, SIDE)
                     acc[pl.ds(start, SIDE), :] += jnp.dot(
                         tile(sent, s), tile(blocks, along), preferred_element_type=jnp.float32
                     )
@@ -169,8 +173,7 @@
 
         lax.fori_loop(0, SLOTS, step, 0)
     if len(refs) > 1:
-        mine[...] = acc[:ROWS]
-        other[...] = acc[ROWS:].astype(other.dtype)
+        out[...] = acc[...].astype(out.dtype)
 
 
 def finish_kernel(types, scores, degree, seed, new):
@@ -224,8 +227,12 @@
     (payload,) = call(
         prepare_kernel,
         [jax.ShapeDtypeStruct((SENT, SIDE), bf16)],
-        smem(5) + [pl.BlockSpec(memory_space=pltpu.HBM)] * 2 + vmem(1),
-        [pltpu.VMEM((ROWS, SIDE), bf16), pltpu.SemaphoreType.DMA((2,))],
+        smem(5) + [pl.BlockSpec(memory_space=pltpu.HBM)] * 3,
+        [
+            pltpu.VMEM((ROWS, SIDE), bf16),
+            pltpu.VMEM((4, SIDE), i32),
+            pltpu.SemaphoreType.DMA((3,)),
+        ],
         ROWS * SIDE,
         MEBI,
     )(
@@ -234,9 +241,10 @@
         tile_attr,
         tile_acct,
         tile_count,
-        pltpu.with_memory_space_constraint(tile_weight.reshape(TILES, SIDE), pltpu.HBM),
-        pltpu.with_memory_space_constraint(scores0, pltpu.HBM),
-        degree,
+        *(
+            pltpu.with_memory_space_constraint(array, pltpu.HBM)
+            for array in (tile_weight.reshape(TILES, SIDE), scores0, degree)
+        ),
     )
     payload1 = lax.ppermute(payload, "acct", SWAP)
     flops = 2 * 10 * SIDE**3
@@ -288,18 +296,27 @@
     g2 = lax.ppermute(g0, "acct", ACROSS)
     acc = jax.ShapeDtypeStruct((2 * ROWS, SIDE), f32)
     (before,) = call(
-        functools.partial(backward_kernel, (0,)), [acc], smem(2) + vmem(3), [], flops, 4 * MEBI
-    )(*slots, g0)
-    mine, other = call(
-        functools.partial(backward_kernel, (1, 2, 3)),
-        [jax.ShapeDtypeStruct((ROWS, SIDE), f32), jax.ShapeDtypeStruct((ROWS, SIDE), bf16)],
-        smem(2) + vmem(6),
-        [pltpu.VMEM(acc.shape, f32)],
+        functools.partial(backward_kernel, (0,), (0, 1)),
+        [acc],
+        smem(2) + vmem(3),
+        [],
         flops,
         4 * MEBI,
-    )(*slots, g1, g2, g3, before)
-
-    returned = (mine + lax.ppermute(other, "acct", SWAP).astype(f32)).astype(bf16)
+    )(*slots, g0)
+
+    def backward(half, dtype):
+        (out,) = call(
+            functools.partial(backward_kernel, (3, 1, 2), (half,)),
+            [jax.ShapeDtypeStruct((ROWS, SIDE), dtype)],
+            smem(1) + vmem(5),
+            [pltpu.VMEM((ROWS, SIDE), f32)],
+            flops,
+            2 * MEBI,
+        )(slots[half], slots[2 + half], g3, g1, g2, before)
+        return out
+
+    other = lax.ppermute(backward(1, bf16), "acct", SWAP)
+    returned = (backward(0, f32) + other.astype(f32)).astype(bf16)
     types = jnp.broadcast_to(returned[None], (4, ROWS, SIDE))
     types = lax.all_to_all(types, "attr", 0, 0, tiled=True)
     (new_scores,) = call(

time: 137 us -> 137 us (level)
  waiting for transfers between devices: 28.3 us -> 38.9 us
  starting transfers between devices: 51.7 us -> 44.1 us
    ppermute x1, waiting for transfers between devices: 7.86 us -> 13.6 us  [per_device(): half = near.astype(f32) + lax.ppermute(near, 'acct', FIRST).astype(f32)]
    ppermute x1, starting transfers between devices: 9.59 us -> 4.55 us  [per_device(): rest = lax.ppermute(half, 'acct', SECOND)]
    ppermute x1, waiting for transfers between devices: 0.01 us -> 4.56 us  [per_device(): g1 = lax.ppermute(g0, 'acct', BESIDE)]
    ppermute x1, waiting for transfers between devices: 5.46 us -> 1.04 us  [per_device(): g2 = lax.ppermute(g0, 'acct', ACROSS)]
    all_to_all x1, blocking collectives: 12 us -> 16.1 us  [per_device(): types = lax.all_to_all(types, 'attr', 0, 0, tiled=True)]
    ppermute x1, waiting for transfers between devices: 5.29 us -> 9.19 us  [per_device(): rest = lax.ppermute(half, 'acct', SECOND)]
    ppermute x1, starting transfers between devices: 1.91 us -> 5.64 us  [per_device(): g1 = lax.ppermute(g0, 'acct', BESIDE)]
    all_to_all x1, blocking collectives: 14.7 us -> 11.7 us  [per_device(): lax.all_to_all(line, 'acct', 0, 0, tiled=True, axis_index_groups=QUADS)]
where the time goes in v7:
time: 137 us; the launch traced here: 136 us
  starting transfers between devices  44.1 us (32%)
  blocking collectives  39.5 us (29%)
  waiting for transfers between devices  38.9 us (28%)
  Pallas kernels  10.9 us (8%)
  between operations  1.54 us (1%)
    all_to_all x1, blocking collectives, per_device(): types = lax.all_to_all(types, 'attr', 0, 0, tiled=True)  16.1 us
    ppermute x1, waiting for transfers between devices, per_device(): half = near.astype(f32) + lax.ppermute(near, 'acct', FIRST).astype(f32)  13.6 us
    all_to_all x1, blocking collectives, per_device(): lax.all_to_all(line, 'acct', 0, 0, tiled=True, axis_index_groups=QUADS)  11.7 us
    all_to_all x1, blocking collectives, per_device(): lax.all_to_all(spread, 'acct', 0, 0, tiled=True, axis_index_groups=QUADS)  11.6 us
    ppermute x1, waiting for transfers between devices, per_device(): rest = lax.ppermute(half, 'acct', SECOND)  9.19 us
    ppermute x1, starting transfers between devices, per_device(): payload1 = lax.ppermute(payload, 'acct', SWAP)  8.79 us
    ppermute x1, starting transfers between devices, per_device(): r3 = lax.ppermute(o3, 'acct', DIAGONAL)  7.77 us
    ppermute x1, starting transfers between devices, per_device(): g1 = lax.ppermute(g0, 'acct', BESIDE)  5.64 us
  transfers between devices with their start and end apart: 10, of which 8 were waited for; matrix products, arithmetic and copies ran while one was open for 0% of the time, Pallas kernels for 4%

profile of v7, /device:TPU:1, one launch (start us, length us, event | category | flops | bytes accessed | tf_op | source)
XLA Modules:
  0.0 136.1 jit_solution(8830285827820313520)
XLA Ops:
  1.3 0.0 copy-start.3
  1.3 0.0 copy-start.4
  1.3 0.0 copy-start.5
  1.3 0.6 copy-done.3
  1.9 0.0 copy-done.4
  2.0 0.0 copy-done.5
  2.0 1.7 %shard_map.104.sent0.refs_2_.refs_1_ = bf16[2576,128]{1,0:T(8,128)(2,1)S(1)} custom-call(s32[1]{0:T(128)} %bitcast.me, s32[1,128]{1,0:T(1,128)S(1)} %copy-done.3, s32[1,16]{1,0:T(1,128)S(1)} %copy-done.4, s32[1,16]{1,0:T(1,128)S(1)} %copy-done.5, s32[1,1]{1,0:T(1,128)S(6)} %copy.11.count, bf16[2048,128]{1,0:T(8,128)(2,1)} %bitcast.15, ...), custom_call_target="tpu_custom_call" | custom-call | flops 65536 | bytes 1048576 | tf_op jit(solution)/shard_map/pallas_call | solution.py:227
  3.7 8.8 %collective-permute-start = (bf16[2576,128]{1,0:T(8,128)(2,1)S(1)}, bf16[2576,128]{1,0:T(8,128)(2,1)S(1)}, u32[]{:S(2)}, u32[]{:S(2)}) collective-permute-start(bf16[2576,128]{1,0:T(8,128)(2,1)S(1)} %shard_map.104.sent0.refs_2_.refs_1_), channel_id=1, source_target_pairs={{0,4},{4,0},{8,12},{12,8},{16,20},{20,16},{24,28},{28,24},{32,36},... | collective-permute-start | bytes 1978376 | tf_op jit(solution)/shard_map/ppermute | solution.py:249
  12.5 1.7 %collective-permute-done.sent1.refs_3_.refs_1_ = bf16[2576,128]{1,0:T(8,128)(2,1)S(1)} collective-permute-done((bf16[2576,128]{1,0:T(8,128)(2,1)S(1)}, bf16[2576,128]{1,0:T(8,128)(2,1)S(1)}, u32[]{:S(2)}, u32[]{:S(2)}) %collective-permute-start) | collective-permute-done | bytes 659488 | tf_op jit(solution)/shard_map/ppermute | solution.py:249
  14.2 1.3 shard_map.107
  15.5 7.8 %collective-permute-start.3 = (bf16[16,128,128]{2,1,0:T(8,128)(2,1)S(1)}, bf16[16,128,128]{2,1,0:T(8,128)(2,1)S(1)}, u32[]{:S(2)}, u32[]{:S(2)}) collective-permute-start(bf16[16,128,128]{2,1,0:T(8,128)(2,1)S(1)} %shard_map.107), channel_id=1, source_target_pairs={{0,40},{8,32},{16,56},{24,48},{32,8},{40,0},{48,24},{56,16},{64,10... | collective-permute-start | bytes 1572872 | tf_op jit(solution)/shard_map/ppermute | solution.py:265
  23.3 1.7 %shard_map.106 = (bf16[16,128,128]{2,1,0:T(8,128)(2,1)S(1)}, bf16[16,128,128]{2,1,0:T(8,128)(2,1)S(1)}) custom-call(s32[1,128]{1,0:T(1,128)S(1)} %slice_convert_fusion.1.tail0.refs_0_, s32[1,128]{1,0:T(1,128)S(1)} %slice_convert_fusion.tail1.refs_1_.refs_0_, bf16[2576,128]{1,0:T(8,128)(2,1)S(1)} %shard_map.104.sent0.refs_2_.refs_1_, ...), custom_call_target="tpu_custom_call" | custom-call | flops 41943040 | bytes 3145728 | tf_op jit(solution)/shard_map/pallas_call | solution.py:255
  24.9 2.5 %collective-permute-start.2 = (bf16[16,128,128]{2,1,0:T(8,128)(2,1)S(1)}, bf16[16,128,128]{2,1,0:T(8,128)(2,1)S(1)}, u32[]{:S(2)}, u32[]{:S(2)}) collective-permute-start(bf16[16,128,128]{2,1,0:T(8,128)(2,1)S(1)} %get-tuple-element.7), channel_id=1, source_target_pairs={{0,8},{8,0},{16,24},{24,16},{32,40},{40,32},{48,56},{56,48},{64,72... | collective-permute-start | bytes 1572872 | tf_op jit(solution)/shard_map/ppermute | solution.py:268
  27.4 2.4 %collective-permute-start.1 = (bf16[16,128,128]{2,1,0:T(8,128)(2,1)S(1)}, bf16[16,128,128]{2,1,0:T(8,128)(2,1)S(1)}, u32[]{:S(2)}, u32[]{:S(2)}) collective-permute-start(bf16[16,128,128]{2,1,0:T(8,128)(2,1)S(1)} %get-tuple-element.6), channel_id=1, source_target_pairs={{0,32},{8,40},{16,48},{24,56},{32,0},{40,8},{48,16},{56,24},{64,96... | collective-permute-start | bytes 1572872 | tf_op jit(solution)/shard_map/ppermute | solution.py:267
  29.8 1.3 shard_map.105
  31.1 0.0 collective-permute-done.3
  31.1 5.0 %collective-permute-done.2 = bf16[16,128,128]{2,1,0:T(8,128)(2,1)S(1)} collective-permute-done((bf16[16,128,128]{2,1,0:T(8,128)(2,1)S(1)}, bf16[16,128,128]{2,1,0:T(8,128)(2,1)S(1)}, u32[]{:S(2)}, u32[]{:S(2)}) %collective-permute-start.2) | collective-permute-done | bytes 524320 | tf_op jit(solution)/shard_map/ppermute | solution.py:268
  36.1 2.5 %collective-permute-done.1 = bf16[16,128,128]{2,1,0:T(8,128)(2,1)S(1)} collective-permute-done((bf16[16,128,128]{2,1,0:T(8,128)(2,1)S(1)}, bf16[16,128,128]{2,1,0:T(8,128)(2,1)S(1)}, u32[]{:S(2)}, u32[]{:S(2)}) %collective-permute-start.1) | collective-permute-done | bytes 524320 | tf_op jit(solution)/shard_map/ppermute | solution.py:267
  38.5 0.3 add_convert_fusion
  38.9 0.0 copy-start.6
  38.9 11.7 %all_to_all.15.parts = bf16[4,4,128,128]{3,2,1,0:T(8,128)(2,1)S(1)} all-to-all(bf16[4,4,128,128]{3,2,1,0:T(8,128)(2,1)S(1)} %bitcast.14), channel_id=1, replica_groups={{0,64,24,88},{128,192,152,216},{256,320,280,344},{384,448,408,472},{32,..., dimensions={0} | all-to-all | bytes 1048576 | tf_op jit(solution)/shard_map/all_to_all | solution.py:272
  50.6 0.0 copy-done.6
  50.6 0.1 shard_map.108
  50.7 1.9 %collective-permute-start.4 = (bf16[528,128]{1,0:T(8,128)(2,1)S(1)}, bf16[528,128]{1,0:T(8,128)(2,1)S(1)}, u32[]{:S(2)}, u32[]{:S(2)}) collective-permute-start(bf16[528,128]{1,0:T(8,128)(2,1)S(1)} %shard_map.108), channel_id=1, source_target_pairs={{0,128},{8,136},{16,144},{24,152},{32,160},{40,168},{48,176},{56,1... | collective-permute-start | bytes 405512 | tf_op jit(solution)/shard_map/ppermute | solution.py:277
  52.6 13.6 %collective-permute-done.4 = bf16[528,128]{1,0:T(8,128)(2,1)S(1)} collective-permute-done((bf16[528,128]{1,0:T(8,128)(2,1)S(1)}, bf16[528,128]{1,0:T(8,128)(2,1)S(1)}, u32[]{:S(2)}, u32[]{:S(2)}) %collective-permute-start.4) | collective-permute-done | bytes 135200 | tf_op jit(solution)/shard_map/ppermute | solution.py:277
  66.3 4.6 %collective-permute-start.5 = (bf16[528,128]{1,0:T(8,128)(2,1)S(1)}, bf16[528,128]{1,0:T(8,128)(2,1)S(1)}, u32[]{:S(2)}, u32[]{:S(2)}) collective-permute-start(bf16[528,128]{1,0:T(8,128)(2,1)S(1)} %add_convert_fusion.1.mine), channel_id=1, source_target_pairs={{0,384},{8,392},{16,400},{24,408},{32,416},{40,424},{48,432},{56,4... | collective-permute-start | bytes 405512 | tf_op jit(solution)/shard_map/ppermute | solution.py:279
  70.9 9.2 %collective-permute-done.5.other = bf16[528,128]{1,0:T(8,128)(2,1)S(1)} collective-permute-done((bf16[528,128]{1,0:T(8,128)(2,1)S(1)}, bf16[528,128]{1,0:T(8,128)(2,1)S(1)}, u32[]{:S(2)}, u32[]{:S(2)}) %collective-permute-start.5) | collective-permute-done | bytes 135200 | tf_op jit(solution)/shard_map/ppermute | solution.py:279
  80.1 0.8 shard_map.109
  80.8 11.6 %all_to_all.16 = bf16[4,512,128]{2,1,0:T(8,128)(2,1)S(1)} all-to-all(bf16[4,512,128]{2,1,0:T(8,128)(2,1)S(1)} %get-tuple-element.8), channel_id=1, replica_groups={{0,64,24,88},{128,192,152,216},{256,320,280,344},{384,448,408,472},{32,..., dimensions={0} | all-to-all | bytes 1048576 | tf_op jit(solution)/shard_map/all_to_all | solution.py:292
  92.4 1.9 %collective-permute-start.6 = (bf16[2048,128]{1,0:T(8,128)(2,1)S(1)}, bf16[2048,128]{1,0:T(8,128)(2,1)S(1)}, u32[]{:S(2)}, u32[]{:S(2)}) collective-permute-start(bf16[2048,128]{1,0:T(8,128)(2,1)S(1)} %bitcast.7), channel_id=1, source_target_pairs={{0,40},{8,32},{16,56},{24,48},{32,8},{40,0},{48,24},{56,16},{64,10... | collective-permute-start | bytes 1572872 | tf_op jit(solution)/shard_map/ppermute | solution.py:294
  94.4 5.6 %collective-permute-start.7 = (bf16[2048,128]{1,0:T(8,128)(2,1)S(1)}, bf16[2048,128]{1,0:T(8,128)(2,1)S(1)}, u32[]{:S(2)}, u32[]{:S(2)}) collective-permute-start(bf16[2048,128]{1,0:T(8,128)(2,1)S(1)} %bitcast.8), channel_id=1, source_target_pairs={{0,32},{8,40},{16,48},{24,56},{32,0},{40,8},{48,16},{56,24},{64,96... | collective-permute-start | bytes 1572872 | tf_op jit(solution)/shard_map/ppermute | solution.py:295
  100.0 3.2 %collective-permute-start.8 = (bf16[2048,128]{1,0:T(8,128)(2,1)S(1)}, bf16[2048,128]{1,0:T(8,128)(2,1)S(1)}, u32[]{:S(2)}, u32[]{:S(2)}) collective-permute-start(bf16[2048,128]{1,0:T(8,128)(2,1)S(1)} %bitcast.9), channel_id=1, source_target_pairs={{0,8},{8,0},{16,24},{24,16},{32,40},{40,32},{48,56},{56,48},{64,72... | collective-permute-start | bytes 1572872 | tf_op jit(solution)/shard_map/ppermute | solution.py:296
  103.2 1.1 shard_map.110.refs_5_
  104.3 1.4 %collective-permute-done.6.refs_2_ = bf16[2048,128]{1,0:T(8,128)(2,1)S(1)} collective-permute-done((bf16[2048,128]{1,0:T(8,128)(2,1)S(1)}, bf16[2048,128]{1,0:T(8,128)(2,1)S(1)}, u32[]{:S(2)}, u32[]{:S(2)}) %collective-permute-start.6) | collective-permute-done | bytes 524320 | tf_op jit(solution)/shard_map/ppermute | solution.py:294
  105.7 4.6 %collective-permute-done.7.refs_3_ = bf16[2048,128]{1,0:T(8,128)(2,1)S(1)} collective-permute-done((bf16[2048,128]{1,0:T(8,128)(2,1)S(1)}, bf16[2048,128]{1,0:T(8,128)(2,1)S(1)}, u32[]{:S(2)}, u32[]{:S(2)}) %collective-permute-start.7) | collective-permute-done | bytes 524320 | tf_op jit(solution)/shard_map/ppermute | solution.py:295
  110.2 1.0 collective-permute-done.8.refs_4_
  111.3 1.0 shard_map.112
  112.3 5.5 %collective-permute-start.9 = (bf16[512,128]{1,0:T(8,128)(2,1)S(1)}, bf16[512,128]{1,0:T(8,128)(2,1)S(1)}, u32[]{:S(2)}, u32[]{:S(2)}) collective-permute-start(bf16[512,128]{1,0:T(8,128)(2,1)S(1)} %shard_map.112), channel_id=1, source_target_pairs={{0,4},{4,0},{8,12},{12,8},{16,20},{20,16},{24,28},{28,24},{32,36},... | collective-permute-start | bytes 393224 | tf_op jit(solution)/shard_map/ppermute | solution.py:318
  117.8 1.1 shard_map.111
  118.9 0.0 collective-permute-done.9
  118.9 0.1 broadcast_in_dim.4
  119.0 0.0 copy-start
  119.0 0.0 copy-start.1
  119.0 0.0 copy-start.2
  119.1 16.1 %all_to_all.17.types = bf16[4,512,128]{2,1,0:T(8,128)(2,1)S(1)} all-to-all(bf16[4,512,128]{2,1,0:T(8,128)(2,1)S(1)} %broadcast_in_dim.4), channel_id=1, replica_groups=mesh['acct'=128,'attr'=4] {'attr'}, dimensions={0} | all-to-all | bytes 1048576 | tf_op jit(solution)/shard_map/all_to_all | solution.py:321
  135.2 0.0 copy-done
  135.2 0.0 copy-done.1
  135.2 0.9 shard_map.113
  (5 shorter events, 0.1 us)
Async XLA Ops:
  1.3 0.7 copy-start.3
  1.3 0.7 copy-start.4
  1.3 0.7 copy-start.5
  3.7 10.5 %collective-permute-start = (bf16[2576,128]{1,0:T(8,128)(2,1)S(1)}, bf16[2576,128]{1,0:T(8,128)(2,1)S(1)}, u32[]{:S(2)}, u32[]{:S(2)}) collective-permute-start(bf16[2576,128]{1,0:T(8,128)(2,1)S(1)} %shard_map.104.sent0.refs_2_.refs_1_), channel_id=1, source_target_pairs={{0,4},{4,0},{8,12},{12,8},{16,20},{20,16},{24,28},{28,24},{32,36},... | collective-permute-start | bytes 1978376 | tf_op jit(solution)/shard_map/ppermute | solution.py:249
  15.5 15.6 %collective-permute-start.3 = (bf16[16,128,128]{2,1,0:T(8,128)(2,1)S(1)}, bf16[16,128,128]{2,1,0:T(8,128)(2,1)S(1)}, u32[]{:S(2)}, u32[]{:S(2)}) collective-permute-start(bf16[16,128,128]{2,1,0:T(8,128)(2,1)S(1)} %shard_map.107), channel_id=1, source_target_pairs={{0,40},{8,32},{16,56},{24,48},{32,8},{40,0},{48,24},{56,16},{64,10... | collective-permute-start | bytes 1572872 | tf_op jit(solution)/shard_map/ppermute | solution.py:265
  24.9 11.1 %collective-permute-start.2 = (bf16[16,128,128]{2,1,0:T(8,128)(2,1)S(1)}, bf16[16,128,128]{2,1,0:T(8,128)(2,1)S(1)}, u32[]{:S(2)}, u32[]{:S(2)}) collective-permute-start(bf16[16,128,128]{2,1,0:T(8,128)(2,1)S(1)} %get-tuple-element.7), channel_id=1, source_target_pairs={{0,8},{8,0},{16,24},{24,16},{32,40},{40,32},{48,56},{56,48},{64,72... | collective-permute-start | bytes 1572872 | tf_op jit(solution)/shard_map/ppermute | solution.py:268
  27.4 11.1 %collective-permute-start.1 = (bf16[16,128,128]{2,1,0:T(8,128)(2,1)S(1)}, bf16[16,128,128]{2,1,0:T(8,128)(2,1)S(1)}, u32[]{:S(2)}, u32[]{:S(2)}) collective-permute-start(bf16[16,128,128]{2,1,0:T(8,128)(2,1)S(1)} %get-tuple-element.6), channel_id=1, source_target_pairs={{0,32},{8,40},{16,48},{24,56},{32,0},{40,8},{48,16},{56,24},{64,96... | collective-permute-start | bytes 1572872 | tf_op jit(solution)/shard_map/ppermute | solution.py:267
  38.9 11.8 %copy-start.6 = (s32[1,128]{1,0:T(1,128)S(1)}, s32[1,128]{1,0:T(1,128)}, u32[]{:S(2)}) copy-start(s32[1,128]{1,0:T(1,128)} %degree.1) | copy-start | bytes 1540
  50.7 15.6 %collective-permute-start.4 = (bf16[528,128]{1,0:T(8,128)(2,1)S(1)}, bf16[528,128]{1,0:T(8,128)(2,1)S(1)}, u32[]{:S(2)}, u32[]{:S(2)}) collective-permute-start(bf16[528,128]{1,0:T(8,128)(2,1)S(1)} %shard_map.108), channel_id=1, source_target_pairs={{0,128},{8,136},{16,144},{24,152},{32,160},{40,168},{48,176},{56,1... | collective-permute-start | bytes 405512 | tf_op jit(solution)/shard_map/ppermute | solution.py:277
  66.3 13.7 %collective-permute-start.5 = (bf16[528,128]{1,0:T(8,128)(2,1)S(1)}, bf16[528,128]{1,0:T(8,128)(2,1)S(1)}, u32[]{:S(2)}, u32[]{:S(2)}) collective-permute-start(bf16[528,128]{1,0:T(8,128)(2,1)S(1)} %add_convert_fusion.1.mine), channel_id=1, source_target_pairs={{0,384},{8,392},{16,400},{24,408},{32,416},{40,424},{48,432},{56,4... | collective-permute-start | bytes 405512 | tf_op jit(solution)/shard_map/ppermute | solution.py:279
  92.4 13.2 %collective-permute-start.6 = (bf16[2048,128]{1,0:T(8,128)(2,1)S(1)}, bf16[2048,128]{1,0:T(8,128)(2,1)S(1)}, u32[]{:S(2)}, u32[]{:S(2)}) collective-permute-start(bf16[2048,128]{1,0:T(8,128)(2,1)S(1)} %bitcast.7), channel_id=1, source_target_pairs={{0,40},{8,32},{16,56},{24,48},{32,8},{40,0},{48,24},{56,16},{64,10... | collective-permute-start | bytes 1572872 | tf_op jit(solution)/shard_map/ppermute | solution.py:294
  94.4 15.9 %collective-permute-start.7 = (bf16[2048,128]{1,0:T(8,128)(2,1)S(1)}, bf16[2048,128]{1,0:T(8,128)(2,1)S(1)}, u32[]{:S(2)}, u32[]{:S(2)}) collective-permute-start(bf16[2048,128]{1,0:T(8,128)(2,1)S(1)} %bitcast.8), channel_id=1, source_target_pairs={{0,32},{8,40},{16,48},{24,56},{32,0},{40,8},{48,16},{56,24},{64,96... | collective-permute-start | bytes 1572872 | tf_op jit(solution)/shard_map/ppermute | solution.py:295
  100.0 11.3 %collective-permute-start.8 = (bf16[2048,128]{1,0:T(8,128)(2,1)S(1)}, bf16[2048,128]{1,0:T(8,128)(2,1)S(1)}, u32[]{:S(2)}, u32[]{:S(2)}) collective-permute-start(bf16[2048,128]{1,0:T(8,128)(2,1)S(1)} %bitcast.9), channel_id=1, source_target_pairs={{0,8},{8,0},{16,24},{24,16},{32,40},{40,32},{48,56},{56,48},{64,72... | collective-permute-start | bytes 1572872 | tf_op jit(solution)/shard_map/ppermute | solution.py:296
  112.3 6.6 %collective-permute-start.9 = (bf16[512,128]{1,0:T(8,128)(2,1)S(1)}, bf16[512,128]{1,0:T(8,128)(2,1)S(1)}, u32[]{:S(2)}, u32[]{:S(2)}) collective-permute-start(bf16[512,128]{1,0:T(8,128)(2,1)S(1)} %shard_map.112), channel_id=1, source_target_pairs={{0,4},{4,0},{8,12},{12,8},{16,20},{20,16},{24,28},{28,24},{32,36},... | collective-permute-start | bytes 393224 | tf_op jit(solution)/shard_map/ppermute | solution.py:318
  119.0 16.2 %copy-start = (bf16[512,128]{1,0:T(8,128)(2,1)S(1)}, bf16[512,128]{1,0:T(8,128)(2,1)}, u32[]{:S(2)}) copy-start(bf16[512,128]{1,0:T(8,128)(2,1)} %scores.3) | copy-start | bytes 393220
  119.0 16.2 %copy-start.1 = (s32[512]{0:T(512)S(1)}, s32[512]{0:T(512)}, u32[]{:S(2)}) copy-start(s32[512]{0:T(512)} %param.11) | copy-start | bytes 6148
  119.0 16.2 %copy-start.2 = (s32[512]{0:T(512)S(1)}, s32[512]{0:T(512)}, u32[]{:S(2)}) copy-start(s32[512]{0:T(512)} %param.10) | copy-start | bytes 6148

commit v8 on v7

--- a/solution.py
+++ b/solution.py
@@ -116,7 +116,7 @@
 
             return carry
 
-        lax.fori_loop(0, SLOTS, step, 0)
+        lax.fori_loop(0, SLOTS, step, 0, unroll=True)
     for n, out in enumerate(outs):
         out[...] = acc[n * LINE : (n + 1) * LINE].astype(out.dtype)
 
@@ -171,7 +171,7 @@
 
             return carry
 
-        lax.fori_loop(0, SLOTS, step, 0)
+        lax.fori_loop(0, SLOTS, step, 0, unroll=True)
     if len(refs) > 1:
         out[...] = acc[...].astype(out.dtype)
 
@@ -261,9 +261,8 @@
             3 * MEBI,
         )(*slots)
 
-    (o3,) = forward((3,))
+    o3, o1, o2 = forward((3, 1, 2))
     r3 = lax.ppermute(o3, "acct", DIAGONAL)
-    o1, o2 = forward((1, 2))
     r1 = lax.ppermute(o1, "acct", BESIDE)
     r2 = lax.ppermute(o2, "acct", ACROSS)
     (o0,) = forward((0,))

time: 137 us -> 136 us (level); the launches traced: 136 us -> 137 us
  waiting for transfers between devices: 38.9 us -> 32.5 us
  starting transfers between devices: 44.1 us -> 48.7 us
  blocking collectives: 39.5 us -> 41.9 us
    ppermute x1, waiting for transfers between devices: 13.6 us -> 9.69 us  [per_device(): half = near.astype(f32) + lax.ppermute(near, 'acct', FIRST).astype(f32)]
    ppermute x1, starting transfers between devices: 4.55 us -> 8.39 us  [per_device(): rest = lax.ppermute(half, 'acct', SECOND)]
    ppermute x1, starting transfers between devices: 1.92 us -> 5.33 us  [per_device(): half = near.astype(f32) + lax.ppermute(near, 'acct', FIRST).astype(f32)]
    ppermute x1, starting transfers between devices: 5.64 us -> 2.45 us  [per_device(): g1 = lax.ppermute(g0, 'acct', BESIDE)]
    ppermute x1, starting transfers between devices: 1.91 us -> 4.61 us  [per_device(): g3 = lax.ppermute(g0, 'acct', DIAGONAL)]
    ppermute x1, waiting for transfers between devices: 9.19 us -> 6.65 us  [per_device(): rest = lax.ppermute(half, 'acct', SECOND)]
    all_to_all x1, blocking collectives: 16.1 us -> 18.1 us  [per_device(): types = lax.all_to_all(types, 'attr', 0, 0, tiled=True)]
    ppermute x1, starting transfers between devices: 5.48 us -> 3.6 us  [per_device(): other = lax.ppermute(backward(1, bf16), 'acct', SWAP)]
  transfers between devices with their start and end apart: 10 -> 10, of which waited for: 8 -> 9; matrix products, arithmetic and copies ran while one was open for 0% -> 0% of each run, Pallas kernels for 4% -> 3%
where the time goes in v8:
time: 136 us; the launch traced here: 137 us
  starting transfers between devices  48.7 us (36%)
  blocking collectives  41.9 us (31%)
  waiting for transfers between devices  32.5 us (24%)
  Pallas kernels  11.7 us (9%)
  between operations  1.52 us (1%)
    all_to_all x1, blocking collectives, per_device(): types = lax.all_to_all(types, 'attr', 0, 0, tiled=True)  18.1 us
    all_to_all x1, blocking collectives, per_device(): lax.all_to_all(spread, 'acct', 0, 0, tiled=True, axis_index_groups=QUADS)  13.2 us
    all_to_all x1, blocking collectives, per_device(): lax.all_to_all(line, 'acct', 0, 0, tiled=True, axis_index_groups=QUADS)  10.5 us
    ppermute x1, waiting for transfers between devices, per_device(): half = near.astype(f32) + lax.ppermute(near, 'acct', FIRST).astype(f32)  9.69 us
    ppermute x1, starting transfers between devices, per_device(): payload1 = lax.ppermute(payload, 'acct', SWAP)  8.79 us
    ppermute x1, starting transfers between devices, per_device(): rest = lax.ppermute(half, 'acct', SECOND)  8.39 us
    ppermute x1, starting transfers between devices, per_device(): r3 = lax.ppermute(o3, 'acct', DIAGONAL)  7.24 us
    ppermute x1, waiting for transfers between devices, per_device(): rest = lax.ppermute(half, 'acct', SECOND)  6.65 us
  transfers between devices with their start and end apart: 10, of which 9 were waited for; matrix products, arithmetic and copies ran while one was open for 0% of the time, Pallas kernels for 3%

profile of v8, /device:TPU:1, one launch (start us, length us, event | category | flops | bytes accessed | tf_op | source)
XLA Modules:
  0.0 137.4 jit_solution(1702376649694384482)
XLA Ops:
  1.3 0.0 copy-start.3
  1.3 0.0 copy-start.4
  1.3 0.0 copy-start.5
  1.3 0.6 copy-done.3
  1.9 0.0 copy-done.4
  2.0 0.0 copy-done.5
  2.0 1.7 %shard_map.104.sent0.refs_2_.refs_1_ = bf16[2576,128]{1,0:T(8,128)(2,1)S(1)} custom-call(s32[1]{0:T(128)} %bitcast.me, s32[1,128]{1,0:T(1,128)S(1)} %copy-done.3, s32[1,16]{1,0:T(1,128)S(1)} %copy-done.4, s32[1,16]{1,0:T(1,128)S(1)} %copy-done.5, s32[1,1]{1,0:T(1,128)S(6)} %copy.11.count, bf16[2048,128]{1,0:T(8,128)(2,1)} %bitcast.15, ...), custom_call_target="tpu_custom_call" | custom-call | flops 65536 | bytes 1048576 | tf_op jit(solution)/shard_map/pallas_call | solution.py:227
  3.7 8.8 %collective-permute-start = (bf16[2576,128]{1,0:T(8,128)(2,1)S(1)}, bf16[2576,128]{1,0:T(8,128)(2,1)S(1)}, u32[]{:S(2)}, u32[]{:S(2)}) collective-permute-start(bf16[2576,128]{1,0:T(8,128)(2,1)S(1)} %shard_map.104.sent0.refs_2_.refs_1_), channel_id=1, source_target_pairs={{0,4},{4,0},{8,12},{12,8},{16,20},{20,16},{24,28},{28,24},{32,36},... | collective-permute-start | bytes 1978376 | tf_op jit(solution)/shard_map/ppermute | solution.py:249
  12.5 1.7 %collective-permute-done.sent1.refs_3_.refs_1_ = bf16[2576,128]{1,0:T(8,128)(2,1)S(1)} collective-permute-done((bf16[2576,128]{1,0:T(8,128)(2,1)S(1)}, bf16[2576,128]{1,0:T(8,128)(2,1)S(1)}, u32[]{:S(2)}, u32[]{:S(2)}) %collective-permute-start) | collective-permute-done | bytes 659488 | tf_op jit(solution)/shard_map/ppermute | solution.py:249
  14.2 2.8 %shard_map.106 = (bf16[16,128,128]{2,1,0:T(8,128)(2,1)S(1)}, bf16[16,128,128]{2,1,0:T(8,128)(2,1)S(1)}, bf16[16,128,128]{2,1,0:T(8,128)(2,1)S(1)}) custom-call(s32[1,128]{1,0:T(1,128)S(1)} %slice_convert_fusion.1.tail0.refs_0_, s32[1,128]{1,0:T(1,128)S(1)} %slice_convert_fusion.tail1.refs_1_.refs_0_, bf16[2576,128]{1,0:T(8,128)(2,1)S(1)} %shard_map.104.sent0.refs_2_.refs_1_, ...), custom_call_target="tpu_custom_call" | custom-call | flops 41943040 | bytes 3145728 | tf_op jit(solution)/shard_map/pallas_call | solution.py:255
  17.0 7.2 %collective-permute-start.3 = (bf16[16,128,128]{2,1,0:T(8,128)(2,1)S(1)}, bf16[16,128,128]{2,1,0:T(8,128)(2,1)S(1)}, u32[]{:S(2)}, u32[]{:S(2)}) collective-permute-start(bf16[16,128,128]{2,1,0:T(8,128)(2,1)S(1)} %get-tuple-element.9), channel_id=1, source_target_pairs={{0,40},{8,32},{16,56},{24,48},{32,8},{40,0},{48,24},{56,16},{64,10... | collective-permute-start | bytes 1572872 | tf_op jit(solution)/shard_map/ppermute | solution.py:265
  24.3 2.6 %collective-permute-start.2 = (bf16[16,128,128]{2,1,0:T(8,128)(2,1)S(1)}, bf16[16,128,128]{2,1,0:T(8,128)(2,1)S(1)}, u32[]{:S(2)}, u32[]{:S(2)}) collective-permute-start(bf16[16,128,128]{2,1,0:T(8,128)(2,1)S(1)} %get-tuple-element.8), channel_id=1, source_target_pairs={{0,8},{8,0},{16,24},{24,16},{32,40},{40,32},{48,56},{56,48},{64,72... | collective-permute-start | bytes 1572872 | tf_op jit(solution)/shard_map/ppermute | solution.py:267
  26.9 1.9 %collective-permute-start.1 = (bf16[16,128,128]{2,1,0:T(8,128)(2,1)S(1)}, bf16[16,128,128]{2,1,0:T(8,128)(2,1)S(1)}, u32[]{:S(2)}, u32[]{:S(2)}) collective-permute-start(bf16[16,128,128]{2,1,0:T(8,128)(2,1)S(1)} %get-tuple-element.7), channel_id=1, source_target_pairs={{0,32},{8,40},{16,48},{24,56},{32,0},{40,8},{48,16},{56,24},{64,96... | collective-permute-start | bytes 1572872 | tf_op jit(solution)/shard_map/ppermute | solution.py:266
  28.9 1.6 %shard_map.105 = bf16[16,128,128]{2,1,0:T(8,128)(2,1)S(1)} custom-call(s32[1,128]{1,0:T(1,128)S(1)} %slice_convert_fusion.1.tail0.refs_0_, s32[1,128]{1,0:T(1,128)S(1)} %slice_convert_fusion.tail1.refs_1_.refs_0_, bf16[2576,128]{1,0:T(8,128)(2,1)S(1)} %shard_map.104.sent0.refs_2_.refs_1_, bf16[2576,128]{1,0:T(8,128)(2,1)S(1)} %collective-permute-done.sent1.refs_3_.refs_1_), custom_call_target="tpu_custom_call" | custom-call | flops 41943040 | bytes 3145728 | tf_op jit(solution)/shard_map/pallas_call | solution.py:255
  30.5 0.4 collective-permute-done.3
  30.9 5.5 %collective-permute-done.2 = bf16[16,128,128]{2,1,0:T(8,128)(2,1)S(1)} collective-permute-done((bf16[16,128,128]{2,1,0:T(8,128)(2,1)S(1)}, bf16[16,128,128]{2,1,0:T(8,128)(2,1)S(1)}, u32[]{:S(2)}, u32[]{:S(2)}) %collective-permute-start.2) | collective-permute-done | bytes 524320 | tf_op jit(solution)/shard_map/ppermute | solution.py:267
  36.5 1.6 %collective-permute-done.1 = bf16[16,128,128]{2,1,0:T(8,128)(2,1)S(1)} collective-permute-done((bf16[16,128,128]{2,1,0:T(8,128)(2,1)S(1)}, bf16[16,128,128]{2,1,0:T(8,128)(2,1)S(1)}, u32[]{:S(2)}, u32[]{:S(2)}) %collective-permute-start.1) | collective-permute-done | bytes 524320 | tf_op jit(solution)/shard_map/ppermute | solution.py:266
  38.1 0.3 add_convert_fusion
  38.4 0.0 copy-start.6
  38.4 10.5 %all_to_all.15.parts = bf16[4,4,128,128]{3,2,1,0:T(8,128)(2,1)S(1)} all-to-all(bf16[4,4,128,128]{3,2,1,0:T(8,128)(2,1)S(1)} %bitcast.14), channel_id=1, replica_groups={{0,64,24,88},{128,192,152,216},{256,320,280,344},{384,448,408,472},{32,..., dimensions={0} | all-to-all | bytes 1048576 | tf_op jit(solution)/shard_map/all_to_all | solution.py:271
  48.9 0.0 copy-done.6
  48.9 0.1 shard_map.107
  49.0 5.3 %collective-permute-start.4 = (bf16[528,128]{1,0:T(8,128)(2,1)S(1)}, bf16[528,128]{1,0:T(8,128)(2,1)S(1)}, u32[]{:S(2)}, u32[]{:S(2)}) collective-permute-start(bf16[528,128]{1,0:T(8,128)(2,1)S(1)} %shard_map.107), channel_id=1, source_target_pairs={{0,128},{8,136},{16,144},{24,152},{32,160},{40,168},{48,176},{56,1... | collective-permute-start | bytes 405512 | tf_op jit(solution)/shard_map/ppermute | solution.py:276
  54.4 9.7 %collective-permute-done.4 = bf16[528,128]{1,0:T(8,128)(2,1)S(1)} collective-permute-done((bf16[528,128]{1,0:T(8,128)(2,1)S(1)}, bf16[528,128]{1,0:T(8,128)(2,1)S(1)}, u32[]{:S(2)}, u32[]{:S(2)}) %collective-permute-start.4) | collective-permute-done | bytes 135200 | tf_op jit(solution)/shard_map/ppermute | solution.py:276
  64.1 8.4 %collective-permute-start.5 = (bf16[528,128]{1,0:T(8,128)(2,1)S(1)}, bf16[528,128]{1,0:T(8,128)(2,1)S(1)}, u32[]{:S(2)}, u32[]{:S(2)}) collective-permute-start(bf16[528,128]{1,0:T(8,128)(2,1)S(1)} %add_convert_fusion.1.mine), channel_id=1, source_target_pairs={{0,384},{8,392},{16,400},{24,408},{32,416},{40,424},{48,432},{56,4... | collective-permute-start | bytes 405512 | tf_op jit(solution)/shard_map/ppermute | solution.py:278
  72.5 6.6 %collective-permute-done.5.other = bf16[528,128]{1,0:T(8,128)(2,1)S(1)} collective-permute-done((bf16[528,128]{1,0:T(8,128)(2,1)S(1)}, bf16[528,128]{1,0:T(8,128)(2,1)S(1)}, u32[]{:S(2)}, u32[]{:S(2)}) %collective-permute-start.5) | collective-permute-done | bytes 135200 | tf_op jit(solution)/shard_map/ppermute | solution.py:278
  79.1 0.8 shard_map.108
  79.9 13.2 %all_to_all.16 = bf16[4,512,128]{2,1,0:T(8,128)(2,1)S(1)} all-to-all(bf16[4,512,128]{2,1,0:T(8,128)(2,1)S(1)} %get-tuple-element.10), channel_id=1, replica_groups={{0,64,24,88},{128,192,152,216},{256,320,280,344},{384,448,408,472},{32,..., dimensions={0} | all-to-all | bytes 1048576 | tf_op jit(solution)/shard_map/all_to_all | solution.py:291
  93.2 4.6 %collective-permute-start.6 = (bf16[2048,128]{1,0:T(8,128)(2,1)S(1)}, bf16[2048,128]{1,0:T(8,128)(2,1)S(1)}, u32[]{:S(2)}, u32[]{:S(2)}) collective-permute-start(bf16[2048,128]{1,0:T(8,128)(2,1)S(1)} %bitcast.7), channel_id=1, source_target_pairs={{0,40},{8,32},{16,56},{24,48},{32,8},{40,0},{48,24},{56,16},{64,10... | collective-permute-start | bytes 1572872 | tf_op jit(solution)/shard_map/ppermute | solution.py:293
  97.8 2.5 %collective-permute-start.7 = (bf16[2048,128]{1,0:T(8,128)(2,1)S(1)}, bf16[2048,128]{1,0:T(8,128)(2,1)S(1)}, u32[]{:S(2)}, u32[]{:S(2)}) collective-permute-start(bf16[2048,128]{1,0:T(8,128)(2,1)S(1)} %bitcast.8), channel_id=1, source_target_pairs={{0,32},{8,40},{16,48},{24,56},{32,0},{40,8},{48,16},{56,24},{64,96... | collective-permute-start | bytes 1572872 | tf_op jit(solution)/shard_map/ppermute | solution.py:294
  100.2 3.7 %collective-permute-start.8 = (bf16[2048,128]{1,0:T(8,128)(2,1)S(1)}, bf16[2048,128]{1,0:T(8,128)(2,1)S(1)}, u32[]{:S(2)}, u32[]{:S(2)}) collective-permute-start(bf16[2048,128]{1,0:T(8,128)(2,1)S(1)} %bitcast.9), channel_id=1, source_target_pairs={{0,8},{8,0},{16,24},{24,16},{32,40},{40,32},{48,56},{56,48},{64,72... | collective-permute-start | bytes 1572872 | tf_op jit(solution)/shard_map/ppermute | solution.py:295
  104.0 1.2 shard_map.109.refs_5_
  105.1 1.3 collective-permute-done.6.refs_2_
  106.5 4.0 %collective-permute-done.7.refs_3_ = bf16[2048,128]{1,0:T(8,128)(2,1)S(1)} collective-permute-done((bf16[2048,128]{1,0:T(8,128)(2,1)S(1)}, bf16[2048,128]{1,0:T(8,128)(2,1)S(1)}, u32[]{:S(2)}, u32[]{:S(2)}) %collective-permute-start.7) | collective-permute-done | bytes 524320 | tf_op jit(solution)/shard_map/ppermute | solution.py:294
  110.5 1.5 %collective-permute-done.8.refs_4_ = bf16[2048,128]{1,0:T(8,128)(2,1)S(1)} collective-permute-done((bf16[2048,128]{1,0:T(8,128)(2,1)S(1)}, bf16[2048,128]{1,0:T(8,128)(2,1)S(1)}, u32[]{:S(2)}, u32[]{:S(2)}) %collective-permute-start.8) | collective-permute-done | bytes 524320 | tf_op jit(solution)/shard_map/ppermute | solution.py:295
  112.0 1.1 shard_map.111
  113.2 3.6 %collective-permute-start.9 = (bf16[512,128]{1,0:T(8,128)(2,1)S(1)}, bf16[512,128]{1,0:T(8,128)(2,1)S(1)}, u32[]{:S(2)}, u32[]{:S(2)}) collective-permute-start(bf16[512,128]{1,0:T(8,128)(2,1)S(1)} %shard_map.111), channel_id=1, source_target_pairs={{0,4},{4,0},{8,12},{12,8},{16,20},{20,16},{24,28},{28,24},{32,36},... | collective-permute-start | bytes 393224 | tf_op jit(solution)/shard_map/ppermute | solution.py:317
  116.8 1.4 %shard_map.110 = f32[512,128]{1,0:T(8,128)S(1)} custom-call(s32[1,128]{1,0:T(1,128)S(1)} %slice_convert_fusion.1.tail0.refs_0_, bf16[2576,128]{1,0:T(8,128)(2,1)S(1)} %shard_map.104.sent0.refs_2_.refs_1_, bf16[2048,128]{1,0:T(8,128)(2,1)S(1)} %collective-permute-done.6.refs_2_, bf16[2048,128]{1,0:T(8,128)(2,1)S(1)} %collective-permute-done.7.refs_3_, ...), custom_call_target="tpu_custom_call" | custom-call | flops 41943040 | bytes 2097152 | tf_op jit(solution)/shard_map/pallas_call | solution.py:307
  118.2 0.0 collective-permute-done.9
  118.3 0.1 broadcast_in_dim.4
  118.3 0.0 copy-start
  118.3 0.0 copy-start.1
  118.4 0.0 copy-start.2
  118.4 18.1 %all_to_all.17.types = bf16[4,512,128]{2,1,0:T(8,128)(2,1)S(1)} all-to-all(bf16[4,512,128]{2,1,0:T(8,128)(2,1)S(1)} %broadcast_in_dim.4), channel_id=1, replica_groups=mesh['acct'=128,'attr'=4] {'attr'}, dimensions={0} | all-to-all | bytes 1048576 | tf_op jit(solution)/shard_map/all_to_all | solution.py:320
  136.5 0.0 copy-done
  136.5 0.0 copy-done.1
  136.5 0.0 copy-done.2
  136.5 0.9 shard_map.112
  (4 shorter events, 0.1 us)
Async XLA Ops:
  1.3 0.7 copy-start.3
  1.3 0.7 copy-start.4
  1.3 0.7 copy-start.5
  3.7 10.5 %collective-permute-start = (bf16[2576,128]{1,0:T(8,128)(2,1)S(1)}, bf16[2576,128]{1,0:T(8,128)(2,1)S(1)}, u32[]{:S(2)}, u32[]{:S(2)}) collective-permute-start(bf16[2576,128]{1,0:T(8,128)(2,1)S(1)} %shard_map.104.sent0.refs_2_.refs_1_), channel_id=1, source_target_pairs={{0,4},{4,0},{8,12},{12,8},{16,20},{20,16},{24,28},{28,24},{32,36},... | collective-permute-start | bytes 1978376 | tf_op jit(solution)/shard_map/ppermute | solution.py:249
  17.0 13.9 %collective-permute-start.3 = (bf16[16,128,128]{2,1,0:T(8,128)(2,1)S(1)}, bf16[16,128,128]{2,1,0:T(8,128)(2,1)S(1)}, u32[]{:S(2)}, u32[]{:S(2)}) collective-permute-start(bf16[16,128,128]{2,1,0:T(8,128)(2,1)S(1)} %get-tuple-element.9), channel_id=1, source_target_pairs={{0,40},{8,32},{16,56},{24,48},{32,8},{40,0},{48,24},{56,16},{64,10... | collective-permute-start | bytes 1572872 | tf_op jit(solution)/shard_map/ppermute | solution.py:265
  24.3 12.2 %collective-permute-start.2 = (bf16[16,128,128]{2,1,0:T(8,128)(2,1)S(1)}, bf16[16,128,128]{2,1,0:T(8,128)(2,1)S(1)}, u32[]{:S(2)}, u32[]{:S(2)}) collective-permute-start(bf16[16,128,128]{2,1,0:T(8,128)(2,1)S(1)} %get-tuple-element.8), channel_id=1, source_target_pairs={{0,8},{8,0},{16,24},{24,16},{32,40},{40,32},{48,56},{56,48},{64,72... | collective-permute-start | bytes 1572872 | tf_op jit(solution)/shard_map/ppermute | solution.py:267
  26.9 11.1 %collective-permute-start.1 = (bf16[16,128,128]{2,1,0:T(8,128)(2,1)S(1)}, bf16[16,128,128]{2,1,0:T(8,128)(2,1)S(1)}, u32[]{:S(2)}, u32[]{:S(2)}) collective-permute-start(bf16[16,128,128]{2,1,0:T(8,128)(2,1)S(1)} %get-tuple-element.7), channel_id=1, source_target_pairs={{0,32},{8,40},{16,48},{24,56},{32,0},{40,8},{48,16},{56,24},{64,96... | collective-permute-start | bytes 1572872 | tf_op jit(solution)/shard_map/ppermute | solution.py:266
  38.4 10.5 %copy-start.6 = (s32[1,128]{1,0:T(1,128)S(1)}, s32[1,128]{1,0:T(1,128)}, u32[]{:S(2)}) copy-start(s32[1,128]{1,0:T(1,128)} %degree.1) | copy-start | bytes 1540
  49.0 15.0 %collective-permute-start.4 = (bf16[528,128]{1,0:T(8,128)(2,1)S(1)}, bf16[528,128]{1,0:T(8,128)(2,1)S(1)}, u32[]{:S(2)}, u32[]{:S(2)}) collective-permute-start(bf16[528,128]{1,0:T(8,128)(2,1)S(1)} %shard_map.107), channel_id=1, source_target_pairs={{0,128},{8,136},{16,144},{24,152},{32,160},{40,168},{48,176},{56,1... | collective-permute-start | bytes 405512 | tf_op jit(solution)/shard_map/ppermute | solution.py:276
  64.1 15.1 %collective-permute-start.5 = (bf16[528,128]{1,0:T(8,128)(2,1)S(1)}, bf16[528,128]{1,0:T(8,128)(2,1)S(1)}, u32[]{:S(2)}, u32[]{:S(2)}) collective-permute-start(bf16[528,128]{1,0:T(8,128)(2,1)S(1)} %add_convert_fusion.1.mine), channel_id=1, source_target_pairs={{0,384},{8,392},{16,400},{24,408},{32,416},{40,424},{48,432},{56,4... | collective-permute-start | bytes 405512 | tf_op jit(solution)/shard_map/ppermute | solution.py:278
  93.2 13.3 %collective-permute-start.6 = (bf16[2048,128]{1,0:T(8,128)(2,1)S(1)}, bf16[2048,128]{1,0:T(8,128)(2,1)S(1)}, u32[]{:S(2)}, u32[]{:S(2)}) collective-permute-start(bf16[2048,128]{1,0:T(8,128)(2,1)S(1)} %bitcast.7), channel_id=1, source_target_pairs={{0,40},{8,32},{16,56},{24,48},{32,8},{40,0},{48,24},{56,16},{64,10... | collective-permute-start | bytes 1572872 | tf_op jit(solution)/shard_map/ppermute | solution.py:293
  97.8 12.7 %collective-permute-start.7 = (bf16[2048,128]{1,0:T(8,128)(2,1)S(1)}, bf16[2048,128]{1,0:T(8,128)(2,1)S(1)}, u32[]{:S(2)}, u32[]{:S(2)}) collective-permute-start(bf16[2048,128]{1,0:T(8,128)(2,1)S(1)} %bitcast.8), channel_id=1, source_target_pairs={{0,32},{8,40},{16,48},{24,56},{32,0},{40,8},{48,16},{56,24},{64,96... | collective-permute-start | bytes 1572872 | tf_op jit(solution)/shard_map/ppermute | solution.py:294
  100.2 11.8 %collective-permute-start.8 = (bf16[2048,128]{1,0:T(8,128)(2,1)S(1)}, bf16[2048,128]{1,0:T(8,128)(2,1)S(1)}, u32[]{:S(2)}, u32[]{:S(2)}) collective-permute-start(bf16[2048,128]{1,0:T(8,128)(2,1)S(1)} %bitcast.9), channel_id=1, source_target_pairs={{0,8},{8,0},{16,24},{24,16},{32,40},{40,32},{48,56},{56,48},{64,72... | collective-permute-start | bytes 1572872 | tf_op jit(solution)/shard_map/ppermute | solution.py:295
  113.2 5.1 %collective-permute-start.9 = (bf16[512,128]{1,0:T(8,128)(2,1)S(1)}, bf16[512,128]{1,0:T(8,128)(2,1)S(1)}, u32[]{:S(2)}, u32[]{:S(2)}) collective-permute-start(bf16[512,128]{1,0:T(8,128)(2,1)S(1)} %shard_map.111), channel_id=1, source_target_pairs={{0,4},{4,0},{8,12},{12,8},{16,20},{20,16},{24,28},{28,24},{32,36},... | collective-permute-start | bytes 393224 | tf_op jit(solution)/shard_map/ppermute | solution.py:317
  118.3 18.2 %copy-start = (bf16[512,128]{1,0:T(8,128)(2,1)S(1)}, bf16[512,128]{1,0:T(8,128)(2,1)}, u32[]{:S(2)}) copy-start(bf16[512,128]{1,0:T(8,128)(2,1)} %scores.3) | copy-start | bytes 393220
  118.3 18.2 %copy-start.1 = (s32[512]{0:T(512)S(1)}, s32[512]{0:T(512)}, u32[]{:S(2)}) copy-start(s32[512]{0:T(512)} %param.11) | copy-start | bytes 6148
  118.4 18.2 %copy-start.2 = (s32[512]{0:T(512)S(1)}, s32[512]{0:T(512)}, u32[]{:S(2)}) copy-start(s32[512]{0:T(512)} %param.10) | copy-start | bytes 6148

commit v9 on v8

--- a/solution.py
+++ b/solution.py
@@ -291,8 +291,8 @@
     g0 = lax.all_to_all(spread, "acct", 0, 0, tiled=True, axis_index_groups=QUADS)
     g0 = g0.reshape(LINE * SIDE, SIDE)
     g3 = lax.ppermute(g0, "acct", DIAGONAL)
+    g2 = lax.ppermute(g0, "acct", ACROSS)
     g1 = lax.ppermute(g0, "acct", BESIDE)
-    g2 = lax.ppermute(g0, "acct", ACROSS)
     acc = jax.ShapeDtypeStruct((2 * ROWS, SIDE), f32)
     (before,) = call(
         functools.partial(backward_kernel, (0,), (0, 1)),
@@ -305,13 +305,13 @@
 
     def backward(half, dtype):
         (out,) = call(
-            functools.partial(backward_kernel, (3, 1, 2), (half,)),
+            functools.partial(backward_kernel, (3, 2, 1), (half,)),
             [jax.ShapeDtypeStruct((ROWS, SIDE), dtype)],
             smem(1) + vmem(5),
             [pltpu.VMEM((ROWS, SIDE), f32)],
             flops,
             2 * MEBI,
-        )(slots[half], slots[2 + half], g3, g1, g2, before)
+        )(slots[half], slots[2 + half], g3, g2, g1, before)
         return out
 
     other = lax.ppermute(backward(1, bf16), "acct", SWAP)

time: 136 us -> 136 us (level); the launches traced: 137 us -> 135 us
  waiting for transfers between devices: 32.5 us -> 28.7 us
  blocking collectives: 41.9 us -> 44.5 us
  Pallas kernels: 11.7 us -> 9.8 us
    ppermute x1, waiting for transfers between devices: 4.02 us -> 0.01 us  [per_device(): g1 = lax.ppermute(g0, 'acct', BESIDE)]
    ppermute x1, waiting for transfers between devices: 6.65 us -> 2.81 us  [per_device(): rest = lax.ppermute(half, 'acct', SECOND)]
    all_to_all x1, blocking collectives: 13.2 us -> 17 us  [per_device(): lax.all_to_all(spread, 'acct', 0, 0, tiled=True, axis_index_groups=QUADS)]
    ppermute x1, waiting for transfers between devices: 1.53 us -> 5.33 us  [per_device(): g2 = lax.ppermute(g0, 'acct', ACROSS)]
    ppermute x1, starting transfers between devices: 5.33 us -> 1.92 us  [per_device(): half = near.astype(f32) + lax.ppermute(near, 'acct', FIRST).astype(f32)]
    ppermute x1, starting transfers between devices: 2.45 us -> 5.47 us  [per_device(): g1 = lax.ppermute(g0, 'acct', BESIDE)]
    all_to_all x1, blocking collectives: 18.1 us -> 15.1 us  [per_device(): types = lax.all_to_all(types, 'attr', 0, 0, tiled=True)]
    ppermute x1, starting transfers between devices: 4.61 us -> 1.91 us  [per_device(): g3 = lax.ppermute(g0, 'acct', DIAGONAL)]
where the time goes in v9:
time: 136 us; the launch traced here: 135 us
  starting transfers between devices  49.6 us (36%)
  blocking collectives  44.5 us (33%)
  waiting for transfers between devices  28.7 us (21%)
  Pallas kernels  9.8 us (7%)
  between operations  1.5 us (1%)
    all_to_all x1, blocking collectives, per_device(): lax.all_to_all(spread, 'acct', 0, 0, tiled=True, axis_index_groups=QUADS)  17 us
    all_to_all x1, blocking collectives, per_device(): types = lax.all_to_all(types, 'attr', 0, 0, tiled=True)  15.1 us
    all_to_all x1, blocking collectives, per_device(): lax.all_to_all(line, 'acct', 0, 0, tiled=True, axis_index_groups=QUADS)  12.3 us
    ppermute x1, waiting for transfers between devices, per_device(): half = near.astype(f32) + lax.ppermute(near, 'acct', FIRST).astype(f32)  10.2 us
    ppermute x1, starting transfers between devices, per_device(): rest = lax.ppermute(half, 'acct', SECOND)  9.54 us
    ppermute x1, starting transfers between devices, per_device(): payload1 = lax.ppermute(payload, 'acct', SWAP)  8.79 us
    ppermute x1, starting transfers between devices, per_device(): r3 = lax.ppermute(o3, 'acct', DIAGONAL)  8.47 us
    ppermute x1, starting transfers between devices, per_device(): other = lax.ppermute(backward(1, bf16), 'acct', SWAP)  5.97 us
  transfers between devices with their start and end apart: 10, of which 9 were waited for; matrix products, arithmetic and copies ran while one was open for 0% of the time, Pallas kernels for 3%

profile of v9, /device:TPU:1, one launch (start us, length us, event | category | flops | bytes accessed | tf_op | source)
XLA Modules:
  0.0 135.2 jit_solution(13334656912495911880)
XLA Ops:
  1.3 0.0 copy-start.3
  1.3 0.0 copy-start.4
  1.3 0.0 copy-start.5
  1.3 0.6 copy-done.3
  1.9 0.0 copy-done.4
  2.0 0.0 copy-done.5
  2.0 1.7 %shard_map.104.sent0.refs_2_.refs_1_ = bf16[2576,128]{1,0:T(8,128)(2,1)S(1)} custom-call(s32[1]{0:T(128)} %bitcast.me, s32[1,128]{1,0:T(1,128)S(1)} %copy-done.3, s32[1,16]{1,0:T(1,128)S(1)} %copy-done.4, s32[1,16]{1,0:T(1,128)S(1)} %copy-done.5, s32[1,1]{1,0:T(1,128)S(6)} %copy.11.count, bf16[2048,128]{1,0:T(8,128)(2,1)} %bitcast.15, ...), custom_call_target="tpu_custom_call" | custom-call | flops 65536 | bytes 1048576 | tf_op jit(solution)/shard_map/pallas_call | solution.py:227
  3.7 8.8 %collective-permute-start = (bf16[2576,128]{1,0:T(8,128)(2,1)S(1)}, bf16[2576,128]{1,0:T(8,128)(2,1)S(1)}, u32[]{:S(2)}, u32[]{:S(2)}) collective-permute-start(bf16[2576,128]{1,0:T(8,128)(2,1)S(1)} %shard_map.104.sent0.refs_2_.refs_1_), channel_id=1, source_target_pairs={{0,4},{4,0},{8,12},{12,8},{16,20},{20,16},{24,28},{28,24},{32,36},... | collective-permute-start | bytes 1978376 | tf_op jit(solution)/shard_map/ppermute | solution.py:249
  12.5 1.7 %collective-permute-done.sent1.refs_3_.refs_1_ = bf16[2576,128]{1,0:T(8,128)(2,1)S(1)} collective-permute-done((bf16[2576,128]{1,0:T(8,128)(2,1)S(1)}, bf16[2576,128]{1,0:T(8,128)(2,1)S(1)}, u32[]{:S(2)}, u32[]{:S(2)}) %collective-permute-start) | collective-permute-done | bytes 659488 | tf_op jit(solution)/shard_map/ppermute | solution.py:249
  14.2 1.4 %shard_map.106 = (bf16[16,128,128]{2,1,0:T(8,128)(2,1)S(1)}, bf16[16,128,128]{2,1,0:T(8,128)(2,1)S(1)}, bf16[16,128,128]{2,1,0:T(8,128)(2,1)S(1)}) custom-call(s32[1,128]{1,0:T(1,128)S(1)} %slice_convert_fusion.1.tail0.refs_0_, s32[1,128]{1,0:T(1,128)S(1)} %slice_convert_fusion.tail1.refs_1_.refs_0_, bf16[2576,128]{1,0:T(8,128)(2,1)S(1)} %shard_map.104.sent0.refs_2_.refs_1_, ...), custom_call_target="tpu_custom_call" | custom-call | flops 41943040 | bytes 3145728 | tf_op jit(solution)/shard_map/pallas_call | solution.py:255
  15.6 8.5 %collective-permute-start.3 = (bf16[16,128,128]{2,1,0:T(8,128)(2,1)S(1)}, bf16[16,128,128]{2,1,0:T(8,128)(2,1)S(1)}, u32[]{:S(2)}, u32[]{:S(2)}) collective-permute-start(bf16[16,128,128]{2,1,0:T(8,128)(2,1)S(1)} %get-tuple-element.9), channel_id=1, source_target_pairs={{0,40},{8,32},{16,56},{24,48},{32,8},{40,0},{48,24},{56,16},{64,10... | collective-permute-start | bytes 1572872 | tf_op jit(solution)/shard_map/ppermute | solution.py:265
  24.1 2.1 %collective-permute-start.2 = (bf16[16,128,128]{2,1,0:T(8,128)(2,1)S(1)}, bf16[16,128,128]{2,1,0:T(8,128)(2,1)S(1)}, u32[]{:S(2)}, u32[]{:S(2)}) collective-permute-start(bf16[16,128,128]{2,1,0:T(8,128)(2,1)S(1)} %get-tuple-element.8), channel_id=1, source_target_pairs={{0,8},{8,0},{16,24},{24,16},{32,40},{40,32},{48,56},{56,48},{64,72... | collective-permute-start | bytes 1572872 | tf_op jit(solution)/shard_map/ppermute | solution.py:267
  26.2 2.0 %collective-permute-start.1 = (bf16[16,128,128]{2,1,0:T(8,128)(2,1)S(1)}, bf16[16,128,128]{2,1,0:T(8,128)(2,1)S(1)}, u32[]{:S(2)}, u32[]{:S(2)}) collective-permute-start(bf16[16,128,128]{2,1,0:T(8,128)(2,1)S(1)} %get-tuple-element.7), channel_id=1, source_target_pairs={{0,32},{8,40},{16,48},{24,56},{32,0},{40,8},{48,16},{56,24},{64,96... | collective-permute-start | bytes 1572872 | tf_op jit(solution)/shard_map/ppermute | solution.py:266
  28.2 1.8 %shard_map.105 = bf16[16,128,128]{2,1,0:T(8,128)(2,1)S(1)} custom-call(s32[1,128]{1,0:T(1,128)S(1)} %slice_convert_fusion.1.tail0.refs_0_, s32[1,128]{1,0:T(1,128)S(1)} %slice_convert_fusion.tail1.refs_1_.refs_0_, bf16[2576,128]{1,0:T(8,128)(2,1)S(1)} %shard_map.104.sent0.refs_2_.refs_1_, bf16[2576,128]{1,0:T(8,128)(2,1)S(1)} %collective-permute-done.sent1.refs_3_.refs_1_), custom_call_target="tpu_custom_call" | custom-call | flops 41943040 | bytes 3145728 | tf_op jit(solution)/shard_map/pallas_call | solution.py:255
  30.1 0.7 collective-permute-done.3
  30.8 5.5 %collective-permute-done.2 = bf16[16,128,128]{2,1,0:T(8,128)(2,1)S(1)} collective-permute-done((bf16[16,128,128]{2,1,0:T(8,128)(2,1)S(1)}, bf16[16,128,128]{2,1,0:T(8,128)(2,1)S(1)}, u32[]{:S(2)}, u32[]{:S(2)}) %collective-permute-start.2) | collective-permute-done | bytes 524320 | tf_op jit(solution)/shard_map/ppermute | solution.py:267
  36.3 1.1 collective-permute-done.1
  37.4 0.3 add_convert_fusion
  37.7 0.0 copy-start.6
  37.7 12.3 %all_to_all.15.parts = bf16[4,4,128,128]{3,2,1,0:T(8,128)(2,1)S(1)} all-to-all(bf16[4,4,128,128]{3,2,1,0:T(8,128)(2,1)S(1)} %bitcast.14), channel_id=1, replica_groups={{0,64,24,88},{128,192,152,216},{256,320,280,344},{384,448,408,472},{32,..., dimensions={0} | all-to-all | bytes 1048576 | tf_op jit(solution)/shard_map/all_to_all | solution.py:271
  50.0 0.0 copy-done.6
  50.0 0.1 shard_map.107
  50.1 1.9 %collective-permute-start.4 = (bf16[528,128]{1,0:T(8,128)(2,1)S(1)}, bf16[528,128]{1,0:T(8,128)(2,1)S(1)}, u32[]{:S(2)}, u32[]{:S(2)}) collective-permute-start(bf16[528,128]{1,0:T(8,128)(2,1)S(1)} %shard_map.107), channel_id=1, source_target_pairs={{0,128},{8,136},{16,144},{24,152},{32,160},{40,168},{48,176},{56,1... | collective-permute-start | bytes 405512 | tf_op jit(solution)/shard_map/ppermute | solution.py:276
  52.0 10.2 %collective-permute-done.4 = bf16[528,128]{1,0:T(8,128)(2,1)S(1)} collective-permute-done((bf16[528,128]{1,0:T(8,128)(2,1)S(1)}, bf16[528,128]{1,0:T(8,128)(2,1)S(1)}, u32[]{:S(2)}, u32[]{:S(2)}) %collective-permute-start.4) | collective-permute-done | bytes 135200 | tf_op jit(solution)/shard_map/ppermute | solution.py:276
  62.3 9.5 %collective-permute-start.5 = (bf16[528,128]{1,0:T(8,128)(2,1)S(1)}, bf16[528,128]{1,0:T(8,128)(2,1)S(1)}, u32[]{:S(2)}, u32[]{:S(2)}) collective-permute-start(bf16[528,128]{1,0:T(8,128)(2,1)S(1)} %add_convert_fusion.1.mine), channel_id=1, source_target_pairs={{0,384},{8,392},{16,400},{24,408},{32,416},{40,424},{48,432},{56,4... | collective-permute-start | bytes 405512 | tf_op jit(solution)/shard_map/ppermute | solution.py:278
  71.8 2.8 %collective-permute-done.5.other = bf16[528,128]{1,0:T(8,128)(2,1)S(1)} collective-permute-done((bf16[528,128]{1,0:T(8,128)(2,1)S(1)}, bf16[528,128]{1,0:T(8,128)(2,1)S(1)}, u32[]{:S(2)}, u32[]{:S(2)}) %collective-permute-start.5) | collective-permute-done | bytes 135200 | tf_op jit(solution)/shard_map/ppermute | solution.py:278
  74.7 0.8 shard_map.108
  75.4 17.0 %all_to_all.16 = bf16[4,512,128]{2,1,0:T(8,128)(2,1)S(1)} all-to-all(bf16[4,512,128]{2,1,0:T(8,128)(2,1)S(1)} %get-tuple-element.10), channel_id=1, replica_groups={{0,64,24,88},{128,192,152,216},{256,320,280,344},{384,448,408,472},{32,..., dimensions={0} | all-to-all | bytes 1048576 | tf_op jit(solution)/shard_map/all_to_all | solution.py:291
  92.5 1.9 %collective-permute-start.6 = (bf16[2048,128]{1,0:T(8,128)(2,1)S(1)}, bf16[2048,128]{1,0:T(8,128)(2,1)S(1)}, u32[]{:S(2)}, u32[]{:S(2)}) collective-permute-start(bf16[2048,128]{1,0:T(8,128)(2,1)S(1)} %bitcast.7), channel_id=1, source_target_pairs={{0,40},{8,32},{16,56},{24,48},{32,8},{40,0},{48,24},{56,16},{64,10... | collective-permute-start | bytes 1572872 | tf_op jit(solution)/shard_map/ppermute | solution.py:293
  94.4 3.4 %collective-permute-start.7 = (bf16[2048,128]{1,0:T(8,128)(2,1)S(1)}, bf16[2048,128]{1,0:T(8,128)(2,1)S(1)}, u32[]{:S(2)}, u32[]{:S(2)}) collective-permute-start(bf16[2048,128]{1,0:T(8,128)(2,1)S(1)} %bitcast.8), channel_id=1, source_target_pairs={{0,8},{8,0},{16,24},{24,16},{32,40},{40,32},{48,56},{56,48},{64,72... | collective-permute-start | bytes 1572872 | tf_op jit(solution)/shard_map/ppermute | solution.py:294
  97.8 5.5 %collective-permute-start.8 = (bf16[2048,128]{1,0:T(8,128)(2,1)S(1)}, bf16[2048,128]{1,0:T(8,128)(2,1)S(1)}, u32[]{:S(2)}, u32[]{:S(2)}) collective-permute-start(bf16[2048,128]{1,0:T(8,128)(2,1)S(1)} %bitcast.9), channel_id=1, source_target_pairs={{0,32},{8,40},{16,48},{24,56},{32,0},{40,8},{48,16},{56,24},{64,96... | collective-permute-start | bytes 1572872 | tf_op jit(solution)/shard_map/ppermute | solution.py:295
  103.3 1.3 shard_map.109.refs_5_
  104.6 1.2 collective-permute-done.6.refs_2_
  105.8 5.3 %collective-permute-done.7.refs_3_ = bf16[2048,128]{1,0:T(8,128)(2,1)S(1)} collective-permute-done((bf16[2048,128]{1,0:T(8,128)(2,1)S(1)}, bf16[2048,128]{1,0:T(8,128)(2,1)S(1)}, u32[]{:S(2)}, u32[]{:S(2)}) %collective-permute-start.7) | collective-permute-done | bytes 524320 | tf_op jit(solution)/shard_map/ppermute | solution.py:294
  111.1 0.0 collective-permute-done.8.refs_4_
  111.2 0.9 shard_map.111
  112.0 6.0 %collective-permute-start.9 = (bf16[512,128]{1,0:T(8,128)(2,1)S(1)}, bf16[512,128]{1,0:T(8,128)(2,1)S(1)}, u32[]{:S(2)}, u32[]{:S(2)}) collective-permute-start(bf16[512,128]{1,0:T(8,128)(2,1)S(1)} %shard_map.111), channel_id=1, source_target_pairs={{0,4},{4,0},{8,12},{12,8},{16,20},{20,16},{24,28},{28,24},{32,36},... | collective-permute-start | bytes 393224 | tf_op jit(solution)/shard_map/ppermute | solution.py:317
  118.0 0.9 shard_map.110
  118.9 0.1 collective-permute-done.9
  119.0 0.1 broadcast_in_dim.4
  119.1 0.0 copy-start
  119.1 0.0 copy-start.1
  119.1 0.0 copy-start.2
  119.1 15.1 %all_to_all.17.types = bf16[4,512,128]{2,1,0:T(8,128)(2,1)S(1)} all-to-all(bf16[4,512,128]{2,1,0:T(8,128)(2,1)S(1)} %broadcast_in_dim.4), channel_id=1, replica_groups=mesh['acct'=128,'attr'=4] {'attr'}, dimensions={0} | all-to-all | bytes 1048576 | tf_op jit(solution)/shard_map/all_to_all | solution.py:320
  134.2 0.0 copy-done
  134.3 0.0 copy-done.1
  134.3 0.0 copy-done.2
  134.3 0.9 shard_map.112
  (4 shorter events, 0.1 us)
Async XLA Ops:
  1.3 0.7 copy-start.3
  1.3 0.7 copy-start.4
  1.3 0.7 copy-start.5
  3.7 10.5 %collective-permute-start = (bf16[2576,128]{1,0:T(8,128)(2,1)S(1)}, bf16[2576,128]{1,0:T(8,128)(2,1)S(1)}, u32[]{:S(2)}, u32[]{:S(2)}) collective-permute-start(bf16[2576,128]{1,0:T(8,128)(2,1)S(1)} %shard_map.104.sent0.refs_2_.refs_1_), channel_id=1, source_target_pairs={{0,4},{4,0},{8,12},{12,8},{16,20},{20,16},{24,28},{28,24},{32,36},... | collective-permute-start | bytes 1978376 | tf_op jit(solution)/shard_map/ppermute | solution.py:249
  15.6 15.1 %collective-permute-start.3 = (bf16[16,128,128]{2,1,0:T(8,128)(2,1)S(1)}, bf16[16,128,128]{2,1,0:T(8,128)(2,1)S(1)}, u32[]{:S(2)}, u32[]{:S(2)}) collective-permute-start(bf16[16,128,128]{2,1,0:T(8,128)(2,1)S(1)} %get-tuple-element.9), channel_id=1, source_target_pairs={{0,40},{8,32},{16,56},{24,48},{32,8},{40,0},{48,24},{56,16},{64,10... | collective-permute-start | bytes 1572872 | tf_op jit(solution)/shard_map/ppermute | solution.py:265
  24.1 12.2 %collective-permute-start.2 = (bf16[16,128,128]{2,1,0:T(8,128)(2,1)S(1)}, bf16[16,128,128]{2,1,0:T(8,128)(2,1)S(1)}, u32[]{:S(2)}, u32[]{:S(2)}) collective-permute-start(bf16[16,128,128]{2,1,0:T(8,128)(2,1)S(1)} %get-tuple-element.8), channel_id=1, source_target_pairs={{0,8},{8,0},{16,24},{24,16},{32,40},{40,32},{48,56},{56,48},{64,72... | collective-permute-start | bytes 1572872 | tf_op jit(solution)/shard_map/ppermute | solution.py:267
  26.2 11.1 %collective-permute-start.1 = (bf16[16,128,128]{2,1,0:T(8,128)(2,1)S(1)}, bf16[16,128,128]{2,1,0:T(8,128)(2,1)S(1)}, u32[]{:S(2)}, u32[]{:S(2)}) collective-permute-start(bf16[16,128,128]{2,1,0:T(8,128)(2,1)S(1)} %get-tuple-element.7), channel_id=1, source_target_pairs={{0,32},{8,40},{16,48},{24,56},{32,0},{40,8},{48,16},{56,24},{64,96... | collective-permute-start | bytes 1572872 | tf_op jit(solution)/shard_map/ppermute | solution.py:266
  37.7 12.3 %copy-start.6 = (s32[1,128]{1,0:T(1,128)S(1)}, s32[1,128]{1,0:T(1,128)}, u32[]{:S(2)}) copy-start(s32[1,128]{1,0:T(1,128)} %degree.1) | copy-start | bytes 1540
  50.1 12.2 %collective-permute-start.4 = (bf16[528,128]{1,0:T(8,128)(2,1)S(1)}, bf16[528,128]{1,0:T(8,128)(2,1)S(1)}, u32[]{:S(2)}, u32[]{:S(2)}) collective-permute-start(bf16[528,128]{1,0:T(8,128)(2,1)S(1)} %shard_map.107), channel_id=1, source_target_pairs={{0,128},{8,136},{16,144},{24,152},{32,160},{40,168},{48,176},{56,1... | collective-permute-start | bytes 405512 | tf_op jit(solution)/shard_map/ppermute | solution.py:276
  62.3 12.4 %collective-permute-start.5 = (bf16[528,128]{1,0:T(8,128)(2,1)S(1)}, bf16[528,128]{1,0:T(8,128)(2,1)S(1)}, u32[]{:S(2)}, u32[]{:S(2)}) collective-permute-start(bf16[528,128]{1,0:T(8,128)(2,1)S(1)} %add_convert_fusion.1.mine), channel_id=1, source_target_pairs={{0,384},{8,392},{16,400},{24,408},{32,416},{40,424},{48,432},{56,4... | collective-permute-start | bytes 405512 | tf_op jit(solution)/shard_map/ppermute | solution.py:278
  92.5 13.3 %collective-permute-start.6 = (bf16[2048,128]{1,0:T(8,128)(2,1)S(1)}, bf16[2048,128]{1,0:T(8,128)(2,1)S(1)}, u32[]{:S(2)}, u32[]{:S(2)}) collective-permute-start(bf16[2048,128]{1,0:T(8,128)(2,1)S(1)} %bitcast.7), channel_id=1, source_target_pairs={{0,40},{8,32},{16,56},{24,48},{32,8},{40,0},{48,24},{56,16},{64,10... | collective-permute-start | bytes 1572872 | tf_op jit(solution)/shard_map/ppermute | solution.py:293
  94.4 16.8 %collective-permute-start.7 = (bf16[2048,128]{1,0:T(8,128)(2,1)S(1)}, bf16[2048,128]{1,0:T(8,128)(2,1)S(1)}, u32[]{:S(2)}, u32[]{:S(2)}) collective-permute-start(bf16[2048,128]{1,0:T(8,128)(2,1)S(1)} %bitcast.8), channel_id=1, source_target_pairs={{0,8},{8,0},{16,24},{24,16},{32,40},{40,32},{48,56},{56,48},{64,72... | collective-permute-start | bytes 1572872 | tf_op jit(solution)/shard_map/ppermute | solution.py:294
  97.8 13.3 %collective-permute-start.8 = (bf16[2048,128]{1,0:T(8,128)(2,1)S(1)}, bf16[2048,128]{1,0:T(8,128)(2,1)S(1)}, u32[]{:S(2)}, u32[]{:S(2)}) collective-permute-start(bf16[2048,128]{1,0:T(8,128)(2,1)S(1)} %bitcast.9), channel_id=1, source_target_pairs={{0,32},{8,40},{16,48},{24,56},{32,0},{40,8},{48,16},{56,24},{64,96... | collective-permute-start | bytes 1572872 | tf_op jit(solution)/shard_map/ppermute | solution.py:295
  112.0 6.9 %collective-permute-start.9 = (bf16[512,128]{1,0:T(8,128)(2,1)S(1)}, bf16[512,128]{1,0:T(8,128)(2,1)S(1)}, u32[]{:S(2)}, u32[]{:S(2)}) collective-permute-start(bf16[512,128]{1,0:T(8,128)(2,1)S(1)} %shard_map.111), channel_id=1, source_target_pairs={{0,4},{4,0},{8,12},{12,8},{16,20},{20,16},{24,28},{28,24},{32,36},... | collective-permute-start | bytes 393224 | tf_op jit(solution)/shard_map/ppermute | solution.py:317
  119.1 15.2 %copy-start = (bf16[512,128]{1,0:T(8,128)(2,1)S(1)}, bf16[512,128]{1,0:T(8,128)(2,1)}, u32[]{:S(2)}) copy-start(bf16[512,128]{1,0:T(8,128)(2,1)} %scores.3) | copy-start | bytes 393220
  119.1 15.2 %copy-start.1 = (s32[512]{0:T(512)S(1)}, s32[512]{0:T(512)}, u32[]{:S(2)}) copy-start(s32[512]{0:T(512)} %param.11) | copy-start | bytes 6148
  119.1 15.1 %copy-start.2 = (s32[512]{0:T(512)S(1)}, s32[512]{0:T(512)}, u32[]{:S(2)}) copy-start(s32[512]{0:T(512)} %param.10) | copy-start | bytes 6148

commit v10 on v8

--- a/solution.py
+++ b/solution.py
@@ -59,13 +59,21 @@
     return jnp.broadcast_to(row, (SIDE, SIDE)).T
 
 
-def prepare_kernel(me, table, attr, acct, count, weights, scores, degrees, payload, rows, degree, sems):
-    tiles = pltpu.make_async_copy(weights, payload.at[pl.ds(0, TILES), :], sems.at[0])
-    prior = pltpu.make_async_copy(scores, rows, sems.at[1])
-    small = pltpu.make_async_copy(degrees, degree, sems.at[2])
-    small.start()
+def prepare_kernel(me, count, *refs):
+    tables, (weights, scores, degrees, payload) = refs[:3], refs[3:7]
+    table, attr, acct, rows, degree, sems = refs[7:]
+    small = [
+        pltpu.make_async_copy(source, target, sems.at[n])
+        for n, (source, target) in enumerate(zip((*tables, degrees), (table, attr, acct, degree)))
+    ]
+    for copy in small:
+        copy.start()
+    tiles = pltpu.make_async_copy(weights, payload.at[pl.ds(0, TILES), :], sems.at[4])
+    prior = pltpu.make_async_copy(scores, rows, sems.at[5])
     prior.start()
     tiles.start()
+    for copy in small:
+        copy.wait()
     core, u, v = where(me[0])
     twin, twin_u, twin_v = where(me[0] ^ 1)
     lane = lax.broadcasted_iota(jnp.int32, (SLOTS, SIDE), 1)
@@ -78,7 +86,6 @@
         tail = jnp.where(lane == s + SLOTS, sent, tail)
         tail = jnp.where(lane == s + 2 * SLOTS, acct[0, s], tail)
     payload[TILES + ROWS :, :] = tail.astype(jnp.float32).astype(payload.dtype)
-    small.wait()
     prior.wait()
     for n in range(4):
         scale = column(lax.rsqrt(degree[n : n + 1, :].astype(jnp.float32)))
@@ -121,22 +128,24 @@
         out[...] = acc[n * LINE : (n + 1) * LINE].astype(out.dtype)
 
 
-def near_kernel(me, parts, degree, sums):
+def near_kernel(me, parts, degree, sums, sent):
     for n in range(4):
         total = parts[0, n].astype(jnp.float32)
         for k in range(1, 4):
             total += parts[k, n].astype(jnp.float32)
-        sums[n * SIDE : (n + 1) * SIDE, :] = total.astype(sums.dtype)
+        sums[n * SIDE : (n + 1) * SIDE, :] = total
+        sent[n * SIDE : (n + 1) * SIDE, :] = total.astype(sent.dtype)
     row = lax.broadcasted_iota(jnp.int32, (SLOTS, SIDE), 0)
     mine = jnp.where(row == where(me[0])[1] >> 2, degree[...].astype(jnp.float32), 0.0)
-    sums[FOUR:, :] = mine.astype(sums.dtype)
+    sums[FOUR:, :] = mine
+    sent[FOUR:, :] = mine.astype(sent.dtype)
 
 
 def far_kernel(me, mine, other, own, spread):
-    degree = mine[FOUR:, :].astype(jnp.float32) + other[FOUR:, :].astype(jnp.float32)
+    degree = mine[FOUR:, :] + other[FOUR:, :].astype(jnp.float32)
     for n in range(4):
         rows = pl.ds(n * SIDE, SIDE)
-        total = mine[rows, :].astype(jnp.float32) + other[rows, :].astype(jnp.float32)
+        total = mine[rows, :] + other[rows, :].astype(jnp.float32)
         scores = (total * column(lax.rsqrt(degree[n : n + 1, :]))).astype(spread.dtype)
         for k in range(4):
             spread[k, rows, :] = scores
@@ -221,29 +230,35 @@
     tile_count,
 ):
     bf16, f32, i32 = jnp.bfloat16, jnp.float32, jnp.int32
-    group = jax.ShapeDtypeStruct((LINE, SIDE, SIDE), bf16)
     degree = acct_degree.reshape(4, SIDE)
     me = lax.axis_index("acct").astype(i32).reshape(1)
     (payload,) = call(
         prepare_kernel,
         [jax.ShapeDtypeStruct((SENT, SIDE), bf16)],
-        smem(5) + [pl.BlockSpec(memory_space=pltpu.HBM)] * 3,
+        smem(2) + [pl.BlockSpec(memory_space=pltpu.HBM)] * 6,
         [
+            pltpu.SMEM((1, SIDE), i32),
+            pltpu.SMEM((1, SLOTS), i32),
+            pltpu.SMEM((1, SLOTS), i32),
             pltpu.VMEM((ROWS, SIDE), bf16),
             pltpu.VMEM((4, SIDE), i32),
-            pltpu.SemaphoreType.DMA((3,)),
+            pltpu.SemaphoreType.DMA((6,)),
         ],
         ROWS * SIDE,
         MEBI,
     )(
         me,
-        attr_owner,
-        tile_attr,
-        tile_acct,
         tile_count,
         *(
             pltpu.with_memory_space_constraint(array, pltpu.HBM)
-            for array in (tile_weight.reshape(TILES, SIDE), scores0, degree)
+            for array in (
+                attr_owner,
+                tile_attr,
+                tile_acct,
+                tile_weight.reshape(TILES, SIDE),
+                scores0,
+                degree,
+            )
         ),
     )
     payload1 = lax.ppermute(payload, "acct", SWAP)
@@ -251,31 +266,34 @@
     tails = [sent[TILES + ROWS :][:1].astype(i32) for sent in (payload, payload1)]
     slots = (*tails, payload, payload1)
 
-    def forward(chips):
+    def forward(chips, dtype):
         return call(
             functools.partial(forward_kernel, chips),
-            [group] * len(chips),
+            [jax.ShapeDtypeStruct((LINE, SIDE, SIDE), dtype)] * len(chips),
             smem(2) + vmem(2),
             [pltpu.VMEM((len(chips) * LINE, SIDE, SIDE), f32)],
             flops,
             3 * MEBI,
         )(*slots)
 
-    o3, o1, o2 = forward((3, 1, 2))
+    o3, o1, o2 = forward((3, 1, 2), bf16)
     r3 = lax.ppermute(o3, "acct", DIAGONAL)
     r1 = lax.ppermute(o1, "acct", BESIDE)
     r2 = lax.ppermute(o2, "acct", ACROSS)
-    (o0,) = forward((0,))
-    line = o0.astype(f32) + r1.astype(f32) + r2.astype(f32) + r3.astype(f32)
+    (o0,) = forward((0,), f32)
+    line = o0 + r3.astype(f32) + r2.astype(f32) + r1.astype(f32)
     line = line.astype(bf16).reshape(4, 4, SIDE, SIDE)
     line = lax.all_to_all(line, "acct", 0, 0, tiled=True, axis_index_groups=QUADS)
-    sums = jax.ShapeDtypeStruct((FOUR + SLOTS, SIDE), bf16)
-    (near,) = call(
-        near_kernel, [sums], smem(1) + vmem(2), [], SIDE * SIDE * LINE, MEBI
+    near, sent = call(
+        near_kernel,
+        [jax.ShapeDtypeStruct((FOUR + SLOTS, SIDE), dtype) for dtype in (f32, bf16)],
+        smem(1) + vmem(2),
+        [],
+        SIDE * SIDE * LINE,
+        MEBI,
     )(me, line, attr_degree)
-    half = near.astype(f32) + lax.ppermute(near, "acct", FIRST).astype(f32)
-    half = half.astype(bf16)
-    rest = lax.ppermute(half, "acct", SECOND)
+    half = near + lax.ppermute(sent, "acct", FIRST).astype(f32)
+    rest = lax.ppermute(half.astype(bf16), "acct", SECOND)
     own_scores, spread = call(
         far_kernel,
         [

time: 136 us -> 134 us (0.985); the launches traced: 137 us -> 134 us
  starting transfers between devices: 48.7 us -> 54.2 us
  waiting for transfers between devices: 32.5 us -> 28.9 us
  blocking collectives: 41.9 us -> 39.3 us
  Pallas kernels: 11.7 us -> 9.43 us
    ppermute x2, waiting for transfers between devices: 16.3 us -> 12.6 us  [the longest x1 6.36 us: per_device(): rest = lax.ppermute(half.astype(bf16), 'acct', SECOND)]
    ppermute x2, starting transfers between devices: 13.7 us -> 17 us  [the longest x1 11.8 us: per_device(): rest = lax.ppermute(half.astype(bf16), 'acct', SECOND)]
    all_to_all x1, blocking collectives: 18.1 us -> 15.6 us  [per_device(): types = lax.all_to_all(types, 'attr', 0, 0, tiled=True)]
    ppermute x1, starting transfers between devices: 7.24 us -> 8.82 us  [per_device(): r3 = lax.ppermute(o3, 'acct', DIAGONAL)]
    pallas_call x4, Pallas kernels: 6.26 us -> 4.7 us  [the longest x2 3.45 us: forward(): call(functools.partial(forward_kernel, chips), [jax.ShapeDtypeStruct((LIN...]
  transfers between devices with their start and end apart: 10 -> 10, of which waited for: 9 -> 10; matrix products, arithmetic and copies ran while one was open for 0% -> 0% of each run, Pallas kernels for 3% -> 3%
where the time goes in v10:
time: 134 us
  starting transfers between devices  54.2 us (40%)
  blocking collectives  39.3 us (29%)
  waiting for transfers between devices  28.9 us (22%)
  Pallas kernels  9.43 us (7%)
  between operations  1.48 us (1%)
    all_to_all x1, blocking collectives, per_device(): types = lax.all_to_all(types, 'attr', 0, 0, tiled=True)  15.6 us
    all_to_all x1, blocking collectives, per_device(): lax.all_to_all(spread, 'acct', 0, 0, tiled=True, axis_index_groups=QUADS)  13.2 us
    ppermute x1, starting transfers between devices, per_device(): rest = lax.ppermute(half.astype(bf16), 'acct', SECOND)  11.8 us
    all_to_all x1, blocking collectives, per_device(): lax.all_to_all(line, 'acct', 0, 0, tiled=True, axis_index_groups=QUADS)  10.5 us
    ppermute x1, starting transfers between devices, per_device(): r3 = lax.ppermute(o3, 'acct', DIAGONAL)  8.82 us
    ppermute x1, starting transfers between devices, per_device(): payload1 = lax.ppermute(payload, 'acct', SWAP)  8.79 us
    ppermute x1, waiting for transfers between devices, per_device(): rest = lax.ppermute(half.astype(bf16), 'acct', SECOND)  6.36 us
    ppermute x1, waiting for transfers between devices, per_device(): half = near + lax.ppermute(sent, 'acct', FIRST).astype(f32)  6.27 us
  transfers between devices with their start and end apart: 10, of which 10 were waited for; matrix products, arithmetic and copies ran while one was open for 0% of the time, Pallas kernels for 3%

profile of v10, /device:TPU:1, one launch (start us, length us, event | category | flops | bytes accessed | tf_op | source)
XLA Modules:
  0.0 133.8 jit_solution(4816387755003234232)
XLA Ops:
  1.3 1.2 shard_map.104.sent0.refs_2_.refs_1_
  2.5 8.8 %collective-permute-start = (bf16[2576,128]{1,0:T(8,128)(2,1)S(1)}, bf16[2576,128]{1,0:T(8,128)(2,1)S(1)}, u32[]{:S(2)}, u32[]{:S(2)}) collective-permute-start(bf16[2576,128]{1,0:T(8,128)(2,1)S(1)} %shard_map.104.sent0.refs_2_.refs_1_), channel_id=1, source_target_pairs={{0,4},{4,0},{8,12},{12,8},{16,20},{20,16},{24,28},{28,24},{32,36},... | collective-permute-start | bytes 1978376 | tf_op jit(solution)/shard_map/ppermute | solution.py:264
  11.3 1.7 %collective-permute-done.sent1.refs_3_.refs_1_ = bf16[2576,128]{1,0:T(8,128)(2,1)S(1)} collective-permute-done((bf16[2576,128]{1,0:T(8,128)(2,1)S(1)}, bf16[2576,128]{1,0:T(8,128)(2,1)S(1)}, u32[]{:S(2)}, u32[]{:S(2)}) %collective-permute-start) | collective-permute-done | bytes 659488 | tf_op jit(solution)/shard_map/ppermute | solution.py:264
  13.0 1.8 %shard_map.106 = (bf16[16,128,128]{2,1,0:T(8,128)(2,1)S(1)}, bf16[16,128,128]{2,1,0:T(8,128)(2,1)S(1)}, bf16[16,128,128]{2,1,0:T(8,128)(2,1)S(1)}) custom-call(s32[1,128]{1,0:T(1,128)S(1)} %slice_convert_fusion.1.tail0.refs_0_, s32[1,128]{1,0:T(1,128)S(1)} %slice_convert_fusion.tail1.refs_1_.refs_0_, bf16[2576,128]{1,0:T(8,128)(2,1)S(1)} %shard_map.104.sent0.refs_2_.refs_1_, ...), custom_call_target="tpu_custom_call" | custom-call | flops 41943040 | bytes 3145728 | tf_op jit(solution)/shard_map/pallas_call | solution.py:270
  14.8 8.8 %collective-permute-start.1 = (bf16[16,128,128]{2,1,0:T(8,128)(2,1)S(1)}, bf16[16,128,128]{2,1,0:T(8,128)(2,1)S(1)}, u32[]{:S(2)}, u32[]{:S(2)}) collective-permute-start(bf16[16,128,128]{2,1,0:T(8,128)(2,1)S(1)} %get-tuple-element.9), channel_id=1, source_target_pairs={{0,40},{8,32},{16,56},{24,48},{32,8},{40,0},{48,24},{56,16},{64,10... | collective-permute-start | bytes 1572872 | tf_op jit(solution)/shard_map/ppermute | solution.py:280
  23.6 2.5 %collective-permute-start.2 = (bf16[16,128,128]{2,1,0:T(8,128)(2,1)S(1)}, bf16[16,128,128]{2,1,0:T(8,128)(2,1)S(1)}, u32[]{:S(2)}, u32[]{:S(2)}) collective-permute-start(bf16[16,128,128]{2,1,0:T(8,128)(2,1)S(1)} %get-tuple-element.10), channel_id=1, source_target_pairs={{0,8},{8,0},{16,24},{24,16},{32,40},{40,32},{48,56},{56,48},{64,72... | collective-permute-start | bytes 1572872 | tf_op jit(solution)/shard_map/ppermute | solution.py:282
  26.1 1.9 %collective-permute-start.3 = (bf16[16,128,128]{2,1,0:T(8,128)(2,1)S(1)}, bf16[16,128,128]{2,1,0:T(8,128)(2,1)S(1)}, u32[]{:S(2)}, u32[]{:S(2)}) collective-permute-start(bf16[16,128,128]{2,1,0:T(8,128)(2,1)S(1)} %get-tuple-element.11), channel_id=1, source_target_pairs={{0,32},{8,40},{16,48},{24,56},{32,0},{40,8},{48,16},{56,24},{64,96... | collective-permute-start | bytes 1572872 | tf_op jit(solution)/shard_map/ppermute | solution.py:281
  28.0 1.7 %shard_map.105 = f32[16,128,128]{2,1,0:T(8,128)S(1)} custom-call(s32[1,128]{1,0:T(1,128)S(1)} %slice_convert_fusion.1.tail0.refs_0_, s32[1,128]{1,0:T(1,128)S(1)} %slice_convert_fusion.tail1.refs_1_.refs_0_, bf16[2576,128]{1,0:T(8,128)(2,1)S(1)} %shard_map.104.sent0.refs_2_.refs_1_, bf16[2576,128]{1,0:T(8,128)(2,1)S(1)} %collective-permute-done.sent1.refs_3_.refs_1_), custom_call_target="tpu_custom_call" | custom-call | flops 41943040 | bytes 3145728 | tf_op jit(solution)/shard_map/pallas_call | solution.py:270
  29.7 0.6 collective-permute-done.1
  30.3 5.5 %collective-permute-done.2 = bf16[16,128,128]{2,1,0:T(8,128)(2,1)S(1)} collective-permute-done((bf16[16,128,128]{2,1,0:T(8,128)(2,1)S(1)}, bf16[16,128,128]{2,1,0:T(8,128)(2,1)S(1)}, u32[]{:S(2)}, u32[]{:S(2)}) %collective-permute-start.2) | collective-permute-done | bytes 524320 | tf_op jit(solution)/shard_map/ppermute | solution.py:282
  35.8 1.4 %collective-permute-done.3 = bf16[16,128,128]{2,1,0:T(8,128)(2,1)S(1)} collective-permute-done((bf16[16,128,128]{2,1,0:T(8,128)(2,1)S(1)}, bf16[16,128,128]{2,1,0:T(8,128)(2,1)S(1)}, u32[]{:S(2)}, u32[]{:S(2)}) %collective-permute-start.3) | collective-permute-done | bytes 524320 | tf_op jit(solution)/shard_map/ppermute | solution.py:281
  37.2 0.3 add_convert_fusion
  37.5 0.0 copy-start.3
  37.5 10.5 %all_to_all.15.parts = bf16[4,4,128,128]{3,2,1,0:T(8,128)(2,1)S(1)} all-to-all(bf16[4,4,128,128]{3,2,1,0:T(8,128)(2,1)S(1)} %bitcast.14), channel_id=1, replica_groups={{0,64,24,88},{128,192,152,216},{256,320,280,344},{384,448,408,472},{32,..., dimensions={0} | all-to-all | bytes 1048576 | tf_op jit(solution)/shard_map/all_to_all | solution.py:286
  48.1 0.0 copy-done.3
  48.1 0.1 shard_map.107
  48.1 5.2 %collective-permute-start.4 = (bf16[528,128]{1,0:T(8,128)(2,1)S(1)}, bf16[528,128]{1,0:T(8,128)(2,1)S(1)}, u32[]{:S(2)}, u32[]{:S(2)}) collective-permute-start(bf16[528,128]{1,0:T(8,128)(2,1)S(1)} %get-tuple-element.13), channel_id=1, source_target_pairs={{0,128},{8,136},{16,144},{24,152},{32,160},{40,168},{48,176},{56,1... | collective-permute-start | bytes 405512 | tf_op jit(solution)/shard_map/ppermute | solution.py:295
  53.4 6.3 %collective-permute-done.4 = bf16[528,128]{1,0:T(8,128)(2,1)S(1)} collective-permute-done((bf16[528,128]{1,0:T(8,128)(2,1)S(1)}, bf16[528,128]{1,0:T(8,128)(2,1)S(1)}, u32[]{:S(2)}, u32[]{:S(2)}) %collective-permute-start.4) | collective-permute-done | bytes 135200 | tf_op jit(solution)/shard_map/ppermute | solution.py:295
  59.7 11.8 %collective-permute-start.5 = (bf16[528,128]{1,0:T(8,128)(2,1)S(1)}, bf16[528,128]{1,0:T(8,128)(2,1)S(1)}, u32[]{:S(2)}, u32[]{:S(2)}) collective-permute-start(bf16[528,128]{1,0:T(8,128)(2,1)S(1)} %get-tuple-element.16), channel_id=1, source_target_pairs={{0,384},{8,392},{16,400},{24,408},{32,416},{40,424},{48,432},{56,4... | collective-permute-start | bytes 405512 | tf_op jit(solution)/shard_map/ppermute | solution.py:296
  71.5 6.4 %collective-permute-done.5.other = bf16[528,128]{1,0:T(8,128)(2,1)S(1)} collective-permute-done((bf16[528,128]{1,0:T(8,128)(2,1)S(1)}, bf16[528,128]{1,0:T(8,128)(2,1)S(1)}, u32[]{:S(2)}, u32[]{:S(2)}) %collective-permute-start.5) | collective-permute-done | bytes 135200 | tf_op jit(solution)/shard_map/ppermute | solution.py:296
  77.8 0.8 shard_map.108
  78.6 13.2 %all_to_all.16 = bf16[4,512,128]{2,1,0:T(8,128)(2,1)S(1)} all-to-all(bf16[4,512,128]{2,1,0:T(8,128)(2,1)S(1)} %get-tuple-element.14), channel_id=1, replica_groups={{0,64,24,88},{128,192,152,216},{256,320,280,344},{384,448,408,472},{32,..., dimensions={0} | all-to-all | bytes 1048576 | tf_op jit(solution)/shard_map/all_to_all | solution.py:309
  91.8 5.1 %collective-permute-start.6 = (bf16[2048,128]{1,0:T(8,128)(2,1)S(1)}, bf16[2048,128]{1,0:T(8,128)(2,1)S(1)}, u32[]{:S(2)}, u32[]{:S(2)}) collective-permute-start(bf16[2048,128]{1,0:T(8,128)(2,1)S(1)} %bitcast.7), channel_id=1, source_target_pairs={{0,40},{8,32},{16,56},{24,48},{32,8},{40,0},{48,24},{56,16},{64,10... | collective-permute-start | bytes 1572872 | tf_op jit(solution)/shard_map/ppermute | solution.py:311
  96.9 2.8 %collective-permute-start.7 = (bf16[2048,128]{1,0:T(8,128)(2,1)S(1)}, bf16[2048,128]{1,0:T(8,128)(2,1)S(1)}, u32[]{:S(2)}, u32[]{:S(2)}) collective-permute-start(bf16[2048,128]{1,0:T(8,128)(2,1)S(1)} %bitcast.8), channel_id=1, source_target_pairs={{0,32},{8,40},{16,48},{24,56},{32,0},{40,8},{48,16},{56,24},{64,96... | collective-permute-start | bytes 1572872 | tf_op jit(solution)/shard_map/ppermute | solution.py:312
  99.7 2.9 %collective-permute-start.8 = (bf16[2048,128]{1,0:T(8,128)(2,1)S(1)}, bf16[2048,128]{1,0:T(8,128)(2,1)S(1)}, u32[]{:S(2)}, u32[]{:S(2)}) collective-permute-start(bf16[2048,128]{1,0:T(8,128)(2,1)S(1)} %bitcast.9), channel_id=1, source_target_pairs={{0,8},{8,0},{16,24},{24,16},{32,40},{40,32},{48,56},{56,48},{64,72... | collective-permute-start | bytes 1572872 | tf_op jit(solution)/shard_map/ppermute | solution.py:313
  102.6 1.2 shard_map.109.refs_5_
  103.8 1.3 collective-permute-done.6.refs_2_
  105.0 4.9 %collective-permute-done.7.refs_3_ = bf16[2048,128]{1,0:T(8,128)(2,1)S(1)} collective-permute-done((bf16[2048,128]{1,0:T(8,128)(2,1)S(1)}, bf16[2048,128]{1,0:T(8,128)(2,1)S(1)}, u32[]{:S(2)}, u32[]{:S(2)}) %collective-permute-start.7) | collective-permute-done | bytes 524320 | tf_op jit(solution)/shard_map/ppermute | solution.py:312
  109.9 0.9 collective-permute-done.8.refs_4_
  110.8 1.0 shard_map.111
  111.8 4.4 %collective-permute-start.9 = (bf16[512,128]{1,0:T(8,128)(2,1)S(1)}, bf16[512,128]{1,0:T(8,128)(2,1)S(1)}, u32[]{:S(2)}, u32[]{:S(2)}) collective-permute-start(bf16[512,128]{1,0:T(8,128)(2,1)S(1)} %shard_map.111), channel_id=1, source_target_pairs={{0,4},{4,0},{8,12},{12,8},{16,20},{20,16},{24,28},{28,24},{32,36},... | collective-permute-start | bytes 393224 | tf_op jit(solution)/shard_map/ppermute | solution.py:335
  116.2 0.9 shard_map.110
  117.1 0.1 collective-permute-done.9
  117.2 0.1 broadcast_in_dim.4
  117.3 0.0 copy-start
  117.3 0.0 copy-start.1
  117.3 0.0 copy-start.2
  117.3 15.6 %all_to_all.17.types = bf16[4,512,128]{2,1,0:T(8,128)(2,1)S(1)} all-to-all(bf16[4,512,128]{2,1,0:T(8,128)(2,1)S(1)} %broadcast_in_dim.4), channel_id=1, replica_groups=mesh['acct'=128,'attr'=4] {'attr'}, dimensions={0} | all-to-all | bytes 1048576 | tf_op jit(solution)/shard_map/all_to_all | solution.py:338
  132.9 0.0 copy-done
  132.9 0.0 copy-done.1
  132.9 0.0 copy-done.2
  132.9 0.9 shard_map.112
  (4 shorter events, 0.1 us)
Async XLA Ops:
  2.5 10.5 %collective-permute-start = (bf16[2576,128]{1,0:T(8,128)(2,1)S(1)}, bf16[2576,128]{1,0:T(8,128)(2,1)S(1)}, u32[]{:S(2)}, u32[]{:S(2)}) collective-permute-start(bf16[2576,128]{1,0:T(8,128)(2,1)S(1)} %shard_map.104.sent0.refs_2_.refs_1_), channel_id=1, source_target_pairs={{0,4},{4,0},{8,12},{12,8},{16,20},{20,16},{24,28},{28,24},{32,36},... | collective-permute-start | bytes 1978376 | tf_op jit(solution)/shard_map/ppermute | solution.py:264
  14.8 15.5 %collective-permute-start.1 = (bf16[16,128,128]{2,1,0:T(8,128)(2,1)S(1)}, bf16[16,128,128]{2,1,0:T(8,128)(2,1)S(1)}, u32[]{:S(2)}, u32[]{:S(2)}) collective-permute-start(bf16[16,128,128]{2,1,0:T(8,128)(2,1)S(1)} %get-tuple-element.9), channel_id=1, source_target_pairs={{0,40},{8,32},{16,56},{24,48},{32,8},{40,0},{48,24},{56,16},{64,10... | collective-permute-start | bytes 1572872 | tf_op jit(solution)/shard_map/ppermute | solution.py:280
  23.6 12.2 %collective-permute-start.2 = (bf16[16,128,128]{2,1,0:T(8,128)(2,1)S(1)}, bf16[16,128,128]{2,1,0:T(8,128)(2,1)S(1)}, u32[]{:S(2)}, u32[]{:S(2)}) collective-permute-start(bf16[16,128,128]{2,1,0:T(8,128)(2,1)S(1)} %get-tuple-element.10), channel_id=1, source_target_pairs={{0,8},{8,0},{16,24},{24,16},{32,40},{40,32},{48,56},{56,48},{64,72... | collective-permute-start | bytes 1572872 | tf_op jit(solution)/shard_map/ppermute | solution.py:282
  26.1 11.1 %collective-permute-start.3 = (bf16[16,128,128]{2,1,0:T(8,128)(2,1)S(1)}, bf16[16,128,128]{2,1,0:T(8,128)(2,1)S(1)}, u32[]{:S(2)}, u32[]{:S(2)}) collective-permute-start(bf16[16,128,128]{2,1,0:T(8,128)(2,1)S(1)} %get-tuple-element.11), channel_id=1, source_target_pairs={{0,32},{8,40},{16,48},{24,56},{32,0},{40,8},{48,16},{56,24},{64,96... | collective-permute-start | bytes 1572872 | tf_op jit(solution)/shard_map/ppermute | solution.py:281
  37.5 10.6 %copy-start.3 = (s32[1,128]{1,0:T(1,128)S(1)}, s32[1,128]{1,0:T(1,128)}, u32[]{:S(2)}) copy-start(s32[1,128]{1,0:T(1,128)} %degree.1) | copy-start | bytes 1540
  48.1 11.5 %collective-permute-start.4 = (bf16[528,128]{1,0:T(8,128)(2,1)S(1)}, bf16[528,128]{1,0:T(8,128)(2,1)S(1)}, u32[]{:S(2)}, u32[]{:S(2)}) collective-permute-start(bf16[528,128]{1,0:T(8,128)(2,1)S(1)} %get-tuple-element.13), channel_id=1, source_target_pairs={{0,128},{8,136},{16,144},{24,152},{32,160},{40,168},{48,176},{56,1... | collective-permute-start | bytes 405512 | tf_op jit(solution)/shard_map/ppermute | solution.py:295
  59.7 18.1 %collective-permute-start.5 = (bf16[528,128]{1,0:T(8,128)(2,1)S(1)}, bf16[528,128]{1,0:T(8,128)(2,1)S(1)}, u32[]{:S(2)}, u32[]{:S(2)}) collective-permute-start(bf16[528,128]{1,0:T(8,128)(2,1)S(1)} %get-tuple-element.16), channel_id=1, source_target_pairs={{0,384},{8,392},{16,400},{24,408},{32,416},{40,424},{48,432},{56,4... | collective-permute-start | bytes 405512 | tf_op jit(solution)/shard_map/ppermute | solution.py:296
  91.8 13.2 %collective-permute-start.6 = (bf16[2048,128]{1,0:T(8,128)(2,1)S(1)}, bf16[2048,128]{1,0:T(8,128)(2,1)S(1)}, u32[]{:S(2)}, u32[]{:S(2)}) collective-permute-start(bf16[2048,128]{1,0:T(8,128)(2,1)S(1)} %bitcast.7), channel_id=1, source_target_pairs={{0,40},{8,32},{16,56},{24,48},{32,8},{40,0},{48,24},{56,16},{64,10... | collective-permute-start | bytes 1572872 | tf_op jit(solution)/shard_map/ppermute | solution.py:311
  96.9 13.0 %collective-permute-start.7 = (bf16[2048,128]{1,0:T(8,128)(2,1)S(1)}, bf16[2048,128]{1,0:T(8,128)(2,1)S(1)}, u32[]{:S(2)}, u32[]{:S(2)}) collective-permute-start(bf16[2048,128]{1,0:T(8,128)(2,1)S(1)} %bitcast.8), channel_id=1, source_target_pairs={{0,32},{8,40},{16,48},{24,56},{32,0},{40,8},{48,16},{56,24},{64,96... | collective-permute-start | bytes 1572872 | tf_op jit(solution)/shard_map/ppermute | solution.py:312
  99.7 11.1 %collective-permute-start.8 = (bf16[2048,128]{1,0:T(8,128)(2,1)S(1)}, bf16[2048,128]{1,0:T(8,128)(2,1)S(1)}, u32[]{:S(2)}, u32[]{:S(2)}) collective-permute-start(bf16[2048,128]{1,0:T(8,128)(2,1)S(1)} %bitcast.9), channel_id=1, source_target_pairs={{0,8},{8,0},{16,24},{24,16},{32,40},{40,32},{48,56},{56,48},{64,72... | collective-permute-start | bytes 1572872 | tf_op jit(solution)/shard_map/ppermute | solution.py:313
  111.8 5.4 %collective-permute-start.9 = (bf16[512,128]{1,0:T(8,128)(2,1)S(1)}, bf16[512,128]{1,0:T(8,128)(2,1)S(1)}, u32[]{:S(2)}, u32[]{:S(2)}) collective-permute-start(bf16[512,128]{1,0:T(8,128)(2,1)S(1)} %shard_map.111), channel_id=1, source_target_pairs={{0,4},{4,0},{8,12},{12,8},{16,20},{20,16},{24,28},{28,24},{32,36},... | collective-permute-start | bytes 393224 | tf_op jit(solution)/shard_map/ppermute | solution.py:335
  117.3 15.6 %copy-start = (bf16[512,128]{1,0:T(8,128)(2,1)S(1)}, bf16[512,128]{1,0:T(8,128)(2,1)}, u32[]{:S(2)}) copy-start(bf16[512,128]{1,0:T(8,128)(2,1)} %scores.1) | copy-start | bytes 393220
  117.3 15.6 %copy-start.1 = (s32[512]{0:T(512)S(1)}, s32[512]{0:T(512)}, u32[]{:S(2)}) copy-start(s32[512]{0:T(512)} %param.11) | copy-start | bytes 6148
  117.3 15.6 %copy-start.2 = (s32[512]{0:T(512)S(1)}, s32[512]{0:T(512)}, u32[]{:S(2)}) copy-start(s32[512]{0:T(512)} %param.10) | copy-start | bytes 6148

commit v11 on v10

--- a/solution.py
+++ b/solution.py
@@ -276,10 +276,12 @@
             3 * MEBI,
         )(*slots)
 
-    o3, o1, o2 = forward((3, 1, 2), bf16)
+    (o3,) = forward((3,), bf16)
     r3 = lax.ppermute(o3, "acct", DIAGONAL)
+    (o2,) = forward((2,), bf16)
+    r2 = lax.ppermute(o2, "acct", ACROSS)
+    (o1,) = forward((1,), bf16)
     r1 = lax.ppermute(o1, "acct", BESIDE)
-    r2 = lax.ppermute(o2, "acct", ACROSS)
     (o0,) = forward((0,), f32)
     line = o0 + r3.astype(f32) + r2.astype(f32) + r1.astype(f32)
     line = line.astype(bf16).reshape(4, 4, SIDE, SIDE)

time: 134 us -> 134 us (level)
  waiting for transfers between devices: 28.9 us -> 41.4 us
  starting transfers between devices: 54.2 us -> 41.8 us
  blocking collectives: 39.3 us -> 37.6 us
  Pallas kernels: 9.43 us -> 11.1 us
    ppermute x1, starting transfers between devices: 11.8 us -> 1.92 us  [per_device(): rest = lax.ppermute(half.astype(bf16), 'acct', SECOND)]
    ppermute x1, waiting for transfers between devices: 6.27 us -> 13.5 us  [per_device(): half = near + lax.ppermute(sent, 'acct', FIRST).astype(f32)]
    ppermute x1, waiting for transfers between devices: 1.27 us -> 5.35 us  [per_device(): g3 = lax.ppermute(g0, 'acct', DIAGONAL)]
    ppermute x1, waiting for transfers between devices: 6.36 us -> 10 us  [per_device(): rest = lax.ppermute(half.astype(bf16), 'acct', SECOND)]
    ppermute x1, starting transfers between devices: 5.23 us -> 1.92 us  [per_device(): half = near + lax.ppermute(sent, 'acct', FIRST).astype(f32)]
    ppermute x1, starting transfers between devices: 2.94 us -> 5.26 us  [per_device(): g2 = lax.ppermute(g0, 'acct', ACROSS)]
    ppermute x1, waiting for transfers between devices: 1.44 us -> 3.15 us  [per_device(): r1 = lax.ppermute(o1, 'acct', BESIDE)]
    all_to_all x1, blocking collectives: 15.6 us -> 14 us  [per_device(): types = lax.all_to_all(types, 'attr', 0, 0, tiled=True)]
  transfers between devices with their start and end apart: 10 -> 10, of which waited for: 10 -> 8; matrix products, arithmetic and copies ran while one was open for 0% -> 0% of each run, Pallas kernels for 3% -> 5%
where the time goes in v11:
time: 134 us
  starting transfers between devices  41.8 us (31%)
  waiting for transfers between devices  41.4 us (31%)
  blocking collectives  37.6 us (28%)
  Pallas kernels  11.1 us (8%)
  between operations  1.51 us (1%)
    all_to_all x1, blocking collectives, per_device(): types = lax.all_to_all(types, 'attr', 0, 0, tiled=True)  14 us
    ppermute x1, waiting for transfers between devices, per_device(): half = near + lax.ppermute(sent, 'acct', FIRST).astype(f32)  13.5 us
    all_to_all x1, blocking collectives, per_device(): lax.all_to_all(spread, 'acct', 0, 0, tiled=True, axis_index_groups=QUADS)  13.1 us
    all_to_all x1, blocking collectives, per_device(): lax.all_to_all(line, 'acct', 0, 0, tiled=True, axis_index_groups=QUADS)  10.5 us
    ppermute x1, waiting for transfers between devices, per_device(): rest = lax.ppermute(half.astype(bf16), 'acct', SECOND)  10 us
    ppermute x1, starting transfers between devices, per_device(): r3 = lax.ppermute(o3, 'acct', DIAGONAL)  9.35 us
    ppermute x1, starting transfers between devices, per_device(): payload1 = lax.ppermute(payload, 'acct', SWAP)  8.79 us
    ppermute x1, waiting for transfers between devices, per_device(): g3 = lax.ppermute(g0, 'acct', DIAGONAL)  5.35 us
  transfers between devices with their start and end apart: 10, of which 8 were waited for; matrix products, arithmetic and copies ran while one was open for 0% of the time, Pallas kernels for 5%

profile of v11, /device:TPU:1, one launch (start us, length us, event | category | flops | bytes accessed | tf_op | source)
XLA Modules:
  0.0 133.8 jit_solution(13381663468588516907)
XLA Ops:
  1.3 1.2 shard_map.104.sent0.refs_2_.refs_1_
  2.5 8.8 %collective-permute-start = (bf16[2576,128]{1,0:T(8,128)(2,1)S(1)}, bf16[2576,128]{1,0:T(8,128)(2,1)S(1)}, u32[]{:S(2)}, u32[]{:S(2)}) collective-permute-start(bf16[2576,128]{1,0:T(8,128)(2,1)S(1)} %shard_map.104.sent0.refs_2_.refs_1_), channel_id=1, source_target_pairs={{0,4},{4,0},{8,12},{12,8},{16,20},{20,16},{24,28},{28,24},{32,36},... | collective-permute-start | bytes 1978376 | tf_op jit(solution)/shard_map/ppermute | solution.py:264
  11.3 1.7 %collective-permute-done.sent1.refs_3_.refs_1_ = bf16[2576,128]{1,0:T(8,128)(2,1)S(1)} collective-permute-done((bf16[2576,128]{1,0:T(8,128)(2,1)S(1)}, bf16[2576,128]{1,0:T(8,128)(2,1)S(1)}, u32[]{:S(2)}, u32[]{:S(2)}) %collective-permute-start) | collective-permute-done | bytes 659488 | tf_op jit(solution)/shard_map/ppermute | solution.py:264
  13.0 0.9 shard_map.106
  13.9 9.4 %collective-permute-start.1 = (bf16[16,128,128]{2,1,0:T(8,128)(2,1)S(1)}, bf16[16,128,128]{2,1,0:T(8,128)(2,1)S(1)}, u32[]{:S(2)}, u32[]{:S(2)}) collective-permute-start(bf16[16,128,128]{2,1,0:T(8,128)(2,1)S(1)} %shard_map.106), channel_id=1, source_target_pairs={{0,40},{8,32},{16,56},{24,48},{32,8},{40,0},{48,24},{56,16},{64,10... | collective-permute-start | bytes 1572872 | tf_op jit(solution)/shard_map/ppermute | solution.py:280
  23.3 0.9 shard_map.107
  24.2 2.1 %collective-permute-start.2 = (bf16[16,128,128]{2,1,0:T(8,128)(2,1)S(1)}, bf16[16,128,128]{2,1,0:T(8,128)(2,1)S(1)}, u32[]{:S(2)}, u32[]{:S(2)}) collective-permute-start(bf16[16,128,128]{2,1,0:T(8,128)(2,1)S(1)} %shard_map.107), channel_id=1, source_target_pairs={{0,8},{8,0},{16,24},{24,16},{32,40},{40,32},{48,56},{56,48},{64,72... | collective-permute-start | bytes 1572872 | tf_op jit(solution)/shard_map/ppermute | solution.py:282
  26.4 1.1 shard_map.108
  27.5 1.9 %collective-permute-start.3 = (bf16[16,128,128]{2,1,0:T(8,128)(2,1)S(1)}, bf16[16,128,128]{2,1,0:T(8,128)(2,1)S(1)}, u32[]{:S(2)}, u32[]{:S(2)}) collective-permute-start(bf16[16,128,128]{2,1,0:T(8,128)(2,1)S(1)} %shard_map.108), channel_id=1, source_target_pairs={{0,32},{8,40},{16,48},{24,56},{32,0},{40,8},{48,16},{56,24},{64,96... | collective-permute-start | bytes 1572872 | tf_op jit(solution)/shard_map/ppermute | solution.py:284
  29.4 2.0 %shard_map.105 = f32[16,128,128]{2,1,0:T(8,128)S(1)} custom-call(s32[1,128]{1,0:T(1,128)S(1)} %slice_convert_fusion.1.tail0.refs_0_, s32[1,128]{1,0:T(1,128)S(1)} %slice_convert_fusion.tail1.refs_1_.refs_0_, bf16[2576,128]{1,0:T(8,128)(2,1)S(1)} %shard_map.104.sent0.refs_2_.refs_1_, bf16[2576,128]{1,0:T(8,128)(2,1)S(1)} %collective-permute-done.sent1.refs_3_.refs_1_), custom_call_target="tpu_custom_call" | custom-call | flops 41943040 | bytes 3145728 | tf_op jit(solution)/shard_map/pallas_call | solution.py:270
  31.4 0.0 collective-permute-done.1
  31.4 4.1 %collective-permute-done.2 = bf16[16,128,128]{2,1,0:T(8,128)(2,1)S(1)} collective-permute-done((bf16[16,128,128]{2,1,0:T(8,128)(2,1)S(1)}, bf16[16,128,128]{2,1,0:T(8,128)(2,1)S(1)}, u32[]{:S(2)}, u32[]{:S(2)}) %collective-permute-start.2) | collective-permute-done | bytes 524320 | tf_op jit(solution)/shard_map/ppermute | solution.py:282
  35.5 3.2 %collective-permute-done.3 = bf16[16,128,128]{2,1,0:T(8,128)(2,1)S(1)} collective-permute-done((bf16[16,128,128]{2,1,0:T(8,128)(2,1)S(1)}, bf16[16,128,128]{2,1,0:T(8,128)(2,1)S(1)}, u32[]{:S(2)}, u32[]{:S(2)}) %collective-permute-start.3) | collective-permute-done | bytes 524320 | tf_op jit(solution)/shard_map/ppermute | solution.py:284
  38.6 0.3 add_convert_fusion
  38.9 0.0 copy-start.3
  38.9 10.5 %all_to_all.15.parts = bf16[4,4,128,128]{3,2,1,0:T(8,128)(2,1)S(1)} all-to-all(bf16[4,4,128,128]{3,2,1,0:T(8,128)(2,1)S(1)} %bitcast.14), channel_id=1, replica_groups={{0,64,24,88},{128,192,152,216},{256,320,280,344},{384,448,408,472},{32,..., dimensions={0} | all-to-all | bytes 1048576 | tf_op jit(solution)/shard_map/all_to_all | solution.py:288
  49.4 0.0 copy-done.3
  49.4 0.1 shard_map.109
  49.5 1.9 %collective-permute-start.4 = (bf16[528,128]{1,0:T(8,128)(2,1)S(1)}, bf16[528,128]{1,0:T(8,128)(2,1)S(1)}, u32[]{:S(2)}, u32[]{:S(2)}) collective-permute-start(bf16[528,128]{1,0:T(8,128)(2,1)S(1)} %get-tuple-element.7), channel_id=1, source_target_pairs={{0,128},{8,136},{16,144},{24,152},{32,160},{40,168},{48,176},{56,1... | collective-permute-start | bytes 405512 | tf_op jit(solution)/shard_map/ppermute | solution.py:297
  51.4 13.5 %collective-permute-done.4 = bf16[528,128]{1,0:T(8,128)(2,1)S(1)} collective-permute-done((bf16[528,128]{1,0:T(8,128)(2,1)S(1)}, bf16[528,128]{1,0:T(8,128)(2,1)S(1)}, u32[]{:S(2)}, u32[]{:S(2)}) %collective-permute-start.4) | collective-permute-done | bytes 135200 | tf_op jit(solution)/shard_map/ppermute | solution.py:297
  65.0 1.9 %collective-permute-start.5 = (bf16[528,128]{1,0:T(8,128)(2,1)S(1)}, bf16[528,128]{1,0:T(8,128)(2,1)S(1)}, u32[]{:S(2)}, u32[]{:S(2)}) collective-permute-start(bf16[528,128]{1,0:T(8,128)(2,1)S(1)} %get-tuple-element.10), channel_id=1, source_target_pairs={{0,384},{8,392},{16,400},{24,408},{32,416},{40,424},{48,432},{56,4... | collective-permute-start | bytes 405512 | tf_op jit(solution)/shard_map/ppermute | solution.py:298
  66.9 10.0 %collective-permute-done.5.other = bf16[528,128]{1,0:T(8,128)(2,1)S(1)} collective-permute-done((bf16[528,128]{1,0:T(8,128)(2,1)S(1)}, bf16[528,128]{1,0:T(8,128)(2,1)S(1)}, u32[]{:S(2)}, u32[]{:S(2)}) %collective-permute-start.5) | collective-permute-done | bytes 135200 | tf_op jit(solution)/shard_map/ppermute | solution.py:298
  76.9 0.8 shard_map.110
  77.7 13.1 %all_to_all.16 = bf16[4,512,128]{2,1,0:T(8,128)(2,1)S(1)} all-to-all(bf16[4,512,128]{2,1,0:T(8,128)(2,1)S(1)} %get-tuple-element.8), channel_id=1, replica_groups={{0,64,24,88},{128,192,152,216},{256,320,280,344},{384,448,408,472},{32,..., dimensions={0} | all-to-all | bytes 1048576 | tf_op jit(solution)/shard_map/all_to_all | solution.py:311
  90.8 5.3 %collective-permute-start.8 = (bf16[2048,128]{1,0:T(8,128)(2,1)S(1)}, bf16[2048,128]{1,0:T(8,128)(2,1)S(1)}, u32[]{:S(2)}, u32[]{:S(2)}) collective-permute-start(bf16[2048,128]{1,0:T(8,128)(2,1)S(1)} %bitcast.7), channel_id=1, source_target_pairs={{0,8},{8,0},{16,24},{24,16},{32,40},{40,32},{48,56},{56,48},{64,72... | collective-permute-start | bytes 1572872 | tf_op jit(solution)/shard_map/ppermute | solution.py:315
  96.1 1.9 %collective-permute-start.7 = (bf16[2048,128]{1,0:T(8,128)(2,1)S(1)}, bf16[2048,128]{1,0:T(8,128)(2,1)S(1)}, u32[]{:S(2)}, u32[]{:S(2)}) collective-permute-start(bf16[2048,128]{1,0:T(8,128)(2,1)S(1)} %bitcast.8), channel_id=1, source_target_pairs={{0,32},{8,40},{16,48},{24,56},{32,0},{40,8},{48,16},{56,24},{64,96... | collective-permute-start | bytes 1572872 | tf_op jit(solution)/shard_map/ppermute | solution.py:314
  98.0 4.3 %collective-permute-start.6 = (bf16[2048,128]{1,0:T(8,128)(2,1)S(1)}, bf16[2048,128]{1,0:T(8,128)(2,1)S(1)}, u32[]{:S(2)}, u32[]{:S(2)}) collective-permute-start(bf16[2048,128]{1,0:T(8,128)(2,1)S(1)} %bitcast.9), channel_id=1, source_target_pairs={{0,40},{8,32},{16,56},{24,48},{32,8},{40,0},{48,24},{56,16},{64,10... | collective-permute-start | bytes 1572872 | tf_op jit(solution)/shard_map/ppermute | solution.py:313
  102.3 1.4 %shard_map.111.refs_5_ = f32[1024,128]{1,0:T(8,128)S(1)} custom-call(s32[1,128]{1,0:T(1,128)S(1)} %slice_convert_fusion.1.tail0.refs_0_, s32[1,128]{1,0:T(1,128)S(1)} %slice_convert_fusion.tail1.refs_1_.refs_0_, bf16[2576,128]{1,0:T(8,128)(2,1)S(1)} %shard_map.104.sent0.refs_2_.refs_1_, bf16[2576,128]{1,0:T(8,128)(2,1)S(1)} %collective-permute-done.sent1.refs_3_.refs_1_, ...), custom_call_target="tpu_custom_call" | custom-call | flops 41943040 | bytes 4194304 | tf_op jit(solution)/shard_map/pallas_call | solution.py:317
  103.7 0.0 collective-permute-done.8.refs_4_
  103.7 3.5 %collective-permute-done.7.refs_3_ = bf16[2048,128]{1,0:T(8,128)(2,1)S(1)} collective-permute-done((bf16[2048,128]{1,0:T(8,128)(2,1)S(1)}, bf16[2048,128]{1,0:T(8,128)(2,1)S(1)}, u32[]{:S(2)}, u32[]{:S(2)}) %collective-permute-start.7) | collective-permute-done | bytes 524320 | tf_op jit(solution)/shard_map/ppermute | solution.py:314
  107.2 5.3 %collective-permute-done.6.refs_2_ = bf16[2048,128]{1,0:T(8,128)(2,1)S(1)} collective-permute-done((bf16[2048,128]{1,0:T(8,128)(2,1)S(1)}, bf16[2048,128]{1,0:T(8,128)(2,1)S(1)}, u32[]{:S(2)}, u32[]{:S(2)}) %collective-permute-start.6) | collective-permute-done | bytes 524320 | tf_op jit(solution)/shard_map/ppermute | solution.py:313
  112.6 0.9 shard_map.113
  113.5 4.2 %collective-permute-start.9 = (bf16[512,128]{1,0:T(8,128)(2,1)S(1)}, bf16[512,128]{1,0:T(8,128)(2,1)S(1)}, u32[]{:S(2)}, u32[]{:S(2)}) collective-permute-start(bf16[512,128]{1,0:T(8,128)(2,1)S(1)} %shard_map.113), channel_id=1, source_target_pairs={{0,4},{4,0},{8,12},{12,8},{16,20},{20,16},{24,28},{28,24},{32,36},... | collective-permute-start | bytes 393224 | tf_op jit(solution)/shard_map/ppermute | solution.py:337
  117.7 0.9 shard_map.112
  118.6 0.1 collective-permute-done.9
  118.7 0.1 broadcast_in_dim.4
  118.8 0.0 copy-start
  118.8 0.0 copy-start.1
  118.8 0.0 copy-start.2
  118.9 14.0 %all_to_all.17.types = bf16[4,512,128]{2,1,0:T(8,128)(2,1)S(1)} all-to-all(bf16[4,512,128]{2,1,0:T(8,128)(2,1)S(1)} %broadcast_in_dim.4), channel_id=1, replica_groups=mesh['acct'=128,'attr'=4] {'attr'}, dimensions={0} | all-to-all | bytes 1048576 | tf_op jit(solution)/shard_map/all_to_all | solution.py:340
  132.9 0.0 copy-done
  132.9 0.0 copy-done.1
  132.9 0.0 copy-done.2
  132.9 0.9 shard_map.114
  (4 shorter events, 0.1 us)
Async XLA Ops:
  2.5 10.5 %collective-permute-start = (bf16[2576,128]{1,0:T(8,128)(2,1)S(1)}, bf16[2576,128]{1,0:T(8,128)(2,1)S(1)}, u32[]{:S(2)}, u32[]{:S(2)}) collective-permute-start(bf16[2576,128]{1,0:T(8,128)(2,1)S(1)} %shard_map.104.sent0.refs_2_.refs_1_), channel_id=1, source_target_pairs={{0,4},{4,0},{8,12},{12,8},{16,20},{20,16},{24,28},{28,24},{32,36},... | collective-permute-start | bytes 1978376 | tf_op jit(solution)/shard_map/ppermute | solution.py:264
  13.9 17.5 %collective-permute-start.1 = (bf16[16,128,128]{2,1,0:T(8,128)(2,1)S(1)}, bf16[16,128,128]{2,1,0:T(8,128)(2,1)S(1)}, u32[]{:S(2)}, u32[]{:S(2)}) collective-permute-start(bf16[16,128,128]{2,1,0:T(8,128)(2,1)S(1)} %shard_map.106), channel_id=1, source_target_pairs={{0,40},{8,32},{16,56},{24,48},{32,8},{40,0},{48,24},{56,16},{64,10... | collective-permute-start | bytes 1572872 | tf_op jit(solution)/shard_map/ppermute | solution.py:280
  24.2 11.2 %collective-permute-start.2 = (bf16[16,128,128]{2,1,0:T(8,128)(2,1)S(1)}, bf16[16,128,128]{2,1,0:T(8,128)(2,1)S(1)}, u32[]{:S(2)}, u32[]{:S(2)}) collective-permute-start(bf16[16,128,128]{2,1,0:T(8,128)(2,1)S(1)} %shard_map.107), channel_id=1, source_target_pairs={{0,8},{8,0},{16,24},{24,16},{32,40},{40,32},{48,56},{56,48},{64,72... | collective-permute-start | bytes 1572872 | tf_op jit(solution)/shard_map/ppermute | solution.py:282
  27.5 11.1 %collective-permute-start.3 = (bf16[16,128,128]{2,1,0:T(8,128)(2,1)S(1)}, bf16[16,128,128]{2,1,0:T(8,128)(2,1)S(1)}, u32[]{:S(2)}, u32[]{:S(2)}) collective-permute-start(bf16[16,128,128]{2,1,0:T(8,128)(2,1)S(1)} %shard_map.108), channel_id=1, source_target_pairs={{0,32},{8,40},{16,48},{24,56},{32,0},{40,8},{48,16},{56,24},{64,96... | collective-permute-start | bytes 1572872 | tf_op jit(solution)/shard_map/ppermute | solution.py:284
  38.9 10.5 %copy-start.3 = (s32[1,128]{1,0:T(1,128)S(1)}, s32[1,128]{1,0:T(1,128)}, u32[]{:S(2)}) copy-start(s32[1,128]{1,0:T(1,128)} %degree.1) | copy-start | bytes 1540
  49.5 15.4 %collective-permute-start.4 = (bf16[528,128]{1,0:T(8,128)(2,1)S(1)}, bf16[528,128]{1,0:T(8,128)(2,1)S(1)}, u32[]{:S(2)}, u32[]{:S(2)}) collective-permute-start(bf16[528,128]{1,0:T(8,128)(2,1)S(1)} %get-tuple-element.7), channel_id=1, source_target_pairs={{0,128},{8,136},{16,144},{24,152},{32,160},{40,168},{48,176},{56,1... | collective-permute-start | bytes 405512 | tf_op jit(solution)/shard_map/ppermute | solution.py:297
  65.0 12.0 %collective-permute-start.5 = (bf16[528,128]{1,0:T(8,128)(2,1)S(1)}, bf16[528,128]{1,0:T(8,128)(2,1)S(1)}, u32[]{:S(2)}, u32[]{:S(2)}) collective-permute-start(bf16[528,128]{1,0:T(8,128)(2,1)S(1)} %get-tuple-element.10), channel_id=1, source_target_pairs={{0,384},{8,392},{16,400},{24,408},{32,416},{40,424},{48,432},{56,4... | collective-permute-start | bytes 405512 | tf_op jit(solution)/shard_map/ppermute | solution.py:298
  90.8 12.9 %collective-permute-start.8 = (bf16[2048,128]{1,0:T(8,128)(2,1)S(1)}, bf16[2048,128]{1,0:T(8,128)(2,1)S(1)}, u32[]{:S(2)}, u32[]{:S(2)}) collective-permute-start(bf16[2048,128]{1,0:T(8,128)(2,1)S(1)} %bitcast.7), channel_id=1, source_target_pairs={{0,8},{8,0},{16,24},{24,16},{32,40},{40,32},{48,56},{56,48},{64,72... | collective-permute-start | bytes 1572872 | tf_op jit(solution)/shard_map/ppermute | solution.py:315
  96.1 11.1 %collective-permute-start.7 = (bf16[2048,128]{1,0:T(8,128)(2,1)S(1)}, bf16[2048,128]{1,0:T(8,128)(2,1)S(1)}, u32[]{:S(2)}, u32[]{:S(2)}) collective-permute-start(bf16[2048,128]{1,0:T(8,128)(2,1)S(1)} %bitcast.8), channel_id=1, source_target_pairs={{0,32},{8,40},{16,48},{24,56},{32,0},{40,8},{48,16},{56,24},{64,96... | collective-permute-start | bytes 1572872 | tf_op jit(solution)/shard_map/ppermute | solution.py:314
  98.0 14.6 %collective-permute-start.6 = (bf16[2048,128]{1,0:T(8,128)(2,1)S(1)}, bf16[2048,128]{1,0:T(8,128)(2,1)S(1)}, u32[]{:S(2)}, u32[]{:S(2)}) collective-permute-start(bf16[2048,128]{1,0:T(8,128)(2,1)S(1)} %bitcast.9), channel_id=1, source_target_pairs={{0,40},{8,32},{16,56},{24,48},{32,8},{40,0},{48,24},{56,16},{64,10... | collective-permute-start | bytes 1572872 | tf_op jit(solution)/shard_map/ppermute | solution.py:313
  113.5 5.2 %collective-permute-start.9 = (bf16[512,128]{1,0:T(8,128)(2,1)S(1)}, bf16[512,128]{1,0:T(8,128)(2,1)S(1)}, u32[]{:S(2)}, u32[]{:S(2)}) collective-permute-start(bf16[512,128]{1,0:T(8,128)(2,1)S(1)} %shard_map.113), channel_id=1, source_target_pairs={{0,4},{4,0},{8,12},{12,8},{16,20},{20,16},{24,28},{28,24},{32,36},... | collective-permute-start | bytes 393224 | tf_op jit(solution)/shard_map/ppermute | solution.py:337
  118.8 14.1 %copy-start = (bf16[512,128]{1,0:T(8,128)(2,1)S(1)}, bf16[512,128]{1,0:T(8,128)(2,1)}, u32[]{:S(2)}) copy-start(bf16[512,128]{1,0:T(8,128)(2,1)} %scores.1) | copy-start | bytes 393220
  118.8 14.1 %copy-start.1 = (s32[512]{0:T(512)S(1)}, s32[512]{0:T(512)}, u32[]{:S(2)}) copy-start(s32[512]{0:T(512)} %param.11) | copy-start | bytes 6148
  118.8 14.0 %copy-start.2 = (s32[512]{0:T(512)S(1)}, s32[512]{0:T(512)}, u32[]{:S(2)}) copy-start(s32[512]{0:T(512)} %param.10) | copy-start | bytes 6148

commit v12 on v10

--- a/solution.py
+++ b/solution.py
@@ -128,24 +128,22 @@
         out[...] = acc[n * LINE : (n + 1) * LINE].astype(out.dtype)
 
 
-def near_kernel(me, parts, degree, sums, sent):
+def near_kernel(me, parts, degree, sums):
     for n in range(4):
         total = parts[0, n].astype(jnp.float32)
         for k in range(1, 4):
             total += parts[k, n].astype(jnp.float32)
-        sums[n * SIDE : (n + 1) * SIDE, :] = total
-        sent[n * SIDE : (n + 1) * SIDE, :] = total.astype(sent.dtype)
+        sums[n * SIDE : (n + 1) * SIDE, :] = total.astype(sums.dtype)
     row = lax.broadcasted_iota(jnp.int32, (SLOTS, SIDE), 0)
     mine = jnp.where(row == where(me[0])[1] >> 2, degree[...].astype(jnp.float32), 0.0)
-    sums[FOUR:, :] = mine
-    sent[FOUR:, :] = mine.astype(sent.dtype)
+    sums[FOUR:, :] = mine.astype(sums.dtype)
 
 
 def far_kernel(me, mine, other, own, spread):
-    degree = mine[FOUR:, :] + other[FOUR:, :].astype(jnp.float32)
+    degree = mine[FOUR:, :].astype(jnp.float32) + other[FOUR:, :].astype(jnp.float32)
     for n in range(4):
         rows = pl.ds(n * SIDE, SIDE)
-        total = mine[rows, :] + other[rows, :].astype(jnp.float32)
+        total = mine[rows, :].astype(jnp.float32) + other[rows, :].astype(jnp.float32)
         scores = (total * column(lax.rsqrt(degree[n : n + 1, :]))).astype(spread.dtype)
         for k in range(4):
             spread[k, rows, :] = scores
@@ -230,6 +228,7 @@
     tile_count,
 ):
     bf16, f32, i32 = jnp.bfloat16, jnp.float32, jnp.int32
+    group = jax.ShapeDtypeStruct((LINE, SIDE, SIDE), bf16)
     degree = acct_degree.reshape(4, SIDE)
     me = lax.axis_index("acct").astype(i32).reshape(1)
     (payload,) = call(
@@ -266,34 +265,31 @@
     tails = [sent[TILES + ROWS :][:1].astype(i32) for sent in (payload, payload1)]
     slots = (*tails, payload, payload1)
 
-    def forward(chips, dtype):
+    def forward(chips):
         return call(
             functools.partial(forward_kernel, chips),
-            [jax.ShapeDtypeStruct((LINE, SIDE, SIDE), dtype)] * len(chips),
+            [group] * len(chips),
             smem(2) + vmem(2),
             [pltpu.VMEM((len(chips) * LINE, SIDE, SIDE), f32)],
             flops,
             3 * MEBI,
         )(*slots)
 
-    o3, o1, o2 = forward((3, 1, 2), bf16)
+    o3, o1, o2 = forward((3, 1, 2))
     r3 = lax.ppermute(o3, "acct", DIAGONAL)
     r1 = lax.ppermute(o1, "acct", BESIDE)
     r2 = lax.ppermute(o2, "acct", ACROSS)
-    (o0,) = forward((0,), f32)
-    line = o0 + r3.astype(f32) + r2.astype(f32) + r1.astype(f32)
+    (o0,) = forward((0,))
+    line = o0.astype(f32) + r1.astype(f32) + r2.astype(f32) + r3.astype(f32)
     line = line.astype(bf16).reshape(4, 4, SIDE, SIDE)
     line = lax.all_to_all(line, "acct", 0, 0, tiled=True, axis_index_groups=QUADS)
-    near, sent = call(
-        near_kernel,
-        [jax.ShapeDtypeStruct((FOUR + SLOTS, SIDE), dtype) for dtype in (f32, bf16)],
-        smem(1) + vmem(2),
-        [],
-        SIDE * SIDE * LINE,
-        MEBI,
+    sums = jax.ShapeDtypeStruct((FOUR + SLOTS, SIDE), bf16)
+    (near,) = call(
+        near_kernel, [sums], smem(1) + vmem(2), [], SIDE * SIDE * LINE, MEBI
     )(me, line, attr_degree)
-    half = near + lax.ppermute(sent, "acct", FIRST).astype(f32)
-    rest = lax.ppermute(half.astype(bf16), "acct", SECOND)
+    half = near.astype(f32) + lax.ppermute(near, "acct", FIRST).astype(f32)
+    half = half.astype(bf16)
+    rest = lax.ppermute(half, "acct", SECOND)
     own_scores, spread = call(
         far_kernel,
         [

time: 134 us -> 133 us (level)
  blocking collectives: 39.3 us -> 36.8 us
  waiting for transfers between devices: 28.9 us -> 30.7 us
    ppermute x1, starting transfers between devices: 5.06 us -> 1.91 us  [per_device(): g3 = lax.ppermute(g0, 'acct', DIAGONAL)]
    ppermute x1, starting transfers between devices: 2.78 us -> 5.62 us  [per_device(): g1 = lax.ppermute(g0, 'acct', BESIDE)]
    all_to_all x1, blocking collectives: 15.6 us -> 14.1 us  [per_device(): types = lax.all_to_all(types, 'attr', 0, 0, tiled=True)]
    ppermute x1, starting transfers between devices: 8.82 us -> 7.42 us  [per_device(): r3 = lax.ppermute(o3, 'acct', DIAGONAL)]
  transfers between devices with their start and end apart: 10 -> 10, of which waited for: 10 -> 9; matrix products, arithmetic and copies ran while one was open for 0% -> 0% of each run, Pallas kernels for 3% -> 2%
where the time goes in v12:
time: 133 us
  starting transfers between devices  53.2 us (40%)
  blocking collectives  36.8 us (28%)
  waiting for transfers between devices  30.7 us (23%)
  Pallas kernels  9.94 us (7%)
  between operations  1.49 us (1%)
    all_to_all x1, blocking collectives, per_device(): types = lax.all_to_all(types, 'attr', 0, 0, tiled=True)  14.1 us
    all_to_all x1, blocking collectives, per_device(): lax.all_to_all(spread, 'acct', 0, 0, tiled=True, axis_index_groups=QUADS)  12.2 us
    all_to_all x1, blocking collectives, per_device(): lax.all_to_all(line, 'acct', 0, 0, tiled=True, axis_index_groups=QUADS)  10.5 us
    ppermute x1, starting transfers between devices, per_device(): rest = lax.ppermute(half, 'acct', SECOND)  10.4 us
    ppermute x1, starting transfers between devices, per_device(): payload1 = lax.ppermute(payload, 'acct', SWAP)  8.79 us
    ppermute x1, starting transfers between devices, per_device(): r3 = lax.ppermute(o3, 'acct', DIAGONAL)  7.42 us
    ppermute x1, waiting for transfers between devices, per_device(): half = near.astype(f32) + lax.ppermute(near, 'acct', FIRST).astype(f32)  6.96 us
    ppermute x1, waiting for transfers between devices, per_device(): rest = lax.ppermute(half, 'acct', SECOND)  6.58 us
  transfers between devices with their start and end apart: 10, of which 9 were waited for; matrix products, arithmetic and copies ran while one was open for 0% of the time, Pallas kernels for 2%

profile of v12, /device:TPU:1, one launch (start us, length us, event | category | flops | bytes accessed | tf_op | source)
XLA Modules:
  0.0 132.7 jit_solution(8702719543489884666)
XLA Ops:
  1.3 1.2 shard_map.104.sent0.refs_2_.refs_1_
  2.5 8.8 %collective-permute-start = (bf16[2576,128]{1,0:T(8,128)(2,1)S(1)}, bf16[2576,128]{1,0:T(8,128)(2,1)S(1)}, u32[]{:S(2)}, u32[]{:S(2)}) collective-permute-start(bf16[2576,128]{1,0:T(8,128)(2,1)S(1)} %shard_map.104.sent0.refs_2_.refs_1_), channel_id=1, source_target_pairs={{0,4},{4,0},{8,12},{12,8},{16,20},{20,16},{24,28},{28,24},{32,36},... | collective-permute-start | bytes 1978376 | tf_op jit(solution)/shard_map/ppermute | solution.py:263
  11.3 1.7 %collective-permute-done.sent1.refs_3_.refs_1_ = bf16[2576,128]{1,0:T(8,128)(2,1)S(1)} collective-permute-done((bf16[2576,128]{1,0:T(8,128)(2,1)S(1)}, bf16[2576,128]{1,0:T(8,128)(2,1)S(1)}, u32[]{:S(2)}, u32[]{:S(2)}) %collective-permute-start) | collective-permute-done | bytes 659488 | tf_op jit(solution)/shard_map/ppermute | solution.py:263
  13.0 2.7 %shard_map.106 = (bf16[16,128,128]{2,1,0:T(8,128)(2,1)S(1)}, bf16[16,128,128]{2,1,0:T(8,128)(2,1)S(1)}, bf16[16,128,128]{2,1,0:T(8,128)(2,1)S(1)}) custom-call(s32[1,128]{1,0:T(1,128)S(1)} %slice_convert_fusion.1.tail0.refs_0_, s32[1,128]{1,0:T(1,128)S(1)} %slice_convert_fusion.tail1.refs_1_.refs_0_, bf16[2576,128]{1,0:T(8,128)(2,1)S(1)} %shard_map.104.sent0.refs_2_.refs_1_, ...), custom_call_target="tpu_custom_call" | custom-call | flops 41943040 | bytes 3145728 | tf_op jit(solution)/shard_map/pallas_call | solution.py:269
  15.7 7.4 %collective-permute-start.3 = (bf16[16,128,128]{2,1,0:T(8,128)(2,1)S(1)}, bf16[16,128,128]{2,1,0:T(8,128)(2,1)S(1)}, u32[]{:S(2)}, u32[]{:S(2)}) collective-permute-start(bf16[16,128,128]{2,1,0:T(8,128)(2,1)S(1)} %get-tuple-element.9), channel_id=1, source_target_pairs={{0,40},{8,32},{16,56},{24,48},{32,8},{40,0},{48,24},{56,16},{64,10... | collective-permute-start | bytes 1572872 | tf_op jit(solution)/shard_map/ppermute | solution.py:279
  23.1 3.5 %collective-permute-start.2 = (bf16[16,128,128]{2,1,0:T(8,128)(2,1)S(1)}, bf16[16,128,128]{2,1,0:T(8,128)(2,1)S(1)}, u32[]{:S(2)}, u32[]{:S(2)}) collective-permute-start(bf16[16,128,128]{2,1,0:T(8,128)(2,1)S(1)} %get-tuple-element.8), channel_id=1, source_target_pairs={{0,8},{8,0},{16,24},{24,16},{32,40},{40,32},{48,56},{56,48},{64,72... | collective-permute-start | bytes 1572872 | tf_op jit(solution)/shard_map/ppermute | solution.py:281
  26.6 1.9 %collective-permute-start.1 = (bf16[16,128,128]{2,1,0:T(8,128)(2,1)S(1)}, bf16[16,128,128]{2,1,0:T(8,128)(2,1)S(1)}, u32[]{:S(2)}, u32[]{:S(2)}) collective-permute-start(bf16[16,128,128]{2,1,0:T(8,128)(2,1)S(1)} %get-tuple-element.7), channel_id=1, source_target_pairs={{0,32},{8,40},{16,48},{24,56},{32,0},{40,8},{48,16},{56,24},{64,96... | collective-permute-start | bytes 1572872 | tf_op jit(solution)/shard_map/ppermute | solution.py:280
  28.5 0.9 shard_map.105
  29.5 0.3 collective-permute-done.3
  29.7 5.5 %collective-permute-done.2 = bf16[16,128,128]{2,1,0:T(8,128)(2,1)S(1)} collective-permute-done((bf16[16,128,128]{2,1,0:T(8,128)(2,1)S(1)}, bf16[16,128,128]{2,1,0:T(8,128)(2,1)S(1)}, u32[]{:S(2)}, u32[]{:S(2)}) %collective-permute-start.2) | collective-permute-done | bytes 524320 | tf_op jit(solution)/shard_map/ppermute | solution.py:281
  35.3 2.5 %collective-permute-done.1 = bf16[16,128,128]{2,1,0:T(8,128)(2,1)S(1)} collective-permute-done((bf16[16,128,128]{2,1,0:T(8,128)(2,1)S(1)}, bf16[16,128,128]{2,1,0:T(8,128)(2,1)S(1)}, u32[]{:S(2)}, u32[]{:S(2)}) %collective-permute-start.1) | collective-permute-done | bytes 524320 | tf_op jit(solution)/shard_map/ppermute | solution.py:280
  37.7 0.3 add_convert_fusion
  38.1 0.0 copy-start.3
  38.1 10.5 %all_to_all.15.parts = bf16[4,4,128,128]{3,2,1,0:T(8,128)(2,1)S(1)} all-to-all(bf16[4,4,128,128]{3,2,1,0:T(8,128)(2,1)S(1)} %bitcast.14), channel_id=1, replica_groups={{0,64,24,88},{128,192,152,216},{256,320,280,344},{384,448,408,472},{32,..., dimensions={0} | all-to-all | bytes 1048576 | tf_op jit(solution)/shard_map/all_to_all | solution.py:285
  48.6 0.0 copy-done.3
  48.6 0.1 shard_map.107
  48.7 5.8 %collective-permute-start.4 = (bf16[528,128]{1,0:T(8,128)(2,1)S(1)}, bf16[528,128]{1,0:T(8,128)(2,1)S(1)}, u32[]{:S(2)}, u32[]{:S(2)}) collective-permute-start(bf16[528,128]{1,0:T(8,128)(2,1)S(1)} %shard_map.107), channel_id=1, source_target_pairs={{0,128},{8,136},{16,144},{24,152},{32,160},{40,168},{48,176},{56,1... | collective-permute-start | bytes 405512 | tf_op jit(solution)/shard_map/ppermute | solution.py:290
  54.5 7.0 %collective-permute-done.4 = bf16[528,128]{1,0:T(8,128)(2,1)S(1)} collective-permute-done((bf16[528,128]{1,0:T(8,128)(2,1)S(1)}, bf16[528,128]{1,0:T(8,128)(2,1)S(1)}, u32[]{:S(2)}, u32[]{:S(2)}) %collective-permute-start.4) | collective-permute-done | bytes 135200 | tf_op jit(solution)/shard_map/ppermute | solution.py:290
  61.5 10.4 %collective-permute-start.5 = (bf16[528,128]{1,0:T(8,128)(2,1)S(1)}, bf16[528,128]{1,0:T(8,128)(2,1)S(1)}, u32[]{:S(2)}, u32[]{:S(2)}) collective-permute-start(bf16[528,128]{1,0:T(8,128)(2,1)S(1)} %add_convert_fusion.1.mine), channel_id=1, source_target_pairs={{0,384},{8,392},{16,400},{24,408},{32,416},{40,424},{48,432},{56,4... | collective-permute-start | bytes 405512 | tf_op jit(solution)/shard_map/ppermute | solution.py:292
  72.0 6.6 %collective-permute-done.5.other = bf16[528,128]{1,0:T(8,128)(2,1)S(1)} collective-permute-done((bf16[528,128]{1,0:T(8,128)(2,1)S(1)}, bf16[528,128]{1,0:T(8,128)(2,1)S(1)}, u32[]{:S(2)}, u32[]{:S(2)}) %collective-permute-start.5) | collective-permute-done | bytes 135200 | tf_op jit(solution)/shard_map/ppermute | solution.py:292
  78.6 0.8 shard_map.108
  79.4 12.2 %all_to_all.16 = bf16[4,512,128]{2,1,0:T(8,128)(2,1)S(1)} all-to-all(bf16[4,512,128]{2,1,0:T(8,128)(2,1)S(1)} %get-tuple-element.10), channel_id=1, replica_groups={{0,64,24,88},{128,192,152,216},{256,320,280,344},{384,448,408,472},{32,..., dimensions={0} | all-to-all | bytes 1048576 | tf_op jit(solution)/shard_map/all_to_all | solution.py:305
  91.5 1.9 %collective-permute-start.6 = (bf16[2048,128]{1,0:T(8,128)(2,1)S(1)}, bf16[2048,128]{1,0:T(8,128)(2,1)S(1)}, u32[]{:S(2)}, u32[]{:S(2)}) collective-permute-start(bf16[2048,128]{1,0:T(8,128)(2,1)S(1)} %bitcast.7), channel_id=1, source_target_pairs={{0,40},{8,32},{16,56},{24,48},{32,8},{40,0},{48,24},{56,16},{64,10... | collective-permute-start | bytes 1572872 | tf_op jit(solution)/shard_map/ppermute | solution.py:307
  93.4 5.6 %collective-permute-start.7 = (bf16[2048,128]{1,0:T(8,128)(2,1)S(1)}, bf16[2048,128]{1,0:T(8,128)(2,1)S(1)}, u32[]{:S(2)}, u32[]{:S(2)}) collective-permute-start(bf16[2048,128]{1,0:T(8,128)(2,1)S(1)} %bitcast.8), channel_id=1, source_target_pairs={{0,32},{8,40},{16,48},{24,56},{32,0},{40,8},{48,16},{56,24},{64,96... | collective-permute-start | bytes 1572872 | tf_op jit(solution)/shard_map/ppermute | solution.py:308
  99.1 3.2 %collective-permute-start.8 = (bf16[2048,128]{1,0:T(8,128)(2,1)S(1)}, bf16[2048,128]{1,0:T(8,128)(2,1)S(1)}, u32[]{:S(2)}, u32[]{:S(2)}) collective-permute-start(bf16[2048,128]{1,0:T(8,128)(2,1)S(1)} %bitcast.9), channel_id=1, source_target_pairs={{0,8},{8,0},{16,24},{24,16},{32,40},{40,32},{48,56},{56,48},{64,72... | collective-permute-start | bytes 1572872 | tf_op jit(solution)/shard_map/ppermute | solution.py:309
  102.3 0.9 shard_map.109.refs_5_
  103.2 1.6 %collective-permute-done.6.refs_2_ = bf16[2048,128]{1,0:T(8,128)(2,1)S(1)} collective-permute-done((bf16[2048,128]{1,0:T(8,128)(2,1)S(1)}, bf16[2048,128]{1,0:T(8,128)(2,1)S(1)}, u32[]{:S(2)}, u32[]{:S(2)}) %collective-permute-start.6) | collective-permute-done | bytes 524320 | tf_op jit(solution)/shard_map/ppermute | solution.py:307
  104.8 4.5 %collective-permute-done.7.refs_3_ = bf16[2048,128]{1,0:T(8,128)(2,1)S(1)} collective-permute-done((bf16[2048,128]{1,0:T(8,128)(2,1)S(1)}, bf16[2048,128]{1,0:T(8,128)(2,1)S(1)}, u32[]{:S(2)}, u32[]{:S(2)}) %collective-permute-start.7) | collective-permute-done | bytes 524320 | tf_op jit(solution)/shard_map/ppermute | solution.py:308
  109.3 1.1 collective-permute-done.8.refs_4_
  110.4 1.5 %shard_map.111 = bf16[512,128]{1,0:T(8,128)(2,1)S(1)} custom-call(s32[1,128]{1,0:T(1,128)S(1)} %slice_convert_fusion.tail1.refs_1_.refs_0_, bf16[2576,128]{1,0:T(8,128)(2,1)S(1)} %collective-permute-done.sent1.refs_3_.refs_1_, bf16[2048,128]{1,0:T(8,128)(2,1)S(1)} %collective-permute-done.6.refs_2_, bf16[2048,128]{1,0:T(8,128)(2,1)S(1)} %collective-permute-done.7.refs_3_, ...), custom_call_target="tpu_custom_call" | custom-call | flops 41943040 | bytes 2097152 | tf_op jit(solution)/shard_map/pallas_call | solution.py:321
  111.9 4.6 %collective-permute-start.9 = (bf16[512,128]{1,0:T(8,128)(2,1)S(1)}, bf16[512,128]{1,0:T(8,128)(2,1)S(1)}, u32[]{:S(2)}, u32[]{:S(2)}) collective-permute-start(bf16[512,128]{1,0:T(8,128)(2,1)S(1)} %shard_map.111), channel_id=1, source_target_pairs={{0,4},{4,0},{8,12},{12,8},{16,20},{20,16},{24,28},{28,24},{32,36},... | collective-permute-start | bytes 393224 | tf_op jit(solution)/shard_map/ppermute | solution.py:331
  116.4 1.0 shard_map.110
  117.5 0.0 collective-permute-done.9
  117.5 0.1 broadcast_in_dim.4
  117.6 0.0 copy-start
  117.6 0.0 copy-start.1
  117.6 0.0 copy-start.2
  117.6 14.1 %all_to_all.17.types = bf16[4,512,128]{2,1,0:T(8,128)(2,1)S(1)} all-to-all(bf16[4,512,128]{2,1,0:T(8,128)(2,1)S(1)} %broadcast_in_dim.4), channel_id=1, replica_groups=mesh['acct'=128,'attr'=4] {'attr'}, dimensions={0} | all-to-all | bytes 1048576 | tf_op jit(solution)/shard_map/all_to_all | solution.py:334
  131.7 0.0 copy-done
  131.7 0.0 copy-done.1
  131.7 0.0 copy-done.2
  131.8 0.9 shard_map.112
  (4 shorter events, 0.1 us)
Async XLA Ops:
  2.5 10.5 %collective-permute-start = (bf16[2576,128]{1,0:T(8,128)(2,1)S(1)}, bf16[2576,128]{1,0:T(8,128)(2,1)S(1)}, u32[]{:S(2)}, u32[]{:S(2)}) collective-permute-start(bf16[2576,128]{1,0:T(8,128)(2,1)S(1)} %shard_map.104.sent0.refs_2_.refs_1_), channel_id=1, source_target_pairs={{0,4},{4,0},{8,12},{12,8},{16,20},{20,16},{24,28},{28,24},{32,36},... | collective-permute-start | bytes 1978376 | tf_op jit(solution)/shard_map/ppermute | solution.py:263
  15.7 14.1 %collective-permute-start.3 = (bf16[16,128,128]{2,1,0:T(8,128)(2,1)S(1)}, bf16[16,128,128]{2,1,0:T(8,128)(2,1)S(1)}, u32[]{:S(2)}, u32[]{:S(2)}) collective-permute-start(bf16[16,128,128]{2,1,0:T(8,128)(2,1)S(1)} %get-tuple-element.9), channel_id=1, source_target_pairs={{0,40},{8,32},{16,56},{24,48},{32,8},{40,0},{48,24},{56,16},{64,10... | collective-permute-start | bytes 1572872 | tf_op jit(solution)/shard_map/ppermute | solution.py:279
  23.1 12.2 %collective-permute-start.2 = (bf16[16,128,128]{2,1,0:T(8,128)(2,1)S(1)}, bf16[16,128,128]{2,1,0:T(8,128)(2,1)S(1)}, u32[]{:S(2)}, u32[]{:S(2)}) collective-permute-start(bf16[16,128,128]{2,1,0:T(8,128)(2,1)S(1)} %get-tuple-element.8), channel_id=1, source_target_pairs={{0,8},{8,0},{16,24},{24,16},{32,40},{40,32},{48,56},{56,48},{64,72... | collective-permute-start | bytes 1572872 | tf_op jit(solution)/shard_map/ppermute | solution.py:281
  26.6 11.1 %collective-permute-start.1 = (bf16[16,128,128]{2,1,0:T(8,128)(2,1)S(1)}, bf16[16,128,128]{2,1,0:T(8,128)(2,1)S(1)}, u32[]{:S(2)}, u32[]{:S(2)}) collective-permute-start(bf16[16,128,128]{2,1,0:T(8,128)(2,1)S(1)} %get-tuple-element.7), channel_id=1, source_target_pairs={{0,32},{8,40},{16,48},{24,56},{32,0},{40,8},{48,16},{56,24},{64,96... | collective-permute-start | bytes 1572872 | tf_op jit(solution)/shard_map/ppermute | solution.py:280
  38.1 10.6 %copy-start.3 = (s32[1,128]{1,0:T(1,128)S(1)}, s32[1,128]{1,0:T(1,128)}, u32[]{:S(2)}) copy-start(s32[1,128]{1,0:T(1,128)} %degree.1) | copy-start | bytes 1540
  48.7 12.8 %collective-permute-start.4 = (bf16[528,128]{1,0:T(8,128)(2,1)S(1)}, bf16[528,128]{1,0:T(8,128)(2,1)S(1)}, u32[]{:S(2)}, u32[]{:S(2)}) collective-permute-start(bf16[528,128]{1,0:T(8,128)(2,1)S(1)} %shard_map.107), channel_id=1, source_target_pairs={{0,128},{8,136},{16,144},{24,152},{32,160},{40,168},{48,176},{56,1... | collective-permute-start | bytes 405512 | tf_op jit(solution)/shard_map/ppermute | solution.py:290
  61.5 17.0 %collective-permute-start.5 = (bf16[528,128]{1,0:T(8,128)(2,1)S(1)}, bf16[528,128]{1,0:T(8,128)(2,1)S(1)}, u32[]{:S(2)}, u32[]{:S(2)}) collective-permute-start(bf16[528,128]{1,0:T(8,128)(2,1)S(1)} %add_convert_fusion.1.mine), channel_id=1, source_target_pairs={{0,384},{8,392},{16,400},{24,408},{32,416},{40,424},{48,432},{56,4... | collective-permute-start | bytes 405512 | tf_op jit(solution)/shard_map/ppermute | solution.py:292
  91.5 13.2 %collective-permute-start.6 = (bf16[2048,128]{1,0:T(8,128)(2,1)S(1)}, bf16[2048,128]{1,0:T(8,128)(2,1)S(1)}, u32[]{:S(2)}, u32[]{:S(2)}) collective-permute-start(bf16[2048,128]{1,0:T(8,128)(2,1)S(1)} %bitcast.7), channel_id=1, source_target_pairs={{0,40},{8,32},{16,56},{24,48},{32,8},{40,0},{48,24},{56,16},{64,10... | collective-permute-start | bytes 1572872 | tf_op jit(solution)/shard_map/ppermute | solution.py:307
  93.4 15.9 %collective-permute-start.7 = (bf16[2048,128]{1,0:T(8,128)(2,1)S(1)}, bf16[2048,128]{1,0:T(8,128)(2,1)S(1)}, u32[]{:S(2)}, u32[]{:S(2)}) collective-permute-start(bf16[2048,128]{1,0:T(8,128)(2,1)S(1)} %bitcast.8), channel_id=1, source_target_pairs={{0,32},{8,40},{16,48},{24,56},{32,0},{40,8},{48,16},{56,24},{64,96... | collective-permute-start | bytes 1572872 | tf_op jit(solution)/shard_map/ppermute | solution.py:308
  99.1 11.3 %collective-permute-start.8 = (bf16[2048,128]{1,0:T(8,128)(2,1)S(1)}, bf16[2048,128]{1,0:T(8,128)(2,1)S(1)}, u32[]{:S(2)}, u32[]{:S(2)}) collective-permute-start(bf16[2048,128]{1,0:T(8,128)(2,1)S(1)} %bitcast.9), channel_id=1, source_target_pairs={{0,8},{8,0},{16,24},{24,16},{32,40},{40,32},{48,56},{56,48},{64,72... | collective-permute-start | bytes 1572872 | tf_op jit(solution)/shard_map/ppermute | solution.py:309
  111.9 5.6 %collective-permute-start.9 = (bf16[512,128]{1,0:T(8,128)(2,1)S(1)}, bf16[512,128]{1,0:T(8,128)(2,1)S(1)}, u32[]{:S(2)}, u32[]{:S(2)}) collective-permute-start(bf16[512,128]{1,0:T(8,128)(2,1)S(1)} %shard_map.111), channel_id=1, source_target_pairs={{0,4},{4,0},{8,12},{12,8},{16,20},{20,16},{24,28},{28,24},{32,36},... | collective-permute-start | bytes 393224 | tf_op jit(solution)/shard_map/ppermute | solution.py:331
  117.6 14.2 %copy-start = (bf16[512,128]{1,0:T(8,128)(2,1)S(1)}, bf16[512,128]{1,0:T(8,128)(2,1)}, u32[]{:S(2)}) copy-start(bf16[512,128]{1,0:T(8,128)(2,1)} %scores.1) | copy-start | bytes 393220
  117.6 14.1 %copy-start.1 = (s32[512]{0:T(512)S(1)}, s32[512]{0:T(512)}, u32[]{:S(2)}) copy-start(s32[512]{0:T(512)} %param.11) | copy-start | bytes 6148
  117.6 14.1 %copy-start.2 = (s32[512]{0:T(512)S(1)}, s32[512]{0:T(512)}, u32[]{:S(2)}) copy-start(s32[512]{0:T(512)} %param.10) | copy-start | bytes 6148

commit v13 on v8

--- a/solution.py
+++ b/solution.py
@@ -261,8 +261,9 @@
             3 * MEBI,
         )(*slots)
 
-    o3, o1, o2 = forward((3, 1, 2))
+    (o3,) = forward((3,))
     r3 = lax.ppermute(o3, "acct", DIAGONAL)
+    o1, o2 = forward((1, 2))
     r1 = lax.ppermute(o1, "acct", BESIDE)
     r2 = lax.ppermute(o2, "acct", ACROSS)
     (o0,) = forward((0,))

time: 136 us -> 135 us (level); the launches traced: 137 us -> 134 us
  starting transfers between devices: 48.7 us -> 46.3 us
    ppermute x1, starting transfers between devices: 8.39 us -> 1.92 us  [per_device(): rest = lax.ppermute(half, 'acct', SECOND)]
    ppermute x1, starting transfers between devices: 2.45 us -> 7.83 us  [per_device(): g1 = lax.ppermute(g0, 'acct', BESIDE)]
    ppermute x1, waiting for transfers between devices: 4.02 us -> 7.14 us  [per_device(): g1 = lax.ppermute(g0, 'acct', BESIDE)]
    ppermute x1, waiting for transfers between devices: 9.69 us -> 7.37 us  [per_device(): half = near.astype(f32) + lax.ppermute(near, 'acct', FIRST).astype(f32)]
    all_to_all x1, blocking collectives: 13.2 us -> 15.5 us  [per_device(): lax.all_to_all(spread, 'acct', 0, 0, tiled=True, axis_index_groups=QUADS)]
    ppermute x1, starting transfers between devices: 3.72 us -> 1.92 us  [per_device(): g2 = lax.ppermute(g0, 'acct', ACROSS)]
    all_to_all x1, blocking collectives: 18.1 us -> 16.4 us  [per_device(): types = lax.all_to_all(types, 'attr', 0, 0, tiled=True)]
    ppermute x1, starting transfers between devices: 7.24 us -> 8.65 us  [per_device(): r3 = lax.ppermute(o3, 'acct', DIAGONAL)]
  transfers between devices with their start and end apart: 10 -> 10, of which waited for: 9 -> 8; matrix products, arithmetic and copies ran while one was open for 0% -> 0% of each run, Pallas kernels for 3% -> 4%
where the time goes in v13:
time: 135 us; the launch traced here: 134 us
  starting transfers between devices  46.3 us (34%)
  blocking collectives  41.7 us (31%)
  waiting for transfers between devices  32.5 us (24%)
  Pallas kernels  10.9 us (8%)
  between operations  1.53 us (1%)
    all_to_all x1, blocking collectives, per_device(): types = lax.all_to_all(types, 'attr', 0, 0, tiled=True)  16.4 us
    all_to_all x1, blocking collectives, per_device(): lax.all_to_all(spread, 'acct', 0, 0, tiled=True, axis_index_groups=QUADS)  15.5 us
    all_to_all x1, blocking collectives, per_device(): lax.all_to_all(line, 'acct', 0, 0, tiled=True, axis_index_groups=QUADS)  9.79 us
    ppermute x1, starting transfers between devices, per_device(): payload1 = lax.ppermute(payload, 'acct', SWAP)  8.79 us
    ppermute x1, starting transfers between devices, per_device(): r3 = lax.ppermute(o3, 'acct', DIAGONAL)  8.65 us
    ppermute x1, starting transfers between devices, per_device(): g1 = lax.ppermute(g0, 'acct', BESIDE)  7.83 us
    ppermute x1, waiting for transfers between devices, per_device(): rest = lax.ppermute(half, 'acct', SECOND)  7.79 us
    ppermute x1, waiting for transfers between devices, per_device(): half = near.astype(f32) + lax.ppermute(near, 'acct', FIRST).astype(f32)  7.37 us
  transfers between devices with their start and end apart: 10, of which 8 were waited for; matrix products, arithmetic and copies ran while one was open for 0% of the time, Pallas kernels for 4%

profile of v13, /device:TPU:1, one launch (start us, length us, event | category | flops | bytes accessed | tf_op | source)
XLA Modules:
  0.0 134.1 jit_solution(267566411937272891)
XLA Ops:
  1.3 0.0 copy-start.3
  1.3 0.0 copy-start.4
  1.3 0.0 copy-start.5
  1.3 0.6 copy-done.3
  1.9 0.0 copy-done.4
  2.0 0.0 copy-done.5
  2.0 1.7 %shard_map.104.sent0.refs_2_.refs_1_ = bf16[2576,128]{1,0:T(8,128)(2,1)S(1)} custom-call(s32[1]{0:T(128)} %bitcast.me, s32[1,128]{1,0:T(1,128)S(1)} %copy-done.3, s32[1,16]{1,0:T(1,128)S(1)} %copy-done.4, s32[1,16]{1,0:T(1,128)S(1)} %copy-done.5, s32[1,1]{1,0:T(1,128)S(6)} %copy.11.count, bf16[2048,128]{1,0:T(8,128)(2,1)} %bitcast.15, ...), custom_call_target="tpu_custom_call" | custom-call | flops 65536 | bytes 1048576 | tf_op jit(solution)/shard_map/pallas_call | solution.py:227
  3.7 8.8 %collective-permute-start = (bf16[2576,128]{1,0:T(8,128)(2,1)S(1)}, bf16[2576,128]{1,0:T(8,128)(2,1)S(1)}, u32[]{:S(2)}, u32[]{:S(2)}) collective-permute-start(bf16[2576,128]{1,0:T(8,128)(2,1)S(1)} %shard_map.104.sent0.refs_2_.refs_1_), channel_id=1, source_target_pairs={{0,4},{4,0},{8,12},{12,8},{16,20},{20,16},{24,28},{28,24},{32,36},... | collective-permute-start | bytes 1978376 | tf_op jit(solution)/shard_map/ppermute | solution.py:249
  12.5 1.7 %collective-permute-done.sent1.refs_3_.refs_1_ = bf16[2576,128]{1,0:T(8,128)(2,1)S(1)} collective-permute-done((bf16[2576,128]{1,0:T(8,128)(2,1)S(1)}, bf16[2576,128]{1,0:T(8,128)(2,1)S(1)}, u32[]{:S(2)}, u32[]{:S(2)}) %collective-permute-start) | collective-permute-done | bytes 659488 | tf_op jit(solution)/shard_map/ppermute | solution.py:249
  14.2 1.1 shard_map.107
  15.3 8.6 %collective-permute-start.3 = (bf16[16,128,128]{2,1,0:T(8,128)(2,1)S(1)}, bf16[16,128,128]{2,1,0:T(8,128)(2,1)S(1)}, u32[]{:S(2)}, u32[]{:S(2)}) collective-permute-start(bf16[16,128,128]{2,1,0:T(8,128)(2,1)S(1)} %shard_map.107), channel_id=1, source_target_pairs={{0,40},{8,32},{16,56},{24,48},{32,8},{40,0},{48,24},{56,16},{64,10... | collective-permute-start | bytes 1572872 | tf_op jit(solution)/shard_map/ppermute | solution.py:265
  24.0 1.5 %shard_map.106 = (bf16[16,128,128]{2,1,0:T(8,128)(2,1)S(1)}, bf16[16,128,128]{2,1,0:T(8,128)(2,1)S(1)}) custom-call(s32[1,128]{1,0:T(1,128)S(1)} %slice_convert_fusion.1.tail0.refs_0_, s32[1,128]{1,0:T(1,128)S(1)} %slice_convert_fusion.tail1.refs_1_.refs_0_, bf16[2576,128]{1,0:T(8,128)(2,1)S(1)} %shard_map.104.sent0.refs_2_.refs_1_, ...), custom_call_target="tpu_custom_call" | custom-call | flops 41943040 | bytes 3145728 | tf_op jit(solution)/shard_map/pallas_call | solution.py:255
  25.5 2.9 %collective-permute-start.2 = (bf16[16,128,128]{2,1,0:T(8,128)(2,1)S(1)}, bf16[16,128,128]{2,1,0:T(8,128)(2,1)S(1)}, u32[]{:S(2)}, u32[]{:S(2)}) collective-permute-start(bf16[16,128,128]{2,1,0:T(8,128)(2,1)S(1)} %get-tuple-element.7), channel_id=1, source_target_pairs={{0,8},{8,0},{16,24},{24,16},{32,40},{40,32},{48,56},{56,48},{64,72... | collective-permute-start | bytes 1572872 | tf_op jit(solution)/shard_map/ppermute | solution.py:268
  28.4 1.9 %collective-permute-start.1 = (bf16[16,128,128]{2,1,0:T(8,128)(2,1)S(1)}, bf16[16,128,128]{2,1,0:T(8,128)(2,1)S(1)}, u32[]{:S(2)}, u32[]{:S(2)}) collective-permute-start(bf16[16,128,128]{2,1,0:T(8,128)(2,1)S(1)} %get-tuple-element.6), channel_id=1, source_target_pairs={{0,32},{8,40},{16,48},{24,56},{32,0},{40,8},{48,16},{56,24},{64,96... | collective-permute-start | bytes 1572872 | tf_op jit(solution)/shard_map/ppermute | solution.py:267
  30.4 1.6 %shard_map.105 = bf16[16,128,128]{2,1,0:T(8,128)(2,1)S(1)} custom-call(s32[1,128]{1,0:T(1,128)S(1)} %slice_convert_fusion.1.tail0.refs_0_, s32[1,128]{1,0:T(1,128)S(1)} %slice_convert_fusion.tail1.refs_1_.refs_0_, bf16[2576,128]{1,0:T(8,128)(2,1)S(1)} %shard_map.104.sent0.refs_2_.refs_1_, bf16[2576,128]{1,0:T(8,128)(2,1)S(1)} %collective-permute-done.sent1.refs_3_.refs_1_), custom_call_target="tpu_custom_call" | custom-call | flops 41943040 | bytes 3145728 | tf_op jit(solution)/shard_map/pallas_call | solution.py:255
  32.0 0.0 collective-permute-done.3
  32.0 4.6 %collective-permute-done.2 = bf16[16,128,128]{2,1,0:T(8,128)(2,1)S(1)} collective-permute-done((bf16[16,128,128]{2,1,0:T(8,128)(2,1)S(1)}, bf16[16,128,128]{2,1,0:T(8,128)(2,1)S(1)}, u32[]{:S(2)}, u32[]{:S(2)}) %collective-permute-start.2) | collective-permute-done | bytes 524320 | tf_op jit(solution)/shard_map/ppermute | solution.py:268
  36.6 2.9 %collective-permute-done.1 = bf16[16,128,128]{2,1,0:T(8,128)(2,1)S(1)} collective-permute-done((bf16[16,128,128]{2,1,0:T(8,128)(2,1)S(1)}, bf16[16,128,128]{2,1,0:T(8,128)(2,1)S(1)}, u32[]{:S(2)}, u32[]{:S(2)}) %collective-permute-start.1) | collective-permute-done | bytes 524320 | tf_op jit(solution)/shard_map/ppermute | solution.py:267
  39.6 0.3 add_convert_fusion
  39.9 0.0 copy-start.6
  39.9 9.8 %all_to_all.15.parts = bf16[4,4,128,128]{3,2,1,0:T(8,128)(2,1)S(1)} all-to-all(bf16[4,4,128,128]{3,2,1,0:T(8,128)(2,1)S(1)} %bitcast.14), channel_id=1, replica_groups={{0,64,24,88},{128,192,152,216},{256,320,280,344},{384,448,408,472},{32,..., dimensions={0} | all-to-all | bytes 1048576 | tf_op jit(solution)/shard_map/all_to_all | solution.py:272
  49.7 0.0 copy-done.6
  49.7 0.1 shard_map.108
  49.8 6.0 %collective-permute-start.4 = (bf16[528,128]{1,0:T(8,128)(2,1)S(1)}, bf16[528,128]{1,0:T(8,128)(2,1)S(1)}, u32[]{:S(2)}, u32[]{:S(2)}) collective-permute-start(bf16[528,128]{1,0:T(8,128)(2,1)S(1)} %shard_map.108), channel_id=1, source_target_pairs={{0,128},{8,136},{16,144},{24,152},{32,160},{40,168},{48,176},{56,1... | collective-permute-start | bytes 405512 | tf_op jit(solution)/shard_map/ppermute | solution.py:277
  55.8 7.4 %collective-permute-done.4 = bf16[528,128]{1,0:T(8,128)(2,1)S(1)} collective-permute-done((bf16[528,128]{1,0:T(8,128)(2,1)S(1)}, bf16[528,128]{1,0:T(8,128)(2,1)S(1)}, u32[]{:S(2)}, u32[]{:S(2)}) %collective-permute-start.4) | collective-permute-done | bytes 135200 | tf_op jit(solution)/shard_map/ppermute | solution.py:277
  63.2 1.9 %collective-permute-start.5 = (bf16[528,128]{1,0:T(8,128)(2,1)S(1)}, bf16[528,128]{1,0:T(8,128)(2,1)S(1)}, u32[]{:S(2)}, u32[]{:S(2)}) collective-permute-start(bf16[528,128]{1,0:T(8,128)(2,1)S(1)} %add_convert_fusion.1.mine), channel_id=1, source_target_pairs={{0,384},{8,392},{16,400},{24,408},{32,416},{40,424},{48,432},{56,4... | collective-permute-start | bytes 405512 | tf_op jit(solution)/shard_map/ppermute | solution.py:279
  65.2 7.8 %collective-permute-done.5.other = bf16[528,128]{1,0:T(8,128)(2,1)S(1)} collective-permute-done((bf16[528,128]{1,0:T(8,128)(2,1)S(1)}, bf16[528,128]{1,0:T(8,128)(2,1)S(1)}, u32[]{:S(2)}, u32[]{:S(2)}) %collective-permute-start.5) | collective-permute-done | bytes 135200 | tf_op jit(solution)/shard_map/ppermute | solution.py:279
  73.0 0.8 shard_map.109
  73.7 15.5 %all_to_all.16 = bf16[4,512,128]{2,1,0:T(8,128)(2,1)S(1)} all-to-all(bf16[4,512,128]{2,1,0:T(8,128)(2,1)S(1)} %get-tuple-element.8), channel_id=1, replica_groups={{0,64,24,88},{128,192,152,216},{256,320,280,344},{384,448,408,472},{32,..., dimensions={0} | all-to-all | bytes 1048576 | tf_op jit(solution)/shard_map/all_to_all | solution.py:292
  89.2 3.3 %collective-permute-start.6 = (bf16[2048,128]{1,0:T(8,128)(2,1)S(1)}, bf16[2048,128]{1,0:T(8,128)(2,1)S(1)}, u32[]{:S(2)}, u32[]{:S(2)}) collective-permute-start(bf16[2048,128]{1,0:T(8,128)(2,1)S(1)} %bitcast.7), channel_id=1, source_target_pairs={{0,40},{8,32},{16,56},{24,48},{32,8},{40,0},{48,24},{56,16},{64,10... | collective-permute-start | bytes 1572872 | tf_op jit(solution)/shard_map/ppermute | solution.py:294
  92.6 7.8 %collective-permute-start.7 = (bf16[2048,128]{1,0:T(8,128)(2,1)S(1)}, bf16[2048,128]{1,0:T(8,128)(2,1)S(1)}, u32[]{:S(2)}, u32[]{:S(2)}) collective-permute-start(bf16[2048,128]{1,0:T(8,128)(2,1)S(1)} %bitcast.8), channel_id=1, source_target_pairs={{0,32},{8,40},{16,48},{24,56},{32,0},{40,8},{48,16},{56,24},{64,96... | collective-permute-start | bytes 1572872 | tf_op jit(solution)/shard_map/ppermute | solution.py:295
  100.4 1.9 %collective-permute-start.8 = (bf16[2048,128]{1,0:T(8,128)(2,1)S(1)}, bf16[2048,128]{1,0:T(8,128)(2,1)S(1)}, u32[]{:S(2)}, u32[]{:S(2)}) collective-permute-start(bf16[2048,128]{1,0:T(8,128)(2,1)S(1)} %bitcast.9), channel_id=1, source_target_pairs={{0,8},{8,0},{16,24},{24,16},{32,40},{40,32},{48,56},{56,48},{64,72... | collective-permute-start | bytes 1572872 | tf_op jit(solution)/shard_map/ppermute | solution.py:296
  102.3 1.2 shard_map.110.refs_5_
  103.5 0.0 collective-permute-done.6.refs_2_
  103.5 7.1 %collective-permute-done.7.refs_3_ = bf16[2048,128]{1,0:T(8,128)(2,1)S(1)} collective-permute-done((bf16[2048,128]{1,0:T(8,128)(2,1)S(1)}, bf16[2048,128]{1,0:T(8,128)(2,1)S(1)}, u32[]{:S(2)}, u32[]{:S(2)}) %collective-permute-start.7) | collective-permute-done | bytes 524320 | tf_op jit(solution)/shard_map/ppermute | solution.py:295
  110.7 0.9 collective-permute-done.8.refs_4_
  111.5 1.1 shard_map.112
  112.7 3.0 %collective-permute-start.9 = (bf16[512,128]{1,0:T(8,128)(2,1)S(1)}, bf16[512,128]{1,0:T(8,128)(2,1)S(1)}, u32[]{:S(2)}, u32[]{:S(2)}) collective-permute-start(bf16[512,128]{1,0:T(8,128)(2,1)S(1)} %shard_map.112), channel_id=1, source_target_pairs={{0,4},{4,0},{8,12},{12,8},{16,20},{20,16},{24,28},{28,24},{32,36},... | collective-permute-start | bytes 393224 | tf_op jit(solution)/shard_map/ppermute | solution.py:318
  115.6 0.9 shard_map.111
  116.5 0.1 collective-permute-done.9
  116.6 0.1 broadcast_in_dim.4
  116.7 0.0 copy-start
  116.7 0.0 copy-start.1
  116.7 0.0 copy-start.2
  116.7 16.4 %all_to_all.17.types = bf16[4,512,128]{2,1,0:T(8,128)(2,1)S(1)} all-to-all(bf16[4,512,128]{2,1,0:T(8,128)(2,1)S(1)} %broadcast_in_dim.4), channel_id=1, replica_groups=mesh['acct'=128,'attr'=4] {'attr'}, dimensions={0} | all-to-all | bytes 1048576 | tf_op jit(solution)/shard_map/all_to_all | solution.py:321
  133.2 0.0 copy-done
  133.2 0.0 copy-done.2
  133.2 0.9 shard_map.113
  (5 shorter events, 0.1 us)
Async XLA Ops:
  1.3 0.7 copy-start.3
  1.3 0.7 copy-start.4
  1.3 0.7 copy-start.5
  3.7 10.5 %collective-permute-start = (bf16[2576,128]{1,0:T(8,128)(2,1)S(1)}, bf16[2576,128]{1,0:T(8,128)(2,1)S(1)}, u32[]{:S(2)}, u32[]{:S(2)}) collective-permute-start(bf16[2576,128]{1,0:T(8,128)(2,1)S(1)} %shard_map.104.sent0.refs_2_.refs_1_), channel_id=1, source_target_pairs={{0,4},{4,0},{8,12},{12,8},{16,20},{20,16},{24,28},{28,24},{32,36},... | collective-permute-start | bytes 1978376 | tf_op jit(solution)/shard_map/ppermute | solution.py:249
  15.3 16.7 %collective-permute-start.3 = (bf16[16,128,128]{2,1,0:T(8,128)(2,1)S(1)}, bf16[16,128,128]{2,1,0:T(8,128)(2,1)S(1)}, u32[]{:S(2)}, u32[]{:S(2)}) collective-permute-start(bf16[16,128,128]{2,1,0:T(8,128)(2,1)S(1)} %shard_map.107), channel_id=1, source_target_pairs={{0,40},{8,32},{16,56},{24,48},{32,8},{40,0},{48,24},{56,16},{64,10... | collective-permute-start | bytes 1572872 | tf_op jit(solution)/shard_map/ppermute | solution.py:265
  25.5 11.1 %collective-permute-start.2 = (bf16[16,128,128]{2,1,0:T(8,128)(2,1)S(1)}, bf16[16,128,128]{2,1,0:T(8,128)(2,1)S(1)}, u32[]{:S(2)}, u32[]{:S(2)}) collective-permute-start(bf16[16,128,128]{2,1,0:T(8,128)(2,1)S(1)} %get-tuple-element.7), channel_id=1, source_target_pairs={{0,8},{8,0},{16,24},{24,16},{32,40},{40,32},{48,56},{56,48},{64,72... | collective-permute-start | bytes 1572872 | tf_op jit(solution)/shard_map/ppermute | solution.py:268
  28.4 11.1 %collective-permute-start.1 = (bf16[16,128,128]{2,1,0:T(8,128)(2,1)S(1)}, bf16[16,128,128]{2,1,0:T(8,128)(2,1)S(1)}, u32[]{:S(2)}, u32[]{:S(2)}) collective-permute-start(bf16[16,128,128]{2,1,0:T(8,128)(2,1)S(1)} %get-tuple-element.6), channel_id=1, source_target_pairs={{0,32},{8,40},{16,48},{24,56},{32,0},{40,8},{48,16},{56,24},{64,96... | collective-permute-start | bytes 1572872 | tf_op jit(solution)/shard_map/ppermute | solution.py:267
  39.9 9.8 %copy-start.6 = (s32[1,128]{1,0:T(1,128)S(1)}, s32[1,128]{1,0:T(1,128)}, u32[]{:S(2)}) copy-start(s32[1,128]{1,0:T(1,128)} %degree.1) | copy-start | bytes 1540
  49.8 13.4 %collective-permute-start.4 = (bf16[528,128]{1,0:T(8,128)(2,1)S(1)}, bf16[528,128]{1,0:T(8,128)(2,1)S(1)}, u32[]{:S(2)}, u32[]{:S(2)}) collective-permute-start(bf16[528,128]{1,0:T(8,128)(2,1)S(1)} %shard_map.108), channel_id=1, source_target_pairs={{0,128},{8,136},{16,144},{24,152},{32,160},{40,168},{48,176},{56,1... | collective-permute-start | bytes 405512 | tf_op jit(solution)/shard_map/ppermute | solution.py:277
  63.2 9.7 %collective-permute-start.5 = (bf16[528,128]{1,0:T(8,128)(2,1)S(1)}, bf16[528,128]{1,0:T(8,128)(2,1)S(1)}, u32[]{:S(2)}, u32[]{:S(2)}) collective-permute-start(bf16[528,128]{1,0:T(8,128)(2,1)S(1)} %add_convert_fusion.1.mine), channel_id=1, source_target_pairs={{0,384},{8,392},{16,400},{24,408},{32,416},{40,424},{48,432},{56,4... | collective-permute-start | bytes 405512 | tf_op jit(solution)/shard_map/ppermute | solution.py:279
  89.2 14.3 %collective-permute-start.6 = (bf16[2048,128]{1,0:T(8,128)(2,1)S(1)}, bf16[2048,128]{1,0:T(8,128)(2,1)S(1)}, u32[]{:S(2)}, u32[]{:S(2)}) collective-permute-start(bf16[2048,128]{1,0:T(8,128)(2,1)S(1)} %bitcast.7), channel_id=1, source_target_pairs={{0,40},{8,32},{16,56},{24,48},{32,8},{40,0},{48,24},{56,16},{64,10... | collective-permute-start | bytes 1572872 | tf_op jit(solution)/shard_map/ppermute | solution.py:294
  92.6 18.1 %collective-permute-start.7 = (bf16[2048,128]{1,0:T(8,128)(2,1)S(1)}, bf16[2048,128]{1,0:T(8,128)(2,1)S(1)}, u32[]{:S(2)}, u32[]{:S(2)}) collective-permute-start(bf16[2048,128]{1,0:T(8,128)(2,1)S(1)} %bitcast.8), channel_id=1, source_target_pairs={{0,32},{8,40},{16,48},{24,56},{32,0},{40,8},{48,16},{56,24},{64,96... | collective-permute-start | bytes 1572872 | tf_op jit(solution)/shard_map/ppermute | solution.py:295
  100.4 11.1 %collective-permute-start.8 = (bf16[2048,128]{1,0:T(8,128)(2,1)S(1)}, bf16[2048,128]{1,0:T(8,128)(2,1)S(1)}, u32[]{:S(2)}, u32[]{:S(2)}) collective-permute-start(bf16[2048,128]{1,0:T(8,128)(2,1)S(1)} %bitcast.9), channel_id=1, source_target_pairs={{0,8},{8,0},{16,24},{24,16},{32,40},{40,32},{48,56},{56,48},{64,72... | collective-permute-start | bytes 1572872 | tf_op jit(solution)/shard_map/ppermute | solution.py:296
  112.7 3.9 %collective-permute-start.9 = (bf16[512,128]{1,0:T(8,128)(2,1)S(1)}, bf16[512,128]{1,0:T(8,128)(2,1)S(1)}, u32[]{:S(2)}, u32[]{:S(2)}) collective-permute-start(bf16[512,128]{1,0:T(8,128)(2,1)S(1)} %shard_map.112), channel_id=1, source_target_pairs={{0,4},{4,0},{8,12},{12,8},{16,20},{20,16},{24,28},{28,24},{32,36},... | collective-permute-start | bytes 393224 | tf_op jit(solution)/shard_map/ppermute | solution.py:318
  116.7 16.5 %copy-start = (bf16[512,128]{1,0:T(8,128)(2,1)S(1)}, bf16[512,128]{1,0:T(8,128)(2,1)}, u32[]{:S(2)}) copy-start(bf16[512,128]{1,0:T(8,128)(2,1)} %scores.3) | copy-start | bytes 393220
  116.7 16.5 %copy-start.1 = (s32[512]{0:T(512)S(1)}, s32[512]{0:T(512)}, u32[]{:S(2)}) copy-start(s32[512]{0:T(512)} %param.11) | copy-start | bytes 6148
  116.7 16.5 %copy-start.2 = (s32[512]{0:T(512)S(1)}, s32[512]{0:T(512)}, u32[]{:S(2)}) copy-start(s32[512]{0:T(512)} %param.10) | copy-start | bytes 6148
